TPU v7x, 128 devices: a whole 4x4x4 slice. The times are simulated.
128 devices in a mesh: row: 16 (over y, x), col: 8 (over z, core).
Axes of the slice: x: 4, y: 4, z: 4, core: 2. Of those that a mesh axis runs over, the one named last changes fastest.
Arguments:
- object_field: float32 [2, 8192, 4096], P(None, 'row', 'col'), may hold values from -6 to 6
- probe: float32 [2, 512, 512], replicated, may hold values from -6 to 6
- amplitudes: float32 [256, 512, 512], P(('row', 'col')), may hold values from 0.1 to 3
- positions: int32 [256, 2], P(('row', 'col')), may hold values from 0 to 7680, as said below
Outputs:
- new_object: float32 [2, 8192, 4096], P(None, 'row', 'col')
- new_probe: float32 [2, 512, 512], replicated
Inputs may be any that keep to these rules, and one draw needn't show every extreme that they name: `positions`: scan position j belongs to device d = j // 2 (row-major over row, col); its row offset is 512 * (d // 8) plus 0 to 511, at most 7680; its column offset is 512 * (d % 8) plus 0 to 511, at most 3584.
All inputs are finite; a program needn't handle non-finite values. Where the computation divides by a largest or mean magnitude, that divisor is 1e-20 or more.
Results may differ from a plain program's by a relative error of at most 0.00016.
Values sent between devices are 32-bit elements; how exact they have to be, the bound alone decides.
No kernel may reach another device: no remote copies, remote signals or barrier semaphores. Data moves between devices by JAX's collectives and lax.ppermute only.
A program may use at most 128 MiB of HBM per device.

v0:
```python
import functools
import math

import jax
import jax.numpy as jnp
import numpy as np
from jax import lax
from jax.experimental import pallas as pl
from jax.experimental.pallas import tpu as pltpu
from jax.sharding import PartitionSpec as P

SIDE = 512
QUARTER = 128
PIECES = 4
PIECE = SIDE // PIECES
BACK = (96, 128, 288)
CHUNKS = ((0, 96, 0, 0), (96, 128, 1, 0), (224, 144, 2, 0), (368, 144, 2, 144))
VMEM_LIMIT = 60 * 1024 * 1024
F32 = jnp.float32
BF16 = jnp.bfloat16


def split_matrices():
    k = np.arange(QUARTER)[:, None]
    n = np.arange(QUARTER)[None, :]
    parts = []
    for p in range(4):
        angle = 2.0 * np.pi * (((4 * k + p) * n) % SIDE) / SIDE
        re, im = np.cos(angle) / np.sqrt(SIDE), -np.sin(angle) / np.sqrt(SIDE)
        parts.append(np.block([[re, -im], [im, re]]))
    left = np.stack(parts)
    out = []
    for matrix in (left, np.swapaxes(left, 1, 2)):
        high = matrix.astype(np.float32).astype(jnp.bfloat16)
        low = (matrix - high.astype(np.float64)).astype(np.float32).astype(jnp.bfloat16)
        out += [np.ascontiguousarray(high), np.ascontiguousarray(low)]
    return out


def order_matrix():
    at = np.arange(SIDE)
    matrix = np.zeros((SIDE, SIDE), np.float32)
    matrix[at, (at % 4) * QUARTER + at // 4] = 1.0
    return matrix.astype(jnp.bfloat16)


def split(value):
    high = value.astype(BF16)
    return high, (value - high.astype(F32)).astype(BF16)


def mm(left, right):
    return jnp.dot(left, right, preferred_element_type=F32)


def fold(x, sign):
    (r0, i0), (r1, i1), (r2, i2), (r3, i3) = x
    sr, si, dr, di = r0 + r2, i0 + i2, r0 - r2, i0 - i2
    tr, ti, er, ei = r1 + r3, i1 + i3, r1 - r3, i1 - i3
    first = (dr + ei, di - er)
    second = (dr - ei, di + er)
    if sign > 0:
        first, second = second, first
    return [(sr + tr, si + ti), first, (sr - tr, si - ti), second]


def ready_kernel(
    where_ref, probe_ref, own_ref, amp_ref, order_ref, rolled_ref, amps_ref, peaks_ref, columns
):
    for item in range(2):
        down, along = where_ref[0, item], where_ref[1, item]
        for part in range(2):
            value = pltpu.roll(probe_ref[part], down, 0)
            rolled_ref[item, part] = pltpu.roll(value, along, 1)
        rows = amp_ref[item]
        high = rows.astype(BF16)
        rest = rows - high.astype(F32)
        middle = rest.astype(BF16)
        low = (rest - middle.astype(F32)).astype(BF16)
        order = order_ref[...]
        moved = mm(high, order) + mm(middle, order) + mm(low, order)
        for q in range(4):
            lanes = slice(q * QUARTER, (q + 1) * QUARTER)
            columns[q] = moved[:, lanes]
            for p in range(4):
                amps_ref[item, p * QUARTER : (p + 1) * QUARTER, lanes] = columns[
                    q, pl.ds(p, QUARTER, stride=4), :
                ]
    own = own_ref[0] ** 2 + own_ref[1] ** 2
    beam = probe_ref[0] ** 2 + probe_ref[1] ** 2
    peaks_ref[0] = jnp.full((8, 128), jnp.max(own), F32)
    peaks_ref[1] = jnp.full((8, 128), jnp.max(beam), F32)


def fore_kernel(
    piece, where_ref, own_ref, right_ref, below_ref, diag_ref, rolled_ref, mh_ref, ml_ref, *refs
):
    spec_ref, wrapped_ref = refs[-3:-1] if len(refs) == 4 else refs[-2:]
    lane = lax.broadcasted_iota(jnp.int32, (PIECE, SIDE), 1)
    row = lax.broadcasted_iota(jnp.int32, (PIECE, SIDE), 0) + piece * PIECE
    for item in range(2):
        down, along = where_ref[0, item], where_ref[1, item]
        above, beside = row < down, lane < along
        value = []
        for part in range(2):
            lower = jnp.where(beside, diag_ref[part], below_ref[part])
            upper = jnp.where(beside, right_ref[part], own_ref[part])
            value.append(jnp.where(above, lower, upper))
            wrapped_ref[item, part] = value[part]
        beam_r, beam_i = rolled_ref[item, 0], rolled_ref[item, 1]
        psi_r = beam_r * value[0] - beam_i * value[1]
        psi_i = beam_r * value[1] + beam_i * value[0]
        blocks = [
            (psi_r[:, q * QUARTER : (q + 1) * QUARTER], psi_i[:, q * QUARTER : (q + 1) * QUARTER])
            for q in range(4)
        ]
        for p, (br, bi) in enumerate(fold(blocks, -1)):
            hi, lo = split(jnp.concatenate([br, bi], axis=1))
            out = mm(hi, mh_ref[p]) + mm(lo, mh_ref[p]) + mm(hi, ml_ref[p])
            spec_ref[item, 0, :, p * QUARTER : (p + 1) * QUARTER] = out[:, :QUARTER]
            spec_ref[item, 1, :, p * QUARTER : (p + 1) * QUARTER] = out[:, QUARTER:]


def fore(piece, where, own, right, below, diag, rolled, matrices, held=None, after=None):
    def rows(*lead):
        zeros = (0,) * len(lead)
        return pl.BlockSpec(lead + (PIECE, SIDE), lambda i: zeros + (piece, 0))

    full = pl.BlockSpec((2, PIECE, SIDE), lambda i: (0, 0, 0))
    whole = pl.BlockSpec((4, 2 * QUARTER, 2 * QUARTER), lambda i: (0, 0, 0))
    four = pl.BlockSpec((2, 2, PIECE, SIDE), lambda i: (0, 0, 0, 0))
    shape = jax.ShapeDtypeStruct((2, 2, PIECE, SIDE), F32)
    operands = [where, own, right, below, diag, rolled, *matrices[2:]]
    in_specs = [sm(), rows(2), rows(2), full, full, rows(2, 2), whole, whole]
    out_shape, out_specs, aliases = [shape, shape], [four, four], {}
    if held is not None:
        aliases = {len(operands): 2}
        operands.append(held)
        in_specs.append(anywhere())
        out_shape.append(jax.ShapeDtypeStruct(held.shape, F32))
        out_specs.append(anywhere())
    if after is not None:
        operands.append(after)
        in_specs.append(anywhere())
    return pl.pallas_call(
        functools.partial(fore_kernel, piece),
        grid=(1,),
        out_shape=out_shape,
        in_specs=in_specs,
        out_specs=out_specs,
        input_output_aliases=aliases,
        compiler_params=params(),
        cost_estimate=pl.CostEstimate(
            flops=4 * 10**8, bytes_accessed=6 * 2**20, transcendentals=0
        ),
    )(*operands)


def update_kernel(where_ref, *refs):
    spec_refs = refs[:PIECES]
    wrapped_hbm = refs[PIECES : 2 * PIECES]
    rolled_hbm, amps_ref, lh_ref, ll_ref, mh_ref, ml_ref = refs[2 * PIECES : 2 * PIECES + 6]
    outs = refs[2 * PIECES + 6 :]
    t_own_ref, t_right_ref = outs[:2]
    count = len(BACK)
    t_below_refs, t_diag_refs = outs[2 : 2 + count], outs[2 + count : 2 + 2 * count]
    keep_ref, send_ref = outs[2 + 2 * count : 4 + 2 * count]
    wrapped, rolled_ref, high, low, grad, sems = outs[4 + 2 * count :]
    core = where_ref[2, 0]
    loads = [
        pltpu.make_async_copy(wrapped_hbm[k], wrapped.at[:, :, k * PIECE : (k + 1) * PIECE], sems.at[k])
        for k in range(PIECES)
    ] + [pltpu.make_async_copy(rolled_hbm, rolled_ref, sems.at[PIECES])]
    for load in loads:
        load.start()

    wide = 2 * QUARTER
    for item in range(2):
        for chunk in range(SIDE // wide):
            cols = slice(chunk * wide, (chunk + 1) * wide)
            blocks = [
                (spec_refs[q][item, 0, :, cols], spec_refs[q][item, 1, :, cols]) for q in range(4)
            ]
            back = []
            for p, (br, bi) in enumerate(fold(blocks, -1)):
                hi, lo = split(jnp.concatenate([br, bi], axis=0))
                out = mm(lh_ref[p], hi) + mm(lh_ref[p], lo) + mm(ll_ref[p], hi)
                sr, si = out[:QUARTER], out[QUARTER:]
                factor = amps_ref[item, p * QUARTER : (p + 1) * QUARTER, cols] * lax.rsqrt(
                    sr * sr + si * si + 0.25
                )
                hi, lo = split(jnp.concatenate([sr * factor, si * factor], axis=0))
                out = mm(mh_ref[p], hi) + mm(mh_ref[p], lo) + mm(ml_ref[p], hi)
                back.append((out[:QUARTER], out[QUARTER:]))
            for q, (xr, xi) in enumerate(fold(back, 1)):
                rows = slice(q * QUARTER, (q + 1) * QUARTER)
                for part, value in enumerate((xr, xi)):
                    hi, lo = split(value)
                    for half in range(2):
                        p = 2 * chunk + half
                        to = slice(p * wide + part * QUARTER, p * wide + (part + 1) * QUARTER)
                        piece = slice(half * QUARTER, (half + 1) * QUARTER)
                        high[item, rows, to] = hi[:, piece]
                        low[item, rows, to] = lo[:, piece]

    for load in loads:
        load.wait()
    for first, size, piece, inside in CHUNKS:
        at, within = slice(first, first + size), slice(inside, inside + size)
        lane = lax.broadcasted_iota(jnp.int32, (size, SIDE), 1)
        row = lax.broadcasted_iota(jnp.int32, (size, SIDE), 0) + first
        for item in range(2):
            down, along = where_ref[0, item], where_ref[1, item]
            above, beside = row < down, lane < along
            back = []
            for p in range(4):
                cols = slice(p * wide, (p + 1) * wide)
                hi, lo = high[item, at, cols], low[item, at, cols]
                out = mm(hi, lh_ref[p]) + mm(lo, lh_ref[p]) + mm(hi, ll_ref[p])
                back.append((out[:, :QUARTER], out[:, QUARTER:]))
            back = fold(back, 1)
            back_r = jnp.concatenate([b[0] for b in back], axis=1)
            back_i = jnp.concatenate([b[1] for b in back], axis=1)
            beam_r, beam_i = rolled_ref[item, 0, at, :], rolled_ref[item, 1, at, :]
            patch_r, patch_i = wrapped[item, 0, at, :], wrapped[item, 1, at, :]
            diff_r = back_r - (beam_r * patch_r - beam_i * patch_i)
            diff_i = back_i - (beam_r * patch_i + beam_i * patch_r)
            term = (beam_r * diff_r + beam_i * diff_i, beam_r * diff_i - beam_i * diff_r)
            grad[item, 0, at, :] = patch_r * diff_r + patch_i * diff_i
            grad[item, 1, at, :] = patch_r * diff_i - patch_i * diff_r
            for part in range(2):
                zero = jnp.zeros_like(term[part])
                upper = jnp.where(above, zero, term[part])
                lower = jnp.where(above, term[part], zero)
                four = (
                    (t_own_ref, (part, at), jnp.where(beside, zero, upper)),
                    (t_right_ref, (part, at), jnp.where(beside, upper, zero)),
                    (t_below_refs[piece], (part, within), jnp.where(beside, zero, lower)),
                    (t_diag_refs[piece], (part, within), jnp.where(beside, lower, zero)),
                )
                for ref, index, value in four:
                    if item == 0:
                        ref[index] = value
                    else:
                        ref[index] += value
    whole = []
    for part in range(2):
        total = None
        for item in range(2):
            down, along = where_ref[0, item], where_ref[1, item]
            value = pltpu.roll(grad[item, part], (SIDE - down) % SIDE, 0)
            value = pltpu.roll(value, (SIDE - along) % SIDE, 1)
            total = value if total is None else total + value
        whole.append(total)
    keep_ref[...] = jnp.where(core == 0, whole[0], whole[1])
    send_ref[...] = jnp.where(core == 0, whole[1], whole[0])


def vm():
    return pl.BlockSpec(memory_space=pltpu.VMEM)


def sm():
    return pl.BlockSpec(memory_space=pltpu.SMEM)


def anywhere():
    return pl.BlockSpec(memory_space=pl.ANY)


def params():
    return pltpu.CompilerParams(vmem_limit_bytes=VMEM_LIMIT)


def ready(where, probe, own, amplitudes):
    return pl.pallas_call(
        ready_kernel,
        out_shape=(
            jax.ShapeDtypeStruct((2, 2, SIDE, SIDE), F32),
            jax.ShapeDtypeStruct((2, SIDE, SIDE), F32),
            jax.ShapeDtypeStruct((2, 8, 128), F32),
        ),
        in_specs=[sm()] + [vm()] * 4,
        out_specs=(vm(), vm(), vm()),
        scratch_shapes=[pltpu.VMEM((4, SIDE, QUARTER), F32)],
        compiler_params=params(),
        cost_estimate=pl.CostEstimate(flops=4 * 10**9, bytes_accessed=14 * 2**20, transcendentals=0),
    )(where, probe, own, amplitudes, jnp.asarray(order_matrix()))


def update(where, specs, wrapped, rolled, amps, matrices):
    full = jax.ShapeDtypeStruct((2, SIDE, SIDE), F32)
    parts = tuple(jax.ShapeDtypeStruct((2, size, SIDE), F32) for size in BACK)
    plane = jax.ShapeDtypeStruct((SIDE, SIDE), F32)
    out_shape = (full, full) + parts + parts + (plane, plane)
    count = len(BACK)
    outs = pl.pallas_call(
        update_kernel,
        out_shape=out_shape,
        in_specs=[sm()] + [vm()] * PIECES + [anywhere()] * (PIECES + 1) + [vm()] * 5,
        out_specs=(vm(),) * len(out_shape),
        scratch_shapes=[
            pltpu.VMEM((2, 2, SIDE, SIDE), F32),
            pltpu.VMEM((2, 2, SIDE, SIDE), F32),
            pltpu.VMEM((2, SIDE, 2 * SIDE), BF16),
            pltpu.VMEM((2, SIDE, 2 * SIDE), BF16),
            pltpu.VMEM((2, 2, SIDE, SIDE), F32),
            pltpu.SemaphoreType.DMA((PIECES + 1,)),
        ],
        compiler_params=params(),
        cost_estimate=pl.CostEstimate(
            flops=5 * 10**9, bytes_accessed=26 * 2**20, transcendentals=2 * SIDE * SIDE
        ),
    )(where, *specs, *wrapped, rolled, amps, *matrices)
    return outs[0], outs[1], outs[2 : 2 + count], outs[2 + count : 2 + 2 * count], outs[-2], outs[-1]


def nothing_kernel(*refs):
    del refs


def tied(values, after):
    count = len(values) + len(after)
    return pl.pallas_call(
        nothing_kernel,
        out_shape=[jax.ShapeDtypeStruct(v.shape, v.dtype) for v in values],
        in_specs=[anywhere()] * count,
        out_specs=[anywhere()] * len(values),
        input_output_aliases={k: k for k in range(len(values))},
    )(*values, *after)


def first_kernel(keep_ref, came_ref, below_ref, diag_ref, half_ref, lower_ref):
    half_ref[...] = keep_ref[...] + came_ref[...]
    lower_ref[...] = below_ref[...] + diag_ref[...]


def first_sums(keep, came, below, diag):
    return pl.pallas_call(
        first_kernel,
        out_shape=[jax.ShapeDtypeStruct(keep.shape, F32), jax.ShapeDtypeStruct(below.shape, F32)],
        in_specs=[vm()] * 4,
        out_specs=[vm()] * 2,
        compiler_params=params(),
        cost_estimate=pl.CostEstimate(flops=2 * keep.size, bytes_accessed=18 * keep.size, transcendentals=0),
    )(keep, came, below, diag)


def share_kernel(peak_ref, terms_ref, start_ref, below_ref, corner_ref, *refs):
    out_ref, lower_ref = refs[-2:]
    lower_ref[...] = below_ref[...] + corner_ref[...]
    total = jnp.sum(terms_ref[...], axis=0)
    value = start_ref[...] + 0.5 * total / (peak_ref[0, 0] + 1e-06)
    out_ref[...] = jnp.broadcast_to(value, out_ref.shape)


def shared(peak, terms, start, below, corner, after):
    return pl.pallas_call(
        share_kernel,
        out_shape=[jax.ShapeDtypeStruct(terms.shape, F32), jax.ShapeDtypeStruct(below.shape, F32)],
        in_specs=[sm()] + [vm()] * 4 + [anywhere()] * len(after),
        out_specs=[vm(), vm()],
        compiler_params=params(),
        cost_estimate=pl.CostEstimate(flops=2 * terms.size, bytes_accessed=20 * terms.size, transcendentals=0),
    )(peak, terms, start, below, corner, *after)


def shifted(value, axis, steps):
    count = lax.axis_size(axis)
    first, last = (max(0, -steps), min(count, count - steps))
    return lax.ppermute(value, axis, [(source, source + steps) for source in range(first, last)])


def other_core(value):
    return lax.ppermute(value, "core", [(0, 1), (1, 0)])


def largest(value):
    spread = jnp.broadcast_to(value[:1][None], (64, 1, QUARTER))
    value = jnp.max(lax.all_to_all(spread, CHIPS, 0, 0), axis=0)
    return jnp.maximum(value, other_core(value))


def base_kernel(scale_ref, own_ref, t_own_ref, base_ref):
    base_ref[...] = own_ref[...] + scale_ref[0, 0] * t_own_ref[...]


def base(scale, own, t_own):
    return pl.pallas_call(
        base_kernel,
        out_shape=jax.ShapeDtypeStruct(own.shape, F32),
        in_specs=[sm(), vm(), vm()],
        out_specs=vm(),
        compiler_params=params(),
        cost_estimate=pl.CostEstimate(flops=2 * own.size, bytes_accessed=12 * own.size, transcendentals=0),
    )(scale, own, t_own)


def object_kernel(scale_ref, base_ref, left_ref, *refs):
    out_ref = refs[-1]
    first = 0
    for ref, size in zip(refs, BACK):
        at = slice(first, first + size)
        out_ref[:, at, :] = base_ref[:, at, :] + scale_ref[0, 0] * (left_ref[:, at, :] + ref[...])
        first += size


def finished_object(scale, start, left, above):
    return pl.pallas_call(
        object_kernel,
        out_shape=jax.ShapeDtypeStruct(start.shape, F32),
        in_specs=[sm(), vm(), vm()] + [vm()] * len(above),
        out_specs=vm(),
        compiler_params=params(),
        cost_estimate=pl.CostEstimate(flops=3 * start.size, bytes_accessed=16 * start.size, transcendentals=0),
    )(scale, start, left, *above)


def probe_kernel(core_ref, mine_ref, other_ref, out_ref):
    core = core_ref[0, 0]
    out_ref[core] = mine_ref[...]
    out_ref[1 - core] = other_ref[...]


def joined(core, mine, other):
    return pl.pallas_call(
        probe_kernel,
        out_shape=jax.ShapeDtypeStruct((2, SIDE, SIDE), F32),
        in_specs=[sm(), vm(), vm()],
        out_specs=vm(),
        compiler_params=params(),
        cost_estimate=pl.CostEstimate(flops=0, bytes_accessed=16 * SIDE * SIDE, transcendentals=0),
    )(core, mine, other)


def on_device(object_field, probe, amplitudes, positions):
    row, col, core = lax.axis_index(ROW), lax.axis_index(COL), lax.axis_index("core")
    where = jnp.stack(
        [positions[:, 0] - row * SIDE, positions[:, 1] - col * SIDE, jnp.stack([core, row]).astype(jnp.int32)]
    )
    matrices = [jnp.asarray(m) for m in split_matrices()]
    pieces = [object_field[:, k * PIECE : (k + 1) * PIECE] for k in range(PIECES)]
    below, diag, specs, wrapped = [None] * 4, [None] * 4, [None] * 4, [None] * 4
    below[0] = shifted(pieces[0], ROW, -1)
    below[1] = shifted(pieces[1], ROW, -1)
    right = shifted(object_field, COL, -1)
    rolled, amps, peaks = ready(where, probe, object_field, amplitudes)
    scale = 0.9 / (peaks[1, :1, :1] + 1e-06)
    below[0], pieces[2] = tied((below[0], pieces[2]), (rolled,))
    diag[0] = shifted(below[0], COL, -1)
    below[2] = shifted(pieces[2], ROW, -1)
    object_peak = largest(peaks[0])
    below[1], pieces[3] = tied((below[1], pieces[3]), (pieces[2], object_peak))
    diag[1] = shifted(below[1], COL, -1)
    below[3] = shifted(pieces[3], ROW, -1)
    specs[0], wrapped[0], below[2] = fore(
        0, where, object_field, right, below[0], diag[0], rolled, matrices, held=below[2]
    )
    diag[2] = shifted(below[2], COL, -1)
    diag[3] = shifted(below[3], COL, -1)
    for k in range(1, PIECES):
        specs[k], wrapped[k] = fore(
            k, where, object_field, right, below[k], diag[k], rolled, matrices
        )
    t_own, t_right, t_below, t_diag, keep, send = update(where, specs, wrapped, rolled, amps, matrices)

    came = other_core(send)
    corner = [shifted(t_diag[0], COL, 1)]
    half, lower = first_sums(keep, came, t_below[0], corner[0])
    share = SIDE // 64
    terms = lax.all_to_all(half.reshape(64, share, SIDE), CHIPS, 0, 0)
    from_above = [shifted(lower, ROW, 1)]
    later = tied((t_diag[1], t_diag[2]), (half,))
    corner += [shifted(t, COL, 1) for t in later]
    from_above.append(shifted(t_below[1] + corner[1], ROW, 1))
    at = lax.axis_index(CHIPS) * share
    start = lax.dynamic_slice(probe, (core, at, jnp.zeros_like(at)), (1, share, SIDE))[0]
    shares, lower = shared(object_peak[:, :1], terms, start, t_below[2], corner[2], from_above)
    mine = lax.all_to_all(shares, CHIPS, 0, 0).reshape(SIDE, SIDE)
    from_above.append(shifted(lower, ROW, 1))
    (t_right,) = tied((t_right,), (shares,))
    from_left = shifted(t_right, COL, 1)
    begun = base(scale, object_field, t_own)
    (mine,) = tied((mine,), (from_above[2], from_left, begun))
    new_probe = joined(core.astype(jnp.int32).reshape(1, 1), mine, other_core(mine))
    new_object = finished_object(scale, begun, from_left, from_above)
    return (new_object, new_probe)


CHIPS = ("y", "x", "z")
ROW = ("y", "x")
COL = ("z", "core")


def solution(mesh):
    chips = jax.sharding.Mesh(mesh.devices.reshape(4, 4, 4, 2), ROW + COL)
    in_specs = (P(None, ROW, COL), P(), P(ROW + COL, None, None), P(ROW + COL, None))
    out_specs = (P(None, ROW, COL), P())
    return jax.shard_map(
        on_device, mesh=chips, in_specs=in_specs, out_specs=out_specs, check_vma=False
    )
```

profile of v0, /device:TPU:33, one launch (start us, length us, event | category | flops | bytes accessed | tf_op | source)
XLA Modules:
  0.0 250.6 jit_solution(15230284646024664165)
XLA Ops:
  0.6 2.6 %collective-permute-start = (f32[2,512,512]{2,1,0:T(8,128)}, f32[2,512,512]{2,1,0:T(8,128)S(1)}, u32[]{:S(2)}, u32[]{:S(2)}) collective-permute-start(f32[2,512,512]{2,1,0:T(8,128)} %own_ref.11), channel_id=1, source_target_pairs={{1,0},{2,1},{3,2},{4,3},{5,4},{6,5},{7,6},{9,8},{10,9},{11,10},{12... | collective-permute-start | bytes 6291464 | tf_op jit(solution)/shard_map/ppermute | solution.py:371
  3.2 2.9 %fusion = (f32[2,128,512]{2,1,0:T(8,128)}, f32[2,128,512]{2,1,0:T(8,128)}, f32[2,128,512]{2,1,0:T(8,128)}, f32[2,128,512]{2,1,0:T(8,128)}) fusion(f32[2,512,512]{2,1,0:T(8,128)} %own_ref.11), kind=kLoop, calls=%fused_computation.7 | loop fusion | bytes 4194304 | tf_op jit(solution)/shard_map/slice | solution.py:442
  6.2 1.3 collective-permute-start.1
  7.5 1.3 collective-permute-start.4
  9.6 9.3 %shard_map.104 = (f32[2,2,512,512]{3,2,1,0:T(8,128)}, f32[2,512,512]{2,1,0:T(8,128)}, f32[2,8,128]{2,1,0:T(8,128)}) custom-call(s32[3,2]{1,0:T(4,128)} %pad_add_fusion.where_ref, f32[2,512,512]{2,1,0:T(8,128)} %probe_ref.1, f32[2,512,512]{2,1,0:T(8,128)} %own_ref.11, f32[2,512,512]{2,1,0:T(8,128)} %amp_ref.1, bf16[512,512]{1,0:T(8,128)(2,1)} %constant.49.clone.order_ref), custom_call_target="tpu_custom_call" | custom-call | flops 4000000000 | bytes 14680064 | tf_op jit(solution)/shard_map/pallas_call | solution.py:276
  19.7 20.6 %all_to_all.15 = f32[64,1,128]{2,1,0:T(1,128)S(1)} all-to-all(f32[64,1,128]{2,1,0:T(1,128)S(1)} %broadcast_in_dim.9), channel_id=1, replica_groups=mesh['y'=4,'x'=4,'z'=4,'core'=2] {'y','x','z'}, dimensions={0} | all-to-all | bytes 65536 | tf_op jit(solution)/shard_map/all_to_all | solution.py:380
  40.3 1.9 collective-permute-start.5
  42.2 0.8 collective-permute-done.5
  44.3 0.8 copy-done.7
  45.1 1.3 collective-permute-start.8
  46.4 2.2 collective-permute-start.2
  48.6 1.3 collective-permute-start.3
  49.9 3.2 %collective-permute-start.6 = (f32[2,128,512]{2,1,0:T(8,128)}, f32[2,128,512]{2,1,0:T(8,128)S(1)}, u32[]{:S(2)}, u32[]{:S(2)}) collective-permute-start(f32[2,128,512]{2,1,0:T(8,128)} %get-tuple-element.39.below_ref), channel_id=1, source_target_pairs={{1,0},{2,1},{3,2},{4,3},{5,4},{6,5},{7,6},{9,8},{10,9},{11,10},{12... | collective-permute-start | bytes 1572872 | tf_op jit(solution)/shard_map/ppermute | solution.py:371
  53.1 7.3 %collective-permute-done.8.below_ref = f32[2,128,512]{2,1,0:T(8,128)S(1)} collective-permute-done((f32[2,128,512]{2,1,0:T(8,128)}, f32[2,128,512]{2,1,0:T(8,128)S(1)}, u32[]{:S(2)}, u32[]{:S(2)}) %collective-permute-start.8) | collective-permute-done | bytes 524320 | tf_op jit(solution)/shard_map/ppermute | solution.py:371
  60.4 3.8 %collective-permute-start.9 = (f32[2,128,512]{2,1,0:T(8,128)S(1)}, f32[2,128,512]{2,1,0:T(8,128)}, u32[]{:S(2)}, u32[]{:S(2)}) collective-permute-start(f32[2,128,512]{2,1,0:T(8,128)S(1)} %collective-permute-done.8.below_ref), channel_id=1, source_target_pairs={{1,0},{2,1},{3,2},{4,3},{5,4},{6,5},{7,6},{9,8},{10,9},{11,10},{12... | collective-permute-start | bytes 1572872 | tf_op jit(solution)/shard_map/ppermute | solution.py:371
  64.2 7.4 %collective-permute-done.3.refs_0_ = f32[2,128,512]{2,1,0:T(8,128)S(1)} collective-permute-done((f32[2,128,512]{2,1,0:T(8,128)}, f32[2,128,512]{2,1,0:T(8,128)S(1)}, u32[]{:S(2)}, u32[]{:S(2)}) %collective-permute-start.3) | collective-permute-done | bytes 524320 | tf_op jit(solution)/shard_map/ppermute | solution.py:371
  71.7 0.8 copy-done.6
  72.5 1.3 copy-done
  73.8 4.0 %shard_map.106 = (f32[2,2,128,512]{3,2,1,0:T(8,128)}, f32[2,2,128,512]{3,2,1,0:T(8,128)}, f32[2,128,512]{2,1,0:T(8,128)}) custom-call(s32[3,2]{1,0:T(4,128)} %pad_add_fusion.where_ref, f32[2,512,512]{2,1,0:T(8,128)} %own_ref.11, f32[2,512,512]{2,1,0:T(8,128)} %copy-done, ...), custom_call_target="tpu_custom_call", output_to_operand_aliasing={{2}: (8, {})} | custom-call | flops 400000000 | bytes 6291456 | tf_op jit(solution)/shard_map/pallas_call | solution.py:145
  77.8 3.2 %collective-permute-start.7 = (f32[2,128,512]{2,1,0:T(8,128)}, f32[2,128,512]{2,1,0:T(8,128)S(1)}, u32[]{:S(2)}, u32[]{:S(2)}) collective-permute-start(f32[2,128,512]{2,1,0:T(8,128)} %get-tuple-element.41.below_ref), channel_id=1, source_target_pairs={{1,0},{2,1},{3,2},{4,3},{5,4},{6,5},{7,6},{9,8},{10,9},{11,10},{12... | collective-permute-start | bytes 1572872 | tf_op jit(solution)/shard_map/ppermute | solution.py:371
  81.8 4.1 %shard_map.108 = (f32[2,2,128,512]{3,2,1,0:T(8,128)}, f32[2,2,128,512]{3,2,1,0:T(8,128)}) custom-call(s32[3,2]{1,0:T(4,128)} %pad_add_fusion.where_ref, f32[2,512,512]{2,1,0:T(8,128)} %own_ref.11, f32[2,512,512]{2,1,0:T(8,128)} %copy-done, f32[2,128,512]{2,1,0:T(8,128)} %get-tuple-element.39.below_ref, f32[2,128,512]{2,1,0:T(8,128)} %copy-done.14, ...), custom_call_target="tpu_custom_call" | custom-call | flops 400000000 | bytes 6291456 | tf_op jit(solution)/shard_map/pallas_call | solution.py:145
  86.0 4.0 %shard_map.110 = (f32[2,2,128,512]{3,2,1,0:T(8,128)}, f32[2,2,128,512]{3,2,1,0:T(8,128)}) custom-call(s32[3,2]{1,0:T(4,128)} %pad_add_fusion.where_ref, f32[2,512,512]{2,1,0:T(8,128)} %own_ref.11, f32[2,512,512]{2,1,0:T(8,128)} %copy-done, f32[2,128,512]{2,1,0:T(8,128)} %copy-done.13, f32[2,128,512]{2,1,0:T(8,128)} %collective-permute-done.9.diag_ref, ...), custom_call_target="tpu_custom_call" | custom-call | flops 400000000 | bytes 6291456 | tf_op jit(solution)/shard_map/pallas_call | solution.py:145
  90.8 4.0 %shard_map.109 = (f32[2,2,128,512]{3,2,1,0:T(8,128)}, f32[2,2,128,512]{3,2,1,0:T(8,128)}) custom-call(s32[3,2]{1,0:T(4,128)} %pad_add_fusion.where_ref, f32[2,512,512]{2,1,0:T(8,128)} %own_ref.11, f32[2,512,512]{2,1,0:T(8,128)} %copy-done, f32[2,128,512]{2,1,0:T(8,128)} %get-tuple-element.41.below_ref, f32[2,128,512]{2,1,0:T(8,128)} %copy-done.16, ...), custom_call_target="tpu_custom_call" | custom-call | flops 400000000 | bytes 6291456 | tf_op jit(solution)/shard_map/pallas_call | solution.py:145
  94.8 18.1 %shard_map.111 = (f32[2,512,512]{2,1,0:T(8,128)}, f32[2,512,512]{2,1,0:T(8,128)}, f32[2,96,512]{2,1,0:T(8,128)}, f32[2,128,512]{2,1,0:T(8,128)}, f32[2,288,512]{...) custom-call(s32[3,2]{1,0:T(4,128)} %pad_add_fusion.where_ref, ...), custom_call_target="tpu_custom_call" | custom-call | flops 5000000000 | bytes 27262976 | tf_op jit(solution)/shard_map/pallas_call | solution.py:297
  113.4 2.1 collective-permute-start.11
  115.5 5.0 %collective-permute-done.11.diag_ref = f32[2,96,512]{2,1,0:T(8,128)S(1)} collective-permute-done((f32[2,96,512]{2,1,0:T(8,128)}, f32[2,96,512]{2,1,0:T(8,128)S(1)}, u32[]{:S(2)}, u32[]{:S(2)}) %collective-permute-start.11) | collective-permute-done | bytes 393248 | tf_op jit(solution)/shard_map/ppermute | solution.py:371
  121.6 3.0 %shard_map.113 = (f32[512,512]{1,0:T(8,128)}, f32[2,96,512]{2,1,0:T(8,128)}) custom-call(f32[512,512]{1,0:T(8,128)} %get-tuple-element.52.keep_ref, f32[512,512]{1,0:T(8,128)} %copy-done.11, f32[2,96,512]{2,1,0:T(8,128)} %get-tuple-element.54.below_ref, f32[2,96,512]{2,1,0:T(8,128)} %copy-done.17), custom_call_target="tpu_custom_call" | custom-call | flops 524288 | bytes 4718592 | tf_op jit(solution)/shard_map/pallas_call | solution.py:339
  124.7 4.4 %collective-permute-start.12 = (f32[2,288,512]{2,1,0:T(8,128)}, f32[2,288,512]{2,1,0:T(8,128)S(1)}, u32[]{:S(2)}, u32[]{:S(2)}) collective-permute-start(f32[2,288,512]{2,1,0:T(8,128)} %get-tuple-element.60), channel_id=1, source_target_pairs={{0,1},{1,2},{2,3},{3,4},{4,5},{5,6},{6,7},{8,9},{9,10},{10,11},{11... | collective-permute-start | bytes 3538952 | tf_op jit(solution)/shard_map/ppermute | solution.py:371
  129.1 1.9 collective-permute-start.14
  131.0 8.1 %all-to-all-start.1 = ((f32[64,8,512]{2,1,0:T(8,128)}), f32[64,8,512]{2,1,0:T(8,128)S(1)}, u32[]{:S(2)}, u32[]{:S(2)}) async-start(f32[64,8,512]{2,1,0:T(8,128)} %bitcast.7), calls=%async_computation.1 | async-start | bytes 2097152 | tf_op jit(solution)/shard_map/all_to_all | solution.py:471
  139.1 19.9 %collective-permute-done.14 = f32[2,128,512]{2,1,0:T(8,128)S(1)} collective-permute-done((f32[2,128,512]{2,1,0:T(8,128)}, f32[2,128,512]{2,1,0:T(8,128)S(1)}, u32[]{:S(2)}, u32[]{:S(2)}) %collective-permute-start.14) | collective-permute-done | bytes 524320 | tf_op jit(solution)/shard_map/ppermute | solution.py:371
  159.0 0.9 add.32
  159.9 2.2 collective-permute-start.15
  162.1 2.2 collective-permute-start.13
  164.4 1.3 dynamic-slice_bitcast_fusion.start_ref
  165.7 14.1 %collective-permute-done.13.refs_0_ = f32[2,96,512]{2,1,0:T(8,128)S(1)} collective-permute-done((f32[2,96,512]{2,1,0:T(8,128)}, f32[2,96,512]{2,1,0:T(8,128)S(1)}, u32[]{:S(2)}, u32[]{:S(2)}) %collective-permute-start.13) | collective-permute-done | bytes 393248 | tf_op jit(solution)/shard_map/ppermute | solution.py:371
  181.4 4.1 %shard_map.115 = (f32[64,8,512]{2,1,0:T(8,128)}, f32[2,288,512]{2,1,0:T(8,128)}) custom-call(f32[1,1]{1,0:T(1,128)} %bitcast.20, f32[64,8,512]{2,1,0:T(8,128)} %copy-done.3, f32[8,512]{1,0:T(8,128)} %dynamic-slice_bitcast_fusion.start_ref, f32[2,288,512]{2,1,0:T(8,128)} %get-tuple-element.57.below_ref, f32[2,288,512]{2,1,0:T(8,128)} %copy-done.9, ...), custom_call_target="tpu_custom_call" | custom-call | flops 524288 | bytes 5242880 | tf_op jit(solution)/shard_map/pallas_call | solution.py:358
  185.5 6.2 %collective-permute-start.16 = (f32[2,512,512]{2,1,0:T(8,128)}, f32[2,512,512]{2,1,0:T(8,128)S(1)}, u32[]{:S(2)}, u32[]{:S(2)}) collective-permute-start(f32[2,512,512]{2,1,0:T(8,128)} %shard_map.116), channel_id=1, source_target_pairs={{0,1},{1,2},{2,3},{3,4},{4,5},{5,6},{6,7},{8,9},{9,10},{10,11},{11... | collective-permute-start | bytes 6291464 | tf_op jit(solution)/shard_map/ppermute | solution.py:371
  191.7 5.0 %collective-permute-start.17 = (f32[2,288,512]{2,1,0:T(8,128)}, f32[2,288,512]{2,1,0:T(8,128)}, u32[]{:S(2)}, u32[]{:S(2)}) collective-permute-start(f32[2,288,512]{2,1,0:T(8,128)} %get-tuple-element.65), channel_id=1, source_target_pairs={{0,8},{8,16},{16,24},{24,32},{32,40},{40,48},{48,56},{56,64},{64,7... | collective-permute-start | bytes 3538952 | tf_op jit(solution)/shard_map/ppermute | solution.py:371
  196.7 7.9 %all-to-all-start.2 = ((f32[64,8,512]{2,1,0:T(8,128)}), f32[64,8,512]{2,1,0:T(8,128)S(1)}, u32[]{:S(2)}, u32[]{:S(2)}) async-start(f32[64,8,512]{2,1,0:T(8,128)} %get-tuple-element.64.refs_1_), calls=%async_computation.2 | async-start | bytes 2097152 | tf_op jit(solution)/shard_map/all_to_all | solution.py:479
  204.6 1.2 slice.32
  206.5 3.8 %shard_map.112.base_ref.refs_3_ = f32[2,512,512]{2,1,0:T(8,128)} custom-call(f32[1,1]{1,0:T(1,128)} %bitcast.3.scale_ref, f32[2,512,512]{2,1,0:T(8,128)} %own_ref.11, f32[2,512,512]{2,1,0:T(8,128)} %get-tuple-element.50.t_own_ref), custom_call_target="tpu_custom_call" | custom-call | flops 1048576 | bytes 6291456 | tf_op jit(solution)/shard_map/pallas_call | solution.py:389
  210.2 28.7 %all-to-all-done.2 = f32[64,8,512]{2,1,0:T(8,128)S(1)} async-done(((f32[64,8,512]{2,1,0:T(8,128)}), f32[64,8,512]{2,1,0:T(8,128)S(1)}, u32[]{:S(2)}, u32[]{:S(2)}) %all-to-all-start.2) | async-done | bytes 1048608 | tf_op jit(solution)/shard_map/all_to_all | solution.py:479
  238.9 0.9 copy-done.1
  240.6 1.5 collective-permute-start.18
  242.1 4.4 %shard_map.117 = f32[2,512,512]{2,1,0:T(8,128)} custom-call(f32[1,1]{1,0:T(1,128)} %bitcast.3.scale_ref, f32[2,512,512]{2,1,0:T(8,128)} %shard_map.112.base_ref.refs_3_, f32[2,512,512]{2,1,0:T(8,128)} %copy-done.2, f32[2,96,512]{2,1,0:T(8,128)} %copy-done.8, f32[2,128,512]{2,1,0:T(8,128)} %copy-done.4, f32[2,288,512]{2,1,0:T(8,128)} %collective-permute-done.17.refs_2_.refs_1_), custom_call_target="tpu_custom_call" | custom-call | flops 1572864 | bytes 8388608 | tf_op jit(solution)/shard_map/pallas_call | solution.py:409
  246.6 1.0 copy-done.10
  247.6 3.0 %shard_map.119 = f32[2,512,512]{2,1,0:T(8,128)} custom-call(s32[1,1]{1,0:T(1,128)} %bitcast.9.core_ref, f32[512,512]{1,0:T(8,128)} %shard_map.118.mine_ref, f32[512,512]{1,0:T(8,128)} %copy-done.10), custom_call_target="tpu_custom_call" | custom-call | bytes 4194304 | tf_op jit(solution)/shard_map/pallas_call | solution.py:426
  (60 shorter events, 8.5 us)
Async XLA Ops:
  0.6 8.2 %copy-start.18 = (s32[2,2]{1,0:T(2,128)S(1)}, s32[2,2]{1,0:T(2,128)}, u32[]{:S(2)}) copy-start(s32[2,2]{1,0:T(2,128)} %param.12) | copy-start | bytes 52
  0.6 71.0 %collective-permute-start = (f32[2,512,512]{2,1,0:T(8,128)}, f32[2,512,512]{2,1,0:T(8,128)S(1)}, u32[]{:S(2)}, u32[]{:S(2)}) collective-permute-start(f32[2,512,512]{2,1,0:T(8,128)} %own_ref.11), channel_id=1, source_target_pairs={{1,0},{2,1},{3,2},{4,3},{5,4},{6,5},{7,6},{9,8},{10,9},{11,10},{12... | collective-permute-start | bytes 6291464 | tf_op jit(solution)/shard_map/ppermute | solution.py:371
  6.2 37.3 %collective-permute-start.1 = (f32[2,128,512]{2,1,0:T(8,128)}, f32[2,128,512]{2,1,0:T(8,128)S(1)}, u32[]{:S(2)}, u32[]{:S(2)}) collective-permute-start(f32[2,128,512]{2,1,0:T(8,128)} %get-tuple-element.71), channel_id=1, source_target_pairs={{8,0},{16,8},{24,16},{32,24},{40,32},{48,40},{56,48},{64,56},{72,6... | collective-permute-start | bytes 1572872 | tf_op jit(solution)/shard_map/ppermute | solution.py:371
  7.5 36.9 %collective-permute-start.4 = (f32[2,128,512]{2,1,0:T(8,128)}, f32[2,128,512]{2,1,0:T(8,128)S(1)}, u32[]{:S(2)}, u32[]{:S(2)}) collective-permute-start(f32[2,128,512]{2,1,0:T(8,128)} %get-tuple-element.69), channel_id=1, source_target_pairs={{8,0},{16,8},{24,16},{32,24},{40,32},{48,40},{56,48},{64,56},{72,6... | collective-permute-start | bytes 1572872 | tf_op jit(solution)/shard_map/ppermute | solution.py:371
  40.3 2.8 %collective-permute-start.5 = (f32[1,128]{1,0:T(1,128)S(1)}, f32[1,128]{1,0:T(1,128)S(1)}, u32[]{:S(2)}, u32[]{:S(2)}) collective-permute-start(f32[1,128]{1,0:T(1,128)S(1)} %bitcast.23), channel_id=1, source_target_pairs={{0,1},{1,0},{2,3},{3,2},{4,5},{5,4},{6,7},{7,6},{8,9},{9,8},{10,11... | collective-permute-start | bytes 1544 | tf_op jit(solution)/shard_map/ppermute | solution.py:375
  43.5 0.8 copy-start.5
  44.3 0.8 copy-start.7
  45.1 15.3 %collective-permute-start.8 = (f32[2,128,512]{2,1,0:T(8,128)}, f32[2,128,512]{2,1,0:T(8,128)S(1)}, u32[]{:S(2)}, u32[]{:S(2)}) collective-permute-start(f32[2,128,512]{2,1,0:T(8,128)} %get-tuple-element.43), channel_id=1, source_target_pairs={{8,0},{16,8},{24,16},{32,24},{40,32},{48,40},{56,48},{64,56},{72,6... | collective-permute-start | bytes 1572872 | tf_op jit(solution)/shard_map/ppermute | solution.py:371
  46.4 17.8 %collective-permute-start.2 = (f32[2,128,512]{2,1,0:T(8,128)}, f32[2,128,512]{2,1,0:T(8,128)S(1)}, u32[]{:S(2)}, u32[]{:S(2)}) collective-permute-start(f32[2,128,512]{2,1,0:T(8,128)} %get-tuple-element.36.below_ref), channel_id=1, source_target_pairs={{1,0},{2,1},{3,2},{4,3},{5,4},{6,5},{7,6},{9,8},{10,9},{11,10},{12... | collective-permute-start | bytes 1572872 | tf_op jit(solution)/shard_map/ppermute | solution.py:371
  48.6 23.0 %collective-permute-start.3 = (f32[2,128,512]{2,1,0:T(8,128)}, f32[2,128,512]{2,1,0:T(8,128)S(1)}, u32[]{:S(2)}, u32[]{:S(2)}) collective-permute-start(f32[2,128,512]{2,1,0:T(8,128)} %get-tuple-element.37.refs_2_), channel_id=1, source_target_pairs={{8,0},{16,8},{24,16},{32,24},{40,32},{48,40},{56,48},{64,56},{72,6... | collective-permute-start | bytes 1572872 | tf_op jit(solution)/shard_map/ppermute | solution.py:371
  49.9 31.1 %collective-permute-start.6 = (f32[2,128,512]{2,1,0:T(8,128)}, f32[2,128,512]{2,1,0:T(8,128)S(1)}, u32[]{:S(2)}, u32[]{:S(2)}) collective-permute-start(f32[2,128,512]{2,1,0:T(8,128)} %get-tuple-element.39.below_ref), channel_id=1, source_target_pairs={{1,0},{2,1},{3,2},{4,3},{5,4},{6,5},{7,6},{9,8},{10,9},{11,10},{12... | collective-permute-start | bytes 1572872 | tf_op jit(solution)/shard_map/ppermute | solution.py:371
  60.4 25.5 %copy-start.13 = (f32[2,128,512]{2,1,0:T(8,128)}, f32[2,128,512]{2,1,0:T(8,128)S(1)}, u32[]{:S(2)}) copy-start(f32[2,128,512]{2,1,0:T(8,128)S(1)} %collective-permute-done.8.below_ref) | copy-start | bytes 1572868
  60.4 25.5 %collective-permute-start.9 = (f32[2,128,512]{2,1,0:T(8,128)S(1)}, f32[2,128,512]{2,1,0:T(8,128)}, u32[]{:S(2)}, u32[]{:S(2)}) collective-permute-start(f32[2,128,512]{2,1,0:T(8,128)S(1)} %collective-permute-done.8.below_ref), channel_id=1, source_target_pairs={{1,0},{2,1},{3,2},{4,3},{5,4},{6,5},{7,6},{9,8},{10,9},{11,10},{12... | collective-permute-start | bytes 1572872 | tf_op jit(solution)/shard_map/ppermute | solution.py:371
  64.2 7.5 %copy-start.15 = (f32[2,128,512]{2,1,0:T(8,128)}, f32[2,128,512]{2,1,0:T(8,128)S(1)}, u32[]{:S(2)}) copy-start(f32[2,128,512]{2,1,0:T(8,128)S(1)} %collective-permute-done.2.diag_ref) | copy-start | bytes 1572868
  71.7 0.8 copy-start.6
  72.5 1.3 copy-start
  77.8 12.2 %collective-permute-start.7 = (f32[2,128,512]{2,1,0:T(8,128)}, f32[2,128,512]{2,1,0:T(8,128)S(1)}, u32[]{:S(2)}, u32[]{:S(2)}) collective-permute-start(f32[2,128,512]{2,1,0:T(8,128)} %get-tuple-element.41.below_ref), channel_id=1, source_target_pairs={{1,0},{2,1},{3,2},{4,3},{5,4},{6,5},{7,6},{9,8},{10,9},{11,10},{12... | collective-permute-start | bytes 1572872 | tf_op jit(solution)/shard_map/ppermute | solution.py:371
  81.0 0.8 copy-start.14
  90.0 0.8 copy-start.16
  112.9 7.6 %collective-permute-start.10 = (f32[512,512]{1,0:T(8,128)}, f32[512,512]{1,0:T(8,128)S(1)}, u32[]{:S(2)}, u32[]{:S(2)}) collective-permute-start(f32[512,512]{1,0:T(8,128)} %get-tuple-element.53), channel_id=1, source_target_pairs={{0,1},{1,0},{2,3},{3,2},{4,5},{5,4},{6,7},{7,6},{8,9},{9,8},{10,11... | collective-permute-start | bytes 3145736 | tf_op jit(solution)/shard_map/ppermute | solution.py:375
  113.4 7.1 %collective-permute-start.11 = (f32[2,96,512]{2,1,0:T(8,128)}, f32[2,96,512]{2,1,0:T(8,128)S(1)}, u32[]{:S(2)}, u32[]{:S(2)}) collective-permute-start(f32[2,96,512]{2,1,0:T(8,128)} %get-tuple-element.55), channel_id=1, source_target_pairs={{0,1},{1,2},{2,3},{3,4},{4,5},{5,6},{6,7},{8,9},{9,10},{10,11},{11... | collective-permute-start | bytes 1179656 | tf_op jit(solution)/shard_map/ppermute | solution.py:371
  120.5 0.7 copy-start.17
  120.6 1.1 copy-start.11
  124.7 34.4 %copy-start.12 = (f32[2,128,512]{2,1,0:T(8,128)S(1)}, f32[2,128,512]{2,1,0:T(8,128)}, u32[]{:S(2)}) copy-start(f32[2,128,512]{2,1,0:T(8,128)} %get-tuple-element.62) | copy-start | bytes 1572868
  124.7 55.2 %collective-permute-start.12 = (f32[2,288,512]{2,1,0:T(8,128)}, f32[2,288,512]{2,1,0:T(8,128)S(1)}, u32[]{:S(2)}, u32[]{:S(2)}) collective-permute-start(f32[2,288,512]{2,1,0:T(8,128)} %get-tuple-element.60), channel_id=1, source_target_pairs={{0,1},{1,2},{2,3},{3,4},{4,5},{5,6},{6,7},{8,9},{9,10},{10,11},{11... | collective-permute-start | bytes 3538952 | tf_op jit(solution)/shard_map/ppermute | solution.py:371
  129.1 29.9 %collective-permute-start.14 = (f32[2,128,512]{2,1,0:T(8,128)}, f32[2,128,512]{2,1,0:T(8,128)S(1)}, u32[]{:S(2)}, u32[]{:S(2)}) collective-permute-start(f32[2,128,512]{2,1,0:T(8,128)} %get-tuple-element.63), channel_id=1, source_target_pairs={{0,1},{1,2},{2,3},{3,4},{4,5},{5,6},{6,7},{8,9},{9,10},{10,11},{11... | collective-permute-start | bytes 1572872 | tf_op jit(solution)/shard_map/ppermute | solution.py:371
  131.0 48.8 %all-to-all-start.1 = ((f32[64,8,512]{2,1,0:T(8,128)}), f32[64,8,512]{2,1,0:T(8,128)S(1)}, u32[]{:S(2)}, u32[]{:S(2)}) async-start(f32[64,8,512]{2,1,0:T(8,128)} %bitcast.7), calls=%async_computation.1 | async-start | bytes 2097152 | tf_op jit(solution)/shard_map/all_to_all | solution.py:471
  159.9 19.9 %collective-permute-start.15 = (f32[2,128,512]{2,1,0:T(8,128)}, f32[2,128,512]{2,1,0:T(8,128)S(1)}, u32[]{:S(2)}, u32[]{:S(2)}) collective-permute-start(f32[2,128,512]{2,1,0:T(8,128)} %add.32), channel_id=1, source_target_pairs={{0,8},{8,16},{16,24},{24,32},{32,40},{40,48},{48,56},{56,64},{64,7... | collective-permute-start | bytes 1572872 | tf_op jit(solution)/shard_map/ppermute | solution.py:371
  162.1 17.7 %collective-permute-start.13 = (f32[2,96,512]{2,1,0:T(8,128)}, f32[2,96,512]{2,1,0:T(8,128)S(1)}, u32[]{:S(2)}, u32[]{:S(2)}) collective-permute-start(f32[2,96,512]{2,1,0:T(8,128)} %get-tuple-element.61), channel_id=1, source_target_pairs={{0,8},{8,16},{16,24},{24,32},{32,40},{40,48},{48,56},{56,64},{64,7... | collective-permute-start | bytes 1179656 | tf_op jit(solution)/shard_map/ppermute | solution.py:371
  179.8 0.8 copy-start.8
  179.8 1.1 copy-start.3
  179.8 1.3 copy-start.4
  179.8 1.6 copy-start.9
  185.5 53.4 %collective-permute-start.16 = (f32[2,512,512]{2,1,0:T(8,128)}, f32[2,512,512]{2,1,0:T(8,128)S(1)}, u32[]{:S(2)}, u32[]{:S(2)}) collective-permute-start(f32[2,512,512]{2,1,0:T(8,128)} %shard_map.116), channel_id=1, source_target_pairs={{0,1},{1,2},{2,3},{3,4},{4,5},{5,6},{6,7},{8,9},{9,10},{10,11},{11... | collective-permute-start | bytes 6291464 | tf_op jit(solution)/shard_map/ppermute | solution.py:371
  191.7 47.2 %collective-permute-start.17 = (f32[2,288,512]{2,1,0:T(8,128)}, f32[2,288,512]{2,1,0:T(8,128)}, u32[]{:S(2)}, u32[]{:S(2)}) collective-permute-start(f32[2,288,512]{2,1,0:T(8,128)} %get-tuple-element.65), channel_id=1, source_target_pairs={{0,8},{8,16},{16,24},{24,32},{32,40},{40,48},{48,56},{56,64},{64,7... | collective-permute-start | bytes 3538952 | tf_op jit(solution)/shard_map/ppermute | solution.py:371
  196.7 42.2 %all-to-all-start.2 = ((f32[64,8,512]{2,1,0:T(8,128)}), f32[64,8,512]{2,1,0:T(8,128)S(1)}, u32[]{:S(2)}, u32[]{:S(2)}) async-start(f32[64,8,512]{2,1,0:T(8,128)} %get-tuple-element.64.refs_1_), calls=%async_computation.2 | async-start | bytes 2097152 | tf_op jit(solution)/shard_map/all_to_all | solution.py:479
  238.9 1.0 copy-start.1
  238.9 1.7 copy-start.2
  240.6 5.9 %collective-permute-start.18 = (f32[512,512]{1,0:T(8,128)}, f32[512,512]{1,0:T(8,128)S(1)}, u32[]{:S(2)}, u32[]{:S(2)}) collective-permute-start(f32[512,512]{1,0:T(8,128)} %shard_map.118.mine_ref), channel_id=1, source_target_pairs={{0,1},{1,0},{2,3},{3,2},{4,5},{5,4},{6,7},{7,6},{8,9},{9,8},{10,11... | collective-permute-start | bytes 3145736 | tf_op jit(solution)/shard_map/ppermute | solution.py:375
  246.6 1.0 copy-start.10
where the time goes:
time: 255 us; the launch traced here: 251 us
  waiting for transfers between devices  83.3 us (33%)
  starting transfers between devices  64.2 us (25%)
  Pallas kernels  61.9 us (24%)
  blocking collectives  20.6 us (8%)
  local copies, waits for them, and re-layouts  16.8 us (7%)
    ppermute x16, waiting for transfers between devices, shifted(): lax.ppermute(value, axis, [(source, source + steps) for source in range(f...  53.7 us
    ppermute x16, starting transfers between devices, shifted(): lax.ppermute(value, axis, [(source, source + steps) for source in range(f...  44.2 us
    all_to_all x1, waiting for transfers between devices, on_device(): mine = lax.all_to_all(shares, CHIPS, 0, 0).reshape(SIDE, SIDE)  28.7 us
    all_to_all x1, blocking collectives, largest(): value = jnp.max(lax.all_to_all(spread, CHIPS, 0, 0), axis=0)  20.6 us
    pallas_call x1, Pallas kernels, update(): pl.pallas_call(update_kernel, out_shape=out_shape, in_specs=[sm()] + [vm(...  18.1 us
    pallas_call x4, Pallas kernels, fore(): pl.pallas_call(functools.partial(fore_kernel, piece), grid=(1,), out_shap...  16.2 us
    unnamed x38, local copies, waits for them, and re-layouts  10.7 us
    pallas_call x1, Pallas kernels, ready(): pl.pallas_call(ready_kernel, out_shape=(jax.ShapeDtypeStruct((2, 2, SIDE,...  9.34 us
  transfers between devices with their start and end apart: 21, of which 7 were waited for; matrix products, arithmetic and copies ran while one was open for 3% of the time, Pallas kernels for 12%

commit v1 on v0

--- a/solution.py
+++ b/solution.py
@@ -15,7 +15,7 @@
 PIECE = SIDE // PIECES
 BACK = (96, 128, 288)
 CHUNKS = ((0, 96, 0, 0), (96, 128, 1, 0), (224, 144, 2, 0), (368, 144, 2, 144))
-VMEM_LIMIT = 60 * 1024 * 1024
+WIDE = SIDE + 128
 F32 = jnp.float32
 BF16 = jnp.bfloat16
 
@@ -93,9 +93,10 @@
 
 
 def fore_kernel(
-    piece, where_ref, own_ref, right_ref, below_ref, diag_ref, rolled_ref, mh_ref, ml_ref, *refs
+    piece, where_ref, own_ref, right_ref, below_ref, diag_ref, rolled_ref, mh_ref, ml_ref,
+    spec_ref, wrapped_ref, token_ref,
 ):
-    spec_ref, wrapped_ref = refs[-3:-1] if len(refs) == 4 else refs[-2:]
+    token_ref[...] = jnp.zeros_like(token_ref)
     lane = lax.broadcasted_iota(jnp.int32, (PIECE, SIDE), 1)
     row = lax.broadcasted_iota(jnp.int32, (PIECE, SIDE), 0) + piece * PIECE
     for item in range(2):
@@ -121,7 +122,7 @@
             spec_ref[item, 1, :, p * QUARTER : (p + 1) * QUARTER] = out[:, QUARTER:]
 
 
-def fore(piece, where, own, right, below, diag, rolled, matrices, held=None, after=None):
+def fore(piece, where, own, right, below, diag, rolled, matrices):
     def rows(*lead):
         zeros = (0,) * len(lead)
         return pl.BlockSpec(lead + (PIECE, SIDE), lambda i: zeros + (piece, 0))
@@ -130,49 +131,30 @@
     whole = pl.BlockSpec((4, 2 * QUARTER, 2 * QUARTER), lambda i: (0, 0, 0))
     four = pl.BlockSpec((2, 2, PIECE, SIDE), lambda i: (0, 0, 0, 0))
     shape = jax.ShapeDtypeStruct((2, 2, PIECE, SIDE), F32)
-    operands = [where, own, right, below, diag, rolled, *matrices[2:]]
-    in_specs = [sm(), rows(2), rows(2), full, full, rows(2, 2), whole, whole]
-    out_shape, out_specs, aliases = [shape, shape], [four, four], {}
-    if held is not None:
-        aliases = {len(operands): 2}
-        operands.append(held)
-        in_specs.append(anywhere())
-        out_shape.append(jax.ShapeDtypeStruct(held.shape, F32))
-        out_specs.append(anywhere())
-    if after is not None:
-        operands.append(after)
-        in_specs.append(anywhere())
     return pl.pallas_call(
         functools.partial(fore_kernel, piece),
         grid=(1,),
-        out_shape=out_shape,
-        in_specs=in_specs,
-        out_specs=out_specs,
-        input_output_aliases=aliases,
-        compiler_params=params(),
+        out_shape=[shape, shape, jax.ShapeDtypeStruct((8, 128), F32)],
+        in_specs=[sm(), rows(2), rows(2), full, full, rows(2, 2), whole, whole],
+        out_specs=[four, four, pl.BlockSpec((8, 128), lambda i: (0, 0))],
+        compiler_params=params(20),
         cost_estimate=pl.CostEstimate(
             flops=4 * 10**8, bytes_accessed=6 * 2**20, transcendentals=0
         ),
-    )(*operands)
+    )(where, own, right, below, diag, rolled, *matrices[2:])
 
 
 def update_kernel(where_ref, *refs):
     spec_refs = refs[:PIECES]
-    wrapped_hbm = refs[PIECES : 2 * PIECES]
-    rolled_hbm, amps_ref, lh_ref, ll_ref, mh_ref, ml_ref = refs[2 * PIECES : 2 * PIECES + 6]
-    outs = refs[2 * PIECES + 6 :]
-    t_own_ref, t_right_ref = outs[:2]
+    wrapped_refs = refs[PIECES : 2 * PIECES]
+    rolled_ref, amps_ref, peaks_ref, lh_ref, ll_ref, mh_ref, ml_ref = refs[2 * PIECES : 2 * PIECES + 7]
+    outs = refs[2 * PIECES + 7 :]
     count = len(BACK)
-    t_below_refs, t_diag_refs = outs[2 : 2 + count], outs[2 + count : 2 + 2 * count]
+    t_own_hbm, t_right_hbm = outs[:2]
+    t_below_hbm, t_diag_hbm = outs[2 : 2 + count], outs[2 + count : 2 + 2 * count]
     keep_ref, send_ref = outs[2 + 2 * count : 4 + 2 * count]
-    wrapped, rolled_ref, high, low, grad, sems = outs[4 + 2 * count :]
+    high, low, grad, terms, out_sems = outs[4 + 2 * count :]
     core = where_ref[2, 0]
-    loads = [
-        pltpu.make_async_copy(wrapped_hbm[k], wrapped.at[:, :, k * PIECE : (k + 1) * PIECE], sems.at[k])
-        for k in range(PIECES)
-    ] + [pltpu.make_async_copy(rolled_hbm, rolled_ref, sems.at[PIECES])]
-    for load in loads:
-        load.start()
 
     wide = 2 * QUARTER
     for item in range(2):
@@ -203,8 +185,7 @@
                         high[item, rows, to] = hi[:, piece]
                         low[item, rows, to] = lo[:, piece]
 
-    for load in loads:
-        load.wait()
+    stores = []
     for first, size, piece, inside in CHUNKS:
         at, within = slice(first, first + size), slice(inside, inside + size)
         lane = lax.broadcasted_iota(jnp.int32, (size, SIDE), 1)
@@ -222,7 +203,15 @@
             back_r = jnp.concatenate([b[0] for b in back], axis=1)
             back_i = jnp.concatenate([b[1] for b in back], axis=1)
             beam_r, beam_i = rolled_ref[item, 0, at, :], rolled_ref[item, 1, at, :]
-            patch_r, patch_i = wrapped[item, 0, at, :], wrapped[item, 1, at, :]
+            patch = []
+            for part in range(2):
+                spans = [
+                    (k, max(first, k * PIECE) - k * PIECE, min(first + size, (k + 1) * PIECE) - k * PIECE)
+                    for k in range(PIECES)
+                ]
+                values = [wrapped_refs[k][item, part, lo:hi] for k, lo, hi in spans if lo < hi]
+                patch.append(values[0] if len(values) == 1 else jnp.concatenate(values, axis=0))
+            patch_r, patch_i = patch
             diff_r = back_r - (beam_r * patch_r - beam_i * patch_i)
             diff_i = back_i - (beam_r * patch_i + beam_i * patch_r)
             term = (beam_r * diff_r + beam_i * diff_i, beam_r * diff_i - beam_i * diff_r)
@@ -233,16 +222,26 @@
                 upper = jnp.where(above, zero, term[part])
                 lower = jnp.where(above, term[part], zero)
                 four = (
-                    (t_own_ref, (part, at), jnp.where(beside, zero, upper)),
-                    (t_right_ref, (part, at), jnp.where(beside, upper, zero)),
-                    (t_below_refs[piece], (part, within), jnp.where(beside, zero, lower)),
-                    (t_diag_refs[piece], (part, within), jnp.where(beside, lower, zero)),
+                    jnp.where(beside, zero, upper),
+                    jnp.where(beside, upper, zero),
+                    jnp.where(beside, zero, lower),
+                    jnp.where(beside, lower, zero),
                 )
-                for ref, index, value in four:
+                for k, value in enumerate(four):
                     if item == 0:
-                        ref[index] = value
+                        terms[k, part, at] = value
                     else:
-                        ref[index] += value
+                        terms[k, part, at] += value
+        targets = (
+            t_own_hbm.at[:, at],
+            t_right_hbm.at[:, at],
+            t_below_hbm[piece].at[:, within],
+            t_diag_hbm[piece].at[:, within],
+        )
+        for k, target in enumerate(targets):
+            store = pltpu.make_async_copy(terms.at[k, :, at], target, out_sems.at[len(stores)])
+            store.start()
+            stores.append(store)
     whole = []
     for part in range(2):
         total = None
@@ -252,8 +251,13 @@
             value = pltpu.roll(value, (SIDE - along) % SIDE, 1)
             total = value if total is None else total + value
         whole.append(total)
-    keep_ref[...] = jnp.where(core == 0, whole[0], whole[1])
-    send_ref[...] = jnp.where(core == 0, whole[1], whole[0])
+    keep_ref[:, :SIDE] = jnp.where(core == 0, whole[0], whole[1])
+    send_ref[:, :SIDE] = jnp.where(core == 0, whole[1], whole[0])
+    peak = jnp.broadcast_to(peaks_ref[0, :1, :], (SIDE, 128))
+    keep_ref[:, SIDE:] = peak
+    send_ref[:, SIDE:] = peak
+    for store in stores:
+        store.wait()
 
 
 def vm():
@@ -268,8 +272,8 @@
     return pl.BlockSpec(memory_space=pl.ANY)
 
 
-def params():
-    return pltpu.CompilerParams(vmem_limit_bytes=VMEM_LIMIT)
+def params(mebibytes=16):
+    return pltpu.CompilerParams(vmem_limit_bytes=mebibytes * 2**20)
 
 
 def ready(where, probe, own, amplitudes):
@@ -281,37 +285,38 @@
             jax.ShapeDtypeStruct((2, 8, 128), F32),
         ),
         in_specs=[sm()] + [vm()] * 4,
-        out_specs=(vm(), vm(), vm()),
+        out_specs=(vm(),) * 3,
         scratch_shapes=[pltpu.VMEM((4, SIDE, QUARTER), F32)],
-        compiler_params=params(),
+        compiler_params=params(32),
         cost_estimate=pl.CostEstimate(flops=4 * 10**9, bytes_accessed=14 * 2**20, transcendentals=0),
     )(where, probe, own, amplitudes, jnp.asarray(order_matrix()))
 
 
-def update(where, specs, wrapped, rolled, amps, matrices):
+def update(where, specs, wrapped, rolled, amps, peaks, matrices):
     full = jax.ShapeDtypeStruct((2, SIDE, SIDE), F32)
     parts = tuple(jax.ShapeDtypeStruct((2, size, SIDE), F32) for size in BACK)
-    plane = jax.ShapeDtypeStruct((SIDE, SIDE), F32)
+    plane = jax.ShapeDtypeStruct((SIDE, WIDE), F32)
     out_shape = (full, full) + parts + parts + (plane, plane)
     count = len(BACK)
+    four = pltpu.VMEM((2, 2, SIDE, SIDE), F32)
+    half = pltpu.VMEM((2, SIDE, 2 * SIDE), BF16)
     outs = pl.pallas_call(
         update_kernel,
         out_shape=out_shape,
-        in_specs=[sm()] + [vm()] * PIECES + [anywhere()] * (PIECES + 1) + [vm()] * 5,
-        out_specs=(vm(),) * len(out_shape),
+        in_specs=[sm()] + [vm()] * (2 * PIECES + 7),
+        out_specs=(anywhere(),) * (2 + 2 * count) + (vm(), vm()),
         scratch_shapes=[
-            pltpu.VMEM((2, 2, SIDE, SIDE), F32),
-            pltpu.VMEM((2, 2, SIDE, SIDE), F32),
-            pltpu.VMEM((2, SIDE, 2 * SIDE), BF16),
-            pltpu.VMEM((2, SIDE, 2 * SIDE), BF16),
-            pltpu.VMEM((2, 2, SIDE, SIDE), F32),
-            pltpu.SemaphoreType.DMA((PIECES + 1,)),
+            half,
+            half,
+            four,
+            pltpu.VMEM((4, 2, SIDE, SIDE), F32),
+            pltpu.SemaphoreType.DMA((4 * len(CHUNKS),)),
         ],
-        compiler_params=params(),
+        compiler_params=params(36),
         cost_estimate=pl.CostEstimate(
             flops=5 * 10**9, bytes_accessed=26 * 2**20, transcendentals=2 * SIDE * SIDE
         ),
-    )(where, *specs, *wrapped, rolled, amps, *matrices)
+    )(where, *specs, *wrapped, rolled, amps, peaks, *matrices)
     return outs[0], outs[1], outs[2 : 2 + count], outs[2 + count : 2 + 2 * count], outs[-2], outs[-1]
 
 
@@ -331,7 +336,8 @@
 
 
 def first_kernel(keep_ref, came_ref, below_ref, diag_ref, half_ref, lower_ref):
-    half_ref[...] = keep_ref[...] + came_ref[...]
+    half_ref[:, :SIDE] = keep_ref[:, :SIDE] + came_ref[:, :SIDE]
+    half_ref[:, SIDE:] = jnp.maximum(keep_ref[:, SIDE:], came_ref[:, SIDE:])
     lower_ref[...] = below_ref[...] + diag_ref[...]
 
 
@@ -346,23 +352,42 @@
     )(keep, came, below, diag)
 
 
-def share_kernel(peak_ref, terms_ref, start_ref, below_ref, corner_ref, *refs):
-    out_ref, lower_ref = refs[-2:]
+def lower_kernel(below_ref, corner_ref, after_ref, lower_ref):
+    del after_ref
     lower_ref[...] = below_ref[...] + corner_ref[...]
-    total = jnp.sum(terms_ref[...], axis=0)
-    value = start_ref[...] + 0.5 * total / (peak_ref[0, 0] + 1e-06)
-    out_ref[...] = jnp.broadcast_to(value, out_ref.shape)
-
-
-def shared(peak, terms, start, below, corner, after):
+
+
+def lowered(below, corner, after):
+    return pl.pallas_call(
+        lower_kernel,
+        out_shape=jax.ShapeDtypeStruct(below.shape, F32),
+        in_specs=[vm(), vm(), anywhere()],
+        out_specs=vm(),
+        compiler_params=params(),
+        cost_estimate=pl.CostEstimate(flops=below.size, bytes_accessed=12 * below.size, transcendentals=0),
+    )(below, corner, after)
+
+
+def share_kernel(terms_ref, start_ref, *refs):
+    out_ref = refs[-1]
+    total = jnp.sum(terms_ref[:, :, :SIDE], axis=0)
+    peak = jnp.max(terms_ref[:, :, SIDE:], axis=0)
+    for q in range(4):
+        lanes = slice(q * QUARTER, (q + 1) * QUARTER)
+        value = start_ref[:, lanes] + 0.5 * total[:, lanes] / (peak + 1e-06)
+        out_ref[:, :, lanes] = jnp.broadcast_to(value, out_ref.shape[:2] + (QUARTER,))
+
+
+def shared(terms, start, after):
+    count, share, _ = terms.shape
     return pl.pallas_call(
         share_kernel,
-        out_shape=[jax.ShapeDtypeStruct(terms.shape, F32), jax.ShapeDtypeStruct(below.shape, F32)],
-        in_specs=[sm()] + [vm()] * 4 + [anywhere()] * len(after),
-        out_specs=[vm(), vm()],
+        out_shape=jax.ShapeDtypeStruct((count, share, SIDE), F32),
+        in_specs=[vm()] * 2 + [anywhere()] * len(after),
+        out_specs=vm(),
         compiler_params=params(),
-        cost_estimate=pl.CostEstimate(flops=2 * terms.size, bytes_accessed=20 * terms.size, transcendentals=0),
-    )(peak, terms, start, below, corner, *after)
+        cost_estimate=pl.CostEstimate(flops=2 * terms.size, bytes_accessed=8 * terms.size, transcendentals=0),
+    )(terms, start, *after)
 
 
 def shifted(value, axis, steps):
@@ -373,12 +398,6 @@
 
 def other_core(value):
     return lax.ppermute(value, "core", [(0, 1), (1, 0)])
-
-
-def largest(value):
-    spread = jnp.broadcast_to(value[:1][None], (64, 1, QUARTER))
-    value = jnp.max(lax.all_to_all(spread, CHIPS, 0, 0), axis=0)
-    return jnp.maximum(value, other_core(value))
 
 
 def base_kernel(scale_ref, own_ref, t_own_ref, base_ref):
@@ -440,46 +459,40 @@
     )
     matrices = [jnp.asarray(m) for m in split_matrices()]
     pieces = [object_field[:, k * PIECE : (k + 1) * PIECE] for k in range(PIECES)]
-    below, diag, specs, wrapped = [None] * 4, [None] * 4, [None] * 4, [None] * 4
-    below[0] = shifted(pieces[0], ROW, -1)
-    below[1] = shifted(pieces[1], ROW, -1)
+    below = [shifted(piece, ROW, -1) for piece in pieces]
     right = shifted(object_field, COL, -1)
     rolled, amps, peaks = ready(where, probe, object_field, amplitudes)
     scale = 0.9 / (peaks[1, :1, :1] + 1e-06)
-    below[0], pieces[2] = tied((below[0], pieces[2]), (rolled,))
-    diag[0] = shifted(below[0], COL, -1)
-    below[2] = shifted(pieces[2], ROW, -1)
-    object_peak = largest(peaks[0])
-    below[1], pieces[3] = tied((below[1], pieces[3]), (pieces[2], object_peak))
-    diag[1] = shifted(below[1], COL, -1)
-    below[3] = shifted(pieces[3], ROW, -1)
-    specs[0], wrapped[0], below[2] = fore(
-        0, where, object_field, right, below[0], diag[0], rolled, matrices, held=below[2]
+    specs, wrapped, tokens = [], [], [peaks]
+    for k in range(PIECES):
+        if k == 1:
+            (below[1],) = tied((below[1],), (below[0], peaks))
+        elif k > 1:
+            (below[k],) = tied((below[k],), (below[k - 1], tokens[k - 2]))
+        corner = shifted(below[k], COL, -1)
+        spec, wrap, token = fore(k, where, object_field, right, below[k], corner, rolled, matrices)
+        specs.append(spec)
+        wrapped.append(wrap)
+        tokens[k:] = [token]
+    t_own, t_right, t_below, t_diag, keep, send = update(
+        where, specs, wrapped, rolled, amps, peaks, matrices
     )
-    diag[2] = shifted(below[2], COL, -1)
-    diag[3] = shifted(below[3], COL, -1)
-    for k in range(1, PIECES):
-        specs[k], wrapped[k] = fore(
-            k, where, object_field, right, below[k], diag[k], rolled, matrices
-        )
-    t_own, t_right, t_below, t_diag, keep, send = update(where, specs, wrapped, rolled, amps, matrices)
 
     came = other_core(send)
-    corner = [shifted(t_diag[0], COL, 1)]
+    corner = [shifted(t, COL, 1) for t in t_diag]
     half, lower = first_sums(keep, came, t_below[0], corner[0])
     share = SIDE // 64
-    terms = lax.all_to_all(half.reshape(64, share, SIDE), CHIPS, 0, 0)
+    terms = lax.all_to_all(half.reshape(64, share, WIDE), CHIPS, 0, 0)
     from_above = [shifted(lower, ROW, 1)]
-    later = tied((t_diag[1], t_diag[2]), (half,))
-    corner += [shifted(t, COL, 1) for t in later]
-    from_above.append(shifted(t_below[1] + corner[1], ROW, 1))
+    lower = lowered(t_below[1], corner[1], from_above[0])
+    from_above.append(shifted(lower, ROW, 1))
+    lower = lowered(t_below[2], corner[2], lower)
+    from_above.append(shifted(lower, ROW, 1))
+    from_left = shifted(t_right, COL, 1)
     at = lax.axis_index(CHIPS) * share
     start = lax.dynamic_slice(probe, (core, at, jnp.zeros_like(at)), (1, share, SIDE))[0]
-    shares, lower = shared(object_peak[:, :1], terms, start, t_below[2], corner[2], from_above)
+    shares = shared(terms, start, from_above[:2] + [lower])
     mine = lax.all_to_all(shares, CHIPS, 0, 0).reshape(SIDE, SIDE)
-    from_above.append(shifted(lower, ROW, 1))
-    (t_right,) = tied((t_right,), (shares,))
-    from_left = shifted(t_right, COL, 1)
     begun = base(scale, object_field, t_own)
     (mine,) = tied((mine,), (from_above[2], from_left, begun))
     new_probe = joined(core.astype(jnp.int32).reshape(1, 1), mine, other_core(mine))

time: 255 us -> 233 us (0.914)
  Pallas kernels: 61.9 us -> 39.9 us
  blocking collectives: 20.6 us -> 0 us
  local copies, waits for them, and re-layouts: 16.8 us -> 33.5 us
  starting transfers between devices: 64.2 us -> 69.8 us
    all_to_all x1 -> x0, blocking collectives: 20.6 us -> none  [largest(): value = jnp.max(lax.all_to_all(spread, CHIPS, 0, 0), axis=0)]
    unnamed x38 -> x84, local copies, waits for them, and re-layouts: 10.7 us -> 29.4 us
    ppermute x16, waiting for transfers between devices: 53.7 us -> 66.6 us  [shifted(): lax.ppermute(value, axis, [(source, source + steps) for source in range(f...]
    all_to_all x1, waiting for transfers between devices: 28.7 us -> 16.7 us  [on_device(): mine = lax.all_to_all(shares, CHIPS, 0, 0).reshape(SIDE, SIDE)]
    pallas_call x4, Pallas kernels: 16.2 us -> 10.1 us  [fore(): pl.pallas_call(functools.partial(fore_kernel, piece), grid=(1,), out_shap...]
    pallas_call x1, Pallas kernels: 9.34 us -> 4.52 us  [ready(): pl.pallas_call(ready_kernel, out_shape=(jax.ShapeDtypeStruct((2, 2, SIDE,...]
    all_to_all x1, starting transfers between devices: 8.14 us -> 12.3 us  [on_device(): terms = lax.all_to_all(half.reshape(64, share, WIDE), CHIPS, 0, 0)]
    pallas_call x1, Pallas kernels: 3.75 us -> 0.21 us  [base(): pl.pallas_call(base_kernel, out_shape=jax.ShapeDtypeStruct(own.shape, F32...]
  transfers between devices with their start and end apart: 21 -> 20, of which waited for: 7 -> 9; matrix products, arithmetic and copies ran while one was open for 3% -> 2% of each run, Pallas kernels for 12% -> 8%
where the time goes in v1:
time: 233 us; the launch traced here: 229 us
  waiting for transfers between devices  83.3 us (36%)
  starting transfers between devices  69.8 us (30%)
  Pallas kernels  39.9 us (17%)
  local copies, waits for them, and re-layouts  33.5 us (14%)
    ppermute x16, waiting for transfers between devices, shifted(): lax.ppermute(value, axis, [(source, source + steps) for source in range(f...  66.6 us
    ppermute x16, starting transfers between devices, shifted(): lax.ppermute(value, axis, [(source, source + steps) for source in range(f...  41.8 us
    unnamed x84, local copies, waits for them, and re-layouts  29.4 us
    all_to_all x1, waiting for transfers between devices, on_device(): mine = lax.all_to_all(shares, CHIPS, 0, 0).reshape(SIDE, SIDE)  16.7 us
    pallas_call x1, Pallas kernels, update(): pl.pallas_call(update_kernel, out_shape=out_shape, in_specs=[sm()] + [vm(...  16.2 us
    all_to_all x1, starting transfers between devices, on_device(): terms = lax.all_to_all(half.reshape(64, share, WIDE), CHIPS, 0, 0)  12.3 us
    all_to_all x1, starting transfers between devices, on_device(): mine = lax.all_to_all(shares, CHIPS, 0, 0).reshape(SIDE, SIDE)  10.8 us
    pallas_call x4, Pallas kernels, fore(): pl.pallas_call(functools.partial(fore_kernel, piece), grid=(1,), out_shap...  10.1 us
  transfers between devices with their start and end apart: 20, of which 9 were waited for; matrix products, arithmetic and copies ran while one was open for 2% of the time, Pallas kernels for 8%

profile of v1, /device:TPU:33, one launch (start us, length us, event | category | flops | bytes accessed | tf_op | source)
XLA Modules:
  0.0 228.6 jit_solution(12038159430586380527)
XLA Ops:
  0.6 2.7 %collective-permute-start = (f32[2,512,512]{2,1,0:T(8,128)}, f32[2,512,512]{2,1,0:T(8,128)}, u32[]{:S(2)}, u32[]{:S(2)}) collective-permute-start(f32[2,512,512]{2,1,0:T(8,128)} %own_ref.11), channel_id=1, source_target_pairs={{1,0},{2,1},{3,2},{4,3},{5,4},{6,5},{7,6},{9,8},{10,9},{11,10},{12... | collective-permute-start | bytes 6291464 | tf_op jit(solution)/shard_map/ppermute | solution.py:396
  3.4 2.9 %fusion = (f32[2,128,512]{2,1,0:T(8,128)}, f32[2,128,512]{2,1,0:T(8,128)}, f32[2,128,512]{2,1,0:T(8,128)}, f32[2,128,512]{2,1,0:T(8,128)}) fusion(f32[2,512,512]{2,1,0:T(8,128)} %own_ref.11), kind=kLoop, calls=%fused_computation.5 | loop fusion | bytes 4194304 | tf_op jit(solution)/shard_map/slice | solution.py:461
  6.3 1.3 collective-permute-start.1
  7.6 1.3 collective-permute-start.3
  8.9 1.3 collective-permute-start.5
  10.5 11.5 %collective-permute-done.1.below_ref.refs_1_ = f32[2,128,512]{2,1,0:T(8,128)} collective-permute-done((f32[2,128,512]{2,1,0:T(8,128)}, f32[2,128,512]{2,1,0:T(8,128)}, u32[]{:S(2)}, u32[]{:S(2)}) %collective-permute-start.1) | collective-permute-done | bytes 524320 | tf_op jit(solution)/shard_map/ppermute | solution.py:396
  22.0 3.1 %collective-permute-start.2 = (f32[2,128,512]{2,1,0:T(8,128)}, f32[2,128,512]{2,1,0:T(8,128)}, u32[]{:S(2)}, u32[]{:S(2)}) collective-permute-start(f32[2,128,512]{2,1,0:T(8,128)} %collective-permute-done.1.below_ref.refs_1_), channel_id=1, source_target_pairs={{1,0},{2,1},{3,2},{4,3},{5,4},{6,5},{7,6},{9,8},{10,9},{11,10},{12... | collective-permute-start | bytes 1572872 | tf_op jit(solution)/shard_map/ppermute | solution.py:396
  25.1 1.6 copy-done.25
  26.7 1.6 copy-done.26
  29.3 4.5 %shard_map.104 = (f32[2,2,512,512]{3,2,1,0:T(8,128)S(1)}, f32[2,512,512]{2,1,0:T(8,128)S(1)}, f32[2,8,128]{2,1,0:T(8,128)S(1)}) custom-call(s32[3,2]{1,0:T(4,128)S(1)} %pad_add_fusion.where_ref, f32[2,512,512]{2,1,0:T(8,128)S(1)} %copy-done.25, f32[2,512,512]{2,1,0:T(8,128)S(1)} %copy-done, f32[2,512,512]{2,1,0:T(8,128)S(1)} %copy-done.26, ...), custom_call_target="tpu_custom_call" | custom-call | flops 4000000000 | bytes 14680064 | tf_op jit(solution)/shard_map/pallas_call | solution.py:280
  33.9 2.0 copy-done.1
  36.4 1.3 copy-done.40
  37.8 1.9 collective-permute-start.4
  39.7 1.3 collective-permute-start.7
  41.0 2.2 copy-done.2
  43.2 2.3 shard_map.105
  48.9 2.2 copy-done.3
  51.1 2.3 shard_map.107
  53.9 1.0 copy-done.31
  55.9 2.5 %collective-permute-start.8 = (f32[2,128,512]{2,1,0:T(8,128)}, f32[2,128,512]{2,1,0:T(8,128)S(1)}, u32[]{:S(2)}, u32[]{:S(2)}) collective-permute-start(f32[2,128,512]{2,1,0:T(8,128)} %shard_map.110.below_ref), channel_id=1, source_target_pairs={{1,0},{2,1},{3,2},{4,3},{5,4},{6,5},{7,6},{9,8},{10,9},{11,10},{12... | collective-permute-start | bytes 1572872 | tf_op jit(solution)/shard_map/ppermute | solution.py:396
  58.4 2.1 collective-permute-start.6
  60.5 6.5 %collective-permute-done.8.diag_ref = f32[2,128,512]{2,1,0:T(8,128)S(1)} collective-permute-done((f32[2,128,512]{2,1,0:T(8,128)}, f32[2,128,512]{2,1,0:T(8,128)S(1)}, u32[]{:S(2)}, u32[]{:S(2)}) %collective-permute-start.8) | collective-permute-done | bytes 524320 | tf_op jit(solution)/shard_map/ppermute | solution.py:396
  67.0 2.2 copy-done.4
  69.2 2.6 %shard_map.111 = (f32[2,2,128,512]{3,2,1,0:T(8,128)S(1)}, f32[2,2,128,512]{3,2,1,0:T(8,128)S(1)}, f32[8,128]{1,0:T(8,128)}) custom-call(s32[3,2]{1,0:T(4,128)S(1)} %pad_add_fusion.where_ref, f32[2,512,512]{2,1,0:T(8,128)S(1)} %copy-done, f32[2,512,512]{2,1,0:T(8,128)} %collective-permute-done.right_ref, f32[2,128,512]{2,1,0:T(8,128)} %shard_map.110.below_ref, ...), custom_call_target="tpu_custom_call" | custom-call | flops 400000000 | bytes 6291456 | tf_op jit(solution)/shard_map/pallas_call | solution.py:134
  72.6 3.0 %shard_map.109 = (f32[2,2,128,512]{3,2,1,0:T(8,128)S(1)}, f32[2,2,128,512]{3,2,1,0:T(8,128)S(1)}, f32[8,128]{1,0:T(8,128)}) custom-call(s32[3,2]{1,0:T(4,128)S(1)} %pad_add_fusion.where_ref, f32[2,512,512]{2,1,0:T(8,128)S(1)} %copy-done, f32[2,512,512]{2,1,0:T(8,128)} %collective-permute-done.right_ref, f32[2,128,512]{2,1,0:T(8,128)} %shard_map.108.below_ref.refs_1_, ...), custom_call_target="tpu_custom_call" | custom-call | flops 400000000 | bytes 6291456 | tf_op jit(solution)/shard_map/pallas_call | solution.py:134
  75.7 16.2 %shard_map.112 = (f32[2,512,512]{2,1,0:T(8,128)}, f32[2,512,512]{2,1,0:T(8,128)}, f32[2,96,512]{2,1,0:T(8,128)S(1)}, f32[2,128,512]{2,1,0:T(8,128)S(1)}, f32[2,2...) custom-call(s32[3,2]{1,0:T(4,128)S(1)} %pad_add_fusion.where_ref, ...), custom_call_target="tpu_custom_call" | custom-call | flops 5000000000 | bytes 27262976 | tf_op jit(solution)/shard_map/pallas_call | solution.py:303
  92.1 4.3 %collective-permute-start.11 = (f32[2,96,512]{2,1,0:T(8,128)S(1)}, f32[2,96,512]{2,1,0:T(8,128)S(1)}, u32[]{:S(2)}, u32[]{:S(2)}) collective-permute-start(f32[2,96,512]{2,1,0:T(8,128)S(1)} %get-tuple-element.45), channel_id=1, source_target_pairs={{0,1},{1,2},{2,3},{3,4},{4,5},{5,6},{6,7},{8,9},{9,10},{10,11},{11... | collective-permute-start | bytes 1179656 | tf_op jit(solution)/shard_map/ppermute | solution.py:396
  96.4 1.9 collective-permute-start.15
  98.3 2.8 %collective-permute-done.11.diag_ref = f32[2,96,512]{2,1,0:T(8,128)S(1)} collective-permute-done((f32[2,96,512]{2,1,0:T(8,128)S(1)}, f32[2,96,512]{2,1,0:T(8,128)S(1)}, u32[]{:S(2)}, u32[]{:S(2)}) %collective-permute-start.11) | collective-permute-done | bytes 393248 | tf_op jit(solution)/shard_map/ppermute | solution.py:396
  102.0 1.0 copy-done.16
  103.1 12.3 %all-to-all-start = ((f32[64,8,640]{2,1,0:T(8,128)}), f32[64,8,640]{2,1,0:T(8,128)S(1)}, u32[]{:S(2)}, u32[]{:S(2)}) async-start(f32[64,8,640]{2,1,0:T(8,128)} %bitcast.13), calls=%async_computation | async-start | bytes 2621440 | tf_op jit(solution)/shard_map/all_to_all | solution.py:485
  115.4 6.6 %collective-permute-start.9 = (f32[2,512,512]{2,1,0:T(8,128)}, f32[2,512,512]{2,1,0:T(8,128)}, u32[]{:S(2)}, u32[]{:S(2)}) collective-permute-start(f32[2,512,512]{2,1,0:T(8,128)} %get-tuple-element.41), channel_id=1, source_target_pairs={{0,1},{1,2},{2,3},{3,4},{4,5},{5,6},{6,7},{8,9},{9,10},{10,11},{11... | collective-permute-start | bytes 6291464 | tf_op jit(solution)/shard_map/ppermute | solution.py:396
  122.0 1.9 collective-permute-start.13
  123.9 3.1 %collective-permute-start.12 = (f32[2,96,512]{2,1,0:T(8,128)}, f32[2,96,512]{2,1,0:T(8,128)S(1)}, u32[]{:S(2)}, u32[]{:S(2)}) collective-permute-start(f32[2,96,512]{2,1,0:T(8,128)} %copy-done.36), channel_id=1, source_target_pairs={{0,8},{8,16},{16,24},{24,32},{32,40},{40,48},{48,56},{56,64},{64,7... | collective-permute-start | bytes 1179656 | tf_op jit(solution)/shard_map/ppermute | solution.py:396
  127.1 32.9 %collective-permute-done.13.corner_ref = f32[2,128,512]{2,1,0:T(8,128)S(1)} collective-permute-done((f32[2,128,512]{2,1,0:T(8,128)}, f32[2,128,512]{2,1,0:T(8,128)S(1)}, u32[]{:S(2)}, u32[]{:S(2)}) %collective-permute-start.13) | collective-permute-done | bytes 524320 | tf_op jit(solution)/shard_map/ppermute | solution.py:396
  162.6 3.6 %collective-permute-start.14 = (f32[2,128,512]{2,1,0:T(8,128)}, f32[2,128,512]{2,1,0:T(8,128)}, u32[]{:S(2)}, u32[]{:S(2)}) collective-permute-start(f32[2,128,512]{2,1,0:T(8,128)} %shard_map.115.after_ref), channel_id=1, source_target_pairs={{0,8},{8,16},{16,24},{24,32},{32,40},{40,48},{48,56},{56,64},{64,7... | collective-permute-start | bytes 1572872 | tf_op jit(solution)/shard_map/ppermute | solution.py:396
  166.2 2.4 %shard_map.116.refs_2_ = f32[2,288,512]{2,1,0:T(8,128)} custom-call(f32[2,288,512]{2,1,0:T(8,128)S(1)} %copy-done.18, f32[2,288,512]{2,1,0:T(8,128)} %collective-permute-done.15.corner_ref, f32[2,128,512]{2,1,0:T(8,128)} %shard_map.115.after_ref), custom_call_target="tpu_custom_call" | custom-call | flops 294912 | bytes 3538944 | tf_op jit(solution)/shard_map/pallas_call | solution.py:361
  168.7 3.0 %collective-permute-start.16 = (f32[2,288,512]{2,1,0:T(8,128)}, f32[2,288,512]{2,1,0:T(8,128)}, u32[]{:S(2)}, u32[]{:S(2)}) collective-permute-start(f32[2,288,512]{2,1,0:T(8,128)} %shard_map.116.refs_2_), channel_id=1, source_target_pairs={{0,8},{8,16},{16,24},{24,32},{32,40},{40,48},{48,56},{56,64},{64,7... | collective-permute-start | bytes 3538952 | tf_op jit(solution)/shard_map/ppermute | solution.py:396
  172.3 3.3 %collective-permute-done.14.refs_1_ = f32[2,128,512]{2,1,0:T(8,128)} collective-permute-done((f32[2,128,512]{2,1,0:T(8,128)}, f32[2,128,512]{2,1,0:T(8,128)}, u32[]{:S(2)}, u32[]{:S(2)}) %collective-permute-start.14) | collective-permute-done | bytes 524320 | tf_op jit(solution)/shard_map/ppermute | solution.py:396
  176.9 1.1 copy-done.11
  177.9 10.8 %all-to-all-start.1 = ((f32[64,8,512]{2,1,0:T(8,128)}), f32[64,8,512]{2,1,0:T(8,128)S(1)}, u32[]{:S(2)}, u32[]{:S(2)}) async-start(f32[64,8,512]{2,1,0:T(8,128)} %copy-done.11), calls=%async_computation.1 | async-start | bytes 2097152 | tf_op jit(solution)/shard_map/all_to_all | solution.py:495
  189.9 1.6 copy-done.15
  191.8 1.3 copy-done.5
  193.1 7.9 %collective-permute-done.16.refs_2_.refs_1_ = f32[2,288,512]{2,1,0:T(8,128)} collective-permute-done((f32[2,288,512]{2,1,0:T(8,128)}, f32[2,288,512]{2,1,0:T(8,128)}, u32[]{:S(2)}, u32[]{:S(2)}) %collective-permute-start.16) | collective-permute-done | bytes 1179680 | tf_op jit(solution)/shard_map/ppermute | solution.py:396
  201.0 16.7 %all-to-all-done.1 = f32[64,8,512]{2,1,0:T(8,128)S(1)} async-done(((f32[64,8,512]{2,1,0:T(8,128)}), f32[64,8,512]{2,1,0:T(8,128)S(1)}, u32[]{:S(2)}, u32[]{:S(2)}) %all-to-all-start.1) | async-done | bytes 1048608 | tf_op jit(solution)/shard_map/all_to_all | solution.py:495
  218.6 4.8 %collective-permute-start.17 = (f32[512,512]{1,0:T(8,128)}, f32[512,512]{1,0:T(8,128)S(1)}, u32[]{:S(2)}, u32[]{:S(2)}) collective-permute-start(f32[512,512]{1,0:T(8,128)} %shard_map.119.mine_ref), channel_id=1, source_target_pairs={{0,1},{1,0},{2,3},{3,2},{4,5},{5,4},{6,7},{7,6},{8,9},{9,8},{10,11... | collective-permute-start | bytes 3145736 | tf_op jit(solution)/shard_map/ppermute | solution.py:400
  223.4 3.7 %shard_map.117 = f32[2,512,512]{2,1,0:T(8,128)} custom-call(f32[1,1]{1,0:T(1,128)} %bitcast.3.scale_ref, f32[2,512,512]{2,1,0:T(8,128)S(1)} %copy-done.6, f32[2,512,512]{2,1,0:T(8,128)} %collective-permute-done.9.left_ref.refs_2_, f32[2,96,512]{2,1,0:T(8,128)S(1)} %copy-done.14, f32[2,128,512]{2,1,0:T(8,128)} %collective-permute-done.14.refs_1_, ...), custom_call_target="tpu_custom_call" | custom-call | flops 1572864 | bytes 8388608 | tf_op jit(solution)/shard_map/pallas_call | solution.py:428
  227.1 1.5 shard_map.120
  (99 shorter events, 15.0 us)
Async XLA Ops:
  0.6 24.5 %copy-start = (f32[2,512,512]{2,1,0:T(8,128)S(1)}, f32[2,512,512]{2,1,0:T(8,128)}, u32[]{:S(2)}) copy-start(f32[2,512,512]{2,1,0:T(8,128)} %own_ref.11) | copy-start | bytes 6291460
  0.6 9.5 %copy-start.41 = (s32[2,2]{1,0:T(2,128)S(1)}, s32[2,2]{1,0:T(2,128)}, u32[]{:S(2)}) copy-start(s32[2,2]{1,0:T(2,128)} %param.12) | copy-start | bytes 52
  0.6 40.4 %collective-permute-start = (f32[2,512,512]{2,1,0:T(8,128)}, f32[2,512,512]{2,1,0:T(8,128)}, u32[]{:S(2)}, u32[]{:S(2)}) collective-permute-start(f32[2,512,512]{2,1,0:T(8,128)} %own_ref.11), channel_id=1, source_target_pairs={{1,0},{2,1},{3,2},{4,3},{5,4},{6,5},{7,6},{9,8},{10,9},{11,10},{12... | collective-permute-start | bytes 6291464 | tf_op jit(solution)/shard_map/ppermute | solution.py:396
  6.3 15.7 %collective-permute-start.1 = (f32[2,128,512]{2,1,0:T(8,128)}, f32[2,128,512]{2,1,0:T(8,128)}, u32[]{:S(2)}, u32[]{:S(2)}) collective-permute-start(f32[2,128,512]{2,1,0:T(8,128)} %get-tuple-element.57), channel_id=1, source_target_pairs={{8,0},{16,8},{24,16},{32,24},{40,32},{48,40},{56,48},{64,56},{72,6... | collective-permute-start | bytes 1572872 | tf_op jit(solution)/shard_map/ppermute | solution.py:396
  7.6 30.2 %collective-permute-start.3 = (f32[2,128,512]{2,1,0:T(8,128)}, f32[2,128,512]{2,1,0:T(8,128)}, u32[]{:S(2)}, u32[]{:S(2)}) collective-permute-start(f32[2,128,512]{2,1,0:T(8,128)} %get-tuple-element.56), channel_id=1, source_target_pairs={{8,0},{16,8},{24,16},{32,24},{40,32},{48,40},{56,48},{64,56},{72,6... | collective-permute-start | bytes 1572872 | tf_op jit(solution)/shard_map/ppermute | solution.py:396
  8.9 39.2 %collective-permute-start.5 = (f32[2,128,512]{2,1,0:T(8,128)}, f32[2,128,512]{2,1,0:T(8,128)}, u32[]{:S(2)}, u32[]{:S(2)}) collective-permute-start(f32[2,128,512]{2,1,0:T(8,128)} %get-tuple-element.55), channel_id=1, source_target_pairs={{8,0},{16,8},{24,16},{32,24},{40,32},{48,40},{56,48},{64,56},{72,6... | collective-permute-start | bytes 1572872 | tf_op jit(solution)/shard_map/ppermute | solution.py:396
  10.5 30.6 %copy-start.9 = (bf16[4,256,256]{2,1,0:T(8,128)(2,1)S(1)}, bf16[4,256,256]{2,1,0:T(8,128)(2,1)}, u32[]{:S(2)}) copy-start(bf16[4,256,256]{2,1,0:T(8,128)(2,1)} %constant.45.clone.mh_ref.refs_13_) | copy-start | bytes 1572868
  10.5 30.6 %copy-start.10 = (bf16[4,256,256]{2,1,0:T(8,128)(2,1)S(1)}, bf16[4,256,256]{2,1,0:T(8,128)(2,1)}, u32[]{:S(2)}) copy-start(bf16[4,256,256]{2,1,0:T(8,128)(2,1)} %constant.46.clone.ml_ref.refs_14_) | copy-start | bytes 1572868
  22.0 19.0 %collective-permute-start.2 = (f32[2,128,512]{2,1,0:T(8,128)}, f32[2,128,512]{2,1,0:T(8,128)}, u32[]{:S(2)}, u32[]{:S(2)}) collective-permute-start(f32[2,128,512]{2,1,0:T(8,128)} %collective-permute-done.1.below_ref.refs_1_), channel_id=1, source_target_pairs={{1,0},{2,1},{3,2},{4,3},{5,4},{6,5},{7,6},{9,8},{10,9},{11,10},{12... | collective-permute-start | bytes 1572872 | tf_op jit(solution)/shard_map/ppermute | solution.py:396
  25.1 1.6 copy-start.25
  26.7 1.6 copy-start.26
  33.9 2.0 copy-start.1
  36.4 1.3 copy-start.40
  37.8 11.1 %collective-permute-start.4 = (f32[2,128,512]{2,1,0:T(8,128)}, f32[2,128,512]{2,1,0:T(8,128)}, u32[]{:S(2)}, u32[]{:S(2)}) collective-permute-start(f32[2,128,512]{2,1,0:T(8,128)} %shard_map.106.below_ref.refs_1_), channel_id=1, source_target_pairs={{1,0},{2,1},{3,2},{4,3},{5,4},{6,5},{7,6},{9,8},{10,9},{11,10},{12... | collective-permute-start | bytes 1572872 | tf_op jit(solution)/shard_map/ppermute | solution.py:396
  39.7 16.2 %collective-permute-start.7 = (f32[2,128,512]{2,1,0:T(8,128)}, f32[2,128,512]{2,1,0:T(8,128)}, u32[]{:S(2)}, u32[]{:S(2)}) collective-permute-start(f32[2,128,512]{2,1,0:T(8,128)} %get-tuple-element.54), channel_id=1, source_target_pairs={{8,0},{16,8},{24,16},{32,24},{40,32},{48,40},{56,48},{64,56},{72,6... | collective-permute-start | bytes 1572872 | tf_op jit(solution)/shard_map/ppermute | solution.py:396
  41.0 2.2 copy-start.2
  48.9 2.2 copy-start.3
  55.9 11.1 %collective-permute-start.8 = (f32[2,128,512]{2,1,0:T(8,128)}, f32[2,128,512]{2,1,0:T(8,128)S(1)}, u32[]{:S(2)}, u32[]{:S(2)}) collective-permute-start(f32[2,128,512]{2,1,0:T(8,128)} %shard_map.110.below_ref), channel_id=1, source_target_pairs={{1,0},{2,1},{3,2},{4,3},{5,4},{6,5},{7,6},{9,8},{10,9},{11,10},{12... | collective-permute-start | bytes 1572872 | tf_op jit(solution)/shard_map/ppermute | solution.py:396
  58.4 14.2 %collective-permute-start.6 = (f32[2,128,512]{2,1,0:T(8,128)}, f32[2,128,512]{2,1,0:T(8,128)S(1)}, u32[]{:S(2)}, u32[]{:S(2)}) collective-permute-start(f32[2,128,512]{2,1,0:T(8,128)} %shard_map.108.below_ref.refs_1_), channel_id=1, source_target_pairs={{1,0},{2,1},{3,2},{4,3},{5,4},{6,5},{7,6},{9,8},{10,9},{11,10},{12... | collective-permute-start | bytes 1572872 | tf_op jit(solution)/shard_map/ppermute | solution.py:396
  67.0 2.2 copy-start.4
  71.8 3.9 %copy-start.22 = (f32[2,8,128]{2,1,0:T(8,128)S(1)}, f32[2,8,128]{2,1,0:T(8,128)}, u32[]{:S(2)}) copy-start(f32[2,8,128]{2,1,0:T(8,128)} %copy-done.21) | copy-start | bytes 24580
  71.8 3.9 %copy-start.28 = (f32[2,2,128,512]{3,2,1,0:T(8,128)S(1)}, f32[2,2,128,512]{3,2,1,0:T(8,128)}, u32[]{:S(2)}) copy-start(f32[2,2,128,512]{3,2,1,0:T(8,128)} %copy-done.27) | copy-start | bytes 3145732
  71.8 3.9 %copy-start.30 = (f32[2,2,128,512]{3,2,1,0:T(8,128)S(1)}, f32[2,2,128,512]{3,2,1,0:T(8,128)}, u32[]{:S(2)}) copy-start(f32[2,2,128,512]{3,2,1,0:T(8,128)} %copy-done.29) | copy-start | bytes 3145732
  71.8 3.9 %copy-start.32 = (f32[2,2,128,512]{3,2,1,0:T(8,128)S(1)}, f32[2,2,128,512]{3,2,1,0:T(8,128)}, u32[]{:S(2)}) copy-start(f32[2,2,128,512]{3,2,1,0:T(8,128)} %copy-done.31) | copy-start | bytes 3145732
  71.8 3.9 %copy-start.34 = (f32[2,2,128,512]{3,2,1,0:T(8,128)S(1)}, f32[2,2,128,512]{3,2,1,0:T(8,128)}, u32[]{:S(2)}) copy-start(f32[2,2,128,512]{3,2,1,0:T(8,128)} %copy-done.33) | copy-start | bytes 3145732
  71.8 3.9 %copy-start.37 = (bf16[4,256,256]{2,1,0:T(8,128)(2,1)S(1)}, bf16[4,256,256]{2,1,0:T(8,128)(2,1)}, u32[]{:S(2)}) copy-start(bf16[4,256,256]{2,1,0:T(8,128)(2,1)} %constant.43.clone.refs_11_) | copy-start | bytes 1572868
  71.8 3.9 %copy-start.38 = (bf16[4,256,256]{2,1,0:T(8,128)(2,1)S(1)}, bf16[4,256,256]{2,1,0:T(8,128)(2,1)}, u32[]{:S(2)}) copy-start(bf16[4,256,256]{2,1,0:T(8,128)(2,1)} %constant.44.clone.refs_12_) | copy-start | bytes 1572868
  91.9 9.3 %copy-start.17 = (f32[2,288,512]{2,1,0:T(8,128)}, f32[2,288,512]{2,1,0:T(8,128)S(1)}, u32[]{:S(2)}) copy-start(f32[2,288,512]{2,1,0:T(8,128)S(1)} %get-tuple-element.49.below_ref) | copy-start | bytes 3538948
  91.9 10.1 %copy-start.19 = (f32[2,128,512]{2,1,0:T(8,128)}, f32[2,128,512]{2,1,0:T(8,128)S(1)}, u32[]{:S(2)}) copy-start(f32[2,128,512]{2,1,0:T(8,128)S(1)} %get-tuple-element.47.below_ref) | copy-start | bytes 1572868
  92.0 10.1 %copy-start.35 = (f32[2,128,512]{2,1,0:T(8,128)}, f32[2,128,512]{2,1,0:T(8,128)S(1)}, u32[]{:S(2)}) copy-start(f32[2,128,512]{2,1,0:T(8,128)S(1)} %get-tuple-element.48) | copy-start | bytes 1572868
  92.0 9.1 %collective-permute-start.10 = (f32[512,640]{1,0:T(8,128)S(1)}, f32[512,640]{1,0:T(8,128)S(1)}, u32[]{:S(2)}, u32[]{:S(2)}) collective-permute-start(f32[512,640]{1,0:T(8,128)S(1)} %get-tuple-element.43), channel_id=1, source_target_pairs={{0,1},{1,0},{2,3},{3,2},{4,5},{5,4},{6,7},{7,6},{8,9},{9,8},{10,11... | collective-permute-start | bytes 3932168 | tf_op jit(solution)/shard_map/ppermute | solution.py:400
  92.1 9.0 %collective-permute-start.11 = (f32[2,96,512]{2,1,0:T(8,128)S(1)}, f32[2,96,512]{2,1,0:T(8,128)S(1)}, u32[]{:S(2)}, u32[]{:S(2)}) collective-permute-start(f32[2,96,512]{2,1,0:T(8,128)S(1)} %get-tuple-element.45), channel_id=1, source_target_pairs={{0,1},{1,2},{2,3},{3,4},{4,5},{5,6},{6,7},{8,9},{9,10},{10,11},{11... | collective-permute-start | bytes 1179656 | tf_op jit(solution)/shard_map/ppermute | solution.py:396
  96.4 69.9 %collective-permute-start.15 = (f32[2,288,512]{2,1,0:T(8,128)}, f32[2,288,512]{2,1,0:T(8,128)}, u32[]{:S(2)}, u32[]{:S(2)}) collective-permute-start(f32[2,288,512]{2,1,0:T(8,128)} %get-tuple-element.50), channel_id=1, source_target_pairs={{0,1},{1,2},{2,3},{3,4},{4,5},{5,6},{6,7},{8,9},{9,10},{10,11},{11... | collective-permute-start | bytes 3538952 | tf_op jit(solution)/shard_map/ppermute | solution.py:396
  103.1 72.6 %all-to-all-start = ((f32[64,8,640]{2,1,0:T(8,128)}), f32[64,8,640]{2,1,0:T(8,128)S(1)}, u32[]{:S(2)}, u32[]{:S(2)}) async-start(f32[64,8,640]{2,1,0:T(8,128)} %bitcast.13), calls=%async_computation | async-start | bytes 2621440 | tf_op jit(solution)/shard_map/all_to_all | solution.py:485
  115.4 50.8 %copy-start.18 = (f32[2,288,512]{2,1,0:T(8,128)S(1)}, f32[2,288,512]{2,1,0:T(8,128)}, u32[]{:S(2)}) copy-start(f32[2,288,512]{2,1,0:T(8,128)} %copy-done.17) | copy-start | bytes 3538948
  115.4 77.6 %collective-permute-start.9 = (f32[2,512,512]{2,1,0:T(8,128)}, f32[2,512,512]{2,1,0:T(8,128)}, u32[]{:S(2)}, u32[]{:S(2)}) collective-permute-start(f32[2,512,512]{2,1,0:T(8,128)} %get-tuple-element.41), channel_id=1, source_target_pairs={{0,1},{1,2},{2,3},{3,4},{4,5},{5,6},{6,7},{8,9},{9,10},{10,11},{11... | collective-permute-start | bytes 6291464 | tf_op jit(solution)/shard_map/ppermute | solution.py:396
  122.0 38.0 %collective-permute-start.13 = (f32[2,128,512]{2,1,0:T(8,128)}, f32[2,128,512]{2,1,0:T(8,128)S(1)}, u32[]{:S(2)}, u32[]{:S(2)}) collective-permute-start(f32[2,128,512]{2,1,0:T(8,128)} %copy-done.35), channel_id=1, source_target_pairs={{0,1},{1,2},{2,3},{3,4},{4,5},{5,6},{6,7},{8,9},{9,10},{10,11},{11... | collective-permute-start | bytes 1572872 | tf_op jit(solution)/shard_map/ppermute | solution.py:396
  123.9 36.0 %collective-permute-start.12 = (f32[2,96,512]{2,1,0:T(8,128)}, f32[2,96,512]{2,1,0:T(8,128)S(1)}, u32[]{:S(2)}, u32[]{:S(2)}) collective-permute-start(f32[2,96,512]{2,1,0:T(8,128)} %copy-done.36), channel_id=1, source_target_pairs={{0,8},{8,16},{16,24},{24,32},{32,40},{40,48},{48,56},{56,64},{64,7... | collective-permute-start | bytes 1179656 | tf_op jit(solution)/shard_map/ppermute | solution.py:396
  162.6 13.0 %collective-permute-start.14 = (f32[2,128,512]{2,1,0:T(8,128)}, f32[2,128,512]{2,1,0:T(8,128)}, u32[]{:S(2)}, u32[]{:S(2)}) collective-permute-start(f32[2,128,512]{2,1,0:T(8,128)} %shard_map.115.after_ref), channel_id=1, source_target_pairs={{0,8},{8,16},{16,24},{24,32},{32,40},{40,48},{48,56},{56,64},{64,7... | collective-permute-start | bytes 1572872 | tf_op jit(solution)/shard_map/ppermute | solution.py:396
  168.7 32.3 %collective-permute-start.16 = (f32[2,288,512]{2,1,0:T(8,128)}, f32[2,288,512]{2,1,0:T(8,128)}, u32[]{:S(2)}, u32[]{:S(2)}) collective-permute-start(f32[2,288,512]{2,1,0:T(8,128)} %shard_map.116.refs_2_), channel_id=1, source_target_pairs={{0,8},{8,16},{16,24},{24,32},{32,40},{40,48},{48,56},{56,64},{64,7... | collective-permute-start | bytes 3538952 | tf_op jit(solution)/shard_map/ppermute | solution.py:396
  176.9 1.1 copy-start.11
  177.9 39.7 %all-to-all-start.1 = ((f32[64,8,512]{2,1,0:T(8,128)}), f32[64,8,512]{2,1,0:T(8,128)S(1)}, u32[]{:S(2)}, u32[]{:S(2)}) async-start(f32[64,8,512]{2,1,0:T(8,128)} %copy-done.11), calls=%async_computation.1 | async-start | bytes 2097152 | tf_op jit(solution)/shard_map/all_to_all | solution.py:495
  189.9 1.6 copy-start.15
  191.7 1.3 copy-start.5
  218.6 4.8 %copy-start.6 = (f32[2,512,512]{2,1,0:T(8,128)S(1)}, f32[2,512,512]{2,1,0:T(8,128)}, u32[]{:S(2)}) copy-start(f32[2,512,512]{2,1,0:T(8,128)} %copy-done.5) | copy-start | bytes 6291460
  218.6 4.8 %copy-start.14 = (f32[2,96,512]{2,1,0:T(8,128)S(1)}, f32[2,96,512]{2,1,0:T(8,128)}, u32[]{:S(2)}) copy-start(f32[2,96,512]{2,1,0:T(8,128)} %copy-done.12) | copy-start | bytes 1179652
  218.6 8.5 %copy-start.8 = (f32[512,512]{1,0:T(8,128)S(1)}, f32[512,512]{1,0:T(8,128)}, u32[]{:S(2)}) copy-start(f32[512,512]{1,0:T(8,128)} %shard_map.119.mine_ref) | copy-start | bytes 3145732
  218.6 8.5 %collective-permute-start.17 = (f32[512,512]{1,0:T(8,128)}, f32[512,512]{1,0:T(8,128)S(1)}, u32[]{:S(2)}, u32[]{:S(2)}) collective-permute-start(f32[512,512]{1,0:T(8,128)} %shard_map.119.mine_ref), channel_id=1, source_target_pairs={{0,1},{1,0},{2,3},{3,2},{4,5},{5,4},{6,7},{7,6},{8,9},{9,8},{10,11... | collective-permute-start | bytes 3145736 | tf_op jit(solution)/shard_map/ppermute | solution.py:400
  (14 other events, 12.4 us)

commit v2 on v1

--- a/solution.py
+++ b/solution.py
@@ -11,11 +11,11 @@
 
 SIDE = 512
 QUARTER = 128
-PIECES = 4
-PIECE = SIDE // PIECES
-BACK = (96, 128, 288)
-CHUNKS = ((0, 96, 0, 0), (96, 128, 1, 0), (224, 144, 2, 0), (368, 144, 2, 144))
+SIZES = (192, 192, 128)
+FIRSTS = (0, 192, 384)
+PIECES = len(SIZES)
 WIDE = SIDE + 128
+COST = pl.CostEstimate(flops=0, bytes_accessed=0, transcendentals=0)
 F32 = jnp.float32
 BF16 = jnp.bfloat16
 
@@ -65,13 +65,17 @@
 
 
 def ready_kernel(
-    where_ref, probe_ref, own_ref, amp_ref, order_ref, rolled_ref, amps_ref, peaks_ref, columns
+    where_ref, probe_ref, own_ref, amp_ref, order_ref, *refs
 ):
+    rolled_refs = refs[:PIECES]
+    amps_ref, peaks_ref, columns = refs[PIECES:]
     for item in range(2):
         down, along = where_ref[0, item], where_ref[1, item]
         for part in range(2):
             value = pltpu.roll(probe_ref[part], down, 0)
-            rolled_ref[item, part] = pltpu.roll(value, along, 1)
+            value = pltpu.roll(value, along, 1)
+            for ref, first, size in zip(rolled_refs, FIRSTS, SIZES):
+                ref[item, part] = value[first : first + size]
         rows = amp_ref[item]
         high = rows.astype(BF16)
         rest = rows - high.astype(F32)
@@ -97,8 +101,8 @@
     spec_ref, wrapped_ref, token_ref,
 ):
     token_ref[...] = jnp.zeros_like(token_ref)
-    lane = lax.broadcasted_iota(jnp.int32, (PIECE, SIDE), 1)
-    row = lax.broadcasted_iota(jnp.int32, (PIECE, SIDE), 0) + piece * PIECE
+    lane = lax.broadcasted_iota(jnp.int32, (SIZES[piece], SIDE), 1)
+    row = lax.broadcasted_iota(jnp.int32, (SIZES[piece], SIDE), 0) + FIRSTS[piece]
     for item in range(2):
         down, along = where_ref[0, item], where_ref[1, item]
         above, beside = row < down, lane < along
@@ -123,37 +127,39 @@
 
 
 def fore(piece, where, own, right, below, diag, rolled, matrices):
-    def rows(*lead):
-        zeros = (0,) * len(lead)
-        return pl.BlockSpec(lead + (PIECE, SIDE), lambda i: zeros + (piece, 0))
-
-    full = pl.BlockSpec((2, PIECE, SIDE), lambda i: (0, 0, 0))
+    size = SIZES[piece]
+    at = FIRSTS[piece] // size
+    rows = pl.BlockSpec((2, size, SIDE), lambda i: (0, at, 0))
+    full = pl.BlockSpec((2, size, SIDE), lambda i: (0, 0, 0))
     whole = pl.BlockSpec((4, 2 * QUARTER, 2 * QUARTER), lambda i: (0, 0, 0))
-    four = pl.BlockSpec((2, 2, PIECE, SIDE), lambda i: (0, 0, 0, 0))
-    shape = jax.ShapeDtypeStruct((2, 2, PIECE, SIDE), F32)
+    four = pl.BlockSpec((2, 2, size, SIDE), lambda i: (0, 0, 0, 0))
+    shape = jax.ShapeDtypeStruct((2, 2, size, SIDE), F32)
     return pl.pallas_call(
         functools.partial(fore_kernel, piece),
         grid=(1,),
         out_shape=[shape, shape, jax.ShapeDtypeStruct((8, 128), F32)],
-        in_specs=[sm(), rows(2), rows(2), full, full, rows(2, 2), whole, whole],
+        in_specs=[sm(), rows, rows, full, full, four, whole, whole],
         out_specs=[four, four, pl.BlockSpec((8, 128), lambda i: (0, 0))],
         compiler_params=params(20),
-        cost_estimate=pl.CostEstimate(
-            flops=4 * 10**8, bytes_accessed=6 * 2**20, transcendentals=0
-        ),
+        cost_estimate=COST,
     )(where, own, right, below, diag, rolled, *matrices[2:])
 
 
+def rows_of(refs, item, part, first, last, lanes=slice(None)):
+    values = []
+    for ref, start, size in zip(refs, FIRSTS, SIZES):
+        low, high = max(first, start) - start, min(last, start + size) - start
+        if low < high:
+            values.append(ref[item, part, low:high, lanes])
+    return values[0] if len(values) == 1 else jnp.concatenate(values, axis=0)
+
+
 def update_kernel(where_ref, *refs):
-    spec_refs = refs[:PIECES]
-    wrapped_refs = refs[PIECES : 2 * PIECES]
-    rolled_ref, amps_ref, peaks_ref, lh_ref, ll_ref, mh_ref, ml_ref = refs[2 * PIECES : 2 * PIECES + 7]
-    outs = refs[2 * PIECES + 7 :]
-    count = len(BACK)
-    t_own_hbm, t_right_hbm = outs[:2]
-    t_below_hbm, t_diag_hbm = outs[2 : 2 + count], outs[2 + count : 2 + 2 * count]
-    keep_ref, send_ref = outs[2 + 2 * count : 4 + 2 * count]
-    high, low, grad, terms, out_sems = outs[4 + 2 * count :]
+    spec_refs, wrapped_refs, rolled_refs = refs[:PIECES], refs[PIECES : 2 * PIECES], refs[2 * PIECES : 3 * PIECES]
+    amps_ref, peaks_ref, lh_ref, ll_ref, mh_ref, ml_ref = refs[3 * PIECES : 3 * PIECES + 6]
+    outs = refs[3 * PIECES + 6 :]
+    targets, keep_ref, send_ref = outs[:4], outs[4], outs[5]
+    high, low, grad, terms, out_sems = outs[6:]
     core = where_ref[2, 0]
 
     wide = 2 * QUARTER
@@ -161,7 +167,11 @@
         for chunk in range(SIDE // wide):
             cols = slice(chunk * wide, (chunk + 1) * wide)
             blocks = [
-                (spec_refs[q][item, 0, :, cols], spec_refs[q][item, 1, :, cols]) for q in range(4)
+                tuple(
+                    rows_of(spec_refs, item, part, q * QUARTER, (q + 1) * QUARTER, cols)
+                    for part in range(2)
+                )
+                for q in range(4)
             ]
             back = []
             for p, (br, bi) in enumerate(fold(blocks, -1)):
@@ -186,8 +196,8 @@
                         low[item, rows, to] = lo[:, piece]
 
     stores = []
-    for first, size, piece, inside in CHUNKS:
-        at, within = slice(first, first + size), slice(inside, inside + size)
+    for piece, (first, size) in enumerate(zip(FIRSTS, SIZES)):
+        at = slice(first, first + size)
         lane = lax.broadcasted_iota(jnp.int32, (size, SIDE), 1)
         row = lax.broadcasted_iota(jnp.int32, (size, SIDE), 0) + first
         for item in range(2):
@@ -202,16 +212,8 @@
             back = fold(back, 1)
             back_r = jnp.concatenate([b[0] for b in back], axis=1)
             back_i = jnp.concatenate([b[1] for b in back], axis=1)
-            beam_r, beam_i = rolled_ref[item, 0, at, :], rolled_ref[item, 1, at, :]
-            patch = []
-            for part in range(2):
-                spans = [
-                    (k, max(first, k * PIECE) - k * PIECE, min(first + size, (k + 1) * PIECE) - k * PIECE)
-                    for k in range(PIECES)
-                ]
-                values = [wrapped_refs[k][item, part, lo:hi] for k, lo, hi in spans if lo < hi]
-                patch.append(values[0] if len(values) == 1 else jnp.concatenate(values, axis=0))
-            patch_r, patch_i = patch
+            beam_r, beam_i = rolled_refs[piece][item, 0], rolled_refs[piece][item, 1]
+            patch_r, patch_i = wrapped_refs[piece][item, 0], wrapped_refs[piece][item, 1]
             diff_r = back_r - (beam_r * patch_r - beam_i * patch_i)
             diff_i = back_i - (beam_r * patch_i + beam_i * patch_r)
             term = (beam_r * diff_r + beam_i * diff_i, beam_r * diff_i - beam_i * diff_r)
@@ -232,14 +234,8 @@
                         terms[k, part, at] = value
                     else:
                         terms[k, part, at] += value
-        targets = (
-            t_own_hbm.at[:, at],
-            t_right_hbm.at[:, at],
-            t_below_hbm[piece].at[:, within],
-            t_diag_hbm[piece].at[:, within],
-        )
         for k, target in enumerate(targets):
-            store = pltpu.make_async_copy(terms.at[k, :, at], target, out_sems.at[len(stores)])
+            store = pltpu.make_async_copy(terms.at[k, :, at], target.at[:, at], out_sems.at[len(stores)])
             store.start()
             stores.append(store)
     whole = []
@@ -279,45 +275,40 @@
 def ready(where, probe, own, amplitudes):
     return pl.pallas_call(
         ready_kernel,
-        out_shape=(
-            jax.ShapeDtypeStruct((2, 2, SIDE, SIDE), F32),
+        out_shape=tuple(jax.ShapeDtypeStruct((2, 2, size, SIDE), F32) for size in SIZES)
+        + (
             jax.ShapeDtypeStruct((2, SIDE, SIDE), F32),
             jax.ShapeDtypeStruct((2, 8, 128), F32),
         ),
         in_specs=[sm()] + [vm()] * 4,
-        out_specs=(vm(),) * 3,
+        out_specs=(vm(),) * (PIECES + 2),
         scratch_shapes=[pltpu.VMEM((4, SIDE, QUARTER), F32)],
         compiler_params=params(32),
-        cost_estimate=pl.CostEstimate(flops=4 * 10**9, bytes_accessed=14 * 2**20, transcendentals=0),
+        cost_estimate=COST,
     )(where, probe, own, amplitudes, jnp.asarray(order_matrix()))
 
 
 def update(where, specs, wrapped, rolled, amps, peaks, matrices):
     full = jax.ShapeDtypeStruct((2, SIDE, SIDE), F32)
-    parts = tuple(jax.ShapeDtypeStruct((2, size, SIDE), F32) for size in BACK)
     plane = jax.ShapeDtypeStruct((SIDE, WIDE), F32)
-    out_shape = (full, full) + parts + parts + (plane, plane)
-    count = len(BACK)
+    out_shape = (full,) * 4 + (plane, plane)
     four = pltpu.VMEM((2, 2, SIDE, SIDE), F32)
     half = pltpu.VMEM((2, SIDE, 2 * SIDE), BF16)
-    outs = pl.pallas_call(
+    return pl.pallas_call(
         update_kernel,
         out_shape=out_shape,
-        in_specs=[sm()] + [vm()] * (2 * PIECES + 7),
-        out_specs=(anywhere(),) * (2 + 2 * count) + (vm(), vm()),
+        in_specs=[sm()] + [vm()] * (3 * PIECES + 6),
+        out_specs=(anywhere(),) * 4 + (vm(), vm()),
         scratch_shapes=[
             half,
             half,
             four,
             pltpu.VMEM((4, 2, SIDE, SIDE), F32),
-            pltpu.SemaphoreType.DMA((4 * len(CHUNKS),)),
+            pltpu.SemaphoreType.DMA((4 * PIECES,)),
         ],
         compiler_params=params(36),
-        cost_estimate=pl.CostEstimate(
-            flops=5 * 10**9, bytes_accessed=26 * 2**20, transcendentals=2 * SIDE * SIDE
-        ),
-    )(where, *specs, *wrapped, rolled, amps, peaks, *matrices)
-    return outs[0], outs[1], outs[2 : 2 + count], outs[2 + count : 2 + 2 * count], outs[-2], outs[-1]
+        cost_estimate=COST,
+    )(where, *specs, *wrapped, *rolled, amps, peaks, *matrices)
 
 
 def nothing_kernel(*refs):
@@ -332,24 +323,24 @@
         in_specs=[anywhere()] * count,
         out_specs=[anywhere()] * len(values),
         input_output_aliases={k: k for k in range(len(values))},
+        cost_estimate=COST,
     )(*values, *after)
 
 
-def first_kernel(keep_ref, came_ref, below_ref, diag_ref, half_ref, lower_ref):
+def first_kernel(keep_ref, came_ref, half_ref):
     half_ref[:, :SIDE] = keep_ref[:, :SIDE] + came_ref[:, :SIDE]
     half_ref[:, SIDE:] = jnp.maximum(keep_ref[:, SIDE:], came_ref[:, SIDE:])
-    lower_ref[...] = below_ref[...] + diag_ref[...]
-
-
-def first_sums(keep, came, below, diag):
+
+
+def first_sum(keep, came):
     return pl.pallas_call(
         first_kernel,
-        out_shape=[jax.ShapeDtypeStruct(keep.shape, F32), jax.ShapeDtypeStruct(below.shape, F32)],
-        in_specs=[vm()] * 4,
-        out_specs=[vm()] * 2,
-        compiler_params=params(),
-        cost_estimate=pl.CostEstimate(flops=2 * keep.size, bytes_accessed=18 * keep.size, transcendentals=0),
-    )(keep, came, below, diag)
+        out_shape=jax.ShapeDtypeStruct(keep.shape, F32),
+        in_specs=[vm()] * 2,
+        out_specs=vm(),
+        compiler_params=params(),
+        cost_estimate=COST,
+    )(keep, came)
 
 
 def lower_kernel(below_ref, corner_ref, after_ref, lower_ref):
@@ -364,7 +355,7 @@
         in_specs=[vm(), vm(), anywhere()],
         out_specs=vm(),
         compiler_params=params(),
-        cost_estimate=pl.CostEstimate(flops=below.size, bytes_accessed=12 * below.size, transcendentals=0),
+        cost_estimate=COST,
     )(below, corner, after)
 
 
@@ -386,7 +377,7 @@
         in_specs=[vm()] * 2 + [anywhere()] * len(after),
         out_specs=vm(),
         compiler_params=params(),
-        cost_estimate=pl.CostEstimate(flops=2 * terms.size, bytes_accessed=8 * terms.size, transcendentals=0),
+        cost_estimate=COST,
     )(terms, start, *after)
 
 
@@ -411,28 +402,23 @@
         in_specs=[sm(), vm(), vm()],
         out_specs=vm(),
         compiler_params=params(),
-        cost_estimate=pl.CostEstimate(flops=2 * own.size, bytes_accessed=12 * own.size, transcendentals=0),
+        cost_estimate=COST,
     )(scale, own, t_own)
 
 
-def object_kernel(scale_ref, base_ref, left_ref, *refs):
-    out_ref = refs[-1]
-    first = 0
-    for ref, size in zip(refs, BACK):
-        at = slice(first, first + size)
-        out_ref[:, at, :] = base_ref[:, at, :] + scale_ref[0, 0] * (left_ref[:, at, :] + ref[...])
-        first += size
+def object_kernel(scale_ref, base_ref, left_ref, above_ref, out_ref):
+    out_ref[...] = base_ref[...] + scale_ref[0, 0] * (left_ref[...] + above_ref[...])
 
 
 def finished_object(scale, start, left, above):
     return pl.pallas_call(
         object_kernel,
         out_shape=jax.ShapeDtypeStruct(start.shape, F32),
-        in_specs=[sm(), vm(), vm()] + [vm()] * len(above),
-        out_specs=vm(),
-        compiler_params=params(),
-        cost_estimate=pl.CostEstimate(flops=3 * start.size, bytes_accessed=16 * start.size, transcendentals=0),
-    )(scale, start, left, *above)
+        in_specs=[sm()] + [vm()] * 3,
+        out_specs=vm(),
+        compiler_params=params(),
+        cost_estimate=COST,
+    )(scale, start, left, above)
 
 
 def probe_kernel(core_ref, mine_ref, other_ref, out_ref):
@@ -448,7 +434,7 @@
         in_specs=[sm(), vm(), vm()],
         out_specs=vm(),
         compiler_params=params(),
-        cost_estimate=pl.CostEstimate(flops=0, bytes_accessed=16 * SIDE * SIDE, transcendentals=0),
+        cost_estimate=COST,
     )(core, mine, other)
 
 
@@ -458,43 +444,39 @@
         [positions[:, 0] - row * SIDE, positions[:, 1] - col * SIDE, jnp.stack([core, row]).astype(jnp.int32)]
     )
     matrices = [jnp.asarray(m) for m in split_matrices()]
-    pieces = [object_field[:, k * PIECE : (k + 1) * PIECE] for k in range(PIECES)]
+    pieces = [object_field[:, first : first + size] for first, size in zip(FIRSTS, SIZES)]
     below = [shifted(piece, ROW, -1) for piece in pieces]
     right = shifted(object_field, COL, -1)
-    rolled, amps, peaks = ready(where, probe, object_field, amplitudes)
+    *rolled, amps, peaks = ready(where, probe, object_field, amplitudes)
     scale = 0.9 / (peaks[1, :1, :1] + 1e-06)
-    specs, wrapped, tokens = [], [], [peaks]
+    specs, wrapped, tokens = [], [], []
     for k in range(PIECES):
-        if k == 1:
-            (below[1],) = tied((below[1],), (below[0], peaks))
-        elif k > 1:
-            (below[k],) = tied((below[k],), (below[k - 1], tokens[k - 2]))
+        after = (tokens[k - 1],) if k > 1 else (peaks,)
+        after += (below[k - 1],) if k else ()
+        (below[k],) = tied((below[k],), after)
         corner = shifted(below[k], COL, -1)
-        spec, wrap, token = fore(k, where, object_field, right, below[k], corner, rolled, matrices)
+        spec, wrap, token = fore(k, where, object_field, right, below[k], corner, rolled[k], matrices)
         specs.append(spec)
         wrapped.append(wrap)
-        tokens[k:] = [token]
+        tokens.append(token)
     t_own, t_right, t_below, t_diag, keep, send = update(
         where, specs, wrapped, rolled, amps, peaks, matrices
     )
 
-    came = other_core(send)
-    corner = [shifted(t, COL, 1) for t in t_diag]
-    half, lower = first_sums(keep, came, t_below[0], corner[0])
+    corner = shifted(t_diag, COL, 1)
+    half = first_sum(keep, other_core(send))
     share = SIDE // 64
     terms = lax.all_to_all(half.reshape(64, share, WIDE), CHIPS, 0, 0)
-    from_above = [shifted(lower, ROW, 1)]
-    lower = lowered(t_below[1], corner[1], from_above[0])
-    from_above.append(shifted(lower, ROW, 1))
-    lower = lowered(t_below[2], corner[2], lower)
-    from_above.append(shifted(lower, ROW, 1))
+    lower = lowered(t_below, corner, half)
+    from_above = shifted(lower, ROW, 1)
+    (t_right,) = tied((t_right,), (lower,))
     from_left = shifted(t_right, COL, 1)
     at = lax.axis_index(CHIPS) * share
     start = lax.dynamic_slice(probe, (core, at, jnp.zeros_like(at)), (1, share, SIDE))[0]
-    shares = shared(terms, start, from_above[:2] + [lower])
+    shares = shared(terms, start, [lower])
     mine = lax.all_to_all(shares, CHIPS, 0, 0).reshape(SIDE, SIDE)
     begun = base(scale, object_field, t_own)
-    (mine,) = tied((mine,), (from_above[2], from_left, begun))
+    (mine,) = tied((mine,), (from_above, from_left, begun))
     new_probe = joined(core.astype(jnp.int32).reshape(1, 1), mine, other_core(mine))
     new_object = finished_object(scale, begun, from_left, from_above)
     return (new_object, new_probe)

time: 233 us -> 223 us (0.957)
  starting transfers between devices: 69.8 us -> 46.7 us
  waiting for transfers between devices: 83.3 us -> 105 us
  local copies, waits for them, and re-layouts: 33.5 us -> 29.6 us
  Pallas kernels: 39.9 us -> 36.4 us
    all_to_all x1, waiting for transfers between devices: 16.7 us -> 47 us  [on_device(): mine = lax.all_to_all(shares, CHIPS, 0, 0).reshape(SIDE, SIDE)]
    ppermute x16 -> x10, starting transfers between devices: 41.8 us -> 24.3 us  [shifted(): lax.ppermute(value, axis, [(source, source + steps) for source in range(f...]
    ppermute x16 -> x10, waiting for transfers between devices: 66.6 us -> 52.7 us  [shifted(): lax.ppermute(value, axis, [(source, source + steps) for source in range(f...]
    ppermute x2, waiting for transfers between devices: 0.01 us -> 5.42 us  [other_core(): return lax.ppermute(value, 'core', [(0, 1), (1, 0)])]
    ppermute x2, starting transfers between devices: 4.9 us -> 0.8 us  [other_core(): return lax.ppermute(value, 'core', [(0, 1), (1, 0)])]
    unnamed x84 -> x68, local copies, waits for them, and re-layouts: 29.4 us -> 25.6 us
    pallas_call x4 -> x3, Pallas kernels: 10.1 us -> 8.74 us  [fore(): pl.pallas_call(functools.partial(fore_kernel, piece), grid=(1,), out_shap...]
  transfers between devices with their start and end apart: 20 -> 14, of which waited for: 9 -> 7; matrix products, arithmetic and copies ran while one was open for 2% -> 2% of each run, Pallas kernels for 8% -> 8%
where the time goes in v2:
time: 223 us; the launch traced here: 220 us
  waiting for transfers between devices  105 us (47%)
  starting transfers between devices  46.7 us (21%)
  Pallas kernels  36.4 us (16%)
  local copies, waits for them, and re-layouts  29.6 us (13%)
    ppermute x10, waiting for transfers between devices, shifted(): lax.ppermute(value, axis, [(source, source + steps) for source in range(f...  52.7 us
    all_to_all x1, waiting for transfers between devices, on_device(): mine = lax.all_to_all(shares, CHIPS, 0, 0).reshape(SIDE, SIDE)  47 us
    unnamed x68, local copies, waits for them, and re-layouts  25.6 us
    ppermute x10, starting transfers between devices, shifted(): lax.ppermute(value, axis, [(source, source + steps) for source in range(f...  24.3 us
    pallas_call x1, Pallas kernels, update(): pl.pallas_call(update_kernel, out_shape=out_shape, in_specs=[sm()] + [vm(...  14.4 us
    all_to_all x1, starting transfers between devices, on_device(): terms = lax.all_to_all(half.reshape(64, share, WIDE), CHIPS, 0, 0)  11.6 us
    all_to_all x1, starting transfers between devices, on_device(): mine = lax.all_to_all(shares, CHIPS, 0, 0).reshape(SIDE, SIDE)  10 us
    pallas_call x3, Pallas kernels, fore(): pl.pallas_call(functools.partial(fore_kernel, piece), grid=(1,), out_shap...  8.74 us
  transfers between devices with their start and end apart: 14, of which 7 were waited for; matrix products, arithmetic and copies ran while one was open for 2% of the time, Pallas kernels for 8%

profile of v2, /device:TPU:33, one launch (start us, length us, event | category | flops | bytes accessed | tf_op | source)
XLA Modules:
  0.0 219.7 jit_solution(12375094574691014535)
XLA Ops:
  0.7 2.7 %collective-permute-start = (f32[2,512,512]{2,1,0:T(8,128)}, f32[2,512,512]{2,1,0:T(8,128)}, u32[]{:S(2)}, u32[]{:S(2)}) collective-permute-start(f32[2,512,512]{2,1,0:T(8,128)} %own_ref.9), channel_id=1, source_target_pairs={{1,0},{2,1},{3,2},{4,3},{5,4},{6,5},{7,6},{9,8},{10,9},{11,10},{12... | collective-permute-start | bytes 6291464 | tf_op jit(solution)/shard_map/ppermute | solution.py:387
  3.4 2.8 %fusion = (f32[2,192,512]{2,1,0:T(8,128)}, f32[2,192,512]{2,1,0:T(8,128)}) fusion(f32[2,512,512]{2,1,0:T(8,128)} %own_ref.9), kind=kLoop, calls=%fused_computation.5 | loop fusion | bytes 3145728 | tf_op jit(solution)/shard_map/slice | solution.py:447
  6.2 1.3 collective-permute-start.1
  7.4 1.3 collective-permute-start.3
  9.1 1.6 copy-done.18
  10.6 1.6 copy-done.20
  12.2 4.5 %shard_map.104 = (f32[2,2,192,512]{3,2,1,0:T(8,128)S(1)}, f32[2,2,192,512]{3,2,1,0:T(8,128)S(1)}, f32[2,2,128,512]{3,2,1,0:T(8,128)S(1)}, f32[2,512,512]{2,1,0:T(8,128)S(1)}, f32[2,8,128]{2,1,0:T(8,128)S(1)}) custom-call(s32[3,2]{1,0:T(4,128)S(1)} %pad_add_fusion.where_ref, f32[2,512,512]{2,1,0:T(8,128)S(1)} %copy-done.18, f32[2,512,512]{2,1,0:T(8,128)S(1)} %copy-done, ...), custom_call_target="tpu_custom_call" | custom-call | tf_op jit(solution)/shard_map/pallas_call | solution.py:276
  16.8 1.1 copy-done.9
  17.9 1.2 copy-done.12
  19.1 1.0 copy-done.16
  20.1 1.3 copy-done.22
  22.0 5.5 %collective-permute-done.1.refs_0_ = f32[2,192,512]{2,1,0:T(8,128)} collective-permute-done((f32[2,192,512]{2,1,0:T(8,128)}, f32[2,192,512]{2,1,0:T(8,128)}, u32[]{:S(2)}, u32[]{:S(2)}) %collective-permute-start.1) | collective-permute-done | bytes 786464 | tf_op jit(solution)/shard_map/ppermute | solution.py:387
  27.5 16.8 %collective-permute-done.3.refs_0_ = f32[2,192,512]{2,1,0:T(8,128)} collective-permute-done((f32[2,192,512]{2,1,0:T(8,128)}, f32[2,192,512]{2,1,0:T(8,128)}, u32[]{:S(2)}, u32[]{:S(2)}) %collective-permute-start.3) | collective-permute-done | bytes 786464 | tf_op jit(solution)/shard_map/ppermute | solution.py:387
  44.4 2.7 %collective-permute-start.4 = (f32[2,192,512]{2,1,0:T(8,128)}, f32[2,192,512]{2,1,0:T(8,128)S(1)}, u32[]{:S(2)}, u32[]{:S(2)}) collective-permute-start(f32[2,192,512]{2,1,0:T(8,128)} %shard_map.107.below_ref.refs_2_), channel_id=1, source_target_pairs={{1,0},{2,1},{3,2},{4,3},{5,4},{6,5},{7,6},{9,8},{10,9},{11,10},{12... | collective-permute-start | bytes 2359304 | tf_op jit(solution)/shard_map/ppermute | solution.py:387
  47.1 1.3 collective-permute-start.5
  48.4 1.9 collective-permute-start.2
  50.3 8.5 %collective-permute-done.4.diag_ref = f32[2,192,512]{2,1,0:T(8,128)S(1)} collective-permute-done((f32[2,192,512]{2,1,0:T(8,128)}, f32[2,192,512]{2,1,0:T(8,128)S(1)}, u32[]{:S(2)}, u32[]{:S(2)}) %collective-permute-start.4) | collective-permute-done | bytes 786464 | tf_op jit(solution)/shard_map/ppermute | solution.py:387
  58.9 1.4 copy-done.13
  60.3 2.6 %shard_map.108 = (f32[2,2,192,512]{3,2,1,0:T(8,128)S(1)}, f32[2,2,192,512]{3,2,1,0:T(8,128)S(1)}, f32[8,128]{1,0:T(8,128)S(1)}) custom-call(s32[3,2]{1,0:T(4,128)S(1)} %pad_add_fusion.where_ref, f32[2,512,512]{2,1,0:T(8,128)S(1)} %copy-done, f32[2,512,512]{2,1,0:T(8,128)} %collective-permute-done.right_ref, f32[2,192,512]{2,1,0:T(8,128)} %shard_map.107.below_ref.refs_2_, ...), custom_call_target="tpu_custom_call" | custom-call | tf_op jit(solution)/shard_map/pallas_call | solution.py:137
  62.9 1.2 copy-done.23
  64.1 1.2 copy-done.25
  65.9 2.1 collective-permute-start.6
  68.0 1.4 copy-done.10
  69.4 3.4 %shard_map.106 = (f32[2,2,192,512]{3,2,1,0:T(8,128)S(1)}, f32[2,2,192,512]{3,2,1,0:T(8,128)S(1)}, f32[8,128]{1,0:T(8,128)}) custom-call(s32[3,2]{1,0:T(4,128)S(1)} %pad_add_fusion.where_ref, f32[2,512,512]{2,1,0:T(8,128)S(1)} %copy-done, f32[2,512,512]{2,1,0:T(8,128)} %collective-permute-done.right_ref, f32[2,192,512]{2,1,0:T(8,128)} %shard_map.105.below_ref.refs_2_, ...), custom_call_target="tpu_custom_call" | custom-call | tf_op jit(solution)/shard_map/pallas_call | solution.py:137
  72.8 3.8 %collective-permute-done.6.diag_ref = f32[2,128,512]{2,1,0:T(8,128)S(1)} collective-permute-done((f32[2,128,512]{2,1,0:T(8,128)}, f32[2,128,512]{2,1,0:T(8,128)S(1)}, u32[]{:S(2)}, u32[]{:S(2)}) %collective-permute-start.6) | collective-permute-done | bytes 524320 | tf_op jit(solution)/shard_map/ppermute | solution.py:387
  76.7 2.7 %shard_map.110 = (f32[2,2,128,512]{3,2,1,0:T(8,128)S(1)}, f32[2,2,128,512]{3,2,1,0:T(8,128)S(1)}, f32[8,128]{1,0:T(8,128)}) custom-call(s32[3,2]{1,0:T(4,128)S(1)} %pad_add_fusion.where_ref, f32[2,512,512]{2,1,0:T(8,128)S(1)} %copy-done, f32[2,512,512]{2,1,0:T(8,128)} %collective-permute-done.right_ref, f32[2,128,512]{2,1,0:T(8,128)} %shard_map.109.below_ref, ...), custom_call_target="tpu_custom_call" | custom-call | tf_op jit(solution)/shard_map/pallas_call | solution.py:137
  80.0 14.4 %shard_map.111 = (f32[2,512,512]{2,1,0:T(8,128)}, f32[2,512,512]{2,1,0:T(8,128)}, f32[2,512,512]{2,1,0:T(8,128)}, f32[2,512,512]{2,1,0:T(8,128)}, f32[512,640]{1,0:T(8,128)S(1)}, /*index=5*/f32[512,640]{1,0:T(8,128)S(1)}) custom-call(s32[3,2]{1,0:T(4,128)S(1)} %pad_add_fusion.where_ref, f32[2,2,192,512]{3,2,1,0:T(8,128)S(1)} %get-tuple-element.22.refs_0_, ...), custom_call_target="tpu_custom_call" | custom-call | tf_op jit(solution)/shard_map/pallas_call | solution.py:297
  94.4 1.9 collective-permute-start.7
  96.9 5.4 %collective-permute-done.8.came_ref = f32[512,640]{1,0:T(8,128)S(1)} collective-permute-done((f32[512,640]{1,0:T(8,128)S(1)}, f32[512,640]{1,0:T(8,128)S(1)}, u32[]{:S(2)}, u32[]{:S(2)}) %collective-permute-start.8) | collective-permute-done | bytes 1310752 | tf_op jit(solution)/shard_map/ppermute | solution.py:391
  102.3 1.2 shard_map.113.after_ref
  103.5 11.6 %all-to-all-start = ((f32[64,8,640]{2,1,0:T(8,128)}), f32[64,8,640]{2,1,0:T(8,128)S(1)}, u32[]{:S(2)}, u32[]{:S(2)}) async-start(f32[64,8,640]{2,1,0:T(8,128)} %bitcast.5), calls=%async_computation | async-start | bytes 2621440 | tf_op jit(solution)/shard_map/all_to_all | solution.py:469
  115.1 18.1 %collective-permute-done.7.corner_ref = f32[2,512,512]{2,1,0:T(8,128)} collective-permute-done((f32[2,512,512]{2,1,0:T(8,128)}, f32[2,512,512]{2,1,0:T(8,128)}, u32[]{:S(2)}, u32[]{:S(2)}) %collective-permute-start.7) | collective-permute-done | bytes 2097184 | tf_op jit(solution)/shard_map/ppermute | solution.py:387
  133.3 1.6 copy-done.21
  134.8 1.8 shard_map.114.refs_1_.refs_0_
  136.7 1.3 copy-done.1
  138.0 4.6 %collective-permute-start.9 = (f32[2,512,512]{2,1,0:T(8,128)}, f32[2,512,512]{2,1,0:T(8,128)}, u32[]{:S(2)}, u32[]{:S(2)}) collective-permute-start(f32[2,512,512]{2,1,0:T(8,128)} %shard_map.115), channel_id=1, source_target_pairs={{0,1},{1,2},{2,3},{3,4},{4,5},{5,6},{6,7},{8,9},{9,10},{10,11},{11... | collective-permute-start | bytes 6291464 | tf_op jit(solution)/shard_map/ppermute | solution.py:387
  142.5 4.5 %collective-permute-start.10 = (f32[2,512,512]{2,1,0:T(8,128)}, f32[2,512,512]{2,1,0:T(8,128)}, u32[]{:S(2)}, u32[]{:S(2)}) collective-permute-start(f32[2,512,512]{2,1,0:T(8,128)} %copy-done.1), channel_id=1, source_target_pairs={{0,8},{8,16},{16,24},{24,32},{32,40},{40,48},{48,56},{56,64},{64,7... | collective-permute-start | bytes 6291464 | tf_op jit(solution)/shard_map/ppermute | solution.py:387
  147.1 0.7 dynamic-slice_bitcast_fusion.start_ref
  147.8 1.6 copy-done.2
  149.6 1.0 copy-done.15
  150.5 10.0 %all-to-all-start.1 = ((f32[64,8,512]{2,1,0:T(8,128)}), f32[64,8,512]{2,1,0:T(8,128)S(1)}, u32[]{:S(2)}, u32[]{:S(2)}) async-start(f32[64,8,512]{2,1,0:T(8,128)} %copy-done.15), calls=%async_computation.1 | async-start | bytes 2097152 | tf_op jit(solution)/shard_map/all_to_all | solution.py:477
  161.8 1.6 copy-done.19
  163.6 1.3 copy-done.3
  164.9 47.0 %all-to-all-done.1 = f32[64,8,512]{2,1,0:T(8,128)S(1)} async-done(((f32[64,8,512]{2,1,0:T(8,128)}), f32[64,8,512]{2,1,0:T(8,128)S(1)}, u32[]{:S(2)}, u32[]{:S(2)}) %all-to-all-start.1) | async-done | bytes 1048608 | tf_op jit(solution)/shard_map/all_to_all | solution.py:477
  211.9 1.0 copy-done.5
  213.1 1.4 copy-done.4
  214.4 3.8 %shard_map.116 = f32[2,512,512]{2,1,0:T(8,128)} custom-call(f32[1,1]{1,0:T(1,128)} %bitcast.3.scale_ref, f32[2,512,512]{2,1,0:T(8,128)S(1)} %copy-done.4, f32[2,512,512]{2,1,0:T(8,128)} %collective-permute-done.9.left_ref.refs_2_, f32[2,512,512]{2,1,0:T(8,128)} %collective-permute-done.10.above_ref.refs_1_), custom_call_target="tpu_custom_call" | custom-call | tf_op jit(solution)/shard_map/pallas_call | solution.py:414
  218.3 1.5 shard_map.119
  (71 shorter events, 3.9 us)
Async XLA Ops:
  0.6 8.4 %copy-start.29 = (bf16[512,512]{1,0:T(8,128)(2,1)S(1)}, bf16[512,512]{1,0:T(8,128)(2,1)}, u32[]{:S(2)}) copy-start(bf16[512,512]{1,0:T(8,128)(2,1)} %constant.47.clone.order_ref) | copy-start | bytes 1572868
  0.6 8.4 %copy-start = (f32[2,512,512]{2,1,0:T(8,128)S(1)}, f32[2,512,512]{2,1,0:T(8,128)}, u32[]{:S(2)}) copy-start(f32[2,512,512]{2,1,0:T(8,128)} %own_ref.9) | copy-start | bytes 6291460
  0.7 8.2 %copy-start.33 = (s32[2,2]{1,0:T(2,128)S(1)}, s32[2,2]{1,0:T(2,128)}, u32[]{:S(2)}) copy-start(s32[2,2]{1,0:T(2,128)} %param.12) | copy-start | bytes 52
  0.7 58.2 %collective-permute-start = (f32[2,512,512]{2,1,0:T(8,128)}, f32[2,512,512]{2,1,0:T(8,128)}, u32[]{:S(2)}, u32[]{:S(2)}) collective-permute-start(f32[2,512,512]{2,1,0:T(8,128)} %own_ref.9), channel_id=1, source_target_pairs={{1,0},{2,1},{3,2},{4,3},{5,4},{6,5},{7,6},{9,8},{10,9},{11,10},{12... | collective-permute-start | bytes 6291464 | tf_op jit(solution)/shard_map/ppermute | solution.py:387
  6.2 21.4 %collective-permute-start.1 = (f32[2,192,512]{2,1,0:T(8,128)}, f32[2,192,512]{2,1,0:T(8,128)}, u32[]{:S(2)}, u32[]{:S(2)}) collective-permute-start(f32[2,192,512]{2,1,0:T(8,128)} %get-tuple-element.41), channel_id=1, source_target_pairs={{8,0},{16,8},{24,16},{32,24},{40,32},{48,40},{56,48},{64,56},{72,6... | collective-permute-start | bytes 2359304 | tf_op jit(solution)/shard_map/ppermute | solution.py:387
  7.4 36.9 %collective-permute-start.3 = (f32[2,192,512]{2,1,0:T(8,128)}, f32[2,192,512]{2,1,0:T(8,128)}, u32[]{:S(2)}, u32[]{:S(2)}) collective-permute-start(f32[2,192,512]{2,1,0:T(8,128)} %get-tuple-element.40), channel_id=1, source_target_pairs={{8,0},{16,8},{24,16},{32,24},{40,32},{48,40},{56,48},{64,56},{72,6... | collective-permute-start | bytes 2359304 | tf_op jit(solution)/shard_map/ppermute | solution.py:387
  9.0 1.6 copy-start.18
  10.6 1.6 copy-start.20
  16.8 1.1 copy-start.9
  17.9 1.2 copy-start.12
  19.1 1.0 copy-start.16
  20.1 1.3 copy-start.22
  21.4 0.6 copy-start.30
  27.5 31.4 %copy-start.7 = (bf16[4,256,256]{2,1,0:T(8,128)(2,1)S(1)}, bf16[4,256,256]{2,1,0:T(8,128)(2,1)}, u32[]{:S(2)}) copy-start(bf16[4,256,256]{2,1,0:T(8,128)(2,1)} %constant.45.clone.mh_ref.refs_13_) | copy-start | bytes 1572868
  27.5 31.4 %copy-start.8 = (bf16[4,256,256]{2,1,0:T(8,128)(2,1)S(1)}, bf16[4,256,256]{2,1,0:T(8,128)(2,1)}, u32[]{:S(2)}) copy-start(bf16[4,256,256]{2,1,0:T(8,128)(2,1)} %constant.46.clone.ml_ref.refs_14_) | copy-start | bytes 1572868
  44.4 14.5 %collective-permute-start.4 = (f32[2,192,512]{2,1,0:T(8,128)}, f32[2,192,512]{2,1,0:T(8,128)S(1)}, u32[]{:S(2)}, u32[]{:S(2)}) collective-permute-start(f32[2,192,512]{2,1,0:T(8,128)} %shard_map.107.below_ref.refs_2_), channel_id=1, source_target_pairs={{1,0},{2,1},{3,2},{4,3},{5,4},{6,5},{7,6},{9,8},{10,9},{11,10},{12... | collective-permute-start | bytes 2359304 | tf_op jit(solution)/shard_map/ppermute | solution.py:387
  47.1 18.8 %collective-permute-start.5 = (f32[2,128,512]{2,1,0:T(8,128)S(1)}, f32[2,128,512]{2,1,0:T(8,128)}, u32[]{:S(2)}, u32[]{:S(2)}) collective-permute-start(f32[2,128,512]{2,1,0:T(8,128)S(1)} %slice.23), channel_id=1, source_target_pairs={{8,0},{16,8},{24,16},{32,24},{40,32},{48,40},{56,48},{64,56},{72,6... | collective-permute-start | bytes 1572872 | tf_op jit(solution)/shard_map/ppermute | solution.py:387
  48.4 19.6 %collective-permute-start.2 = (f32[2,192,512]{2,1,0:T(8,128)}, f32[2,192,512]{2,1,0:T(8,128)}, u32[]{:S(2)}, u32[]{:S(2)}) collective-permute-start(f32[2,192,512]{2,1,0:T(8,128)} %shard_map.105.below_ref.refs_2_), channel_id=1, source_target_pairs={{1,0},{2,1},{3,2},{4,3},{5,4},{6,5},{7,6},{9,8},{10,9},{11,10},{12... | collective-permute-start | bytes 2359304 | tf_op jit(solution)/shard_map/ppermute | solution.py:387
  58.9 1.4 copy-start.13
  62.9 1.2 copy-start.23
  64.1 1.2 copy-start.25
  65.3 0.6 copy-start.32
  65.9 10.7 %collective-permute-start.6 = (f32[2,128,512]{2,1,0:T(8,128)}, f32[2,128,512]{2,1,0:T(8,128)S(1)}, u32[]{:S(2)}, u32[]{:S(2)}) collective-permute-start(f32[2,128,512]{2,1,0:T(8,128)} %shard_map.109.below_ref), channel_id=1, source_target_pairs={{1,0},{2,1},{3,2},{4,3},{5,4},{6,5},{7,6},{9,8},{10,9},{11,10},{12... | collective-permute-start | bytes 1572872 | tf_op jit(solution)/shard_map/ppermute | solution.py:387
  68.0 1.4 copy-start.10
  69.4 7.2 %copy-start.17 = (f32[2,2,128,512]{3,2,1,0:T(8,128)S(1)}, f32[2,2,128,512]{3,2,1,0:T(8,128)}, u32[]{:S(2)}) copy-start(f32[2,2,128,512]{3,2,1,0:T(8,128)} %copy-done.16) | copy-start | bytes 3145732
  76.6 2.8 %copy-start.11 = (f32[2,2,192,512]{3,2,1,0:T(8,128)S(1)}, f32[2,2,192,512]{3,2,1,0:T(8,128)}, u32[]{:S(2)}) copy-start(f32[2,2,192,512]{3,2,1,0:T(8,128)} %copy-done.9) | copy-start | bytes 4718596
  76.6 2.8 %copy-start.14 = (f32[2,2,192,512]{3,2,1,0:T(8,128)S(1)}, f32[2,2,192,512]{3,2,1,0:T(8,128)}, u32[]{:S(2)}) copy-start(f32[2,2,192,512]{3,2,1,0:T(8,128)} %copy-done.12) | copy-start | bytes 4718596
  76.6 2.8 %copy-start.24 = (f32[2,2,192,512]{3,2,1,0:T(8,128)S(1)}, f32[2,2,192,512]{3,2,1,0:T(8,128)}, u32[]{:S(2)}) copy-start(f32[2,2,192,512]{3,2,1,0:T(8,128)} %copy-done.23) | copy-start | bytes 4718596
  76.6 3.1 %copy-start.26 = (f32[2,2,192,512]{3,2,1,0:T(8,128)S(1)}, f32[2,2,192,512]{3,2,1,0:T(8,128)}, u32[]{:S(2)}) copy-start(f32[2,2,192,512]{3,2,1,0:T(8,128)} %copy-done.25) | copy-start | bytes 4718596
  76.6 3.2 %copy-start.27 = (bf16[4,256,256]{2,1,0:T(8,128)(2,1)S(1)}, bf16[4,256,256]{2,1,0:T(8,128)(2,1)}, u32[]{:S(2)}) copy-start(bf16[4,256,256]{2,1,0:T(8,128)(2,1)} %constant.43.clone.refs_11_) | copy-start | bytes 1572868
  76.6 3.3 %copy-start.28 = (bf16[4,256,256]{2,1,0:T(8,128)(2,1)S(1)}, bf16[4,256,256]{2,1,0:T(8,128)(2,1)}, u32[]{:S(2)}) copy-start(bf16[4,256,256]{2,1,0:T(8,128)(2,1)} %constant.44.clone.refs_12_) | copy-start | bytes 1572868
  76.6 3.3 %copy-start.31 = (f32[2,8,128]{2,1,0:T(8,128)S(1)}, f32[2,8,128]{2,1,0:T(8,128)}, u32[]{:S(2)}) copy-start(f32[2,8,128]{2,1,0:T(8,128)} %copy-done.30) | copy-start | bytes 24580
  94.4 38.8 %collective-permute-start.7 = (f32[2,512,512]{2,1,0:T(8,128)}, f32[2,512,512]{2,1,0:T(8,128)}, u32[]{:S(2)}, u32[]{:S(2)}) collective-permute-start(f32[2,512,512]{2,1,0:T(8,128)} %get-tuple-element.35), channel_id=1, source_target_pairs={{0,1},{1,2},{2,3},{3,4},{4,5},{5,6},{6,7},{8,9},{9,10},{10,11},{11... | collective-permute-start | bytes 6291464 | tf_op jit(solution)/shard_map/ppermute | solution.py:387
  96.3 6.0 %collective-permute-start.8 = (f32[512,640]{1,0:T(8,128)S(1)}, f32[512,640]{1,0:T(8,128)S(1)}, u32[]{:S(2)}, u32[]{:S(2)}) collective-permute-start(f32[512,640]{1,0:T(8,128)S(1)} %get-tuple-element.37), channel_id=1, source_target_pairs={{0,1},{1,0},{2,3},{3,2},{4,5},{5,4},{6,7},{7,6},{8,9},{9,8},{10,11... | collective-permute-start | bytes 3932168 | tf_op jit(solution)/shard_map/ppermute | solution.py:391
  103.5 44.3 %all-to-all-start = ((f32[64,8,640]{2,1,0:T(8,128)}), f32[64,8,640]{2,1,0:T(8,128)S(1)}, u32[]{:S(2)}, u32[]{:S(2)}) async-start(f32[64,8,640]{2,1,0:T(8,128)} %bitcast.5), calls=%async_computation | async-start | bytes 2621440 | tf_op jit(solution)/shard_map/all_to_all | solution.py:469
  133.2 1.6 copy-start.21
  136.6 1.3 copy-start.1
  138.0 73.9 %collective-permute-start.9 = (f32[2,512,512]{2,1,0:T(8,128)}, f32[2,512,512]{2,1,0:T(8,128)}, u32[]{:S(2)}, u32[]{:S(2)}) collective-permute-start(f32[2,512,512]{2,1,0:T(8,128)} %shard_map.115), channel_id=1, source_target_pairs={{0,1},{1,2},{2,3},{3,4},{4,5},{5,6},{6,7},{8,9},{9,10},{10,11},{11... | collective-permute-start | bytes 6291464 | tf_op jit(solution)/shard_map/ppermute | solution.py:387
  142.5 69.4 %collective-permute-start.10 = (f32[2,512,512]{2,1,0:T(8,128)}, f32[2,512,512]{2,1,0:T(8,128)}, u32[]{:S(2)}, u32[]{:S(2)}) collective-permute-start(f32[2,512,512]{2,1,0:T(8,128)} %copy-done.1), channel_id=1, source_target_pairs={{0,8},{8,16},{16,24},{24,32},{32,40},{40,48},{48,56},{56,64},{64,7... | collective-permute-start | bytes 6291464 | tf_op jit(solution)/shard_map/ppermute | solution.py:387
  147.8 1.6 copy-start.2
  149.6 1.0 copy-start.15
  150.5 61.4 %all-to-all-start.1 = ((f32[64,8,512]{2,1,0:T(8,128)}), f32[64,8,512]{2,1,0:T(8,128)S(1)}, u32[]{:S(2)}, u32[]{:S(2)}) async-start(f32[64,8,512]{2,1,0:T(8,128)} %copy-done.15), calls=%async_computation.1 | async-start | bytes 2097152 | tf_op jit(solution)/shard_map/all_to_all | solution.py:477
  161.8 1.6 copy-start.19
  163.6 1.3 copy-start.3
  211.9 1.0 copy-start.5
  212.9 1.6 copy-start.4
  212.9 5.4 %copy-start.6 = (f32[512,512]{1,0:T(8,128)S(1)}, f32[512,512]{1,0:T(8,128)}, u32[]{:S(2)}) copy-start(f32[512,512]{1,0:T(8,128)} %shard_map.118.mine_ref) | copy-start | bytes 3145732
  212.9 5.4 %collective-permute-start.11 = (f32[512,512]{1,0:T(8,128)}, f32[512,512]{1,0:T(8,128)S(1)}, u32[]{:S(2)}, u32[]{:S(2)}) collective-permute-start(f32[512,512]{1,0:T(8,128)} %shard_map.118.mine_ref), channel_id=1, source_target_pairs={{0,1},{1,0},{2,3},{3,2},{4,5},{5,4},{6,7},{7,6},{8,9},{9,8},{10,11... | collective-permute-start | bytes 3145736 | tf_op jit(solution)/shard_map/ppermute | solution.py:391

commit v3 on v2

--- a/solution.py
+++ b/solution.py
@@ -11,10 +11,11 @@
 
 SIDE = 512
 QUARTER = 128
-SIZES = (192, 192, 128)
-FIRSTS = (0, 192, 384)
+SIZES = (128,) * 4
+FIRSTS = (0, 128, 256, 384)
+BACK = (128, 384)
+WIDE = SIDE + 128
 PIECES = len(SIZES)
-WIDE = SIDE + 128
 COST = pl.CostEstimate(flops=0, bytes_accessed=0, transcendentals=0)
 F32 = jnp.float32
 BF16 = jnp.bfloat16
@@ -128,8 +129,7 @@
 
 def fore(piece, where, own, right, below, diag, rolled, matrices):
     size = SIZES[piece]
-    at = FIRSTS[piece] // size
-    rows = pl.BlockSpec((2, size, SIDE), lambda i: (0, at, 0))
+    tile = pl.BlockSpec((2, size, SIDE), lambda i: (0, piece, 0))
     full = pl.BlockSpec((2, size, SIDE), lambda i: (0, 0, 0))
     whole = pl.BlockSpec((4, 2 * QUARTER, 2 * QUARTER), lambda i: (0, 0, 0))
     four = pl.BlockSpec((2, 2, size, SIDE), lambda i: (0, 0, 0, 0))
@@ -138,7 +138,7 @@
         functools.partial(fore_kernel, piece),
         grid=(1,),
         out_shape=[shape, shape, jax.ShapeDtypeStruct((8, 128), F32)],
-        in_specs=[sm(), rows, rows, full, full, four, whole, whole],
+        in_specs=[sm(), tile, tile, full, full, four, whole, whole],
         out_specs=[four, four, pl.BlockSpec((8, 128), lambda i: (0, 0))],
         compiler_params=params(20),
         cost_estimate=COST,
@@ -158,8 +158,8 @@
     spec_refs, wrapped_refs, rolled_refs = refs[:PIECES], refs[PIECES : 2 * PIECES], refs[2 * PIECES : 3 * PIECES]
     amps_ref, peaks_ref, lh_ref, ll_ref, mh_ref, ml_ref = refs[3 * PIECES : 3 * PIECES + 6]
     outs = refs[3 * PIECES + 6 :]
-    targets, keep_ref, send_ref = outs[:4], outs[4], outs[5]
-    high, low, grad, terms, out_sems = outs[6:]
+    targets, keep_ref, send_ref = outs[:6], outs[6], outs[7]
+    high, low, grad, terms, out_sems = outs[8:]
     core = where_ref[2, 0]
 
     wide = 2 * QUARTER
@@ -196,7 +196,8 @@
                         low[item, rows, to] = lo[:, piece]
 
     stores = []
-    for piece, (first, size) in enumerate(zip(FIRSTS, SIZES)):
+    size = QUARTER
+    for first in range(0, SIDE, size):
         at = slice(first, first + size)
         lane = lax.broadcasted_iota(jnp.int32, (size, SIDE), 1)
         row = lax.broadcasted_iota(jnp.int32, (size, SIDE), 0) + first
@@ -212,8 +213,8 @@
             back = fold(back, 1)
             back_r = jnp.concatenate([b[0] for b in back], axis=1)
             back_i = jnp.concatenate([b[1] for b in back], axis=1)
-            beam_r, beam_i = rolled_refs[piece][item, 0], rolled_refs[piece][item, 1]
-            patch_r, patch_i = wrapped_refs[piece][item, 0], wrapped_refs[piece][item, 1]
+            beam_r, beam_i = (rows_of(rolled_refs, item, part, first, first + size) for part in range(2))
+            patch_r, patch_i = (rows_of(wrapped_refs, item, part, first, first + size) for part in range(2))
             diff_r = back_r - (beam_r * patch_r - beam_i * patch_i)
             diff_i = back_i - (beam_r * patch_i + beam_i * patch_r)
             term = (beam_r * diff_r + beam_i * diff_i, beam_r * diff_i - beam_i * diff_r)
@@ -234,8 +235,16 @@
                         terms[k, part, at] = value
                     else:
                         terms[k, part, at] += value
-        for k, target in enumerate(targets):
-            store = pltpu.make_async_copy(terms.at[k, :, at], target.at[:, at], out_sems.at[len(stores)])
+        half = int(first >= BACK[0])
+        within = slice(first - half * BACK[0], first - half * BACK[0] + size)
+        parts = (
+            targets[0].at[:, at],
+            targets[1].at[:, at],
+            targets[2 + half].at[:, within],
+            targets[4 + half].at[:, within],
+        )
+        for k, target in enumerate(parts):
+            store = pltpu.make_async_copy(terms.at[k, :, at], target, out_sems.at[len(stores)])
             store.start()
             stores.append(store)
     whole = []
@@ -291,20 +300,21 @@
 def update(where, specs, wrapped, rolled, amps, peaks, matrices):
     full = jax.ShapeDtypeStruct((2, SIDE, SIDE), F32)
     plane = jax.ShapeDtypeStruct((SIDE, WIDE), F32)
-    out_shape = (full,) * 4 + (plane, plane)
+    parts = tuple(jax.ShapeDtypeStruct((2, size, SIDE), F32) for size in BACK)
+    out_shape = (full,) * 2 + parts * 2 + (plane, plane)
     four = pltpu.VMEM((2, 2, SIDE, SIDE), F32)
     half = pltpu.VMEM((2, SIDE, 2 * SIDE), BF16)
     return pl.pallas_call(
         update_kernel,
         out_shape=out_shape,
         in_specs=[sm()] + [vm()] * (3 * PIECES + 6),
-        out_specs=(anywhere(),) * 4 + (vm(), vm()),
+        out_specs=(anywhere(),) * 6 + (vm(), vm()),
         scratch_shapes=[
             half,
             half,
             four,
             pltpu.VMEM((4, 2, SIDE, SIDE), F32),
-            pltpu.SemaphoreType.DMA((4 * PIECES,)),
+            pltpu.SemaphoreType.DMA((16,)),
         ],
         compiler_params=params(36),
         cost_estimate=COST,
@@ -327,20 +337,21 @@
     )(*values, *after)
 
 
-def first_kernel(keep_ref, came_ref, half_ref):
+def first_kernel(keep_ref, came_ref, below_ref, corner_ref, half_ref, lower_ref):
     half_ref[:, :SIDE] = keep_ref[:, :SIDE] + came_ref[:, :SIDE]
     half_ref[:, SIDE:] = jnp.maximum(keep_ref[:, SIDE:], came_ref[:, SIDE:])
-
-
-def first_sum(keep, came):
+    lower_ref[...] = below_ref[...] + corner_ref[...]
+
+
+def first_sums(keep, came, below, corner):
     return pl.pallas_call(
         first_kernel,
-        out_shape=jax.ShapeDtypeStruct(keep.shape, F32),
-        in_specs=[vm()] * 2,
-        out_specs=vm(),
+        out_shape=(jax.ShapeDtypeStruct(keep.shape, F32), jax.ShapeDtypeStruct(below.shape, F32)),
+        in_specs=[vm()] * 4,
+        out_specs=(vm(), vm()),
         compiler_params=params(),
         cost_estimate=COST,
-    )(keep, came)
+    )(keep, came, below, corner)
 
 
 def lower_kernel(below_ref, corner_ref, after_ref, lower_ref):
@@ -391,34 +402,42 @@
     return lax.ppermute(value, "core", [(0, 1), (1, 0)])
 
 
-def base_kernel(scale_ref, own_ref, t_own_ref, base_ref):
+def base_kernel(scale_ref, own_ref, t_own_ref, base_ref, token_ref):
     base_ref[...] = own_ref[...] + scale_ref[0, 0] * t_own_ref[...]
+    token_ref[...] = jnp.zeros_like(token_ref)
 
 
 def base(scale, own, t_own):
+    rows = pl.BlockSpec((2, QUARTER, SIDE), lambda i: (0, i, 0))
     return pl.pallas_call(
         base_kernel,
-        out_shape=jax.ShapeDtypeStruct(own.shape, F32),
-        in_specs=[sm(), vm(), vm()],
-        out_specs=vm(),
+        grid=(4,),
+        out_shape=(jax.ShapeDtypeStruct(own.shape, F32), jax.ShapeDtypeStruct((8, 128), F32)),
+        in_specs=[sm(), rows, rows],
+        out_specs=(rows, pl.BlockSpec((8, 128), lambda i: (0, 0))),
         compiler_params=params(),
         cost_estimate=COST,
     )(scale, own, t_own)
 
 
-def object_kernel(scale_ref, base_ref, left_ref, above_ref, out_ref):
-    out_ref[...] = base_ref[...] + scale_ref[0, 0] * (left_ref[...] + above_ref[...])
+def object_kernel(scale_ref, base_ref, left_ref, first_ref, second_ref, out_ref):
+    above = jnp.where(pl.program_id(0) < 1, first_ref[...], second_ref[...])
+    out_ref[...] = base_ref[...] + scale_ref[0, 0] * (left_ref[...] + above)
 
 
 def finished_object(scale, start, left, above):
+    rows = pl.BlockSpec((2, QUARTER, SIDE), lambda i: (0, i, 0))
+    first = pl.BlockSpec((2, QUARTER, SIDE), lambda i: (0, 0, 0))
+    second = pl.BlockSpec((2, QUARTER, SIDE), lambda i: (0, jnp.maximum(i, 1) - 1, 0))
     return pl.pallas_call(
         object_kernel,
+        grid=(4,),
         out_shape=jax.ShapeDtypeStruct(start.shape, F32),
-        in_specs=[sm()] + [vm()] * 3,
-        out_specs=vm(),
+        in_specs=[sm(), rows, rows, first, second],
+        out_specs=rows,
         compiler_params=params(),
         cost_estimate=COST,
-    )(scale, start, left, above)
+    )(scale, start, left, *above)
 
 
 def probe_kernel(core_ref, mine_ref, other_ref, out_ref):
@@ -445,38 +464,40 @@
     )
     matrices = [jnp.asarray(m) for m in split_matrices()]
     pieces = [object_field[:, first : first + size] for first, size in zip(FIRSTS, SIZES)]
-    below = [shifted(piece, ROW, -1) for piece in pieces]
     right = shifted(object_field, COL, -1)
     *rolled, amps, peaks = ready(where, probe, object_field, amplitudes)
     scale = 0.9 / (peaks[1, :1, :1] + 1e-06)
     specs, wrapped, tokens = [], [], []
-    for k in range(PIECES):
-        after = (tokens[k - 1],) if k > 1 else (peaks,)
-        after += (below[k - 1],) if k else ()
-        (below[k],) = tied((below[k],), after)
-        corner = shifted(below[k], COL, -1)
-        spec, wrap, token = fore(k, where, object_field, right, below[k], corner, rolled[k], matrices)
+    for k, piece in enumerate(pieces):
+        below = shifted(piece, ROW, -1)
+        if k == 3:
+            (below,) = tied((below,), tokens[:2])
+        corner = shifted(below, COL, -1)
+        spec, wrap, token = fore(k, where, object_field, right, below, corner, rolled[k], matrices)
         specs.append(spec)
         wrapped.append(wrap)
         tokens.append(token)
-    t_own, t_right, t_below, t_diag, keep, send = update(
+    t_own, t_right, *parts, keep, send = update(
         where, specs, wrapped, rolled, amps, peaks, matrices
     )
 
-    corner = shifted(t_diag, COL, 1)
-    half = first_sum(keep, other_core(send))
+    corner = shifted(parts[2], COL, 1)
+    half, lower = first_sums(keep, other_core(send), parts[0], corner)
+    (corner,) = tied((parts[3],), (half,))
+    corner = shifted(corner, COL, 1)
     share = SIDE // 64
     terms = lax.all_to_all(half.reshape(64, share, WIDE), CHIPS, 0, 0)
-    lower = lowered(t_below, corner, half)
-    from_above = shifted(lower, ROW, 1)
+    from_above = [shifted(lower, ROW, 1)]
+    at = lax.axis_index(CHIPS) * share
+    start = lax.dynamic_slice(probe, (core, at, jnp.zeros_like(at)), (1, share, SIDE))[0]
+    shares = shared(terms, start, [from_above[0], corner])
+    lower = lowered(parts[1], corner, shares)
+    from_above.append(shifted(lower, ROW, 1))
     (t_right,) = tied((t_right,), (lower,))
     from_left = shifted(t_right, COL, 1)
-    at = lax.axis_index(CHIPS) * share
-    start = lax.dynamic_slice(probe, (core, at, jnp.zeros_like(at)), (1, share, SIDE))[0]
-    shares = shared(terms, start, [lower])
     mine = lax.all_to_all(shares, CHIPS, 0, 0).reshape(SIDE, SIDE)
-    begun = base(scale, object_field, t_own)
-    (mine,) = tied((mine,), (from_above, from_left, begun))
+    begun, token = base(scale, object_field, t_own)
+    (mine,) = tied((mine,), (from_above[1], from_left, token))
     new_probe = joined(core.astype(jnp.int32).reshape(1, 1), mine, other_core(mine))
     new_object = finished_object(scale, begun, from_left, from_above)
     return (new_object, new_probe)

time: 223 us -> 220 us (0.987)
  starting transfers between devices: 46.7 us -> 62.1 us
  waiting for transfers between devices: 105 us -> 89.9 us
  local copies, waits for them, and re-layouts: 29.6 us -> 24.2 us
    ppermute x10 -> x14, starting transfers between devices: 24.3 us -> 40.1 us  [shifted(): lax.ppermute(value, axis, [(source, source + steps) for source in range(f...]
    all_to_all x1, waiting for transfers between devices: 47 us -> 39.5 us  [on_device(): mine = lax.all_to_all(shares, CHIPS, 0, 0).reshape(SIDE, SIDE)]
    ppermute x2, waiting for transfers between devices: 5.42 us -> 0.01 us  [other_core(): return lax.ppermute(value, 'core', [(0, 1), (1, 0)])]
    unnamed x68 -> x78, local copies, waits for them, and re-layouts: 25.6 us -> 20.3 us
    ppermute x10 -> x14, waiting for transfers between devices: 52.7 us -> 50.3 us  [shifted(): lax.ppermute(value, axis, [(source, source + steps) for source in range(f...]
    pallas_call x3 -> x4, Pallas kernels: 8.74 us -> 10.1 us  [fore(): pl.pallas_call(functools.partial(fore_kernel, piece), grid=(1,), out_shap...]
  transfers between devices with their start and end apart: 14 -> 18, of which waited for: 7 -> 6; matrix products, arithmetic and copies ran while one was open for 2% -> 2% of each run, Pallas kernels for 8% -> 8%
where the time goes in v3:
time: 220 us; the launch traced here: 216 us
  waiting for transfers between devices  89.9 us (41%)
  starting transfers between devices  62.1 us (28%)
  Pallas kernels  37.9 us (17%)
  local copies, waits for them, and re-layouts  24.2 us (11%)
    ppermute x14, waiting for transfers between devices, shifted(): lax.ppermute(value, axis, [(source, source + steps) for source in range(f...  50.3 us
    ppermute x14, starting transfers between devices, shifted(): lax.ppermute(value, axis, [(source, source + steps) for source in range(f...  40.1 us
    all_to_all x1, waiting for transfers between devices, on_device(): mine = lax.all_to_all(shares, CHIPS, 0, 0).reshape(SIDE, SIDE)  39.5 us
    unnamed x78, local copies, waits for them, and re-layouts  20.3 us
    pallas_call x1, Pallas kernels, update(): pl.pallas_call(update_kernel, out_shape=out_shape, in_specs=[sm()] + [vm(...  13.5 us
    all_to_all x1, starting transfers between devices, on_device(): terms = lax.all_to_all(half.reshape(64, share, WIDE), CHIPS, 0, 0)  11.4 us
    all_to_all x1, starting transfers between devices, on_device(): mine = lax.all_to_all(shares, CHIPS, 0, 0).reshape(SIDE, SIDE)  10.1 us
    pallas_call x4, Pallas kernels, fore(): pl.pallas_call(functools.partial(fore_kernel, piece), grid=(1,), out_shap...  10.1 us
  transfers between devices with their start and end apart: 18, of which 6 were waited for; matrix products, arithmetic and copies ran while one was open for 2% of the time, Pallas kernels for 8%

profile of v3, /device:TPU:33, one launch (start us, length us, event | category | flops | bytes accessed | tf_op | source)
XLA Modules:
  0.0 216.3 jit_solution(2082679377469582338)
XLA Ops:
  0.6 2.7 %collective-permute-start = (f32[2,512,512]{2,1,0:T(8,128)}, f32[2,512,512]{2,1,0:T(8,128)}, u32[]{:S(2)}, u32[]{:S(2)}) collective-permute-start(f32[2,512,512]{2,1,0:T(8,128)} %own_ref.11), channel_id=1, source_target_pairs={{1,0},{2,1},{3,2},{4,3},{5,4},{6,5},{7,6},{9,8},{10,9},{11,10},{12... | collective-permute-start | bytes 6291464 | tf_op jit(solution)/shard_map/ppermute | solution.py:398
  3.4 2.7 %fusion = (f32[2,128,512]{2,1,0:T(8,128)}, f32[2,128,512]{2,1,0:T(8,128)}, f32[2,128,512]{2,1,0:T(8,128)S(1)}, f32[2,128,512]{2,1,0:T(8,128)S(1)}) fusion(f32[2,512,512]{2,1,0:T(8,128)} %own_ref.11), kind=kLoop, calls=%fused_computation.5 | loop fusion | bytes 4194304 | tf_op jit(solution)/shard_map/slice | solution.py:466
  6.1 1.3 collective-permute-start.3
  7.4 1.3 collective-permute-start.1
  8.7 1.3 collective-permute-start.5
  10.0 11.6 %collective-permute-done.3.below_ref = f32[2,128,512]{2,1,0:T(8,128)} collective-permute-done((f32[2,128,512]{2,1,0:T(8,128)S(1)}, f32[2,128,512]{2,1,0:T(8,128)}, u32[]{:S(2)}, u32[]{:S(2)}) %collective-permute-start.3) | collective-permute-done | bytes 524320 | tf_op jit(solution)/shard_map/ppermute | solution.py:398
  21.6 3.1 %collective-permute-start.4 = (f32[2,128,512]{2,1,0:T(8,128)}, f32[2,128,512]{2,1,0:T(8,128)}, u32[]{:S(2)}, u32[]{:S(2)}) collective-permute-start(f32[2,128,512]{2,1,0:T(8,128)} %collective-permute-done.3.below_ref), channel_id=1, source_target_pairs={{1,0},{2,1},{3,2},{4,3},{5,4},{6,5},{7,6},{9,8},{10,9},{11,10},{12... | collective-permute-start | bytes 1572872 | tf_op jit(solution)/shard_map/ppermute | solution.py:398
  24.7 8.1 %collective-permute-done.1.below_ref = f32[2,128,512]{2,1,0:T(8,128)} collective-permute-done((f32[2,128,512]{2,1,0:T(8,128)S(1)}, f32[2,128,512]{2,1,0:T(8,128)}, u32[]{:S(2)}, u32[]{:S(2)}) %collective-permute-start.1) | collective-permute-done | bytes 524320 | tf_op jit(solution)/shard_map/ppermute | solution.py:398
  32.8 3.1 %collective-permute-start.2 = (f32[2,128,512]{2,1,0:T(8,128)}, f32[2,128,512]{2,1,0:T(8,128)}, u32[]{:S(2)}, u32[]{:S(2)}) collective-permute-start(f32[2,128,512]{2,1,0:T(8,128)} %collective-permute-done.1.below_ref), channel_id=1, source_target_pairs={{1,0},{2,1},{3,2},{4,3},{5,4},{6,5},{7,6},{9,8},{10,9},{11,10},{12... | collective-permute-start | bytes 1572872 | tf_op jit(solution)/shard_map/ppermute | solution.py:398
  35.9 1.3 collective-permute-start.7
  37.5 1.6 copy-done.16
  39.1 1.6 copy-done.17
  40.7 1.0 copy-done.33
  41.8 4.5 %shard_map.104 = (f32[2,2,128,512]{3,2,1,0:T(8,128)S(1)}, f32[2,2,128,512]{3,2,1,0:T(8,128)S(1)}, f32[2,2,128,512]{3,2,1,0:T(8,128)S(1)}, f32[2,2,128,512]{3,2,1...) custom-call(s32[3,2]{1,0:T(4,128)S(1)} %pad_add_fusion.where_ref, f32[2,512,512]{2,1,0:T(8,128)S(1)} %copy-done.16, ...), custom_call_target="tpu_custom_call" | custom-call | tf_op jit(solution)/shard_map/pallas_call | solution.py:285
  46.4 1.9 collective-permute-start.6
  48.3 2.3 %shard_map.106 = (f32[2,2,128,512]{3,2,1,0:T(8,128)S(1)}, f32[2,2,128,512]{3,2,1,0:T(8,128)S(1)}, f32[8,128]{1,0:T(8,128)S(1)}) custom-call(s32[3,2]{1,0:T(4,128)S(1)} %pad_add_fusion.where_ref, f32[2,512,512]{2,1,0:T(8,128)S(1)} %copy-done, f32[2,512,512]{2,1,0:T(8,128)} %collective-permute-done.right_ref, f32[2,128,512]{2,1,0:T(8,128)} %collective-permute-done.3.below_ref, ...), custom_call_target="tpu_custom_call" | custom-call | tf_op jit(solution)/shard_map/pallas_call | solution.py:137
  50.7 1.0 copy-done.23
  51.7 1.0 copy-done.25
  52.6 2.3 %shard_map.105 = (f32[2,2,128,512]{3,2,1,0:T(8,128)S(1)}, f32[2,2,128,512]{3,2,1,0:T(8,128)S(1)}, f32[8,128]{1,0:T(8,128)S(1)}) custom-call(s32[3,2]{1,0:T(4,128)S(1)} %pad_add_fusion.where_ref, f32[2,512,512]{2,1,0:T(8,128)S(1)} %copy-done, f32[2,512,512]{2,1,0:T(8,128)} %collective-permute-done.right_ref, f32[2,128,512]{2,1,0:T(8,128)} %collective-permute-done.1.below_ref, ...), custom_call_target="tpu_custom_call" | custom-call | tf_op jit(solution)/shard_map/pallas_call | solution.py:137
  54.9 1.0 copy-done.27
  55.9 1.0 copy-done.29
  57.5 2.1 collective-permute-start.8
  59.6 1.2 copy-done.12
  60.8 2.9 %shard_map.107 = (f32[2,2,128,512]{3,2,1,0:T(8,128)S(1)}, f32[2,2,128,512]{3,2,1,0:T(8,128)S(1)}, f32[8,128]{1,0:T(8,128)}) custom-call(s32[3,2]{1,0:T(4,128)S(1)} %pad_add_fusion.where_ref, f32[2,512,512]{2,1,0:T(8,128)S(1)} %copy-done, f32[2,512,512]{2,1,0:T(8,128)} %collective-permute-done.right_ref, f32[2,128,512]{2,1,0:T(8,128)} %collective-permute-done.5.below_ref, ...), custom_call_target="tpu_custom_call" | custom-call | tf_op jit(solution)/shard_map/pallas_call | solution.py:137
  63.7 4.5 %collective-permute-done.8.diag_ref = f32[2,128,512]{2,1,0:T(8,128)S(1)} collective-permute-done((f32[2,128,512]{2,1,0:T(8,128)}, f32[2,128,512]{2,1,0:T(8,128)S(1)}, u32[]{:S(2)}, u32[]{:S(2)}) %collective-permute-start.8) | collective-permute-done | bytes 524320 | tf_op jit(solution)/shard_map/ppermute | solution.py:398
  68.2 2.7 %shard_map.109 = (f32[2,2,128,512]{3,2,1,0:T(8,128)S(1)}, f32[2,2,128,512]{3,2,1,0:T(8,128)S(1)}, f32[8,128]{1,0:T(8,128)}) custom-call(s32[3,2]{1,0:T(4,128)S(1)} %pad_add_fusion.where_ref, f32[2,512,512]{2,1,0:T(8,128)S(1)} %copy-done, f32[2,512,512]{2,1,0:T(8,128)} %collective-permute-done.right_ref, f32[2,128,512]{2,1,0:T(8,128)} %shard_map.108.below_ref, ...), custom_call_target="tpu_custom_call" | custom-call | tf_op jit(solution)/shard_map/pallas_call | solution.py:137
  71.6 13.5 %shard_map.110 = (f32[2,512,512]{2,1,0:T(8,128)}, f32[2,512,512]{2,1,0:T(8,128)}, f32[2,128,512]{2,1,0:T(8,128)S(1)}, f32[2,384,512]{2,1,0:T(8,128)}, f32[2,128,...) custom-call(s32[3,2]{1,0:T(4,128)S(1)} %pad_add_fusion.where_ref, ...), custom_call_target="tpu_custom_call" | custom-call | tf_op jit(solution)/shard_map/pallas_call | solution.py:307
  85.2 3.9 %collective-permute-start.10 = (f32[2,128,512]{2,1,0:T(8,128)S(1)}, f32[2,128,512]{2,1,0:T(8,128)S(1)}, u32[]{:S(2)}, u32[]{:S(2)}) collective-permute-start(f32[2,128,512]{2,1,0:T(8,128)S(1)} %get-tuple-element.54), channel_id=1, source_target_pairs={{0,1},{1,2},{2,3},{3,4},{4,5},{5,6},{6,7},{8,9},{9,10},{10,11},{11... | collective-permute-start | bytes 1572872 | tf_op jit(solution)/shard_map/ppermute | solution.py:398
  89.1 6.1 %collective-permute-done.10.corner_ref = f32[2,128,512]{2,1,0:T(8,128)S(1)} collective-permute-done((f32[2,128,512]{2,1,0:T(8,128)S(1)}, f32[2,128,512]{2,1,0:T(8,128)S(1)}, u32[]{:S(2)}, u32[]{:S(2)}) %collective-permute-start.10) | collective-permute-done | bytes 524320 | tf_op jit(solution)/shard_map/ppermute | solution.py:398
  95.2 1.2 shard_map.112
  96.5 0.8 copy-done.37
  97.3 4.4 %collective-permute-start.11 = (f32[2,384,512]{2,1,0:T(8,128)}, f32[2,384,512]{2,1,0:T(8,128)}, u32[]{:S(2)}, u32[]{:S(2)}) collective-permute-start(f32[2,384,512]{2,1,0:T(8,128)} %shard_map.113), channel_id=1, source_target_pairs={{0,1},{1,2},{2,3},{3,4},{4,5},{5,6},{6,7},{8,9},{9,10},{10,11},{11... | collective-permute-start | bytes 4718600 | tf_op jit(solution)/shard_map/ppermute | solution.py:398
  101.7 11.4 %all-to-all-start = ((f32[64,8,640]{2,1,0:T(8,128)}), f32[64,8,640]{2,1,0:T(8,128)S(1)}, u32[]{:S(2)}, u32[]{:S(2)}) async-start(f32[64,8,640]{2,1,0:T(8,128)} %bitcast.4), calls=%async_computation | async-start | bytes 2621440 | tf_op jit(solution)/shard_map/all_to_all | solution.py:489
  113.1 3.9 %collective-permute-start.12 = (f32[2,128,512]{2,1,0:T(8,128)}, f32[2,128,512]{2,1,0:T(8,128)}, u32[]{:S(2)}, u32[]{:S(2)}) collective-permute-start(f32[2,128,512]{2,1,0:T(8,128)} %copy-done.37), channel_id=1, source_target_pairs={{0,8},{8,16},{16,24},{24,32},{32,40},{40,48},{48,56},{56,64},{64,7... | collective-permute-start | bytes 1572872 | tf_op jit(solution)/shard_map/ppermute | solution.py:398
  117.7 19.9 %collective-permute-done.12.refs_0_.first_ref = f32[2,128,512]{2,1,0:T(8,128)} collective-permute-done((f32[2,128,512]{2,1,0:T(8,128)}, f32[2,128,512]{2,1,0:T(8,128)}, u32[]{:S(2)}, u32[]{:S(2)}) %collective-permute-start.12) | collective-permute-done | bytes 524320 | tf_op jit(solution)/shard_map/ppermute | solution.py:398
  137.9 1.6 copy-done.22
  139.4 1.6 shard_map.115.refs_1_
  141.0 1.1 copy-done.6
  142.2 4.6 %collective-permute-start.13 = (f32[2,512,512]{2,1,0:T(8,128)}, f32[2,512,512]{2,1,0:T(8,128)}, u32[]{:S(2)}, u32[]{:S(2)}) collective-permute-start(f32[2,512,512]{2,1,0:T(8,128)} %shard_map.116), channel_id=1, source_target_pairs={{0,1},{1,2},{2,3},{3,4},{4,5},{5,6},{6,7},{8,9},{9,10},{10,11},{11... | collective-permute-start | bytes 6291464 | tf_op jit(solution)/shard_map/ppermute | solution.py:398
  146.7 5.3 %collective-permute-start.14 = (f32[2,384,512]{2,1,0:T(8,128)}, f32[2,384,512]{2,1,0:T(8,128)}, u32[]{:S(2)}, u32[]{:S(2)}) collective-permute-start(f32[2,384,512]{2,1,0:T(8,128)} %copy-done.6), channel_id=1, source_target_pairs={{0,8},{8,16},{16,24},{24,32},{32,40},{40,48},{48,56},{56,64},{64,7... | collective-permute-start | bytes 4718600 | tf_op jit(solution)/shard_map/ppermute | solution.py:398
  152.1 10.1 %all-to-all-start.1 = ((f32[64,8,512]{2,1,0:T(8,128)}), f32[64,8,512]{2,1,0:T(8,128)S(1)}, u32[]{:S(2)}, u32[]{:S(2)}) async-start(f32[64,8,512]{2,1,0:T(8,128)} %copy-done.5), calls=%async_computation.1 | async-start | bytes 2097152 | tf_op jit(solution)/shard_map/all_to_all | solution.py:498
  163.4 1.6 copy-done.18
  165.7 1.3 copy-done.19
  167.6 39.5 %all-to-all-done.1 = f32[64,8,512]{2,1,0:T(8,128)S(1)} async-done(((f32[64,8,512]{2,1,0:T(8,128)}), f32[64,8,512]{2,1,0:T(8,128)S(1)}, u32[]{:S(2)}, u32[]{:S(2)}) %all-to-all-start.1) | async-done | bytes 1048608 | tf_op jit(solution)/shard_map/all_to_all | solution.py:498
  207.2 1.1 copy-done.3
  208.6 1.6 copy-done.20
  210.2 4.6 %shard_map.117 = f32[2,512,512]{2,1,0:T(8,128)} custom-call(f32[1,1]{1,0:T(1,128)} %bitcast.3.scale_ref, f32[2,512,512]{2,1,0:T(8,128)S(1)} %copy-done.20, f32[2,512,512]{2,1,0:T(8,128)} %collective-permute-done.13.left_ref.refs_2_, f32[2,128,512]{2,1,0:T(8,128)} %collective-permute-done.12.refs_0_.first_ref, ...), custom_call_target="tpu_custom_call" | custom-call | tf_op jit(solution)/shard_map/pallas_call | solution.py:432
  214.8 1.5 shard_map.119
  (88 shorter events, 4.8 us)
Async XLA Ops:
  0.6 36.9 %copy-start = (f32[2,512,512]{2,1,0:T(8,128)S(1)}, f32[2,512,512]{2,1,0:T(8,128)}, u32[]{:S(2)}) copy-start(f32[2,512,512]{2,1,0:T(8,128)} %own_ref.11) | copy-start | bytes 6291460
  0.6 36.7 %copy-start.38 = (s32[2,2]{1,0:T(2,128)S(1)}, s32[2,2]{1,0:T(2,128)}, u32[]{:S(2)}) copy-start(s32[2,2]{1,0:T(2,128)} %param.12) | copy-start | bytes 52
  0.6 47.7 %collective-permute-start = (f32[2,512,512]{2,1,0:T(8,128)}, f32[2,512,512]{2,1,0:T(8,128)}, u32[]{:S(2)}, u32[]{:S(2)}) collective-permute-start(f32[2,512,512]{2,1,0:T(8,128)} %own_ref.11), channel_id=1, source_target_pairs={{1,0},{2,1},{3,2},{4,3},{5,4},{6,5},{7,6},{9,8},{10,9},{11,10},{12... | collective-permute-start | bytes 6291464 | tf_op jit(solution)/shard_map/ppermute | solution.py:398
  6.1 15.5 %collective-permute-start.3 = (f32[2,128,512]{2,1,0:T(8,128)S(1)}, f32[2,128,512]{2,1,0:T(8,128)}, u32[]{:S(2)}, u32[]{:S(2)}) collective-permute-start(f32[2,128,512]{2,1,0:T(8,128)S(1)} %get-tuple-element.62), channel_id=1, source_target_pairs={{8,0},{16,8},{24,16},{32,24},{40,32},{48,40},{56,48},{64,56},{72,6... | collective-permute-start | bytes 1572872 | tf_op jit(solution)/shard_map/ppermute | solution.py:398
  7.4 25.5 %collective-permute-start.1 = (f32[2,128,512]{2,1,0:T(8,128)S(1)}, f32[2,128,512]{2,1,0:T(8,128)}, u32[]{:S(2)}, u32[]{:S(2)}) collective-permute-start(f32[2,128,512]{2,1,0:T(8,128)S(1)} %get-tuple-element.63), channel_id=1, source_target_pairs={{8,0},{16,8},{24,16},{32,24},{40,32},{48,40},{56,48},{64,56},{72,6... | collective-permute-start | bytes 1572872 | tf_op jit(solution)/shard_map/ppermute | solution.py:398
  8.7 37.7 %collective-permute-start.5 = (f32[2,128,512]{2,1,0:T(8,128)}, f32[2,128,512]{2,1,0:T(8,128)}, u32[]{:S(2)}, u32[]{:S(2)}) collective-permute-start(f32[2,128,512]{2,1,0:T(8,128)} %get-tuple-element.61), channel_id=1, source_target_pairs={{8,0},{16,8},{24,16},{32,24},{40,32},{48,40},{56,48},{64,56},{72,6... | collective-permute-start | bytes 1572872 | tf_op jit(solution)/shard_map/ppermute | solution.py:398
  21.6 26.7 %collective-permute-start.4 = (f32[2,128,512]{2,1,0:T(8,128)}, f32[2,128,512]{2,1,0:T(8,128)}, u32[]{:S(2)}, u32[]{:S(2)}) collective-permute-start(f32[2,128,512]{2,1,0:T(8,128)} %collective-permute-done.3.below_ref), channel_id=1, source_target_pairs={{1,0},{2,1},{3,2},{4,3},{5,4},{6,5},{7,6},{9,8},{10,9},{11,10},{12... | collective-permute-start | bytes 1572872 | tf_op jit(solution)/shard_map/ppermute | solution.py:398
  32.8 19.8 %collective-permute-start.2 = (f32[2,128,512]{2,1,0:T(8,128)}, f32[2,128,512]{2,1,0:T(8,128)}, u32[]{:S(2)}, u32[]{:S(2)}) collective-permute-start(f32[2,128,512]{2,1,0:T(8,128)} %collective-permute-done.1.below_ref), channel_id=1, source_target_pairs={{1,0},{2,1},{3,2},{4,3},{5,4},{6,5},{7,6},{9,8},{10,9},{11,10},{12... | collective-permute-start | bytes 1572872 | tf_op jit(solution)/shard_map/ppermute | solution.py:398
  35.9 21.5 %collective-permute-start.7 = (f32[2,128,512]{2,1,0:T(8,128)}, f32[2,128,512]{2,1,0:T(8,128)}, u32[]{:S(2)}, u32[]{:S(2)}) collective-permute-start(f32[2,128,512]{2,1,0:T(8,128)} %get-tuple-element.60), channel_id=1, source_target_pairs={{8,0},{16,8},{24,16},{32,24},{40,32},{48,40},{56,48},{64,56},{72,6... | collective-permute-start | bytes 1572872 | tf_op jit(solution)/shard_map/ppermute | solution.py:398
  37.5 1.6 copy-start.16
  39.1 1.6 copy-start.17
  41.8 6.6 %copy-start.1 = (bf16[4,256,256]{2,1,0:T(8,128)(2,1)S(1)}, bf16[4,256,256]{2,1,0:T(8,128)(2,1)}, u32[]{:S(2)}) copy-start(bf16[4,256,256]{2,1,0:T(8,128)(2,1)} %constant.45.clone.mh_ref.refs_16_) | copy-start | bytes 1572868
  41.8 6.6 %copy-start.2 = (bf16[4,256,256]{2,1,0:T(8,128)(2,1)S(1)}, bf16[4,256,256]{2,1,0:T(8,128)(2,1)}, u32[]{:S(2)}) copy-start(bf16[4,256,256]{2,1,0:T(8,128)(2,1)} %constant.46.clone.ml_ref.refs_17_) | copy-start | bytes 1572868
  46.3 4.3 %copy-start.9 = (f32[2,2,128,512]{3,2,1,0:T(8,128)}, f32[2,2,128,512]{3,2,1,0:T(8,128)S(1)}, u32[]{:S(2)}) copy-start(f32[2,2,128,512]{3,2,1,0:T(8,128)S(1)} %get-tuple-element.33.rolled_ref.refs_9_) | copy-start | bytes 3145732
  46.3 4.3 %copy-start.11 = (f32[2,2,128,512]{3,2,1,0:T(8,128)}, f32[2,2,128,512]{3,2,1,0:T(8,128)S(1)}, u32[]{:S(2)}) copy-start(f32[2,2,128,512]{3,2,1,0:T(8,128)S(1)} %get-tuple-element.35.rolled_ref.refs_10_) | copy-start | bytes 3145732
  46.3 4.3 %copy-start.14 = (f32[2,2,128,512]{3,2,1,0:T(8,128)}, f32[2,2,128,512]{3,2,1,0:T(8,128)S(1)}, u32[]{:S(2)}) copy-start(f32[2,2,128,512]{3,2,1,0:T(8,128)S(1)} %get-tuple-element.39.rolled_ref.refs_11_) | copy-start | bytes 3145732
  46.3 4.3 %copy-start.21 = (f32[2,512,512]{2,1,0:T(8,128)}, f32[2,512,512]{2,1,0:T(8,128)S(1)}, u32[]{:S(2)}) copy-start(f32[2,512,512]{2,1,0:T(8,128)S(1)} %get-tuple-element.45.refs_12_) | copy-start | bytes 6291460
  46.3 6.3 %copy-start.7 = (f32[2,2,128,512]{3,2,1,0:T(8,128)}, f32[2,2,128,512]{3,2,1,0:T(8,128)S(1)}, u32[]{:S(2)}) copy-start(f32[2,2,128,512]{3,2,1,0:T(8,128)S(1)} %get-tuple-element.31.rolled_ref.refs_8_) | copy-start | bytes 3145732
  46.4 13.2 %collective-permute-start.6 = (f32[2,128,512]{2,1,0:T(8,128)}, f32[2,128,512]{2,1,0:T(8,128)}, u32[]{:S(2)}, u32[]{:S(2)}) collective-permute-start(f32[2,128,512]{2,1,0:T(8,128)} %collective-permute-done.5.below_ref), channel_id=1, source_target_pairs={{1,0},{2,1},{3,2},{4,3},{5,4},{6,5},{7,6},{9,8},{10,9},{11,10},{12... | collective-permute-start | bytes 1572872 | tf_op jit(solution)/shard_map/ppermute | solution.py:398
  52.6 2.3 %copy-start.34 = (f32[8,128]{1,0:T(8,128)}, f32[8,128]{1,0:T(8,128)S(1)}, u32[]{:S(2)}) copy-start(f32[8,128]{1,0:T(8,128)S(1)} %get-tuple-element.38.refs_2_) | copy-start | bytes 12292
  57.5 10.7 %collective-permute-start.8 = (f32[2,128,512]{2,1,0:T(8,128)}, f32[2,128,512]{2,1,0:T(8,128)S(1)}, u32[]{:S(2)}, u32[]{:S(2)}) collective-permute-start(f32[2,128,512]{2,1,0:T(8,128)} %shard_map.108.below_ref), channel_id=1, source_target_pairs={{1,0},{2,1},{3,2},{4,3},{5,4},{6,5},{7,6},{9,8},{10,9},{11,10},{12... | collective-permute-start | bytes 1572872 | tf_op jit(solution)/shard_map/ppermute | solution.py:398
  59.6 1.2 copy-start.12
  60.8 7.4 %copy-start.15 = (f32[2,2,128,512]{3,2,1,0:T(8,128)S(1)}, f32[2,2,128,512]{3,2,1,0:T(8,128)}, u32[]{:S(2)}) copy-start(f32[2,2,128,512]{3,2,1,0:T(8,128)} %copy-done.14) | copy-start | bytes 3145732
  60.8 10.2 %copy-start.31 = (bf16[4,256,256]{2,1,0:T(8,128)(2,1)S(1)}, bf16[4,256,256]{2,1,0:T(8,128)(2,1)}, u32[]{:S(2)}) copy-start(bf16[4,256,256]{2,1,0:T(8,128)(2,1)} %constant.43.clone.refs_14_) | copy-start | bytes 1572868
  60.8 10.2 %copy-start.32 = (bf16[4,256,256]{2,1,0:T(8,128)(2,1)S(1)}, bf16[4,256,256]{2,1,0:T(8,128)(2,1)}, u32[]{:S(2)}) copy-start(bf16[4,256,256]{2,1,0:T(8,128)(2,1)} %constant.44.clone.refs_15_) | copy-start | bytes 1572868
  68.2 2.8 %copy-start.8 = (f32[2,2,128,512]{3,2,1,0:T(8,128)S(1)}, f32[2,2,128,512]{3,2,1,0:T(8,128)}, u32[]{:S(2)}) copy-start(f32[2,2,128,512]{3,2,1,0:T(8,128)} %copy-done.7) | copy-start | bytes 3145732
  68.2 2.8 %copy-start.10 = (f32[2,2,128,512]{3,2,1,0:T(8,128)S(1)}, f32[2,2,128,512]{3,2,1,0:T(8,128)}, u32[]{:S(2)}) copy-start(f32[2,2,128,512]{3,2,1,0:T(8,128)} %copy-done.9) | copy-start | bytes 3145732
  68.2 2.8 %copy-start.13 = (f32[2,2,128,512]{3,2,1,0:T(8,128)S(1)}, f32[2,2,128,512]{3,2,1,0:T(8,128)}, u32[]{:S(2)}) copy-start(f32[2,2,128,512]{3,2,1,0:T(8,128)} %copy-done.11) | copy-start | bytes 3145732
  68.2 2.8 %copy-start.24 = (f32[2,2,128,512]{3,2,1,0:T(8,128)S(1)}, f32[2,2,128,512]{3,2,1,0:T(8,128)}, u32[]{:S(2)}) copy-start(f32[2,2,128,512]{3,2,1,0:T(8,128)} %copy-done.23) | copy-start | bytes 3145732
  68.2 2.8 %copy-start.26 = (f32[2,2,128,512]{3,2,1,0:T(8,128)S(1)}, f32[2,2,128,512]{3,2,1,0:T(8,128)}, u32[]{:S(2)}) copy-start(f32[2,2,128,512]{3,2,1,0:T(8,128)} %copy-done.25) | copy-start | bytes 3145732
  68.2 3.1 %copy-start.28 = (f32[2,2,128,512]{3,2,1,0:T(8,128)S(1)}, f32[2,2,128,512]{3,2,1,0:T(8,128)}, u32[]{:S(2)}) copy-start(f32[2,2,128,512]{3,2,1,0:T(8,128)} %copy-done.27) | copy-start | bytes 3145732
  68.2 3.4 %copy-start.30 = (f32[2,2,128,512]{3,2,1,0:T(8,128)S(1)}, f32[2,2,128,512]{3,2,1,0:T(8,128)}, u32[]{:S(2)}) copy-start(f32[2,2,128,512]{3,2,1,0:T(8,128)} %copy-done.29) | copy-start | bytes 3145732
  85.1 10.1 %collective-permute-start.9 = (f32[512,640]{1,0:T(8,128)S(1)}, f32[512,640]{1,0:T(8,128)S(1)}, u32[]{:S(2)}, u32[]{:S(2)}) collective-permute-start(f32[512,640]{1,0:T(8,128)S(1)} %get-tuple-element.52), channel_id=1, source_target_pairs={{0,1},{1,0},{2,3},{3,2},{4,5},{5,4},{6,7},{7,6},{8,9},{9,8},{10,11... | collective-permute-start | bytes 3932168 | tf_op jit(solution)/shard_map/ppermute | solution.py:402
  85.2 10.0 %collective-permute-start.10 = (f32[2,128,512]{2,1,0:T(8,128)S(1)}, f32[2,128,512]{2,1,0:T(8,128)S(1)}, u32[]{:S(2)}, u32[]{:S(2)}) collective-permute-start(f32[2,128,512]{2,1,0:T(8,128)S(1)} %get-tuple-element.54), channel_id=1, source_target_pairs={{0,1},{1,2},{2,3},{3,4},{4,5},{5,6},{6,7},{8,9},{9,10},{10,11},{11... | collective-permute-start | bytes 1572872 | tf_op jit(solution)/shard_map/ppermute | solution.py:398
  97.3 40.3 %collective-permute-start.11 = (f32[2,384,512]{2,1,0:T(8,128)}, f32[2,384,512]{2,1,0:T(8,128)}, u32[]{:S(2)}, u32[]{:S(2)}) collective-permute-start(f32[2,384,512]{2,1,0:T(8,128)} %shard_map.113), channel_id=1, source_target_pairs={{0,1},{1,2},{2,3},{3,4},{4,5},{5,6},{6,7},{8,9},{9,10},{10,11},{11... | collective-permute-start | bytes 4718600 | tf_op jit(solution)/shard_map/ppermute | solution.py:398
  101.7 36.0 %all-to-all-start = ((f32[64,8,640]{2,1,0:T(8,128)}), f32[64,8,640]{2,1,0:T(8,128)S(1)}, u32[]{:S(2)}, u32[]{:S(2)}) async-start(f32[64,8,640]{2,1,0:T(8,128)} %bitcast.4), calls=%async_computation | async-start | bytes 2621440 | tf_op jit(solution)/shard_map/all_to_all | solution.py:489
  113.1 24.5 %collective-permute-start.12 = (f32[2,128,512]{2,1,0:T(8,128)}, f32[2,128,512]{2,1,0:T(8,128)}, u32[]{:S(2)}, u32[]{:S(2)}) collective-permute-start(f32[2,128,512]{2,1,0:T(8,128)} %copy-done.37), channel_id=1, source_target_pairs={{0,8},{8,16},{16,24},{24,32},{32,40},{40,48},{48,56},{56,64},{64,7... | collective-permute-start | bytes 1572872 | tf_op jit(solution)/shard_map/ppermute | solution.py:398
  137.6 1.8 copy-start.22
  137.8 3.2 %copy-start.5 = (f32[64,8,512]{2,1,0:T(8,128)}, f32[64,8,512]{2,1,0:T(8,128)S(1)}, u32[]{:S(2)}) copy-start(f32[64,8,512]{2,1,0:T(8,128)S(1)} %shard_map.114.after_ref) | copy-start | bytes 3145732
  141.0 1.1 copy-start.6
  142.2 65.0 %collective-permute-start.13 = (f32[2,512,512]{2,1,0:T(8,128)}, f32[2,512,512]{2,1,0:T(8,128)}, u32[]{:S(2)}, u32[]{:S(2)}) collective-permute-start(f32[2,512,512]{2,1,0:T(8,128)} %shard_map.116), channel_id=1, source_target_pairs={{0,1},{1,2},{2,3},{3,4},{4,5},{5,6},{6,7},{8,9},{9,10},{10,11},{11... | collective-permute-start | bytes 6291464 | tf_op jit(solution)/shard_map/ppermute | solution.py:398
  146.7 60.5 %collective-permute-start.14 = (f32[2,384,512]{2,1,0:T(8,128)}, f32[2,384,512]{2,1,0:T(8,128)}, u32[]{:S(2)}, u32[]{:S(2)}) collective-permute-start(f32[2,384,512]{2,1,0:T(8,128)} %copy-done.6), channel_id=1, source_target_pairs={{0,8},{8,16},{16,24},{24,32},{32,40},{40,48},{48,56},{56,64},{64,7... | collective-permute-start | bytes 4718600 | tf_op jit(solution)/shard_map/ppermute | solution.py:398
  152.1 55.1 %all-to-all-start.1 = ((f32[64,8,512]{2,1,0:T(8,128)}), f32[64,8,512]{2,1,0:T(8,128)S(1)}, u32[]{:S(2)}, u32[]{:S(2)}) async-start(f32[64,8,512]{2,1,0:T(8,128)} %copy-done.5), calls=%async_computation.1 | async-start | bytes 2097152 | tf_op jit(solution)/shard_map/all_to_all | solution.py:498
  163.4 1.6 copy-start.18
  165.7 1.3 copy-start.19
  208.3 6.5 %collective-permute-start.15 = (f32[512,512]{1,0:T(8,128)}, f32[512,512]{1,0:T(8,128)S(1)}, u32[]{:S(2)}, u32[]{:S(2)}) collective-permute-start(f32[512,512]{1,0:T(8,128)} %shard_map.118.mine_ref), channel_id=1, source_target_pairs={{0,1},{1,0},{2,3},{3,2},{4,5},{5,4},{6,7},{7,6},{8,9},{9,8},{10,11... | collective-permute-start | bytes 3145736 | tf_op jit(solution)/shard_map/ppermute | solution.py:402
  208.6 1.6 copy-start.20
  210.2 4.6 %copy-start.4 = (f32[512,512]{1,0:T(8,128)S(1)}, f32[512,512]{1,0:T(8,128)}, u32[]{:S(2)}) copy-start(f32[512,512]{1,0:T(8,128)} %shard_map.118.mine_ref) | copy-start | bytes 3145732
  (9 other events, 8.0 us)

commit v4 on v3

--- a/solution.py
+++ b/solution.py
@@ -13,7 +13,8 @@
 QUARTER = 128
 SIZES = (128,) * 4
 FIRSTS = (0, 128, 256, 384)
-BACK = (128, 384)
+BACK = (320, 192)
+CHUNKS = ((0, 160), (160, 160), (320, 192))
 WIDE = SIDE + 128
 PIECES = len(SIZES)
 COST = pl.CostEstimate(flops=0, bytes_accessed=0, transcendentals=0)
@@ -196,8 +197,7 @@
                         low[item, rows, to] = lo[:, piece]
 
     stores = []
-    size = QUARTER
-    for first in range(0, SIDE, size):
+    for first, size in CHUNKS:
         at = slice(first, first + size)
         lane = lax.broadcasted_iota(jnp.int32, (size, SIDE), 1)
         row = lax.broadcasted_iota(jnp.int32, (size, SIDE), 0) + first
@@ -314,7 +314,7 @@
             half,
             four,
             pltpu.VMEM((4, 2, SIDE, SIDE), F32),
-            pltpu.SemaphoreType.DMA((16,)),
+            pltpu.SemaphoreType.DMA((4 * len(CHUNKS),)),
         ],
         compiler_params=params(36),
         cost_estimate=COST,
@@ -420,21 +420,22 @@
     )(scale, own, t_own)
 
 
-def object_kernel(scale_ref, base_ref, left_ref, first_ref, second_ref, out_ref):
-    above = jnp.where(pl.program_id(0) < 1, first_ref[...], second_ref[...])
-    out_ref[...] = base_ref[...] + scale_ref[0, 0] * (left_ref[...] + above)
+def object_kernel(scale_ref, base_ref, left_ref, *refs):
+    out_ref, first = refs[-1], 0
+    for ref, size in zip(refs, BACK):
+        at = slice(first, first + size)
+        out_ref[at] = base_ref[at] + scale_ref[0, 0] * (left_ref[at] + ref[...])
+        first += size
 
 
 def finished_object(scale, start, left, above):
-    rows = pl.BlockSpec((2, QUARTER, SIDE), lambda i: (0, i, 0))
-    first = pl.BlockSpec((2, QUARTER, SIDE), lambda i: (0, 0, 0))
-    second = pl.BlockSpec((2, QUARTER, SIDE), lambda i: (0, jnp.maximum(i, 1) - 1, 0))
+    parts = [pl.BlockSpec((None, size, SIDE), lambda i: (i, 0, 0)) for size in (SIDE, SIDE) + BACK]
     return pl.pallas_call(
         object_kernel,
-        grid=(4,),
+        grid=(2,),
         out_shape=jax.ShapeDtypeStruct(start.shape, F32),
-        in_specs=[sm(), rows, rows, first, second],
-        out_specs=rows,
+        in_specs=[sm()] + parts,
+        out_specs=parts[0],
         compiler_params=params(),
         cost_estimate=COST,
     )(scale, start, left, *above)
@@ -471,7 +472,7 @@
     for k, piece in enumerate(pieces):
         below = shifted(piece, ROW, -1)
         if k == 3:
-            (below,) = tied((below,), tokens[:2])
+            (below,) = tied((below,), (peaks,))
         corner = shifted(below, COL, -1)
         spec, wrap, token = fore(k, where, object_field, right, below, corner, rolled[k], matrices)
         specs.append(spec)

time: 220 us -> 218 us (level)
  starting transfers between devices: 62.1 us -> 56.2 us
  Pallas kernels: 37.9 us -> 41.5 us
    all_to_all x1, waiting for transfers between devices: 39.5 us -> 3.21 us  [on_device(): mine = lax.all_to_all(shares, CHIPS, 0, 0).reshape(SIDE, SIDE)]
    all_to_all x1, waiting for transfers between devices: 0.01 us -> 19.2 us  [on_device(): terms = lax.all_to_all(half.reshape(64, share, WIDE), CHIPS, 0, 0)]
    ppermute x14, waiting for transfers between devices: 50.3 us -> 69.1 us  [shifted(): lax.ppermute(value, axis, [(source, source + steps) for source in range(f...]
    pallas_call x1, Pallas kernels: 13.5 us -> 16.4 us  [update(): pl.pallas_call(update_kernel, out_shape=out_shape, in_specs=[sm()] + [vm(...]
    ppermute x14, starting transfers between devices: 40.1 us -> 37.6 us  [shifted(): lax.ppermute(value, axis, [(source, source + steps) for source in range(f...]
    unnamed x78 -> x64, local copies, waits for them, and re-layouts: 20.3 us -> 19.7 us
  transfers between devices with their start and end apart: 18 -> 18, of which waited for: 6 -> 8; matrix products, arithmetic and copies ran while one was open for 2% -> 2% of each run, Pallas kernels for 8% -> 8%
where the time goes in v4:
time: 218 us; the launch traced here: 215 us
  waiting for transfers between devices  91.5 us (42%)
  starting transfers between devices  56.2 us (26%)
  Pallas kernels  41.5 us (19%)
  local copies, waits for them, and re-layouts  23.9 us (11%)
    ppermute x14, waiting for transfers between devices, shifted(): lax.ppermute(value, axis, [(source, source + steps) for source in range(f...  69.1 us
    ppermute x14, starting transfers between devices, shifted(): lax.ppermute(value, axis, [(source, source + steps) for source in range(f...  37.6 us
    unnamed x64, local copies, waits for them, and re-layouts  19.7 us
    all_to_all x1, waiting for transfers between devices, on_device(): terms = lax.all_to_all(half.reshape(64, share, WIDE), CHIPS, 0, 0)  19.2 us
    pallas_call x1, Pallas kernels, update(): pl.pallas_call(update_kernel, out_shape=out_shape, in_specs=[sm()] + [vm(...  16.4 us
    pallas_call x4, Pallas kernels, fore(): pl.pallas_call(functools.partial(fore_kernel, piece), grid=(1,), out_shap...  10.8 us
    all_to_all x1, starting transfers between devices, on_device(): terms = lax.all_to_all(half.reshape(64, share, WIDE), CHIPS, 0, 0)  10.5 us
    all_to_all x1, starting transfers between devices, on_device(): mine = lax.all_to_all(shares, CHIPS, 0, 0).reshape(SIDE, SIDE)  8.04 us
  transfers between devices with their start and end apart: 18, of which 8 were waited for; matrix products, arithmetic and copies ran while one was open for 2% of the time, Pallas kernels for 8%

profile of v4, /device:TPU:33, one launch (start us, length us, event | category | flops | bytes accessed | tf_op | source)
XLA Modules:
  0.0 215.1 jit_solution(8489435825040024478)
XLA Ops:
  0.6 2.7 %collective-permute-start = (f32[2,512,512]{2,1,0:T(8,128)}, f32[2,512,512]{2,1,0:T(8,128)}, u32[]{:S(2)}, u32[]{:S(2)}) collective-permute-start(f32[2,512,512]{2,1,0:T(8,128)} %own_ref.11), channel_id=1, source_target_pairs={{1,0},{2,1},{3,2},{4,3},{5,4},{6,5},{7,6},{9,8},{10,9},{11,10},{12... | collective-permute-start | bytes 6291464 | tf_op jit(solution)/shard_map/ppermute | solution.py:398
  3.4 3.0 %fusion = (f32[2,128,512]{2,1,0:T(8,128)}, f32[2,128,512]{2,1,0:T(8,128)}, f32[2,128,512]{2,1,0:T(8,128)}, f32[2,128,512]{2,1,0:T(8,128)}) fusion(f32[2,512,512]{2,1,0:T(8,128)} %own_ref.11), kind=kLoop, calls=%fused_computation.5 | loop fusion | bytes 4194304 | tf_op jit(solution)/shard_map/slice | solution.py:467
  6.4 1.3 collective-permute-start.7
  7.6 1.3 collective-permute-start.3
  8.9 1.3 collective-permute-start.5
  10.2 1.3 collective-permute-start.1
  11.9 1.6 copy-done.15
  13.4 1.6 copy-done.16
  15.0 1.0 copy-done.27
  16.1 4.5 %shard_map.104 = (f32[2,2,128,512]{3,2,1,0:T(8,128)S(1)}, f32[2,2,128,512]{3,2,1,0:T(8,128)S(1)}, f32[2,2,128,512]{3,2,1,0:T(8,128)S(1)}, f32[2,2,128,512]{3,2,1...) custom-call(s32[3,2]{1,0:T(4,128)S(1)} %pad_add_fusion.where_ref, f32[2,512,512]{2,1,0:T(8,128)S(1)} %copy-done.15, ...), custom_call_target="tpu_custom_call" | custom-call | tf_op jit(solution)/shard_map/pallas_call | solution.py:285
  21.6 1.0 copy-done.7
  23.6 1.0 copy-done.11
  24.6 1.3 copy-done.20
  26.5 1.9 collective-permute-start.8
  28.4 4.9 %collective-permute-done.3.below_ref = f32[2,128,512]{2,1,0:T(8,128)} collective-permute-done((f32[2,128,512]{2,1,0:T(8,128)}, f32[2,128,512]{2,1,0:T(8,128)}, u32[]{:S(2)}, u32[]{:S(2)}) %collective-permute-start.3) | collective-permute-done | bytes 524320 | tf_op jit(solution)/shard_map/ppermute | solution.py:398
  33.3 3.1 %collective-permute-start.4 = (f32[2,128,512]{2,1,0:T(8,128)}, f32[2,128,512]{2,1,0:T(8,128)S(1)}, u32[]{:S(2)}, u32[]{:S(2)}) collective-permute-start(f32[2,128,512]{2,1,0:T(8,128)} %collective-permute-done.3.below_ref), channel_id=1, source_target_pairs={{1,0},{2,1},{3,2},{4,3},{5,4},{6,5},{7,6},{9,8},{10,9},{11,10},{12... | collective-permute-start | bytes 1572872 | tf_op jit(solution)/shard_map/ppermute | solution.py:398
  36.4 8.2 %collective-permute-done.5.below_ref = f32[2,128,512]{2,1,0:T(8,128)} collective-permute-done((f32[2,128,512]{2,1,0:T(8,128)}, f32[2,128,512]{2,1,0:T(8,128)}, u32[]{:S(2)}, u32[]{:S(2)}) %collective-permute-start.5) | collective-permute-done | bytes 524320 | tf_op jit(solution)/shard_map/ppermute | solution.py:398
  44.6 3.1 %collective-permute-start.6 = (f32[2,128,512]{2,1,0:T(8,128)}, f32[2,128,512]{2,1,0:T(8,128)S(1)}, u32[]{:S(2)}, u32[]{:S(2)}) collective-permute-start(f32[2,128,512]{2,1,0:T(8,128)} %collective-permute-done.5.below_ref), channel_id=1, source_target_pairs={{1,0},{2,1},{3,2},{4,3},{5,4},{6,5},{7,6},{9,8},{10,9},{11,10},{12... | collective-permute-start | bytes 1572872 | tf_op jit(solution)/shard_map/ppermute | solution.py:398
  47.7 8.2 %collective-permute-done.1.below_ref = f32[2,128,512]{2,1,0:T(8,128)} collective-permute-done((f32[2,128,512]{2,1,0:T(8,128)}, f32[2,128,512]{2,1,0:T(8,128)}, u32[]{:S(2)}, u32[]{:S(2)}) %collective-permute-start.1) | collective-permute-done | bytes 524320 | tf_op jit(solution)/shard_map/ppermute | solution.py:398
  55.8 2.9 %collective-permute-start.2 = (f32[2,128,512]{2,1,0:T(8,128)}, f32[2,128,512]{2,1,0:T(8,128)S(1)}, u32[]{:S(2)}, u32[]{:S(2)}) collective-permute-start(f32[2,128,512]{2,1,0:T(8,128)} %collective-permute-done.1.below_ref), channel_id=1, source_target_pairs={{1,0},{2,1},{3,2},{4,3},{5,4},{6,5},{7,6},{9,8},{10,9},{11,10},{12... | collective-permute-start | bytes 1572872 | tf_op jit(solution)/shard_map/ppermute | solution.py:398
  58.7 1.2 copy-done.12
  60.0 2.7 %shard_map.109 = (f32[2,2,128,512]{3,2,1,0:T(8,128)S(1)}, f32[2,2,128,512]{3,2,1,0:T(8,128)S(1)}, f32[8,128]{1,0:T(8,128)}) custom-call(s32[3,2]{1,0:T(4,128)S(1)} %pad_add_fusion.where_ref, f32[2,512,512]{2,1,0:T(8,128)S(1)} %copy-done, f32[2,512,512]{2,1,0:T(8,128)} %collective-permute-done.right_ref, f32[2,128,512]{2,1,0:T(8,128)} %shard_map.108.below_ref, ...), custom_call_target="tpu_custom_call" | custom-call | tf_op jit(solution)/shard_map/pallas_call | solution.py:138
  62.7 2.7 %shard_map.106 = (f32[2,2,128,512]{3,2,1,0:T(8,128)S(1)}, f32[2,2,128,512]{3,2,1,0:T(8,128)S(1)}, f32[8,128]{1,0:T(8,128)}) custom-call(s32[3,2]{1,0:T(4,128)S(1)} %pad_add_fusion.where_ref, f32[2,512,512]{2,1,0:T(8,128)S(1)} %copy-done, f32[2,512,512]{2,1,0:T(8,128)} %collective-permute-done.right_ref, f32[2,128,512]{2,1,0:T(8,128)} %collective-permute-done.3.below_ref, ...), custom_call_target="tpu_custom_call" | custom-call | tf_op jit(solution)/shard_map/pallas_call | solution.py:138
  65.4 2.7 %shard_map.107 = (f32[2,2,128,512]{3,2,1,0:T(8,128)S(1)}, f32[2,2,128,512]{3,2,1,0:T(8,128)S(1)}, f32[8,128]{1,0:T(8,128)}) custom-call(s32[3,2]{1,0:T(4,128)S(1)} %pad_add_fusion.where_ref, f32[2,512,512]{2,1,0:T(8,128)S(1)} %copy-done, f32[2,512,512]{2,1,0:T(8,128)} %collective-permute-done.right_ref, f32[2,128,512]{2,1,0:T(8,128)} %collective-permute-done.5.below_ref, ...), custom_call_target="tpu_custom_call" | custom-call | tf_op jit(solution)/shard_map/pallas_call | solution.py:138
  68.1 2.8 %shard_map.105 = (f32[2,2,128,512]{3,2,1,0:T(8,128)S(1)}, f32[2,2,128,512]{3,2,1,0:T(8,128)S(1)}, f32[8,128]{1,0:T(8,128)}) custom-call(s32[3,2]{1,0:T(4,128)S(1)} %pad_add_fusion.where_ref, f32[2,512,512]{2,1,0:T(8,128)S(1)} %copy-done, f32[2,512,512]{2,1,0:T(8,128)} %collective-permute-done.right_ref, f32[2,128,512]{2,1,0:T(8,128)} %collective-permute-done.1.below_ref, ...), custom_call_target="tpu_custom_call" | custom-call | tf_op jit(solution)/shard_map/pallas_call | solution.py:138
  70.9 16.4 %shard_map.110 = (f32[2,512,512]{2,1,0:T(8,128)}, f32[2,512,512]{2,1,0:T(8,128)}, f32[2,320,512]{2,1,0:T(8,128)S(1)}, f32[2,192,512]{2,1,0:T(8,128)S(1)}, f32[2,...) custom-call(s32[3,2]{1,0:T(4,128)S(1)} %pad_add_fusion.where_ref, ...), custom_call_target="tpu_custom_call" | custom-call | tf_op jit(solution)/shard_map/pallas_call | solution.py:307
  87.4 3.4 %collective-permute-start.10 = (f32[2,320,512]{2,1,0:T(8,128)}, f32[2,320,512]{2,1,0:T(8,128)S(1)}, u32[]{:S(2)}, u32[]{:S(2)}) collective-permute-start(f32[2,320,512]{2,1,0:T(8,128)} %get-tuple-element.50), channel_id=1, source_target_pairs={{0,1},{1,2},{2,3},{3,4},{4,5},{5,6},{6,7},{8,9},{9,10},{10,11},{11... | collective-permute-start | bytes 3932168 | tf_op jit(solution)/shard_map/ppermute | solution.py:398
  90.9 14.8 %collective-permute-done.10.corner_ref = f32[2,320,512]{2,1,0:T(8,128)S(1)} collective-permute-done((f32[2,320,512]{2,1,0:T(8,128)}, f32[2,320,512]{2,1,0:T(8,128)S(1)}, u32[]{:S(2)}, u32[]{:S(2)}) %collective-permute-start.10) | collective-permute-done | bytes 1310752 | tf_op jit(solution)/shard_map/ppermute | solution.py:398
  105.7 1.3 copy-done.21
  107.0 1.8 shard_map.112
  108.7 4.2 %collective-permute-start.12 = (f32[2,320,512]{2,1,0:T(8,128)}, f32[2,320,512]{2,1,0:T(8,128)}, u32[]{:S(2)}, u32[]{:S(2)}) collective-permute-start(f32[2,320,512]{2,1,0:T(8,128)} %get-tuple-element.52), channel_id=1, source_target_pairs={{0,8},{8,16},{16,24},{24,32},{32,40},{40,48},{48,56},{56,64},{64,7... | collective-permute-start | bytes 3932168 | tf_op jit(solution)/shard_map/ppermute | solution.py:398
  112.9 10.5 %all-to-all-start = ((f32[64,8,640]{2,1,0:T(8,128)}), f32[64,8,640]{2,1,0:T(8,128)S(1)}, u32[]{:S(2)}, u32[]{:S(2)}) async-start(f32[64,8,640]{2,1,0:T(8,128)} %bitcast.4), calls=%async_computation | async-start | bytes 2621440 | tf_op jit(solution)/shard_map/all_to_all | solution.py:490
  123.5 5.3 %collective-permute-start.11 = (f32[2,192,512]{2,1,0:T(8,128)}, f32[2,192,512]{2,1,0:T(8,128)}, u32[]{:S(2)}, u32[]{:S(2)}) collective-permute-start(f32[2,192,512]{2,1,0:T(8,128)} %shard_map.113), channel_id=1, source_target_pairs={{0,1},{1,2},{2,3},{3,4},{4,5},{5,6},{6,7},{8,9},{9,10},{10,11},{11... | collective-permute-start | bytes 2359304 | tf_op jit(solution)/shard_map/ppermute | solution.py:398
  129.5 15.1 %collective-permute-done.11.refs_1_.corner_ref = f32[2,192,512]{2,1,0:T(8,128)} collective-permute-done((f32[2,192,512]{2,1,0:T(8,128)}, f32[2,192,512]{2,1,0:T(8,128)}, u32[]{:S(2)}, u32[]{:S(2)}) %collective-permute-start.11) | collective-permute-done | bytes 786464 | tf_op jit(solution)/shard_map/ppermute | solution.py:398
  144.6 19.2 %all-to-all-done.terms_ref = f32[64,8,640]{2,1,0:T(8,128)S(1)} async-done(((f32[64,8,640]{2,1,0:T(8,128)}), f32[64,8,640]{2,1,0:T(8,128)S(1)}, u32[]{:S(2)}, u32[]{:S(2)}) %all-to-all-start) | async-done | bytes 1310752 | tf_op jit(solution)/shard_map/all_to_all | solution.py:490
  163.8 1.2 shard_map.114.after_ref
  165.0 1.2 shard_map.115.refs_1_
  167.2 1.9 collective-permute-start.13
  169.1 8.0 %all-to-all-start.1 = ((f32[64,8,512]{2,1,0:T(8,128)}), f32[64,8,512]{2,1,0:T(8,128)S(1)}, u32[]{:S(2)}, u32[]{:S(2)}) async-start(f32[64,8,512]{2,1,0:T(8,128)} %shard_map.114.after_ref), calls=%async_computation.1 | async-start | bytes 2097152 | tf_op jit(solution)/shard_map/all_to_all | solution.py:499
  177.1 4.0 %collective-permute-start.14 = (f32[2,192,512]{2,1,0:T(8,128)}, f32[2,192,512]{2,1,0:T(8,128)}, u32[]{:S(2)}, u32[]{:S(2)}) collective-permute-start(f32[2,192,512]{2,1,0:T(8,128)} %copy-done.14), channel_id=1, source_target_pairs={{0,8},{8,16},{16,24},{24,32},{32,40},{40,48},{48,56},{56,64},{64,7... | collective-permute-start | bytes 2359304 | tf_op jit(solution)/shard_map/ppermute | solution.py:398
  182.3 1.6 copy-done.17
  184.6 1.3 copy-done.18
  186.5 17.9 %collective-permute-done.14.refs_1_ = f32[2,192,512]{2,1,0:T(8,128)} collective-permute-done((f32[2,192,512]{2,1,0:T(8,128)}, f32[2,192,512]{2,1,0:T(8,128)}, u32[]{:S(2)}, u32[]{:S(2)}) %collective-permute-start.14) | collective-permute-done | bytes 786464 | tf_op jit(solution)/shard_map/ppermute | solution.py:398
  204.5 3.2 %all-to-all-done.1 = f32[64,8,512]{2,1,0:T(8,128)S(1)} async-done(((f32[64,8,512]{2,1,0:T(8,128)}), f32[64,8,512]{2,1,0:T(8,128)S(1)}, u32[]{:S(2)}, u32[]{:S(2)}) %all-to-all-start.1) | async-done | bytes 1048608 | tf_op jit(solution)/shard_map/all_to_all | solution.py:499
  207.7 1.0 copy-done.3
  208.7 1.6 copy-done.19
  210.3 3.3 %shard_map.117 = f32[2,512,512]{2,1,0:T(8,128)} custom-call(f32[1,1]{1,0:T(1,128)} %bitcast.3.scale_ref, f32[2,512,512]{2,1,0:T(8,128)S(1)} %copy-done.19, f32[2,512,512]{2,1,0:T(8,128)} %collective-permute-done.13.left_ref.refs_2_, f32[2,320,512]{2,1,0:T(8,128)} %collective-permute-done.12.refs_0_, f32[2,192,512]{2,1,0:T(8,128)} %collective-permute-done.14.refs_1_), custom_call_target="tpu_custom_call" | custom-call | tf_op jit(solution)/shard_map/pallas_call | solution.py:433
  213.6 1.5 shard_map.119
  (74 shorter events, 6.5 us)
Async XLA Ops:
  0.6 11.2 %copy-start = (f32[2,512,512]{2,1,0:T(8,128)S(1)}, f32[2,512,512]{2,1,0:T(8,128)}, u32[]{:S(2)}) copy-start(f32[2,512,512]{2,1,0:T(8,128)} %own_ref.11) | copy-start | bytes 6291460
  0.6 11.0 %copy-start.31 = (s32[2,2]{1,0:T(2,128)S(1)}, s32[2,2]{1,0:T(2,128)}, u32[]{:S(2)}) copy-start(s32[2,2]{1,0:T(2,128)} %param.12) | copy-start | bytes 52
  0.6 58.0 %collective-permute-start = (f32[2,512,512]{2,1,0:T(8,128)}, f32[2,512,512]{2,1,0:T(8,128)}, u32[]{:S(2)}, u32[]{:S(2)}) collective-permute-start(f32[2,512,512]{2,1,0:T(8,128)} %own_ref.11), channel_id=1, source_target_pairs={{1,0},{2,1},{3,2},{4,3},{5,4},{6,5},{7,6},{9,8},{10,9},{11,10},{12... | collective-permute-start | bytes 6291464 | tf_op jit(solution)/shard_map/ppermute | solution.py:398
  6.4 20.1 %collective-permute-start.7 = (f32[2,128,512]{2,1,0:T(8,128)}, f32[2,128,512]{2,1,0:T(8,128)}, u32[]{:S(2)}, u32[]{:S(2)}) collective-permute-start(f32[2,128,512]{2,1,0:T(8,128)} %get-tuple-element.56), channel_id=1, source_target_pairs={{8,0},{16,8},{24,16},{32,24},{40,32},{48,40},{56,48},{64,56},{72,6... | collective-permute-start | bytes 1572872 | tf_op jit(solution)/shard_map/ppermute | solution.py:398
  7.6 25.7 %collective-permute-start.3 = (f32[2,128,512]{2,1,0:T(8,128)}, f32[2,128,512]{2,1,0:T(8,128)}, u32[]{:S(2)}, u32[]{:S(2)}) collective-permute-start(f32[2,128,512]{2,1,0:T(8,128)} %get-tuple-element.58), channel_id=1, source_target_pairs={{8,0},{16,8},{24,16},{32,24},{40,32},{48,40},{56,48},{64,56},{72,6... | collective-permute-start | bytes 1572872 | tf_op jit(solution)/shard_map/ppermute | solution.py:398
  8.9 35.6 %collective-permute-start.5 = (f32[2,128,512]{2,1,0:T(8,128)}, f32[2,128,512]{2,1,0:T(8,128)}, u32[]{:S(2)}, u32[]{:S(2)}) collective-permute-start(f32[2,128,512]{2,1,0:T(8,128)} %get-tuple-element.57), channel_id=1, source_target_pairs={{8,0},{16,8},{24,16},{32,24},{40,32},{48,40},{56,48},{64,56},{72,6... | collective-permute-start | bytes 1572872 | tf_op jit(solution)/shard_map/ppermute | solution.py:398
  10.2 45.6 %collective-permute-start.1 = (f32[2,128,512]{2,1,0:T(8,128)}, f32[2,128,512]{2,1,0:T(8,128)}, u32[]{:S(2)}, u32[]{:S(2)}) collective-permute-start(f32[2,128,512]{2,1,0:T(8,128)} %get-tuple-element.59), channel_id=1, source_target_pairs={{8,0},{16,8},{24,16},{32,24},{40,32},{48,40},{56,48},{64,56},{72,6... | collective-permute-start | bytes 1572872 | tf_op jit(solution)/shard_map/ppermute | solution.py:398
  11.8 1.6 copy-start.15
  13.4 1.6 copy-start.16
  15.0 1.0 copy-start.27
  16.1 42.6 %copy-start.1 = (bf16[4,256,256]{2,1,0:T(8,128)(2,1)S(1)}, bf16[4,256,256]{2,1,0:T(8,128)(2,1)}, u32[]{:S(2)}) copy-start(bf16[4,256,256]{2,1,0:T(8,128)(2,1)} %constant.45.clone.mh_ref.refs_16_) | copy-start | bytes 1572868
  16.1 42.6 %copy-start.2 = (bf16[4,256,256]{2,1,0:T(8,128)(2,1)S(1)}, bf16[4,256,256]{2,1,0:T(8,128)(2,1)}, u32[]{:S(2)}) copy-start(bf16[4,256,256]{2,1,0:T(8,128)(2,1)} %constant.46.clone.ml_ref.refs_17_) | copy-start | bytes 1572868
  20.6 1.0 copy-start.5
  21.6 1.0 copy-start.7
  22.6 1.0 copy-start.9
  23.6 1.0 copy-start.11
  24.6 1.3 copy-start.20
  26.5 32.2 %collective-permute-start.8 = (f32[2,128,512]{2,1,0:T(8,128)}, f32[2,128,512]{2,1,0:T(8,128)S(1)}, u32[]{:S(2)}, u32[]{:S(2)}) collective-permute-start(f32[2,128,512]{2,1,0:T(8,128)} %shard_map.108.below_ref), channel_id=1, source_target_pairs={{1,0},{2,1},{3,2},{4,3},{5,4},{6,5},{7,6},{9,8},{10,9},{11,10},{12... | collective-permute-start | bytes 1572872 | tf_op jit(solution)/shard_map/ppermute | solution.py:398
  33.3 29.3 %collective-permute-start.4 = (f32[2,128,512]{2,1,0:T(8,128)}, f32[2,128,512]{2,1,0:T(8,128)S(1)}, u32[]{:S(2)}, u32[]{:S(2)}) collective-permute-start(f32[2,128,512]{2,1,0:T(8,128)} %collective-permute-done.3.below_ref), channel_id=1, source_target_pairs={{1,0},{2,1},{3,2},{4,3},{5,4},{6,5},{7,6},{9,8},{10,9},{11,10},{12... | collective-permute-start | bytes 1572872 | tf_op jit(solution)/shard_map/ppermute | solution.py:398
  44.6 20.8 %collective-permute-start.6 = (f32[2,128,512]{2,1,0:T(8,128)}, f32[2,128,512]{2,1,0:T(8,128)S(1)}, u32[]{:S(2)}, u32[]{:S(2)}) collective-permute-start(f32[2,128,512]{2,1,0:T(8,128)} %collective-permute-done.5.below_ref), channel_id=1, source_target_pairs={{1,0},{2,1},{3,2},{4,3},{5,4},{6,5},{7,6},{9,8},{10,9},{11,10},{12... | collective-permute-start | bytes 1572872 | tf_op jit(solution)/shard_map/ppermute | solution.py:398
  55.8 12.3 %collective-permute-start.2 = (f32[2,128,512]{2,1,0:T(8,128)}, f32[2,128,512]{2,1,0:T(8,128)S(1)}, u32[]{:S(2)}, u32[]{:S(2)}) collective-permute-start(f32[2,128,512]{2,1,0:T(8,128)} %collective-permute-done.1.below_ref), channel_id=1, source_target_pairs={{1,0},{2,1},{3,2},{4,3},{5,4},{6,5},{7,6},{9,8},{10,9},{11,10},{12... | collective-permute-start | bytes 1572872 | tf_op jit(solution)/shard_map/ppermute | solution.py:398
  58.7 1.2 copy-start.12
  60.0 2.7 %copy-start.8 = (f32[2,2,128,512]{3,2,1,0:T(8,128)S(1)}, f32[2,2,128,512]{3,2,1,0:T(8,128)}, u32[]{:S(2)}) copy-start(f32[2,2,128,512]{3,2,1,0:T(8,128)} %copy-done.7) | copy-start | bytes 3145732
  62.7 2.7 %copy-start.10 = (f32[2,2,128,512]{3,2,1,0:T(8,128)S(1)}, f32[2,2,128,512]{3,2,1,0:T(8,128)}, u32[]{:S(2)}) copy-start(f32[2,2,128,512]{3,2,1,0:T(8,128)} %copy-done.9) | copy-start | bytes 3145732
  65.4 2.7 %copy-start.6 = (f32[2,2,128,512]{3,2,1,0:T(8,128)S(1)}, f32[2,2,128,512]{3,2,1,0:T(8,128)}, u32[]{:S(2)}) copy-start(f32[2,2,128,512]{3,2,1,0:T(8,128)} %copy-done.5) | copy-start | bytes 3145732
  68.1 2.8 %copy-start.13 = (f32[2,2,128,512]{3,2,1,0:T(8,128)S(1)}, f32[2,2,128,512]{3,2,1,0:T(8,128)}, u32[]{:S(2)}) copy-start(f32[2,2,128,512]{3,2,1,0:T(8,128)} %copy-done.11) | copy-start | bytes 3145732
  68.1 2.8 %copy-start.25 = (bf16[4,256,256]{2,1,0:T(8,128)(2,1)S(1)}, bf16[4,256,256]{2,1,0:T(8,128)(2,1)}, u32[]{:S(2)}) copy-start(bf16[4,256,256]{2,1,0:T(8,128)(2,1)} %constant.43.clone.refs_14_) | copy-start | bytes 1572868
  68.1 2.8 %copy-start.26 = (bf16[4,256,256]{2,1,0:T(8,128)(2,1)S(1)}, bf16[4,256,256]{2,1,0:T(8,128)(2,1)}, u32[]{:S(2)}) copy-start(bf16[4,256,256]{2,1,0:T(8,128)(2,1)} %constant.44.clone.refs_15_) | copy-start | bytes 1572868
  68.1 2.8 %copy-start.29 = (f32[2,8,128]{2,1,0:T(8,128)S(1)}, f32[2,8,128]{2,1,0:T(8,128)}, u32[]{:S(2)}) copy-start(f32[2,8,128]{2,1,0:T(8,128)} %copy-done.28) | copy-start | bytes 24580
  87.3 21.4 %copy-start.22 = (f32[2,192,512]{2,1,0:T(8,128)}, f32[2,192,512]{2,1,0:T(8,128)S(1)}, u32[]{:S(2)}) copy-start(f32[2,192,512]{2,1,0:T(8,128)S(1)} %get-tuple-element.46.refs_0_) | copy-start | bytes 2359300
  87.3 21.4 %copy-start.23 = (f32[2,192,512]{2,1,0:T(8,128)}, f32[2,192,512]{2,1,0:T(8,128)S(1)}, u32[]{:S(2)}) copy-start(f32[2,192,512]{2,1,0:T(8,128)S(1)} %get-tuple-element.45.below_ref) | copy-start | bytes 2359300
  87.4 18.3 %collective-permute-start.10 = (f32[2,320,512]{2,1,0:T(8,128)}, f32[2,320,512]{2,1,0:T(8,128)S(1)}, u32[]{:S(2)}, u32[]{:S(2)}) collective-permute-start(f32[2,320,512]{2,1,0:T(8,128)} %get-tuple-element.50), channel_id=1, source_target_pairs={{0,1},{1,2},{2,3},{3,4},{4,5},{5,6},{6,7},{8,9},{9,10},{10,11},{11... | collective-permute-start | bytes 3932168 | tf_op jit(solution)/shard_map/ppermute | solution.py:398
  90.8 14.8 %collective-permute-start.9 = (f32[512,640]{1,0:T(8,128)}, f32[512,640]{1,0:T(8,128)S(1)}, u32[]{:S(2)}, u32[]{:S(2)}) collective-permute-start(f32[512,640]{1,0:T(8,128)} %get-tuple-element.48), channel_id=1, source_target_pairs={{0,1},{1,0},{2,3},{3,2},{4,5},{5,4},{6,7},{7,6},{8,9},{9,8},{10,11... | collective-permute-start | bytes 3932168 | tf_op jit(solution)/shard_map/ppermute | solution.py:402
  105.7 1.3 copy-start.21
  108.7 55.1 %collective-permute-start.12 = (f32[2,320,512]{2,1,0:T(8,128)}, f32[2,320,512]{2,1,0:T(8,128)}, u32[]{:S(2)}, u32[]{:S(2)}) collective-permute-start(f32[2,320,512]{2,1,0:T(8,128)} %get-tuple-element.52), channel_id=1, source_target_pairs={{0,8},{8,16},{16,24},{24,32},{32,40},{40,48},{48,56},{56,64},{64,7... | collective-permute-start | bytes 3932168 | tf_op jit(solution)/shard_map/ppermute | solution.py:398
  112.9 50.9 %all-to-all-start = ((f32[64,8,640]{2,1,0:T(8,128)}), f32[64,8,640]{2,1,0:T(8,128)S(1)}, u32[]{:S(2)}, u32[]{:S(2)}) async-start(f32[64,8,640]{2,1,0:T(8,128)} %bitcast.4), calls=%async_computation | async-start | bytes 2621440 | tf_op jit(solution)/shard_map/all_to_all | solution.py:490
  123.5 21.1 %collective-permute-start.11 = (f32[2,192,512]{2,1,0:T(8,128)}, f32[2,192,512]{2,1,0:T(8,128)}, u32[]{:S(2)}, u32[]{:S(2)}) collective-permute-start(f32[2,192,512]{2,1,0:T(8,128)} %shard_map.113), channel_id=1, source_target_pairs={{0,1},{1,2},{2,3},{3,4},{4,5},{5,6},{6,7},{8,9},{9,10},{10,11},{11... | collective-permute-start | bytes 2359304 | tf_op jit(solution)/shard_map/ppermute | solution.py:398
  163.8 1.2 copy-start.24
  166.2 0.9 copy-start.14
  167.2 40.5 %collective-permute-start.13 = (f32[2,512,512]{2,1,0:T(8,128)}, f32[2,512,512]{2,1,0:T(8,128)}, u32[]{:S(2)}, u32[]{:S(2)}) collective-permute-start(f32[2,512,512]{2,1,0:T(8,128)} %shard_map.116), channel_id=1, source_target_pairs={{0,1},{1,2},{2,3},{3,4},{4,5},{5,6},{6,7},{8,9},{9,10},{10,11},{11... | collective-permute-start | bytes 6291464 | tf_op jit(solution)/shard_map/ppermute | solution.py:398
  169.1 38.6 %all-to-all-start.1 = ((f32[64,8,512]{2,1,0:T(8,128)}), f32[64,8,512]{2,1,0:T(8,128)S(1)}, u32[]{:S(2)}, u32[]{:S(2)}) async-start(f32[64,8,512]{2,1,0:T(8,128)} %shard_map.114.after_ref), calls=%async_computation.1 | async-start | bytes 2097152 | tf_op jit(solution)/shard_map/all_to_all | solution.py:499
  177.1 27.3 %collective-permute-start.14 = (f32[2,192,512]{2,1,0:T(8,128)}, f32[2,192,512]{2,1,0:T(8,128)}, u32[]{:S(2)}, u32[]{:S(2)}) collective-permute-start(f32[2,192,512]{2,1,0:T(8,128)} %copy-done.14), channel_id=1, source_target_pairs={{0,8},{8,16},{16,24},{24,32},{32,40},{40,48},{48,56},{56,64},{64,7... | collective-permute-start | bytes 2359304 | tf_op jit(solution)/shard_map/ppermute | solution.py:398
  182.3 1.6 copy-start.17
  184.6 1.3 copy-start.18
  207.7 1.0 copy-start.3
  208.7 4.9 %collective-permute-start.15 = (f32[512,512]{1,0:T(8,128)}, f32[512,512]{1,0:T(8,128)S(1)}, u32[]{:S(2)}, u32[]{:S(2)}) collective-permute-start(f32[512,512]{1,0:T(8,128)} %shard_map.118.mine_ref), channel_id=1, source_target_pairs={{0,1},{1,0},{2,3},{3,2},{4,5},{5,4},{6,7},{7,6},{8,9},{9,8},{10,11... | collective-permute-start | bytes 3145736 | tf_op jit(solution)/shard_map/ppermute | solution.py:402
  208.7 1.6 copy-start.19
  210.3 3.4 %copy-start.4 = (f32[512,512]{1,0:T(8,128)S(1)}, f32[512,512]{1,0:T(8,128)}, u32[]{:S(2)}) copy-start(f32[512,512]{1,0:T(8,128)} %shard_map.118.mine_ref) | copy-start | bytes 3145732
  (2 other events, 1.2 us)

commit v5 on v2

--- a/solution.py
+++ b/solution.py
@@ -11,10 +11,10 @@
 
 SIDE = 512
 QUARTER = 128
-SIZES = (192, 192, 128)
-FIRSTS = (0, 192, 384)
+SIZES = (128,) * 4
+FIRSTS = (0, 128, 256, 384)
+WIDE = SIDE + 128
 PIECES = len(SIZES)
-WIDE = SIDE + 128
 COST = pl.CostEstimate(flops=0, bytes_accessed=0, transcendentals=0)
 F32 = jnp.float32
 BF16 = jnp.bfloat16
@@ -128,8 +128,7 @@
 
 def fore(piece, where, own, right, below, diag, rolled, matrices):
     size = SIZES[piece]
-    at = FIRSTS[piece] // size
-    rows = pl.BlockSpec((2, size, SIDE), lambda i: (0, at, 0))
+    tile = pl.BlockSpec((2, size, SIDE), lambda i: (0, piece, 0))
     full = pl.BlockSpec((2, size, SIDE), lambda i: (0, 0, 0))
     whole = pl.BlockSpec((4, 2 * QUARTER, 2 * QUARTER), lambda i: (0, 0, 0))
     four = pl.BlockSpec((2, 2, size, SIDE), lambda i: (0, 0, 0, 0))
@@ -138,7 +137,7 @@
         functools.partial(fore_kernel, piece),
         grid=(1,),
         out_shape=[shape, shape, jax.ShapeDtypeStruct((8, 128), F32)],
-        in_specs=[sm(), rows, rows, full, full, four, whole, whole],
+        in_specs=[sm(), tile, tile, full, full, four, whole, whole],
         out_specs=[four, four, pl.BlockSpec((8, 128), lambda i: (0, 0))],
         compiler_params=params(20),
         cost_estimate=COST,
@@ -196,7 +195,7 @@
                         low[item, rows, to] = lo[:, piece]
 
     stores = []
-    for piece, (first, size) in enumerate(zip(FIRSTS, SIZES)):
+    for first, size in zip(FIRSTS, SIZES):
         at = slice(first, first + size)
         lane = lax.broadcasted_iota(jnp.int32, (size, SIDE), 1)
         row = lax.broadcasted_iota(jnp.int32, (size, SIDE), 0) + first
@@ -212,8 +211,8 @@
             back = fold(back, 1)
             back_r = jnp.concatenate([b[0] for b in back], axis=1)
             back_i = jnp.concatenate([b[1] for b in back], axis=1)
-            beam_r, beam_i = rolled_refs[piece][item, 0], rolled_refs[piece][item, 1]
-            patch_r, patch_i = wrapped_refs[piece][item, 0], wrapped_refs[piece][item, 1]
+            beam_r, beam_i = (rows_of(rolled_refs, item, part, first, first + size) for part in range(2))
+            patch_r, patch_i = (rows_of(wrapped_refs, item, part, first, first + size) for part in range(2))
             diff_r = back_r - (beam_r * patch_r - beam_i * patch_i)
             diff_i = back_i - (beam_r * patch_i + beam_i * patch_r)
             term = (beam_r * diff_r + beam_i * diff_i, beam_r * diff_i - beam_i * diff_r)
@@ -359,8 +358,26 @@
     )(below, corner, after)
 
 
-def share_kernel(terms_ref, start_ref, *refs):
+def middle_kernel(terms_ref, *refs):
     out_ref = refs[-1]
+    total = jnp.sum(terms_ref[:, :, :SIDE], axis=0)
+    peak = jnp.max(terms_ref[:, :, SIDE:], axis=0)
+    out_ref[:, :, :SIDE] = jnp.broadcast_to(total, (out_ref.shape[0],) + total.shape)
+    out_ref[:, :, SIDE:] = jnp.broadcast_to(peak, (out_ref.shape[0],) + peak.shape)
+
+
+def middle(terms, count, after):
+    return pl.pallas_call(
+        middle_kernel,
+        out_shape=jax.ShapeDtypeStruct((count,) + terms.shape[1:], F32),
+        in_specs=[vm()] + [anywhere()] * len(after),
+        out_specs=vm(),
+        compiler_params=params(),
+        cost_estimate=COST,
+    )(terms, *after)
+
+
+def share_kernel(terms_ref, start_ref, out_ref):
     total = jnp.sum(terms_ref[:, :, :SIDE], axis=0)
     peak = jnp.max(terms_ref[:, :, SIDE:], axis=0)
     for q in range(4):
@@ -369,16 +386,15 @@
         out_ref[:, :, lanes] = jnp.broadcast_to(value, out_ref.shape[:2] + (QUARTER,))
 
 
-def shared(terms, start, after):
-    count, share, _ = terms.shape
+def shared(terms, start, count):
     return pl.pallas_call(
         share_kernel,
-        out_shape=jax.ShapeDtypeStruct((count, share, SIDE), F32),
-        in_specs=[vm()] * 2 + [anywhere()] * len(after),
+        out_shape=jax.ShapeDtypeStruct((count,) + start.shape, F32),
+        in_specs=[vm()] * 2,
         out_specs=vm(),
         compiler_params=params(),
         cost_estimate=COST,
-    )(terms, start, *after)
+    )(terms, start)
 
 
 def shifted(value, axis, steps):
@@ -391,16 +407,19 @@
     return lax.ppermute(value, "core", [(0, 1), (1, 0)])
 
 
-def base_kernel(scale_ref, own_ref, t_own_ref, base_ref):
+def base_kernel(scale_ref, own_ref, t_own_ref, base_ref, token_ref):
     base_ref[...] = own_ref[...] + scale_ref[0, 0] * t_own_ref[...]
+    token_ref[...] = jnp.zeros_like(token_ref)
 
 
 def base(scale, own, t_own):
+    rows = pl.BlockSpec((2, QUARTER, SIDE), lambda i: (0, i, 0))
     return pl.pallas_call(
         base_kernel,
-        out_shape=jax.ShapeDtypeStruct(own.shape, F32),
-        in_specs=[sm(), vm(), vm()],
-        out_specs=vm(),
+        grid=(4,),
+        out_shape=(jax.ShapeDtypeStruct(own.shape, F32), jax.ShapeDtypeStruct((8, 128), F32)),
+        in_specs=[sm(), rows, rows],
+        out_specs=(rows, pl.BlockSpec((8, 128), lambda i: (0, 0))),
         compiler_params=params(),
         cost_estimate=COST,
     )(scale, own, t_own)
@@ -411,11 +430,13 @@
 
 
 def finished_object(scale, start, left, above):
+    rows = pl.BlockSpec((2, QUARTER, SIDE), lambda i: (0, i, 0))
     return pl.pallas_call(
         object_kernel,
+        grid=(4,),
         out_shape=jax.ShapeDtypeStruct(start.shape, F32),
-        in_specs=[sm()] + [vm()] * 3,
-        out_specs=vm(),
+        in_specs=[sm()] + [rows] * 3,
+        out_specs=rows,
         compiler_params=params(),
         cost_estimate=COST,
     )(scale, start, left, above)
@@ -445,44 +466,44 @@
     )
     matrices = [jnp.asarray(m) for m in split_matrices()]
     pieces = [object_field[:, first : first + size] for first, size in zip(FIRSTS, SIZES)]
-    below = [shifted(piece, ROW, -1) for piece in pieces]
     right = shifted(object_field, COL, -1)
     *rolled, amps, peaks = ready(where, probe, object_field, amplitudes)
     scale = 0.9 / (peaks[1, :1, :1] + 1e-06)
     specs, wrapped, tokens = [], [], []
-    for k in range(PIECES):
-        after = (tokens[k - 1],) if k > 1 else (peaks,)
-        after += (below[k - 1],) if k else ()
-        (below[k],) = tied((below[k],), after)
-        corner = shifted(below[k], COL, -1)
-        spec, wrap, token = fore(k, where, object_field, right, below[k], corner, rolled[k], matrices)
+    for k, piece in enumerate(pieces):
+        below = shifted(piece, ROW, -1)
+        if k in (0, 3):
+            (below,) = tied((below,), tokens[:2] if k else (peaks,))
+        corner = shifted(below, COL, -1)
+        spec, wrap, token = fore(k, where, object_field, right, below, corner, rolled[k], matrices)
         specs.append(spec)
         wrapped.append(wrap)
         tokens.append(token)
-    t_own, t_right, t_below, t_diag, keep, send = update(
+    t_own, t_right, t_below, t_corner, keep, send = update(
         where, specs, wrapped, rolled, amps, peaks, matrices
     )
 
-    corner = shifted(t_diag, COL, 1)
+    corner = shifted(t_corner, COL, 1)
     half = first_sum(keep, other_core(send))
-    share = SIDE // 64
-    terms = lax.all_to_all(half.reshape(64, share, WIDE), CHIPS, 0, 0)
+    share = SIDE // 16
+    terms = lax.all_to_all(half.reshape(16, share, WIDE), SIDES, 0, 0)
     lower = lowered(t_below, corner, half)
     from_above = shifted(lower, ROW, 1)
-    (t_right,) = tied((t_right,), (lower,))
+    terms = middle(terms, 4, (lower,))
+    (t_right,) = tied((t_right,), (terms,))
     from_left = shifted(t_right, COL, 1)
-    at = lax.axis_index(CHIPS) * share
+    terms = lax.all_to_all(terms, "x", 0, 0)
+    at = lax.axis_index(SIDES) * share
     start = lax.dynamic_slice(probe, (core, at, jnp.zeros_like(at)), (1, share, SIDE))[0]
-    shares = shared(terms, start, [lower])
-    mine = lax.all_to_all(shares, CHIPS, 0, 0).reshape(SIDE, SIDE)
-    begun = base(scale, object_field, t_own)
-    (mine,) = tied((mine,), (from_above, from_left, begun))
+    mine = lax.all_to_all(shared(terms, start, 16), SIDES, 0, 0).reshape(SIDE, SIDE)
+    begun, token = base(scale, object_field, t_own)
+    (mine,) = tied((mine,), (from_above, from_left, token))
     new_probe = joined(core.astype(jnp.int32).reshape(1, 1), mine, other_core(mine))
     new_object = finished_object(scale, begun, from_left, from_above)
     return (new_object, new_probe)
 
 
-CHIPS = ("y", "x", "z")
+SIDES = ("y", "z")
 ROW = ("y", "x")
 COL = ("z", "core")
 

time: 223 us -> 224 us (level)
  waiting for transfers between devices: 105 us -> 92.8 us
  starting transfers between devices: 46.7 us -> 53.7 us
  Pallas kernels: 36.4 us -> 41.3 us
    ppermute x10 -> x12, waiting for transfers between devices: 52.7 us -> 42.9 us  [shifted(): lax.ppermute(value, axis, [(source, source + steps) for source in range(f...]
    ppermute x10 -> x12, starting transfers between devices: 24.3 us -> 31.3 us  [shifted(): lax.ppermute(value, axis, [(source, source + steps) for source in range(f...]
    ppermute x2, waiting for transfers between devices: 5.42 us -> 0.01 us  [other_core(): return lax.ppermute(value, 'core', [(0, 1), (1, 0)])]
    all_to_all x2 -> x3, starting transfers between devices: 21.6 us -> 18.6 us  [the longest x1 9.72 us: on_device(): terms = lax.all_to_all(half.reshape(16, share, WIDE), SIDES, 0, 0)]
    ppermute x2, starting transfers between devices: 0.8 us -> 3.81 us  [other_core(): return lax.ppermute(value, 'core', [(0, 1), (1, 0)])]
    all_to_all x2 -> x3, waiting for transfers between devices: 47 us -> 50 us  [the longest x1 38.2 us: on_device(): terms = lax.all_to_all(terms, 'x', 0, 0)]
    pallas_call x3 -> x4, Pallas kernels: 4.23 us -> 5.99 us  [the longest x1 4.37 us: finished_object(): pl.pallas_call(object_kernel, grid=(4,), out_shape=jax.ShapeDtypeStruct(s...]
    pallas_call x3 -> x4, Pallas kernels: 8.74 us -> 10.4 us  [fore(): pl.pallas_call(functools.partial(fore_kernel, piece), grid=(1,), out_shap...]
  transfers between devices with their start and end apart: 14 -> 17, of which waited for: 7 -> 7; matrix products, arithmetic and copies ran while one was open for 2% -> 2% of each run, Pallas kernels for 8% -> 10%
where the time goes in v5:
time: 224 us; the launch traced here: 220 us
  waiting for transfers between devices  92.8 us (41%)
  starting transfers between devices  53.7 us (24%)
  Pallas kernels  41.3 us (18%)
  local copies, waits for them, and re-layouts  30.5 us (14%)
    ppermute x12, waiting for transfers between devices, shifted(): lax.ppermute(value, axis, [(source, source + steps) for source in range(f...  42.9 us
    all_to_all x1, waiting for transfers between devices, on_device(): terms = lax.all_to_all(terms, 'x', 0, 0)  38.2 us
    ppermute x12, starting transfers between devices, shifted(): lax.ppermute(value, axis, [(source, source + steps) for source in range(f...  31.3 us
    unnamed x82, local copies, waits for them, and re-layouts  26.3 us
    pallas_call x1, Pallas kernels, update(): pl.pallas_call(update_kernel, out_shape=out_shape, in_specs=[sm()] + [vm(...  14.6 us
    pallas_call x4, Pallas kernels, fore(): pl.pallas_call(functools.partial(fore_kernel, piece), grid=(1,), out_shap...  10.4 us
    all_to_all x1, starting transfers between devices, on_device(): terms = lax.all_to_all(half.reshape(16, share, WIDE), SIDES, 0, 0)  9.72 us
    all_to_all x1, waiting for transfers between devices, on_device(): lax.all_to_all(shared(terms, start, 16), SIDES, 0, 0).reshape(SIDE, SIDE)  7.82 us
  transfers between devices with their start and end apart: 17, of which 7 were waited for; matrix products, arithmetic and copies ran while one was open for 2% of the time, Pallas kernels for 10%

profile of v5, /device:TPU:33, one launch (start us, length us, event | category | flops | bytes accessed | tf_op | source)
XLA Modules:
  0.0 220.5 jit_solution(13723820954002298760)
XLA Ops:
  0.6 2.7 %collective-permute-start = (f32[2,512,512]{2,1,0:T(8,128)}, f32[2,512,512]{2,1,0:T(8,128)}, u32[]{:S(2)}, u32[]{:S(2)}) collective-permute-start(f32[2,512,512]{2,1,0:T(8,128)} %own_ref.11), channel_id=1, source_target_pairs={{1,0},{2,1},{3,2},{4,3},{5,4},{6,5},{7,6},{9,8},{10,9},{11,10},{12... | collective-permute-start | bytes 6291464 | tf_op jit(solution)/shard_map/ppermute | solution.py:403
  3.4 2.9 %fusion = (f32[2,128,512]{2,1,0:T(8,128)}, f32[2,128,512]{2,1,0:T(8,128)}, f32[2,128,512]{2,1,0:T(8,128)}, f32[2,128,512]{2,1,0:T(8,128)}) fusion(f32[2,512,512]{2,1,0:T(8,128)} %own_ref.11), kind=kLoop, calls=%fused_computation.5 | loop fusion | bytes 4194304 | tf_op jit(solution)/shard_map/slice | solution.py:468
  6.3 1.3 collective-permute-start.3
  7.5 1.3 collective-permute-start.1
  8.8 1.3 collective-permute-start.5
  10.5 11.5 %collective-permute-done.3.below_ref = f32[2,128,512]{2,1,0:T(8,128)} collective-permute-done((f32[2,128,512]{2,1,0:T(8,128)}, f32[2,128,512]{2,1,0:T(8,128)}, u32[]{:S(2)}, u32[]{:S(2)}) %collective-permute-start.3) | collective-permute-done | bytes 524320 | tf_op jit(solution)/shard_map/ppermute | solution.py:403
  22.0 3.1 %collective-permute-start.4 = (f32[2,128,512]{2,1,0:T(8,128)}, f32[2,128,512]{2,1,0:T(8,128)}, u32[]{:S(2)}, u32[]{:S(2)}) collective-permute-start(f32[2,128,512]{2,1,0:T(8,128)} %collective-permute-done.3.below_ref), channel_id=1, source_target_pairs={{1,0},{2,1},{3,2},{4,3},{5,4},{6,5},{7,6},{9,8},{10,9},{11,10},{12... | collective-permute-start | bytes 1572872 | tf_op jit(solution)/shard_map/ppermute | solution.py:403
  25.1 1.6 copy-done.17
  26.7 1.6 copy-done.18
  28.3 1.0 copy-done.34
  29.3 4.5 %shard_map.104 = (f32[2,2,128,512]{3,2,1,0:T(8,128)S(1)}, f32[2,2,128,512]{3,2,1,0:T(8,128)S(1)}, f32[2,2,128,512]{3,2,1,0:T(8,128)S(1)}, f32[2,2,128,512]{3,2,1...) custom-call(s32[3,2]{1,0:T(4,128)S(1)} %pad_add_fusion.where_ref, f32[2,512,512]{2,1,0:T(8,128)S(1)} %copy-done.17, ...), custom_call_target="tpu_custom_call" | custom-call | tf_op jit(solution)/shard_map/pallas_call | solution.py:275
  36.8 1.0 copy-done.14
  37.8 1.3 copy-done.23
  39.7 1.9 collective-permute-start.2
  41.6 1.3 collective-permute-start.7
  42.9 1.5 collective-permute-done.5.below_ref
  44.5 2.7 %collective-permute-start.6 = (f32[2,128,512]{2,1,0:T(8,128)}, f32[2,128,512]{2,1,0:T(8,128)}, u32[]{:S(2)}, u32[]{:S(2)}) collective-permute-start(f32[2,128,512]{2,1,0:T(8,128)} %collective-permute-done.5.below_ref), channel_id=1, source_target_pairs={{1,0},{2,1},{3,2},{4,3},{5,4},{6,5},{7,6},{9,8},{10,9},{11,10},{12... | collective-permute-start | bytes 1572872 | tf_op jit(solution)/shard_map/ppermute | solution.py:403
  47.2 1.2 copy-done.9
  48.4 2.4 %shard_map.107 = (f32[2,2,128,512]{3,2,1,0:T(8,128)S(1)}, f32[2,2,128,512]{3,2,1,0:T(8,128)S(1)}, f32[8,128]{1,0:T(8,128)S(1)}) custom-call(s32[3,2]{1,0:T(4,128)S(1)} %pad_add_fusion.where_ref, f32[2,512,512]{2,1,0:T(8,128)S(1)} %copy-done, f32[2,512,512]{2,1,0:T(8,128)} %collective-permute-done.right_ref, f32[2,128,512]{2,1,0:T(8,128)} %collective-permute-done.3.below_ref, ...), custom_call_target="tpu_custom_call" | custom-call | tf_op jit(solution)/shard_map/pallas_call | solution.py:136
  50.9 1.0 copy-done.24
  51.9 1.0 copy-done.26
  52.9 2.2 shard_map.106
  55.1 1.1 copy-done.28
  57.7 2.5 %collective-permute-start.8 = (f32[2,128,512]{2,1,0:T(8,128)}, f32[2,128,512]{2,1,0:T(8,128)S(1)}, u32[]{:S(2)}, u32[]{:S(2)}) collective-permute-start(f32[2,128,512]{2,1,0:T(8,128)} %shard_map.109.below_ref), channel_id=1, source_target_pairs={{1,0},{2,1},{3,2},{4,3},{5,4},{6,5},{7,6},{9,8},{10,9},{11,10},{12... | collective-permute-start | bytes 1572872 | tf_op jit(solution)/shard_map/ppermute | solution.py:403
  60.3 1.2 copy-done.12
  61.5 2.9 %shard_map.108 = (f32[2,2,128,512]{3,2,1,0:T(8,128)S(1)}, f32[2,2,128,512]{3,2,1,0:T(8,128)S(1)}, f32[8,128]{1,0:T(8,128)}) custom-call(s32[3,2]{1,0:T(4,128)S(1)} %pad_add_fusion.where_ref, f32[2,512,512]{2,1,0:T(8,128)S(1)} %copy-done, f32[2,512,512]{2,1,0:T(8,128)} %collective-permute-done.right_ref, f32[2,128,512]{2,1,0:T(8,128)} %collective-permute-done.5.below_ref, ...), custom_call_target="tpu_custom_call" | custom-call | tf_op jit(solution)/shard_map/pallas_call | solution.py:136
  64.5 4.2 %collective-permute-done.8.diag_ref = f32[2,128,512]{2,1,0:T(8,128)S(1)} collective-permute-done((f32[2,128,512]{2,1,0:T(8,128)}, f32[2,128,512]{2,1,0:T(8,128)S(1)}, u32[]{:S(2)}, u32[]{:S(2)}) %collective-permute-start.8) | collective-permute-done | bytes 524320 | tf_op jit(solution)/shard_map/ppermute | solution.py:403
  68.7 2.8 %shard_map.110 = (f32[2,2,128,512]{3,2,1,0:T(8,128)S(1)}, f32[2,2,128,512]{3,2,1,0:T(8,128)S(1)}, f32[8,128]{1,0:T(8,128)}) custom-call(s32[3,2]{1,0:T(4,128)S(1)} %pad_add_fusion.where_ref, f32[2,512,512]{2,1,0:T(8,128)S(1)} %copy-done, f32[2,512,512]{2,1,0:T(8,128)} %collective-permute-done.right_ref, f32[2,128,512]{2,1,0:T(8,128)} %shard_map.109.below_ref, ...), custom_call_target="tpu_custom_call" | custom-call | tf_op jit(solution)/shard_map/pallas_call | solution.py:136
  72.1 14.6 %shard_map.111 = (f32[2,512,512]{2,1,0:T(8,128)}, f32[2,512,512]{2,1,0:T(8,128)}, f32[2,512,512]{2,1,0:T(8,128)}, f32[2,512,512]{2,1,0:T(8,128)}, f32[512,640]{1,0:T(8,128)S(1)}, /*index=5*/f32[512,640]{1,0:T(8,128)S(1)}) custom-call(s32[3,2]{1,0:T(4,128)S(1)} %pad_add_fusion.where_ref, f32[2,2,128,512]{3,2,1,0:T(8,128)S(1)} %copy-done.29, ...), custom_call_target="tpu_custom_call" | custom-call | tf_op jit(solution)/shard_map/pallas_call | solution.py:296
  86.8 3.8 %collective-permute-start.10 = (f32[2,512,512]{2,1,0:T(8,128)}, f32[2,512,512]{2,1,0:T(8,128)}, u32[]{:S(2)}, u32[]{:S(2)}) collective-permute-start(f32[2,512,512]{2,1,0:T(8,128)} %get-tuple-element.48), channel_id=1, source_target_pairs={{0,1},{1,2},{2,3},{3,4},{4,5},{5,6},{6,7},{8,9},{9,10},{10,11},{11... | collective-permute-start | bytes 6291464 | tf_op jit(solution)/shard_map/ppermute | solution.py:403
  90.6 1.2 shard_map.113.after_ref
  91.8 9.7 %all-to-all-start = ((f32[16,32,640]{2,1,0:T(8,128)}), f32[16,32,640]{2,1,0:T(8,128)S(1)}, u32[]{:S(2)}, u32[]{:S(2)}) async-start(f32[16,32,640]{2,1,0:T(8,128)} %bitcast.4), calls=%async_computation | async-start | bytes 2621440 | tf_op jit(solution)/shard_map/all_to_all | solution.py:489
  101.5 25.6 %collective-permute-done.10.corner_ref = f32[2,512,512]{2,1,0:T(8,128)} collective-permute-done((f32[2,512,512]{2,1,0:T(8,128)}, f32[2,512,512]{2,1,0:T(8,128)}, u32[]{:S(2)}, u32[]{:S(2)}) %collective-permute-start.10) | collective-permute-done | bytes 2097184 | tf_op jit(solution)/shard_map/ppermute | solution.py:403
  127.1 1.6 copy-done.20
  128.6 3.2 %shard_map.114.refs_0_ = f32[2,512,512]{2,1,0:T(8,128)} custom-call(f32[2,512,512]{2,1,0:T(8,128)S(1)} %copy-done.20, f32[2,512,512]{2,1,0:T(8,128)} %collective-permute-done.10.corner_ref, f32[512,640]{1,0:T(8,128)} %shard_map.113.after_ref), custom_call_target="tpu_custom_call" | custom-call | tf_op jit(solution)/shard_map/pallas_call | solution.py:351
  131.8 3.5 %collective-permute-start.12 = (f32[2,512,512]{2,1,0:T(8,128)}, f32[2,512,512]{2,1,0:T(8,128)}, u32[]{:S(2)}, u32[]{:S(2)}) collective-permute-start(f32[2,512,512]{2,1,0:T(8,128)} %shard_map.114.refs_0_), channel_id=1, source_target_pairs={{0,8},{8,16},{16,24},{24,32},{32,40},{40,48},{48,56},{56,64},{64,7... | collective-permute-start | bytes 6291464 | tf_op jit(solution)/shard_map/ppermute | solution.py:403
  135.4 3.9 %all-to-all-done.terms_ref = f32[16,32,640]{2,1,0:T(8,128)S(1)} async-done(((f32[16,32,640]{2,1,0:T(8,128)}), f32[16,32,640]{2,1,0:T(8,128)S(1)}, u32[]{:S(2)}, u32[]{:S(2)}) %all-to-all-start) | async-done | bytes 1310752 | tf_op jit(solution)/shard_map/all_to_all | solution.py:489
  140.1 6.0 %collective-permute-start.11 = (f32[2,512,512]{2,1,0:T(8,128)}, f32[2,512,512]{2,1,0:T(8,128)}, u32[]{:S(2)}, u32[]{:S(2)}) collective-permute-start(f32[2,512,512]{2,1,0:T(8,128)} %shard_map.116), channel_id=1, source_target_pairs={{0,1},{1,2},{2,3},{3,4},{4,5},{5,6},{6,7},{8,9},{9,10},{10,11},{11... | collective-permute-start | bytes 6291464 | tf_op jit(solution)/shard_map/ppermute | solution.py:403
  146.0 3.5 %all-to-all-start.1 = ((f32[4,32,640]{2,1,0:T(8,128)}), f32[4,32,640]{2,1,0:T(8,128)S(1)}, u32[]{:S(2)}, u32[]{:S(2)}) async-start(f32[4,32,640]{2,1,0:T(8,128)} %shard_map.115.refs_1_), calls=%async_computation.1 | async-start | bytes 655360 | tf_op jit(solution)/shard_map/all_to_all | solution.py:495
  150.4 38.2 %all-to-all-done.1.terms_ref = f32[4,32,640]{2,1,0:T(8,128)S(1)} async-done(((f32[4,32,640]{2,1,0:T(8,128)}), f32[4,32,640]{2,1,0:T(8,128)S(1)}, u32[]{:S(2)}, u32[]{:S(2)}) %all-to-all-start.1) | async-done | bytes 327712 | tf_op jit(solution)/shard_map/all_to_all | solution.py:495
  189.7 5.4 %all-to-all-start.2 = ((f32[16,32,512]{2,1,0:T(8,128)}), f32[16,32,512]{2,1,0:T(8,128)S(1)}, u32[]{:S(2)}, u32[]{:S(2)}) async-start(f32[16,32,512]{2,1,0:T(8,128)} %copy-done.16), calls=%async_computation.2 | async-start | bytes 2097152 | tf_op jit(solution)/shard_map/all_to_all | solution.py:498
  196.3 1.6 copy-done.19
  198.6 1.3 copy-done.21
  200.5 7.8 %all-to-all-done.2 = f32[16,32,512]{2,1,0:T(8,128)S(1)} async-done(((f32[16,32,512]{2,1,0:T(8,128)}), f32[16,32,512]{2,1,0:T(8,128)S(1)}, u32[]{:S(2)}, u32[]{:S(2)}) %all-to-all-start.2) | async-done | bytes 1048608 | tf_op jit(solution)/shard_map/all_to_all | solution.py:498
  209.3 3.7 %collective-permute-start.13 = (f32[512,512]{1,0:T(8,128)}, f32[512,512]{1,0:T(8,128)S(1)}, u32[]{:S(2)}, u32[]{:S(2)}) collective-permute-start(f32[512,512]{1,0:T(8,128)} %shard_map.119.mine_ref), channel_id=1, source_target_pairs={{0,1},{1,0},{2,3},{3,2},{4,5},{5,4},{6,7},{7,6},{8,9},{9,8},{10,11... | collective-permute-start | bytes 3145736 | tf_op jit(solution)/shard_map/ppermute | solution.py:407
  213.0 1.6 copy-done.22
  214.6 4.4 %shard_map.117 = f32[2,512,512]{2,1,0:T(8,128)} custom-call(f32[1,1]{1,0:T(1,128)} %bitcast.3.scale_ref, f32[2,512,512]{2,1,0:T(8,128)S(1)} %copy-done.22, f32[2,512,512]{2,1,0:T(8,128)} %collective-permute-done.11.left_ref.refs_2_, f32[2,512,512]{2,1,0:T(8,128)} %collective-permute-done.12.above_ref.refs_1_), custom_call_target="tpu_custom_call" | custom-call | tf_op jit(solution)/shard_map/pallas_call | solution.py:434
  219.0 1.5 shard_map.120
  (91 shorter events, 11.6 us)
Async XLA Ops:
  0.6 24.5 %copy-start = (f32[2,512,512]{2,1,0:T(8,128)S(1)}, f32[2,512,512]{2,1,0:T(8,128)}, u32[]{:S(2)}) copy-start(f32[2,512,512]{2,1,0:T(8,128)} %own_ref.11) | copy-start | bytes 6291460
  0.6 9.6 %copy-start.40 = (s32[2,2]{1,0:T(2,128)S(1)}, s32[2,2]{1,0:T(2,128)}, u32[]{:S(2)}) copy-start(s32[2,2]{1,0:T(2,128)} %param.12) | copy-start | bytes 52
  0.6 46.5 %collective-permute-start = (f32[2,512,512]{2,1,0:T(8,128)}, f32[2,512,512]{2,1,0:T(8,128)}, u32[]{:S(2)}, u32[]{:S(2)}) collective-permute-start(f32[2,512,512]{2,1,0:T(8,128)} %own_ref.11), channel_id=1, source_target_pairs={{1,0},{2,1},{3,2},{4,3},{5,4},{6,5},{7,6},{9,8},{10,9},{11,10},{12... | collective-permute-start | bytes 6291464 | tf_op jit(solution)/shard_map/ppermute | solution.py:403
  6.3 15.7 %collective-permute-start.3 = (f32[2,128,512]{2,1,0:T(8,128)}, f32[2,128,512]{2,1,0:T(8,128)}, u32[]{:S(2)}, u32[]{:S(2)}) collective-permute-start(f32[2,128,512]{2,1,0:T(8,128)} %get-tuple-element.54), channel_id=1, source_target_pairs={{8,0},{16,8},{24,16},{32,24},{40,32},{48,40},{56,48},{64,56},{72,6... | collective-permute-start | bytes 1572872 | tf_op jit(solution)/shard_map/ppermute | solution.py:403
  7.5 32.2 %collective-permute-start.1 = (f32[2,128,512]{2,1,0:T(8,128)}, f32[2,128,512]{2,1,0:T(8,128)}, u32[]{:S(2)}, u32[]{:S(2)}) collective-permute-start(f32[2,128,512]{2,1,0:T(8,128)} %get-tuple-element.55), channel_id=1, source_target_pairs={{8,0},{16,8},{24,16},{32,24},{40,32},{48,40},{56,48},{64,56},{72,6... | collective-permute-start | bytes 1572872 | tf_op jit(solution)/shard_map/ppermute | solution.py:403
  8.8 35.6 %collective-permute-start.5 = (f32[2,128,512]{2,1,0:T(8,128)}, f32[2,128,512]{2,1,0:T(8,128)}, u32[]{:S(2)}, u32[]{:S(2)}) collective-permute-start(f32[2,128,512]{2,1,0:T(8,128)} %get-tuple-element.53), channel_id=1, source_target_pairs={{8,0},{16,8},{24,16},{32,24},{40,32},{48,40},{56,48},{64,56},{72,6... | collective-permute-start | bytes 1572872 | tf_op jit(solution)/shard_map/ppermute | solution.py:403
  10.4 36.8 %copy-start.1 = (bf16[4,256,256]{2,1,0:T(8,128)(2,1)S(1)}, bf16[4,256,256]{2,1,0:T(8,128)(2,1)}, u32[]{:S(2)}) copy-start(bf16[4,256,256]{2,1,0:T(8,128)(2,1)} %constant.43.clone.mh_ref.refs_16_) | copy-start | bytes 1572868
  10.4 36.8 %copy-start.2 = (bf16[4,256,256]{2,1,0:T(8,128)(2,1)S(1)}, bf16[4,256,256]{2,1,0:T(8,128)(2,1)}, u32[]{:S(2)}) copy-start(bf16[4,256,256]{2,1,0:T(8,128)(2,1)} %constant.44.clone.ml_ref.refs_17_) | copy-start | bytes 1572868
  22.0 25.2 %collective-permute-start.4 = (f32[2,128,512]{2,1,0:T(8,128)}, f32[2,128,512]{2,1,0:T(8,128)}, u32[]{:S(2)}, u32[]{:S(2)}) collective-permute-start(f32[2,128,512]{2,1,0:T(8,128)} %collective-permute-done.3.below_ref), channel_id=1, source_target_pairs={{1,0},{2,1},{3,2},{4,3},{5,4},{6,5},{7,6},{9,8},{10,9},{11,10},{12... | collective-permute-start | bytes 1572872 | tf_op jit(solution)/shard_map/ppermute | solution.py:403
  25.1 1.6 copy-start.17
  26.7 1.6 copy-start.18
  28.3 1.0 copy-start.34
  36.8 1.0 copy-start.14
  37.8 1.3 copy-start.23
  39.7 13.2 %collective-permute-start.2 = (f32[2,128,512]{2,1,0:T(8,128)}, f32[2,128,512]{2,1,0:T(8,128)S(1)}, u32[]{:S(2)}, u32[]{:S(2)}) collective-permute-start(f32[2,128,512]{2,1,0:T(8,128)} %shard_map.105.below_ref), channel_id=1, source_target_pairs={{1,0},{2,1},{3,2},{4,3},{5,4},{6,5},{7,6},{9,8},{10,9},{11,10},{12... | collective-permute-start | bytes 1572872 | tf_op jit(solution)/shard_map/ppermute | solution.py:403
  41.6 16.1 %collective-permute-start.7 = (f32[2,128,512]{2,1,0:T(8,128)}, f32[2,128,512]{2,1,0:T(8,128)}, u32[]{:S(2)}, u32[]{:S(2)}) collective-permute-start(f32[2,128,512]{2,1,0:T(8,128)} %get-tuple-element.52), channel_id=1, source_target_pairs={{8,0},{16,8},{24,16},{32,24},{40,32},{48,40},{56,48},{64,56},{72,6... | collective-permute-start | bytes 1572872 | tf_op jit(solution)/shard_map/ppermute | solution.py:403
  44.5 15.8 %collective-permute-start.6 = (f32[2,128,512]{2,1,0:T(8,128)}, f32[2,128,512]{2,1,0:T(8,128)}, u32[]{:S(2)}, u32[]{:S(2)}) collective-permute-start(f32[2,128,512]{2,1,0:T(8,128)} %collective-permute-done.5.below_ref), channel_id=1, source_target_pairs={{1,0},{2,1},{3,2},{4,3},{5,4},{6,5},{7,6},{9,8},{10,9},{11,10},{12... | collective-permute-start | bytes 1572872 | tf_op jit(solution)/shard_map/ppermute | solution.py:403
  47.2 1.2 copy-start.9
  48.4 4.4 %copy-start.6 = (f32[2,2,128,512]{3,2,1,0:T(8,128)S(1)}, f32[2,2,128,512]{3,2,1,0:T(8,128)}, u32[]{:S(2)}) copy-start(f32[2,2,128,512]{3,2,1,0:T(8,128)} %copy-done.5) | copy-start | bytes 3145732
  50.9 1.0 copy-start.24
  52.9 2.2 %copy-start.37 = (f32[8,128]{1,0:T(8,128)}, f32[8,128]{1,0:T(8,128)S(1)}, u32[]{:S(2)}) copy-start(f32[8,128]{1,0:T(8,128)S(1)} %get-tuple-element.34.refs_2_) | copy-start | bytes 12292
  55.1 1.1 copy-start.28
  57.7 11.0 %collective-permute-start.8 = (f32[2,128,512]{2,1,0:T(8,128)}, f32[2,128,512]{2,1,0:T(8,128)S(1)}, u32[]{:S(2)}, u32[]{:S(2)}) collective-permute-start(f32[2,128,512]{2,1,0:T(8,128)} %shard_map.109.below_ref), channel_id=1, source_target_pairs={{1,0},{2,1},{3,2},{4,3},{5,4},{6,5},{7,6},{9,8},{10,9},{11,10},{12... | collective-permute-start | bytes 1572872 | tf_op jit(solution)/shard_map/ppermute | solution.py:403
  60.3 1.2 copy-start.12
  61.5 7.2 %copy-start.15 = (f32[2,2,128,512]{3,2,1,0:T(8,128)S(1)}, f32[2,2,128,512]{3,2,1,0:T(8,128)}, u32[]{:S(2)}) copy-start(f32[2,2,128,512]{3,2,1,0:T(8,128)} %copy-done.14) | copy-start | bytes 3145732
  61.5 10.0 %copy-start.32 = (bf16[4,256,256]{2,1,0:T(8,128)(2,1)S(1)}, bf16[4,256,256]{2,1,0:T(8,128)(2,1)}, u32[]{:S(2)}) copy-start(bf16[4,256,256]{2,1,0:T(8,128)(2,1)} %constant.41.clone.refs_14_) | copy-start | bytes 1572868
  61.5 10.0 %copy-start.33 = (bf16[4,256,256]{2,1,0:T(8,128)(2,1)S(1)}, bf16[4,256,256]{2,1,0:T(8,128)(2,1)}, u32[]{:S(2)}) copy-start(bf16[4,256,256]{2,1,0:T(8,128)(2,1)} %constant.42.clone.refs_15_) | copy-start | bytes 1572868
  68.7 2.9 %copy-start.7 = (f32[2,2,128,512]{3,2,1,0:T(8,128)S(1)}, f32[2,2,128,512]{3,2,1,0:T(8,128)}, u32[]{:S(2)}) copy-start(f32[2,2,128,512]{3,2,1,0:T(8,128)} %copy-done.5) | copy-start | bytes 3145732
  68.7 2.9 %copy-start.10 = (f32[2,2,128,512]{3,2,1,0:T(8,128)S(1)}, f32[2,2,128,512]{3,2,1,0:T(8,128)}, u32[]{:S(2)}) copy-start(f32[2,2,128,512]{3,2,1,0:T(8,128)} %copy-done.8) | copy-start | bytes 3145732
  68.7 2.9 %copy-start.13 = (f32[2,2,128,512]{3,2,1,0:T(8,128)S(1)}, f32[2,2,128,512]{3,2,1,0:T(8,128)}, u32[]{:S(2)}) copy-start(f32[2,2,128,512]{3,2,1,0:T(8,128)} %copy-done.11) | copy-start | bytes 3145732
  68.7 2.9 %copy-start.25 = (f32[2,2,128,512]{3,2,1,0:T(8,128)S(1)}, f32[2,2,128,512]{3,2,1,0:T(8,128)}, u32[]{:S(2)}) copy-start(f32[2,2,128,512]{3,2,1,0:T(8,128)} %copy-done.24) | copy-start | bytes 3145732
  68.7 2.9 %copy-start.27 = (f32[2,2,128,512]{3,2,1,0:T(8,128)S(1)}, f32[2,2,128,512]{3,2,1,0:T(8,128)}, u32[]{:S(2)}) copy-start(f32[2,2,128,512]{3,2,1,0:T(8,128)} %copy-done.26) | copy-start | bytes 3145732
  68.7 3.1 %copy-start.29 = (f32[2,2,128,512]{3,2,1,0:T(8,128)S(1)}, f32[2,2,128,512]{3,2,1,0:T(8,128)}, u32[]{:S(2)}) copy-start(f32[2,2,128,512]{3,2,1,0:T(8,128)} %copy-done.28) | copy-start | bytes 3145732
  68.7 3.4 %copy-start.31 = (f32[2,2,128,512]{3,2,1,0:T(8,128)S(1)}, f32[2,2,128,512]{3,2,1,0:T(8,128)}, u32[]{:S(2)}) copy-start(f32[2,2,128,512]{3,2,1,0:T(8,128)} %copy-done.30) | copy-start | bytes 3145732
  68.7 3.4 %copy-start.36 = (f32[2,8,128]{2,1,0:T(8,128)S(1)}, f32[2,8,128]{2,1,0:T(8,128)}, u32[]{:S(2)}) copy-start(f32[2,8,128]{2,1,0:T(8,128)} %copy-done.35) | copy-start | bytes 24580
  86.7 3.9 %collective-permute-start.9 = (f32[512,640]{1,0:T(8,128)S(1)}, f32[512,640]{1,0:T(8,128)S(1)}, u32[]{:S(2)}, u32[]{:S(2)}) collective-permute-start(f32[512,640]{1,0:T(8,128)S(1)} %get-tuple-element.46), channel_id=1, source_target_pairs={{0,1},{1,0},{2,3},{3,2},{4,5},{5,4},{6,7},{7,6},{8,9},{9,8},{10,11... | collective-permute-start | bytes 3932168 | tf_op jit(solution)/shard_map/ppermute | solution.py:407
  86.8 40.2 %collective-permute-start.10 = (f32[2,512,512]{2,1,0:T(8,128)}, f32[2,512,512]{2,1,0:T(8,128)}, u32[]{:S(2)}, u32[]{:S(2)}) collective-permute-start(f32[2,512,512]{2,1,0:T(8,128)} %get-tuple-element.48), channel_id=1, source_target_pairs={{0,1},{1,2},{2,3},{3,4},{4,5},{5,6},{6,7},{8,9},{9,10},{10,11},{11... | collective-permute-start | bytes 6291464 | tf_op jit(solution)/shard_map/ppermute | solution.py:403
  91.8 47.5 %all-to-all-start = ((f32[16,32,640]{2,1,0:T(8,128)}), f32[16,32,640]{2,1,0:T(8,128)S(1)}, u32[]{:S(2)}, u32[]{:S(2)}) async-start(f32[16,32,640]{2,1,0:T(8,128)} %bitcast.4), calls=%async_computation | async-start | bytes 2621440 | tf_op jit(solution)/shard_map/all_to_all | solution.py:489
  127.1 1.6 copy-start.20
  131.8 76.5 %collective-permute-start.12 = (f32[2,512,512]{2,1,0:T(8,128)}, f32[2,512,512]{2,1,0:T(8,128)}, u32[]{:S(2)}, u32[]{:S(2)}) collective-permute-start(f32[2,512,512]{2,1,0:T(8,128)} %shard_map.114.refs_0_), channel_id=1, source_target_pairs={{0,8},{8,16},{16,24},{24,32},{32,40},{40,48},{48,56},{56,64},{64,7... | collective-permute-start | bytes 6291464 | tf_op jit(solution)/shard_map/ppermute | solution.py:403
  140.1 68.3 %collective-permute-start.11 = (f32[2,512,512]{2,1,0:T(8,128)}, f32[2,512,512]{2,1,0:T(8,128)}, u32[]{:S(2)}, u32[]{:S(2)}) collective-permute-start(f32[2,512,512]{2,1,0:T(8,128)} %shard_map.116), channel_id=1, source_target_pairs={{0,1},{1,2},{2,3},{3,4},{4,5},{5,6},{6,7},{8,9},{9,10},{10,11},{11... | collective-permute-start | bytes 6291464 | tf_op jit(solution)/shard_map/ppermute | solution.py:403
  146.0 42.6 %all-to-all-start.1 = ((f32[4,32,640]{2,1,0:T(8,128)}), f32[4,32,640]{2,1,0:T(8,128)S(1)}, u32[]{:S(2)}, u32[]{:S(2)}) async-start(f32[4,32,640]{2,1,0:T(8,128)} %shard_map.115.refs_1_), calls=%async_computation.1 | async-start | bytes 655360 | tf_op jit(solution)/shard_map/all_to_all | solution.py:495
  189.7 18.6 %all-to-all-start.2 = ((f32[16,32,512]{2,1,0:T(8,128)}), f32[16,32,512]{2,1,0:T(8,128)S(1)}, u32[]{:S(2)}, u32[]{:S(2)}) async-start(f32[16,32,512]{2,1,0:T(8,128)} %copy-done.16), calls=%async_computation.2 | async-start | bytes 2097152 | tf_op jit(solution)/shard_map/all_to_all | solution.py:498
  196.3 1.6 copy-start.19
  198.6 1.3 copy-start.21
  209.3 9.7 %collective-permute-start.13 = (f32[512,512]{1,0:T(8,128)}, f32[512,512]{1,0:T(8,128)S(1)}, u32[]{:S(2)}, u32[]{:S(2)}) collective-permute-start(f32[512,512]{1,0:T(8,128)} %shard_map.119.mine_ref), channel_id=1, source_target_pairs={{0,1},{1,0},{2,3},{3,2},{4,5},{5,4},{6,7},{7,6},{8,9},{9,8},{10,11... | collective-permute-start | bytes 3145736 | tf_op jit(solution)/shard_map/ppermute | solution.py:407
  213.0 1.6 copy-start.22
  214.6 4.4 %copy-start.4 = (f32[512,512]{1,0:T(8,128)S(1)}, f32[512,512]{1,0:T(8,128)}, u32[]{:S(2)}) copy-start(f32[512,512]{1,0:T(8,128)} %shard_map.119.mine_ref) | copy-start | bytes 3145732
  (10 other events, 8.6 us)

commit v6 on v5

--- a/solution.py
+++ b/solution.py
@@ -348,11 +348,13 @@
 
 
 def lowered(below, corner, after):
+    rows = pl.BlockSpec((2, QUARTER, SIDE), lambda i: (0, i, 0))
     return pl.pallas_call(
         lower_kernel,
+        grid=(4,),
         out_shape=jax.ShapeDtypeStruct(below.shape, F32),
-        in_specs=[vm(), vm(), anywhere()],
-        out_specs=vm(),
+        in_specs=[rows, rows, anywhere()],
+        out_specs=rows,
         compiler_params=params(),
         cost_estimate=COST,
     )(below, corner, after)
@@ -473,7 +475,7 @@
     for k, piece in enumerate(pieces):
         below = shifted(piece, ROW, -1)
         if k in (0, 3):
-            (below,) = tied((below,), tokens[:2] if k else (peaks,))
+            (below,) = tied((below,), tokens[:1] if k else (peaks,))
         corner = shifted(below, COL, -1)
         spec, wrap, token = fore(k, where, object_field, right, below, corner, rolled[k], matrices)
         specs.append(spec)
@@ -486,16 +488,17 @@
     corner = shifted(t_corner, COL, 1)
     half = first_sum(keep, other_core(send))
     share = SIDE // 16
-    terms = lax.all_to_all(half.reshape(16, share, WIDE), SIDES, 0, 0)
+    terms = lax.all_to_all(half.reshape(16, share, WIDE), ROW, 0, 0)
     lower = lowered(t_below, corner, half)
     from_above = shifted(lower, ROW, 1)
+    (t_right,) = tied((t_right,), (half,))
+    from_left = shifted(t_right, COL, 1)
     terms = middle(terms, 4, (lower,))
-    (t_right,) = tied((t_right,), (terms,))
-    from_left = shifted(t_right, COL, 1)
-    terms = lax.all_to_all(terms, "x", 0, 0)
-    at = lax.axis_index(SIDES) * share
+    terms = lax.all_to_all(terms, "z", 0, 0)
+    at = lax.axis_index(ROW) * share
     start = lax.dynamic_slice(probe, (core, at, jnp.zeros_like(at)), (1, share, SIDE))[0]
-    mine = lax.all_to_all(shared(terms, start, 16), SIDES, 0, 0).reshape(SIDE, SIDE)
+    shares = shared(terms, start, 16)
+    mine = lax.all_to_all(shares, ROW, 0, 0).reshape(SIDE, SIDE)
     begun, token = base(scale, object_field, t_own)
     (mine,) = tied((mine,), (from_above, from_left, token))
     new_probe = joined(core.astype(jnp.int32).reshape(1, 1), mine, other_core(mine))
@@ -503,7 +506,6 @@
     return (new_object, new_probe)
 
 
-SIDES = ("y", "z")
 ROW = ("y", "x")
 COL = ("z", "core")
 

time: 224 us -> 193 us (0.86)
  waiting for transfers between devices: 92.8 us -> 66.9 us
    ppermute x12, waiting for transfers between devices: 42.9 us -> 21.1 us  [shifted(): lax.ppermute(value, axis, [(source, source + steps) for source in range(f...]
    all_to_all x3, waiting for transfers between devices: 50 us -> 40.5 us  [the longest x1 30.2 us: on_device(): mine = lax.all_to_all(shares, ROW, 0, 0).reshape(SIDE, SIDE)]
    ppermute x2, waiting for transfers between devices: 0.01 us -> 5.42 us  [other_core(): return lax.ppermute(value, 'core', [(0, 1), (1, 0)])]
    ppermute x12, starting transfers between devices: 31.3 us -> 28.5 us  [shifted(): lax.ppermute(value, axis, [(source, source + steps) for source in range(f...]
    all_to_all x3, starting transfers between devices: 18.6 us -> 21.3 us  [the longest x1 8.6 us: on_device(): terms = lax.all_to_all(half.reshape(16, share, WIDE), ROW, 0, 0)]
    unnamed x82 -> x72, local copies, waits for them, and re-layouts: 26.3 us -> 24.4 us
  transfers between devices with their start and end apart: 17 -> 17, of which waited for: 7 -> 9; matrix products, arithmetic and copies ran while one was open for 2% -> 2% of each run, Pallas kernels for 10% -> 12%
where the time goes in v6:
time: 193 us; the launch traced here: 191 us
  waiting for transfers between devices  66.9 us (35%)
  starting transfers between devices  52.2 us (27%)
  Pallas kernels  41.3 us (21%)
  local copies, waits for them, and re-layouts  28.6 us (15%)
    all_to_all x1, waiting for transfers between devices, on_device(): mine = lax.all_to_all(shares, ROW, 0, 0).reshape(SIDE, SIDE)  30.2 us
    ppermute x12, starting transfers between devices, shifted(): lax.ppermute(value, axis, [(source, source + steps) for source in range(f...  28.5 us
    unnamed x72, local copies, waits for them, and re-layouts  24.4 us
    ppermute x12, waiting for transfers between devices, shifted(): lax.ppermute(value, axis, [(source, source + steps) for source in range(f...  21.1 us
    pallas_call x1, Pallas kernels, update(): pl.pallas_call(update_kernel, out_shape=out_shape, in_specs=[sm()] + [vm(...  14.4 us
    pallas_call x4, Pallas kernels, fore(): pl.pallas_call(functools.partial(fore_kernel, piece), grid=(1,), out_shap...  10.5 us
    all_to_all x1, starting transfers between devices, on_device(): terms = lax.all_to_all(half.reshape(16, share, WIDE), ROW, 0, 0)  8.6 us
    all_to_all x1, starting transfers between devices, on_device(): mine = lax.all_to_all(shares, ROW, 0, 0).reshape(SIDE, SIDE)  8.6 us
  transfers between devices with their start and end apart: 17, of which 9 were waited for; matrix products, arithmetic and copies ran while one was open for 2% of the time, Pallas kernels for 12%

profile of v6, /device:TPU:33, one launch (start us, length us, event | category | flops | bytes accessed | tf_op | source)
XLA Modules:
  0.0 191.1 jit_solution(10975489187259901467)
XLA Ops:
  0.6 2.7 %collective-permute-start = (f32[2,512,512]{2,1,0:T(8,128)}, f32[2,512,512]{2,1,0:T(8,128)}, u32[]{:S(2)}, u32[]{:S(2)}) collective-permute-start(f32[2,512,512]{2,1,0:T(8,128)} %own_ref.11), channel_id=1, source_target_pairs={{1,0},{2,1},{3,2},{4,3},{5,4},{6,5},{7,6},{9,8},{10,9},{11,10},{12... | collective-permute-start | bytes 6291464 | tf_op jit(solution)/shard_map/ppermute | solution.py:405
  3.4 2.9 %fusion = (f32[2,128,512]{2,1,0:T(8,128)}, f32[2,128,512]{2,1,0:T(8,128)}, f32[2,128,512]{2,1,0:T(8,128)}, f32[2,128,512]{2,1,0:T(8,128)}) fusion(f32[2,512,512]{2,1,0:T(8,128)} %own_ref.11), kind=kLoop, calls=%fused_computation.5 | loop fusion | bytes 4194304 | tf_op jit(solution)/shard_map/slice | solution.py:470
  6.3 1.3 collective-permute-start.1
  7.5 1.3 collective-permute-start.3
  8.8 1.3 collective-permute-start.5
  10.5 1.6 copy-done.16
  12.0 1.6 copy-done.17
  13.6 1.0 copy-done.30
  14.7 4.5 %shard_map.104 = (f32[2,2,128,512]{3,2,1,0:T(8,128)S(1)}, f32[2,2,128,512]{3,2,1,0:T(8,128)S(1)}, f32[2,2,128,512]{3,2,1,0:T(8,128)S(1)}, f32[2,2,128,512]{3,2,1...) custom-call(s32[3,2]{1,0:T(4,128)S(1)} %pad_add_fusion.where_ref, f32[2,512,512]{2,1,0:T(8,128)S(1)} %copy-done.16, ...), custom_call_target="tpu_custom_call" | custom-call | tf_op jit(solution)/shard_map/pallas_call | solution.py:275
  21.2 1.0 copy-done.11
  23.1 1.3 copy-done.22
  25.0 1.9 %collective-permute-start.2 = (f32[2,128,512]{2,1,0:T(8,128)}, f32[2,128,512]{2,1,0:T(8,128)S(1)}, u32[]{:S(2)}, u32[]{:S(2)}) collective-permute-start(f32[2,128,512]{2,1,0:T(8,128)} %shard_map.105.below_ref), channel_id=1, source_target_pairs={{1,0},{2,1},{3,2},{4,3},{5,4},{6,5},{7,6},{9,8},{10,9},{11,10},{12... | collective-permute-start | bytes 1572872 | tf_op jit(solution)/shard_map/ppermute | solution.py:405
  27.0 1.3 collective-permute-start.7
  28.3 5.0 %collective-permute-done.3.below_ref = f32[2,128,512]{2,1,0:T(8,128)} collective-permute-done((f32[2,128,512]{2,1,0:T(8,128)}, f32[2,128,512]{2,1,0:T(8,128)}, u32[]{:S(2)}, u32[]{:S(2)}) %collective-permute-start.3) | collective-permute-done | bytes 524320 | tf_op jit(solution)/shard_map/ppermute | solution.py:405
  33.2 3.1 %collective-permute-start.4 = (f32[2,128,512]{2,1,0:T(8,128)}, f32[2,128,512]{2,1,0:T(8,128)}, u32[]{:S(2)}, u32[]{:S(2)}) collective-permute-start(f32[2,128,512]{2,1,0:T(8,128)} %collective-permute-done.3.below_ref), channel_id=1, source_target_pairs={{1,0},{2,1},{3,2},{4,3},{5,4},{6,5},{7,6},{9,8},{10,9},{11,10},{12... | collective-permute-start | bytes 1572872 | tf_op jit(solution)/shard_map/ppermute | solution.py:405
  36.3 8.2 %collective-permute-done.5.below_ref = f32[2,128,512]{2,1,0:T(8,128)} collective-permute-done((f32[2,128,512]{2,1,0:T(8,128)}, f32[2,128,512]{2,1,0:T(8,128)}, u32[]{:S(2)}, u32[]{:S(2)}) %collective-permute-start.5) | collective-permute-done | bytes 524320 | tf_op jit(solution)/shard_map/ppermute | solution.py:405
  44.5 3.1 %collective-permute-start.6 = (f32[2,128,512]{2,1,0:T(8,128)}, f32[2,128,512]{2,1,0:T(8,128)}, u32[]{:S(2)}, u32[]{:S(2)}) collective-permute-start(f32[2,128,512]{2,1,0:T(8,128)} %collective-permute-done.5.below_ref), channel_id=1, source_target_pairs={{1,0},{2,1},{3,2},{4,3},{5,4},{6,5},{7,6},{9,8},{10,9},{11,10},{12... | collective-permute-start | bytes 1572872 | tf_op jit(solution)/shard_map/ppermute | solution.py:405
  47.6 1.2 copy-done.6
  48.8 2.2 %shard_map.106 = (f32[2,2,128,512]{3,2,1,0:T(8,128)S(1)}, f32[2,2,128,512]{3,2,1,0:T(8,128)S(1)}, f32[8,128]{1,0:T(8,128)S(1)}) custom-call(s32[3,2]{1,0:T(4,128)S(1)} %pad_add_fusion.where_ref, f32[2,512,512]{2,1,0:T(8,128)S(1)} %copy-done, f32[2,512,512]{2,1,0:T(8,128)} %collective-permute-done.right_ref, f32[2,128,512]{2,1,0:T(8,128)} %shard_map.105.below_ref, ...), custom_call_target="tpu_custom_call" | custom-call | tf_op jit(solution)/shard_map/pallas_call | solution.py:136
  51.0 1.0 copy-done.24
  53.5 2.2 %collective-permute-done.7.refs_0_ = f32[2,128,512]{2,1,0:T(8,128)} collective-permute-done((f32[2,128,512]{2,1,0:T(8,128)}, f32[2,128,512]{2,1,0:T(8,128)}, u32[]{:S(2)}, u32[]{:S(2)}) %collective-permute-start.7) | collective-permute-done | bytes 524320 | tf_op jit(solution)/shard_map/ppermute | solution.py:405
  55.7 2.9 %collective-permute-start.8 = (f32[2,128,512]{2,1,0:T(8,128)}, f32[2,128,512]{2,1,0:T(8,128)S(1)}, u32[]{:S(2)}, u32[]{:S(2)}) collective-permute-start(f32[2,128,512]{2,1,0:T(8,128)} %shard_map.109.below_ref), channel_id=1, source_target_pairs={{1,0},{2,1},{3,2},{4,3},{5,4},{6,5},{7,6},{9,8},{10,9},{11,10},{12... | collective-permute-start | bytes 1572872 | tf_op jit(solution)/shard_map/ppermute | solution.py:405
  58.6 1.2 copy-done.9
  59.8 2.8 %shard_map.107 = (f32[2,2,128,512]{3,2,1,0:T(8,128)S(1)}, f32[2,2,128,512]{3,2,1,0:T(8,128)S(1)}, f32[8,128]{1,0:T(8,128)}) custom-call(s32[3,2]{1,0:T(4,128)S(1)} %pad_add_fusion.where_ref, f32[2,512,512]{2,1,0:T(8,128)S(1)} %copy-done, f32[2,512,512]{2,1,0:T(8,128)} %collective-permute-done.right_ref, f32[2,128,512]{2,1,0:T(8,128)} %collective-permute-done.3.below_ref, ...), custom_call_target="tpu_custom_call" | custom-call | tf_op jit(solution)/shard_map/pallas_call | solution.py:136
  62.6 2.8 %shard_map.108 = (f32[2,2,128,512]{3,2,1,0:T(8,128)S(1)}, f32[2,2,128,512]{3,2,1,0:T(8,128)S(1)}, f32[8,128]{1,0:T(8,128)}) custom-call(s32[3,2]{1,0:T(4,128)S(1)} %pad_add_fusion.where_ref, f32[2,512,512]{2,1,0:T(8,128)S(1)} %copy-done, f32[2,512,512]{2,1,0:T(8,128)} %collective-permute-done.right_ref, f32[2,128,512]{2,1,0:T(8,128)} %collective-permute-done.5.below_ref, ...), custom_call_target="tpu_custom_call" | custom-call | tf_op jit(solution)/shard_map/pallas_call | solution.py:136
  65.5 1.5 collective-permute-done.8.diag_ref
  67.0 2.7 %shard_map.110 = (f32[2,2,128,512]{3,2,1,0:T(8,128)S(1)}, f32[2,2,128,512]{3,2,1,0:T(8,128)S(1)}, f32[8,128]{1,0:T(8,128)}) custom-call(s32[3,2]{1,0:T(4,128)S(1)} %pad_add_fusion.where_ref, f32[2,512,512]{2,1,0:T(8,128)S(1)} %copy-done, f32[2,512,512]{2,1,0:T(8,128)} %collective-permute-done.right_ref, f32[2,128,512]{2,1,0:T(8,128)} %shard_map.109.below_ref, ...), custom_call_target="tpu_custom_call" | custom-call | tf_op jit(solution)/shard_map/pallas_call | solution.py:136
  69.8 14.4 %shard_map.111 = (f32[2,512,512]{2,1,0:T(8,128)}, f32[2,512,512]{2,1,0:T(8,128)}, f32[2,512,512]{2,1,0:T(8,128)}, f32[2,512,512]{2,1,0:T(8,128)}, f32[512,640]{1,0:T(8,128)S(1)}, /*index=5*/f32[512,640]{1,0:T(8,128)S(1)}) custom-call(s32[3,2]{1,0:T(4,128)S(1)} %pad_add_fusion.where_ref, f32[2,2,128,512]{3,2,1,0:T(8,128)S(1)} %copy-done.25, ...), custom_call_target="tpu_custom_call" | custom-call | tf_op jit(solution)/shard_map/pallas_call | solution.py:296
  84.3 1.9 %collective-permute-start.11 = (f32[2,512,512]{2,1,0:T(8,128)}, f32[2,512,512]{2,1,0:T(8,128)}, u32[]{:S(2)}, u32[]{:S(2)}) collective-permute-start(f32[2,512,512]{2,1,0:T(8,128)} %get-tuple-element.46), channel_id=1, source_target_pairs={{0,1},{1,2},{2,3},{3,4},{4,5},{5,6},{6,7},{8,9},{9,10},{10,11},{11... | collective-permute-start | bytes 6291464 | tf_op jit(solution)/shard_map/ppermute | solution.py:405
  86.8 5.4 %collective-permute-done.9.came_ref = f32[512,640]{1,0:T(8,128)S(1)} collective-permute-done((f32[512,640]{1,0:T(8,128)S(1)}, f32[512,640]{1,0:T(8,128)S(1)}, u32[]{:S(2)}, u32[]{:S(2)}) %collective-permute-start.9) | collective-permute-done | bytes 1310752 | tf_op jit(solution)/shard_map/ppermute | solution.py:409
  92.2 1.2 shard_map.113.refs_1_.after_ref
  93.4 8.6 %all-to-all-start = ((f32[16,32,640]{2,1,0:T(8,128)}), f32[16,32,640]{2,1,0:T(8,128)S(1)}, u32[]{:S(2)}, u32[]{:S(2)}) async-start(f32[16,32,640]{2,1,0:T(8,128)} %bitcast.5), calls=%async_computation | async-start | bytes 2621440 | tf_op jit(solution)/shard_map/all_to_all | solution.py:491
  102.0 3.3 %collective-permute-start.10 = (f32[2,512,512]{2,1,0:T(8,128)}, f32[2,512,512]{2,1,0:T(8,128)}, u32[]{:S(2)}, u32[]{:S(2)}) collective-permute-start(f32[2,512,512]{2,1,0:T(8,128)} %shard_map.114), channel_id=1, source_target_pairs={{0,1},{1,2},{2,3},{3,4},{4,5},{5,6},{6,7},{8,9},{9,10},{10,11},{11... | collective-permute-start | bytes 6291464 | tf_op jit(solution)/shard_map/ppermute | solution.py:405
  105.3 4.2 %collective-permute-done.11.corner_ref = f32[2,512,512]{2,1,0:T(8,128)} collective-permute-done((f32[2,512,512]{2,1,0:T(8,128)}, f32[2,512,512]{2,1,0:T(8,128)}, u32[]{:S(2)}, u32[]{:S(2)}) %collective-permute-start.11) | collective-permute-done | bytes 2097184 | tf_op jit(solution)/shard_map/ppermute | solution.py:405
  109.5 1.6 copy-done.19
  111.1 3.9 %shard_map.115.refs_0_ = f32[2,512,512]{2,1,0:T(8,128)} custom-call(f32[2,512,512]{2,1,0:T(8,128)S(1)} %copy-done.19, f32[2,512,512]{2,1,0:T(8,128)} %collective-permute-done.11.corner_ref, f32[512,640]{1,0:T(8,128)} %shard_map.113.refs_1_.after_ref), custom_call_target="tpu_custom_call" | custom-call | tf_op jit(solution)/shard_map/pallas_call | solution.py:352
  115.0 4.5 %collective-permute-start.12 = (f32[2,512,512]{2,1,0:T(8,128)}, f32[2,512,512]{2,1,0:T(8,128)}, u32[]{:S(2)}, u32[]{:S(2)}) collective-permute-start(f32[2,512,512]{2,1,0:T(8,128)} %shard_map.115.refs_0_), channel_id=1, source_target_pairs={{0,8},{8,16},{16,24},{24,32},{32,40},{40,48},{48,56},{56,64},{64,7... | collective-permute-start | bytes 6291464 | tf_op jit(solution)/shard_map/ppermute | solution.py:405
  119.5 3.4 %all-to-all-done.terms_ref = f32[16,32,640]{2,1,0:T(8,128)S(1)} async-done(((f32[16,32,640]{2,1,0:T(8,128)}), f32[16,32,640]{2,1,0:T(8,128)S(1)}, u32[]{:S(2)}, u32[]{:S(2)}) %all-to-all-start) | async-done | bytes 1310752 | tf_op jit(solution)/shard_map/all_to_all | solution.py:491
  123.7 4.1 %all-to-all-start.1 = ((f32[4,32,640]{2,1,0:T(8,128)}), f32[4,32,640]{2,1,0:T(8,128)S(1)}, u32[]{:S(2)}, u32[]{:S(2)}) async-start(f32[4,32,640]{2,1,0:T(8,128)} %copy-done.23), calls=%async_computation.1 | async-start | bytes 655360 | tf_op jit(solution)/shard_map/all_to_all | solution.py:497
  128.6 6.9 %all-to-all-done.1.terms_ref = f32[4,32,640]{2,1,0:T(8,128)S(1)} async-done(((f32[4,32,640]{2,1,0:T(8,128)}), f32[4,32,640]{2,1,0:T(8,128)S(1)}, u32[]{:S(2)}, u32[]{:S(2)}) %all-to-all-start.1) | async-done | bytes 327712 | tf_op jit(solution)/shard_map/all_to_all | solution.py:497
  136.6 8.6 %all-to-all-start.2 = ((f32[16,32,512]{2,1,0:T(8,128)}), f32[16,32,512]{2,1,0:T(8,128)S(1)}, u32[]{:S(2)}, u32[]{:S(2)}) async-start(f32[16,32,512]{2,1,0:T(8,128)} %copy-done.15), calls=%async_computation.2 | async-start | bytes 2097152 | tf_op jit(solution)/shard_map/all_to_all | solution.py:501
  146.4 1.6 copy-done.18
  148.7 1.3 copy-done.20
  150.6 30.2 %all-to-all-done.2 = f32[16,32,512]{2,1,0:T(8,128)S(1)} async-done(((f32[16,32,512]{2,1,0:T(8,128)}), f32[16,32,512]{2,1,0:T(8,128)S(1)}, u32[]{:S(2)}, u32[]{:S(2)}) %all-to-all-start.2) | async-done | bytes 1048608 | tf_op jit(solution)/shard_map/all_to_all | solution.py:501
  181.8 1.8 collective-permute-start.13
  183.6 1.6 copy-done.21
  185.2 4.4 %shard_map.116 = f32[2,512,512]{2,1,0:T(8,128)} custom-call(f32[1,1]{1,0:T(1,128)} %bitcast.3.scale_ref, f32[2,512,512]{2,1,0:T(8,128)S(1)} %copy-done.21, f32[2,512,512]{2,1,0:T(8,128)} %collective-permute-done.10.left_ref.refs_2_, f32[2,512,512]{2,1,0:T(8,128)} %collective-permute-done.12.above_ref.refs_1_), custom_call_target="tpu_custom_call" | custom-call | tf_op jit(solution)/shard_map/pallas_call | solution.py:436
  189.6 1.5 shard_map.120
  (81 shorter events, 11.5 us)
Async XLA Ops:
  0.6 9.8 %copy-start = (f32[2,512,512]{2,1,0:T(8,128)S(1)}, f32[2,512,512]{2,1,0:T(8,128)}, u32[]{:S(2)}) copy-start(f32[2,512,512]{2,1,0:T(8,128)} %own_ref.11) | copy-start | bytes 6291460
  0.6 9.6 %copy-start.35 = (s32[2,2]{1,0:T(2,128)S(1)}, s32[2,2]{1,0:T(2,128)}, u32[]{:S(2)}) copy-start(s32[2,2]{1,0:T(2,128)} %param.12) | copy-start | bytes 52
  0.6 46.9 %collective-permute-start = (f32[2,512,512]{2,1,0:T(8,128)}, f32[2,512,512]{2,1,0:T(8,128)}, u32[]{:S(2)}, u32[]{:S(2)}) collective-permute-start(f32[2,512,512]{2,1,0:T(8,128)} %own_ref.11), channel_id=1, source_target_pairs={{1,0},{2,1},{3,2},{4,3},{5,4},{6,5},{7,6},{9,8},{10,9},{11,10},{12... | collective-permute-start | bytes 6291464 | tf_op jit(solution)/shard_map/ppermute | solution.py:405
  6.3 18.8 %collective-permute-start.1 = (f32[2,128,512]{2,1,0:T(8,128)}, f32[2,128,512]{2,1,0:T(8,128)}, u32[]{:S(2)}, u32[]{:S(2)}) collective-permute-start(f32[2,128,512]{2,1,0:T(8,128)} %get-tuple-element.53), channel_id=1, source_target_pairs={{8,0},{16,8},{24,16},{32,24},{40,32},{48,40},{56,48},{64,56},{72,6... | collective-permute-start | bytes 1572872 | tf_op jit(solution)/shard_map/ppermute | solution.py:405
  7.5 25.7 %collective-permute-start.3 = (f32[2,128,512]{2,1,0:T(8,128)}, f32[2,128,512]{2,1,0:T(8,128)}, u32[]{:S(2)}, u32[]{:S(2)}) collective-permute-start(f32[2,128,512]{2,1,0:T(8,128)} %get-tuple-element.52), channel_id=1, source_target_pairs={{8,0},{16,8},{24,16},{32,24},{40,32},{48,40},{56,48},{64,56},{72,6... | collective-permute-start | bytes 1572872 | tf_op jit(solution)/shard_map/ppermute | solution.py:405
  8.8 35.6 %collective-permute-start.5 = (f32[2,128,512]{2,1,0:T(8,128)}, f32[2,128,512]{2,1,0:T(8,128)}, u32[]{:S(2)}, u32[]{:S(2)}) collective-permute-start(f32[2,128,512]{2,1,0:T(8,128)} %get-tuple-element.51), channel_id=1, source_target_pairs={{8,0},{16,8},{24,16},{32,24},{40,32},{48,40},{56,48},{64,56},{72,6... | collective-permute-start | bytes 1572872 | tf_op jit(solution)/shard_map/ppermute | solution.py:405
  10.4 1.6 copy-start.16
  12.0 1.6 copy-start.17
  13.6 1.0 copy-start.30
  14.7 32.9 %copy-start.1 = (bf16[4,256,256]{2,1,0:T(8,128)(2,1)S(1)}, bf16[4,256,256]{2,1,0:T(8,128)(2,1)}, u32[]{:S(2)}) copy-start(bf16[4,256,256]{2,1,0:T(8,128)(2,1)} %constant.43.clone.mh_ref.refs_16_) | copy-start | bytes 1572868
  14.7 32.9 %copy-start.2 = (bf16[4,256,256]{2,1,0:T(8,128)(2,1)S(1)}, bf16[4,256,256]{2,1,0:T(8,128)(2,1)}, u32[]{:S(2)}) copy-start(bf16[4,256,256]{2,1,0:T(8,128)(2,1)} %constant.44.clone.ml_ref.refs_17_) | copy-start | bytes 1572868
  19.2 1.0 copy-start.5
  20.2 1.0 copy-start.8
  21.2 1.0 copy-start.11
  23.1 1.3 copy-start.22
  25.0 22.5 %collective-permute-start.2 = (f32[2,128,512]{2,1,0:T(8,128)}, f32[2,128,512]{2,1,0:T(8,128)S(1)}, u32[]{:S(2)}, u32[]{:S(2)}) collective-permute-start(f32[2,128,512]{2,1,0:T(8,128)} %shard_map.105.below_ref), channel_id=1, source_target_pairs={{1,0},{2,1},{3,2},{4,3},{5,4},{6,5},{7,6},{9,8},{10,9},{11,10},{12... | collective-permute-start | bytes 1572872 | tf_op jit(solution)/shard_map/ppermute | solution.py:405
  27.0 28.8 %collective-permute-start.7 = (f32[2,128,512]{2,1,0:T(8,128)}, f32[2,128,512]{2,1,0:T(8,128)}, u32[]{:S(2)}, u32[]{:S(2)}) collective-permute-start(f32[2,128,512]{2,1,0:T(8,128)} %get-tuple-element.50), channel_id=1, source_target_pairs={{8,0},{16,8},{24,16},{32,24},{40,32},{48,40},{56,48},{64,56},{72,6... | collective-permute-start | bytes 1572872 | tf_op jit(solution)/shard_map/ppermute | solution.py:405
  33.2 25.3 %collective-permute-start.4 = (f32[2,128,512]{2,1,0:T(8,128)}, f32[2,128,512]{2,1,0:T(8,128)}, u32[]{:S(2)}, u32[]{:S(2)}) collective-permute-start(f32[2,128,512]{2,1,0:T(8,128)} %collective-permute-done.3.below_ref), channel_id=1, source_target_pairs={{1,0},{2,1},{3,2},{4,3},{5,4},{6,5},{7,6},{9,8},{10,9},{11,10},{12... | collective-permute-start | bytes 1572872 | tf_op jit(solution)/shard_map/ppermute | solution.py:405
  44.5 18.2 %collective-permute-start.6 = (f32[2,128,512]{2,1,0:T(8,128)}, f32[2,128,512]{2,1,0:T(8,128)}, u32[]{:S(2)}, u32[]{:S(2)}) collective-permute-start(f32[2,128,512]{2,1,0:T(8,128)} %collective-permute-done.5.below_ref), channel_id=1, source_target_pairs={{1,0},{2,1},{3,2},{4,3},{5,4},{6,5},{7,6},{9,8},{10,9},{11,10},{12... | collective-permute-start | bytes 1572872 | tf_op jit(solution)/shard_map/ppermute | solution.py:405
  47.6 1.2 copy-start.6
  51.0 1.0 copy-start.24
  52.0 1.0 copy-start.26
  55.7 11.3 %collective-permute-start.8 = (f32[2,128,512]{2,1,0:T(8,128)}, f32[2,128,512]{2,1,0:T(8,128)S(1)}, u32[]{:S(2)}, u32[]{:S(2)}) collective-permute-start(f32[2,128,512]{2,1,0:T(8,128)} %shard_map.109.below_ref), channel_id=1, source_target_pairs={{1,0},{2,1},{3,2},{4,3},{5,4},{6,5},{7,6},{9,8},{10,9},{11,10},{12... | collective-permute-start | bytes 1572872 | tf_op jit(solution)/shard_map/ppermute | solution.py:405
  58.6 1.2 copy-start.9
  59.8 2.8 %copy-start.12 = (f32[2,2,128,512]{3,2,1,0:T(8,128)S(1)}, f32[2,2,128,512]{3,2,1,0:T(8,128)}, u32[]{:S(2)}) copy-start(f32[2,2,128,512]{3,2,1,0:T(8,128)} %copy-done.11) | copy-start | bytes 3145732
  62.6 4.3 %copy-start.14 = (f32[2,2,128,512]{3,2,1,0:T(8,128)S(1)}, f32[2,2,128,512]{3,2,1,0:T(8,128)}, u32[]{:S(2)}) copy-start(f32[2,2,128,512]{3,2,1,0:T(8,128)} %copy-done.13) | copy-start | bytes 3145732
  67.0 2.8 %copy-start.7 = (f32[2,2,128,512]{3,2,1,0:T(8,128)S(1)}, f32[2,2,128,512]{3,2,1,0:T(8,128)}, u32[]{:S(2)}) copy-start(f32[2,2,128,512]{3,2,1,0:T(8,128)} %copy-done.5) | copy-start | bytes 3145732
  67.0 2.8 %copy-start.10 = (f32[2,2,128,512]{3,2,1,0:T(8,128)S(1)}, f32[2,2,128,512]{3,2,1,0:T(8,128)}, u32[]{:S(2)}) copy-start(f32[2,2,128,512]{3,2,1,0:T(8,128)} %copy-done.8) | copy-start | bytes 3145732
  67.0 2.8 %copy-start.25 = (f32[2,2,128,512]{3,2,1,0:T(8,128)S(1)}, f32[2,2,128,512]{3,2,1,0:T(8,128)}, u32[]{:S(2)}) copy-start(f32[2,2,128,512]{3,2,1,0:T(8,128)} %copy-done.24) | copy-start | bytes 3145732
  67.0 2.8 %copy-start.27 = (f32[2,2,128,512]{3,2,1,0:T(8,128)S(1)}, f32[2,2,128,512]{3,2,1,0:T(8,128)}, u32[]{:S(2)}) copy-start(f32[2,2,128,512]{3,2,1,0:T(8,128)} %copy-done.26) | copy-start | bytes 3145732
  67.0 2.8 %copy-start.28 = (bf16[4,256,256]{2,1,0:T(8,128)(2,1)S(1)}, bf16[4,256,256]{2,1,0:T(8,128)(2,1)}, u32[]{:S(2)}) copy-start(bf16[4,256,256]{2,1,0:T(8,128)(2,1)} %constant.41.clone.refs_14_) | copy-start | bytes 1572868
  67.0 2.8 %copy-start.29 = (bf16[4,256,256]{2,1,0:T(8,128)(2,1)S(1)}, bf16[4,256,256]{2,1,0:T(8,128)(2,1)}, u32[]{:S(2)}) copy-start(bf16[4,256,256]{2,1,0:T(8,128)(2,1)} %constant.42.clone.refs_15_) | copy-start | bytes 1572868
  67.0 2.8 %copy-start.32 = (f32[2,8,128]{2,1,0:T(8,128)S(1)}, f32[2,8,128]{2,1,0:T(8,128)}, u32[]{:S(2)}) copy-start(f32[2,8,128]{2,1,0:T(8,128)} %copy-done.31) | copy-start | bytes 24580
  84.3 25.2 %collective-permute-start.11 = (f32[2,512,512]{2,1,0:T(8,128)}, f32[2,512,512]{2,1,0:T(8,128)}, u32[]{:S(2)}, u32[]{:S(2)}) collective-permute-start(f32[2,512,512]{2,1,0:T(8,128)} %get-tuple-element.46), channel_id=1, source_target_pairs={{0,1},{1,2},{2,3},{3,4},{4,5},{5,6},{6,7},{8,9},{9,10},{10,11},{11... | collective-permute-start | bytes 6291464 | tf_op jit(solution)/shard_map/ppermute | solution.py:405
  86.2 6.0 %collective-permute-start.9 = (f32[512,640]{1,0:T(8,128)S(1)}, f32[512,640]{1,0:T(8,128)S(1)}, u32[]{:S(2)}, u32[]{:S(2)}) collective-permute-start(f32[512,640]{1,0:T(8,128)S(1)} %get-tuple-element.44), channel_id=1, source_target_pairs={{0,1},{1,0},{2,3},{3,2},{4,5},{5,4},{6,7},{7,6},{8,9},{9,8},{10,11... | collective-permute-start | bytes 3932168 | tf_op jit(solution)/shard_map/ppermute | solution.py:409
  93.4 29.5 %all-to-all-start = ((f32[16,32,640]{2,1,0:T(8,128)}), f32[16,32,640]{2,1,0:T(8,128)S(1)}, u32[]{:S(2)}, u32[]{:S(2)}) async-start(f32[16,32,640]{2,1,0:T(8,128)} %bitcast.5), calls=%async_computation | async-start | bytes 2621440 | tf_op jit(solution)/shard_map/all_to_all | solution.py:491
  102.0 48.6 %collective-permute-start.10 = (f32[2,512,512]{2,1,0:T(8,128)}, f32[2,512,512]{2,1,0:T(8,128)}, u32[]{:S(2)}, u32[]{:S(2)}) collective-permute-start(f32[2,512,512]{2,1,0:T(8,128)} %shard_map.114), channel_id=1, source_target_pairs={{0,1},{1,2},{2,3},{3,4},{4,5},{5,6},{6,7},{8,9},{9,10},{10,11},{11... | collective-permute-start | bytes 6291464 | tf_op jit(solution)/shard_map/ppermute | solution.py:405
  109.5 1.6 copy-start.19
  115.0 65.8 %collective-permute-start.12 = (f32[2,512,512]{2,1,0:T(8,128)}, f32[2,512,512]{2,1,0:T(8,128)}, u32[]{:S(2)}, u32[]{:S(2)}) collective-permute-start(f32[2,512,512]{2,1,0:T(8,128)} %shard_map.115.refs_0_), channel_id=1, source_target_pairs={{0,8},{8,16},{16,24},{24,32},{32,40},{40,48},{48,56},{56,64},{64,7... | collective-permute-start | bytes 6291464 | tf_op jit(solution)/shard_map/ppermute | solution.py:405
  123.7 11.8 %all-to-all-start.1 = ((f32[4,32,640]{2,1,0:T(8,128)}), f32[4,32,640]{2,1,0:T(8,128)S(1)}, u32[]{:S(2)}, u32[]{:S(2)}) async-start(f32[4,32,640]{2,1,0:T(8,128)} %copy-done.23), calls=%async_computation.1 | async-start | bytes 655360 | tf_op jit(solution)/shard_map/all_to_all | solution.py:497
  135.6 1.0 copy-start.15
  136.6 44.2 %all-to-all-start.2 = ((f32[16,32,512]{2,1,0:T(8,128)}), f32[16,32,512]{2,1,0:T(8,128)S(1)}, u32[]{:S(2)}, u32[]{:S(2)}) async-start(f32[16,32,512]{2,1,0:T(8,128)} %copy-done.15), calls=%async_computation.2 | async-start | bytes 2097152 | tf_op jit(solution)/shard_map/all_to_all | solution.py:501
  146.4 1.6 copy-start.18
  148.7 1.3 copy-start.20
  180.8 1.0 copy-start.3
  181.8 7.8 %collective-permute-start.13 = (f32[512,512]{1,0:T(8,128)}, f32[512,512]{1,0:T(8,128)S(1)}, u32[]{:S(2)}, u32[]{:S(2)}) collective-permute-start(f32[512,512]{1,0:T(8,128)} %shard_map.119.mine_ref), channel_id=1, source_target_pairs={{0,1},{1,0},{2,3},{3,2},{4,5},{5,4},{6,7},{7,6},{8,9},{9,8},{10,11... | collective-permute-start | bytes 3145736 | tf_op jit(solution)/shard_map/ppermute | solution.py:409
  183.6 1.6 copy-start.21
  185.2 4.4 %copy-start.4 = (f32[512,512]{1,0:T(8,128)S(1)}, f32[512,512]{1,0:T(8,128)}, u32[]{:S(2)}) copy-start(f32[512,512]{1,0:T(8,128)} %shard_map.119.mine_ref) | copy-start | bytes 3145732
  (5 other events, 3.5 us)

commit v7 on v6

--- a/solution.py
+++ b/solution.py
@@ -11,8 +11,8 @@
 
 SIDE = 512
 QUARTER = 128
-SIZES = (128,) * 4
-FIRSTS = (0, 128, 256, 384)
+SIZES = (144, 144, 128, 96)
+FIRSTS = (0, 144, 288, 416)
 WIDE = SIDE + 128
 PIECES = len(SIZES)
 COST = pl.CostEstimate(flops=0, bytes_accessed=0, transcendentals=0)
@@ -101,6 +101,7 @@
     spec_ref, wrapped_ref, token_ref,
 ):
     token_ref[...] = jnp.zeros_like(token_ref)
+    at = slice(FIRSTS[piece], FIRSTS[piece] + SIZES[piece])
     lane = lax.broadcasted_iota(jnp.int32, (SIZES[piece], SIDE), 1)
     row = lax.broadcasted_iota(jnp.int32, (SIZES[piece], SIDE), 0) + FIRSTS[piece]
     for item in range(2):
@@ -109,7 +110,7 @@
         value = []
         for part in range(2):
             lower = jnp.where(beside, diag_ref[part], below_ref[part])
-            upper = jnp.where(beside, right_ref[part], own_ref[part])
+            upper = jnp.where(beside, right_ref[part, at, :], own_ref[part, at, :])
             value.append(jnp.where(above, lower, upper))
             wrapped_ref[item, part] = value[part]
         beam_r, beam_i = rolled_ref[item, 0], rolled_ref[item, 1]
@@ -128,7 +129,7 @@
 
 def fore(piece, where, own, right, below, diag, rolled, matrices):
     size = SIZES[piece]
-    tile = pl.BlockSpec((2, size, SIDE), lambda i: (0, piece, 0))
+    tile = pl.BlockSpec((2, SIDE, SIDE), lambda i: (0, 0, 0))
     full = pl.BlockSpec((2, size, SIDE), lambda i: (0, 0, 0))
     whole = pl.BlockSpec((4, 2 * QUARTER, 2 * QUARTER), lambda i: (0, 0, 0))
     four = pl.BlockSpec((2, 2, size, SIDE), lambda i: (0, 0, 0, 0))
@@ -195,7 +196,8 @@
                         low[item, rows, to] = lo[:, piece]
 
     stores = []
-    for first, size in zip(FIRSTS, SIZES):
+    size = QUARTER
+    for first in range(0, SIDE, size):
         at = slice(first, first + size)
         lane = lax.broadcasted_iota(jnp.int32, (size, SIDE), 1)
         row = lax.broadcasted_iota(jnp.int32, (size, SIDE), 0) + first
@@ -405,6 +407,12 @@
     return lax.ppermute(value, axis, [(source, source + steps) for source in range(first, last)])
 
 
+def the_long_way(value):
+    for _ in range(2):
+        value = lax.ppermute(value, "x", [(x, (x + 1) % 4) for x in range(4)])
+    return lax.ppermute(value, ROW, [(r // 4 * 4 + (r + 2) % 4, r - 1) for r in range(1, 16)])
+
+
 def other_core(value):
     return lax.ppermute(value, "core", [(0, 1), (1, 0)])
 
@@ -427,8 +435,9 @@
     )(scale, own, t_own)
 
 
-def object_kernel(scale_ref, base_ref, left_ref, above_ref, out_ref):
+def object_kernel(scale_ref, base_ref, left_ref, above_ref, out_ref, token_ref):
     out_ref[...] = base_ref[...] + scale_ref[0, 0] * (left_ref[...] + above_ref[...])
+    token_ref[...] = jnp.zeros_like(token_ref)
 
 
 def finished_object(scale, start, left, above):
@@ -436,9 +445,9 @@
     return pl.pallas_call(
         object_kernel,
         grid=(4,),
-        out_shape=jax.ShapeDtypeStruct(start.shape, F32),
+        out_shape=(jax.ShapeDtypeStruct(start.shape, F32), jax.ShapeDtypeStruct((8, 128), F32)),
         in_specs=[sm()] + [rows] * 3,
-        out_specs=rows,
+        out_specs=(rows, pl.BlockSpec((8, 128), lambda i: (0, 0))),
         compiler_params=params(),
         cost_estimate=COST,
     )(scale, start, left, above)
@@ -473,8 +482,8 @@
     scale = 0.9 / (peaks[1, :1, :1] + 1e-06)
     specs, wrapped, tokens = [], [], []
     for k, piece in enumerate(pieces):
-        below = shifted(piece, ROW, -1)
-        if k in (0, 3):
+        below = the_long_way(piece) if k == 3 else shifted(piece, ROW, -1)
+        if k in (0, 2):
             (below,) = tied((below,), tokens[:1] if k else (peaks,))
         corner = shifted(below, COL, -1)
         spec, wrap, token = fore(k, where, object_field, right, below, corner, rolled[k], matrices)
@@ -499,10 +508,10 @@
     start = lax.dynamic_slice(probe, (core, at, jnp.zeros_like(at)), (1, share, SIDE))[0]
     shares = shared(terms, start, 16)
     mine = lax.all_to_all(shares, ROW, 0, 0).reshape(SIDE, SIDE)
-    begun, token = base(scale, object_field, t_own)
-    (mine,) = tied((mine,), (from_above, from_left, token))
+    begun, _ = base(scale, object_field, t_own)
+    new_object, token = finished_object(scale, begun, from_left, from_above)
+    (mine,) = tied((mine,), (token,))
     new_probe = joined(core.astype(jnp.int32).reshape(1, 1), mine, other_core(mine))
-    new_object = finished_object(scale, begun, from_left, from_above)
     return (new_object, new_probe)
 
 

time: 193 us -> 204 us (1.057)
  starting transfers between devices: 52.2 us -> 69.3 us
  waiting for transfers between devices: 66.9 us -> 61.8 us
  local copies, waits for them, and re-layouts: 28.6 us -> 26 us
  Pallas kernels: 41.3 us -> 43.4 us
    all_to_all x1, waiting for transfers between devices: 30.2 us -> 12 us  [on_device(): mine = lax.all_to_all(shares, ROW, 0, 0).reshape(SIDE, SIDE)]
    ppermute x0 -> x3, waiting for transfers between devices: none -> 9.29 us  [the longest x2 9.29 us: the_long_way(): value = lax.ppermute(value, 'x', [(x, (x + 1) % 4) for x in range(4)])]
    all_to_all x1, starting transfers between devices: 8.6 us -> 17.8 us  [on_device(): terms = lax.all_to_all(half.reshape(16, share, WIDE), ROW, 0, 0)]
    ppermute x0 -> x3, starting transfers between devices: none -> 6.15 us  [the longest x1 3.99 us: the_long_way(): lax.ppermute(value, ROW, [(r // 4 * 4 + (r + 2) % 4, r - 1) for r in rang...]
    all_to_all x1, waiting for transfers between devices: 3.42 us -> 6.62 us  [on_device(): terms = lax.all_to_all(half.reshape(16, share, WIDE), ROW, 0, 0)]
    all_to_all x1, waiting for transfers between devices: 6.86 us -> 3.86 us  [on_device(): terms = lax.all_to_all(terms, 'z', 0, 0)]
    ppermute x2, waiting for transfers between devices: 5.42 us -> 7.92 us  [other_core(): return lax.ppermute(value, 'core', [(0, 1), (1, 0)])]
    all_to_all x1, starting transfers between devices: 8.6 us -> 11 us  [on_device(): mine = lax.all_to_all(shares, ROW, 0, 0).reshape(SIDE, SIDE)]
  transfers between devices with their start and end apart: 17 -> 19, of which waited for: 9 -> 9; matrix products, arithmetic and copies ran while one was open for 2% -> 2% of each run, Pallas kernels for 12% -> 12%
where the time goes in v7:
time: 204 us; the launch traced here: 202 us
  starting transfers between devices  69.3 us (34%)
  waiting for transfers between devices  61.8 us (30%)
  Pallas kernels  43.4 us (21%)
  local copies, waits for them, and re-layouts  26 us (13%)
    ppermute x11, starting transfers between devices, shifted(): lax.ppermute(value, axis, [(source, source + steps) for source in range(f...  26.9 us
    unnamed x68, local copies, waits for them, and re-layouts  22.1 us
    ppermute x11, waiting for transfers between devices, shifted(): lax.ppermute(value, axis, [(source, source + steps) for source in range(f...  22.1 us
    all_to_all x1, starting transfers between devices, on_device(): terms = lax.all_to_all(half.reshape(16, share, WIDE), ROW, 0, 0)  17.8 us
    pallas_call x1, Pallas kernels, update(): pl.pallas_call(update_kernel, out_shape=out_shape, in_specs=[sm()] + [vm(...  14.5 us
    pallas_call x4, Pallas kernels, fore(): pl.pallas_call(functools.partial(fore_kernel, piece), grid=(1,), out_shap...  12.1 us
    all_to_all x1, waiting for transfers between devices, on_device(): mine = lax.all_to_all(shares, ROW, 0, 0).reshape(SIDE, SIDE)  12 us
    all_to_all x1, starting transfers between devices, on_device(): mine = lax.all_to_all(shares, ROW, 0, 0).reshape(SIDE, SIDE)  11 us
  transfers between devices with their start and end apart: 19, of which 9 were waited for; matrix products, arithmetic and copies ran while one was open for 2% of the time, Pallas kernels for 12%

profile of v7, /device:TPU:33, one launch (start us, length us, event | category | flops | bytes accessed | tf_op | source)
XLA Modules:
  0.0 202.4 jit_solution(15507422774001176525)
XLA Ops:
  0.7 2.7 %collective-permute-start = (f32[2,512,512]{2,1,0:T(8,128)}, f32[2,512,512]{2,1,0:T(8,128)}, u32[]{:S(2)}, u32[]{:S(2)}) collective-permute-start(f32[2,512,512]{2,1,0:T(8,128)} %own_ref.11), channel_id=1, source_target_pairs={{1,0},{2,1},{3,2},{4,3},{5,4},{6,5},{7,6},{9,8},{10,9},{11,10},{12... | collective-permute-start | bytes 6291464 | tf_op jit(solution)/shard_map/ppermute | solution.py:407
  3.4 2.3 %fusion = (f32[2,144,512]{2,1,0:T(8,128)}, f32[2,144,512]{2,1,0:T(8,128)}) fusion(f32[2,512,512]{2,1,0:T(8,128)} %own_ref.11), kind=kLoop, calls=%fused_computation.5 | loop fusion | bytes 2359296 | tf_op jit(solution)/shard_map/slice | solution.py:479
  5.7 1.3 collective-permute-start.1
  7.1 2.2 %collective-permute-start.7 = (f32[2,96,512]{2,1,0:T(8,128)S(1)}, f32[2,96,512]{2,1,0:T(8,128)S(1)}, u32[]{:S(2)}, u32[]{:S(2)}) collective-permute-start(f32[2,96,512]{2,1,0:T(8,128)S(1)} %slice.27), channel_id=1, source_target_pairs={{0,8},{8,16},{16,24},{24,0},{1,9},{9,17},{17,25},{25,1},{2,10},{10... | collective-permute-start | bytes 1179656 | tf_op jit(solution)/shard_map/ppermute | solution.py:412
  9.2 1.3 collective-permute-start.3
  10.8 9.3 %collective-permute-done.7 = f32[2,96,512]{2,1,0:T(8,128)S(1)} collective-permute-done((f32[2,96,512]{2,1,0:T(8,128)S(1)}, f32[2,96,512]{2,1,0:T(8,128)S(1)}, u32[]{:S(2)}, u32[]{:S(2)}) %collective-permute-start.7) | collective-permute-done | bytes 393248 | tf_op jit(solution)/shard_map/ppermute | solution.py:412
  20.1 1.6 copy-done.16
  21.7 1.6 copy-done.17
  23.3 4.5 %shard_map.104 = (f32[2,2,144,512]{3,2,1,0:T(8,128)S(1)}, f32[2,2,144,512]{3,2,1,0:T(8,128)S(1)}, f32[2,2,128,512]{3,2,1,0:T(8,128)S(1)}, f32[2,2,96,512]{3,2,1,...) custom-call(s32[3,2]{1,0:T(4,128)S(1)} %pad_add_fusion.where_ref, f32[2,512,512]{2,1,0:T(8,128)S(1)} %copy-done.16, ...), custom_call_target="tpu_custom_call" | custom-call | tf_op jit(solution)/shard_map/pallas_call | solution.py:277
  28.8 1.0 copy-done.8
  31.7 1.3 copy-done.20
  33.7 3.0 %collective-permute-start.2 = (f32[2,144,512]{2,1,0:T(8,128)}, f32[2,144,512]{2,1,0:T(8,128)S(1)}, u32[]{:S(2)}, u32[]{:S(2)}) collective-permute-start(f32[2,144,512]{2,1,0:T(8,128)} %shard_map.105.below_ref), channel_id=1, source_target_pairs={{1,0},{2,1},{3,2},{4,3},{5,4},{6,5},{7,6},{9,8},{10,9},{11,10},{12... | collective-permute-start | bytes 1769480 | tf_op jit(solution)/shard_map/ppermute | solution.py:407
  36.7 1.3 collective-permute-start.5
  38.0 4.0 %collective-permute-start.9 = (f32[2,96,512]{2,1,0:T(8,128)}, f32[2,96,512]{2,1,0:T(8,128)S(1)}, u32[]{:S(2)}, u32[]{:S(2)}) collective-permute-start(f32[2,96,512]{2,1,0:T(8,128)} %collective-permute-done.8), channel_id=1, source_target_pairs={{24,0},{0,8},{8,16},{48,24},{56,32},{32,40},{40,48},{80,56},{88,64... | collective-permute-start | bytes 1179656 | tf_op jit(solution)/shard_map/ppermute | solution.py:413
  42.0 2.5 %collective-permute-start.4 = (f32[2,144,512]{2,1,0:T(8,128)}, f32[2,144,512]{2,1,0:T(8,128)}, u32[]{:S(2)}, u32[]{:S(2)}) collective-permute-start(f32[2,144,512]{2,1,0:T(8,128)} %collective-permute-done.3.below_ref), channel_id=1, source_target_pairs={{1,0},{2,1},{3,2},{4,3},{5,4},{6,5},{7,6},{9,8},{10,9},{11,10},{12... | collective-permute-start | bytes 1769480 | tf_op jit(solution)/shard_map/ppermute | solution.py:407
  44.5 1.8 collective-permute-done.2.diag_ref
  46.4 1.3 copy-done.6
  47.7 2.7 %shard_map.106 = (f32[2,2,144,512]{3,2,1,0:T(8,128)S(1)}, f32[2,2,144,512]{3,2,1,0:T(8,128)S(1)}, f32[8,128]{1,0:T(8,128)S(1)}) custom-call(s32[3,2]{1,0:T(4,128)S(1)} %pad_add_fusion.where_ref, f32[2,512,512]{2,1,0:T(8,128)S(1)} %copy-done, f32[2,512,512]{2,1,0:T(8,128)} %collective-permute-done.right_ref, f32[2,144,512]{2,1,0:T(8,128)} %shard_map.105.below_ref, ...), custom_call_target="tpu_custom_call" | custom-call | tf_op jit(solution)/shard_map/pallas_call | solution.py:137
  51.4 1.1 copy-done.24
  53.0 1.9 collective-permute-start.6
  55.0 2.3 %collective-permute-start.10 = (f32[2,96,512]{2,1,0:T(8,128)S(1)}, f32[2,96,512]{2,1,0:T(8,128)S(1)}, u32[]{:S(2)}, u32[]{:S(2)}) collective-permute-start(f32[2,96,512]{2,1,0:T(8,128)S(1)} %collective-permute-done.9.below_ref), channel_id=1, source_target_pairs={{1,0},{2,1},{3,2},{4,3},{5,4},{6,5},{7,6},{9,8},{10,9},{11,10},{12... | collective-permute-start | bytes 1179656 | tf_op jit(solution)/shard_map/ppermute | solution.py:407
  57.2 1.3 copy-done.9
  58.5 3.3 %shard_map.107 = (f32[2,2,144,512]{3,2,1,0:T(8,128)S(1)}, f32[2,2,144,512]{3,2,1,0:T(8,128)S(1)}, f32[8,128]{1,0:T(8,128)}) custom-call(s32[3,2]{1,0:T(4,128)S(1)} %pad_add_fusion.where_ref, f32[2,512,512]{2,1,0:T(8,128)S(1)} %copy-done, f32[2,512,512]{2,1,0:T(8,128)} %collective-permute-done.right_ref, f32[2,144,512]{2,1,0:T(8,128)} %collective-permute-done.3.below_ref, ...), custom_call_target="tpu_custom_call" | custom-call | tf_op jit(solution)/shard_map/pallas_call | solution.py:137
  61.8 6.1 %collective-permute-done.10.diag_ref = f32[2,96,512]{2,1,0:T(8,128)S(1)} collective-permute-done((f32[2,96,512]{2,1,0:T(8,128)S(1)}, f32[2,96,512]{2,1,0:T(8,128)S(1)}, u32[]{:S(2)}, u32[]{:S(2)}) %collective-permute-start.10) | collective-permute-done | bytes 393248 | tf_op jit(solution)/shard_map/ppermute | solution.py:407
  67.9 2.9 %shard_map.110 = (f32[2,2,96,512]{3,2,1,0:T(8,128)S(1)}, f32[2,2,96,512]{3,2,1,0:T(8,128)S(1)}, f32[8,128]{1,0:T(8,128)}) custom-call(s32[3,2]{1,0:T(4,128)S(1)} %pad_add_fusion.where_ref, f32[2,512,512]{2,1,0:T(8,128)S(1)} %copy-done, f32[2,512,512]{2,1,0:T(8,128)} %collective-permute-done.right_ref, f32[2,96,512]{2,1,0:T(8,128)S(1)} %collective-permute-done.9.below_ref, ...), custom_call_target="tpu_custom_call" | custom-call | tf_op jit(solution)/shard_map/pallas_call | solution.py:137
  70.9 3.1 %shard_map.109 = (f32[2,2,128,512]{3,2,1,0:T(8,128)S(1)}, f32[2,2,128,512]{3,2,1,0:T(8,128)S(1)}, f32[8,128]{1,0:T(8,128)}) custom-call(s32[3,2]{1,0:T(4,128)S(1)} %pad_add_fusion.where_ref, f32[2,512,512]{2,1,0:T(8,128)S(1)} %copy-done, f32[2,512,512]{2,1,0:T(8,128)} %collective-permute-done.right_ref, f32[2,128,512]{2,1,0:T(8,128)} %shard_map.108.below_ref, ...), custom_call_target="tpu_custom_call" | custom-call | tf_op jit(solution)/shard_map/pallas_call | solution.py:137
  74.3 14.5 %shard_map.111 = (f32[2,512,512]{2,1,0:T(8,128)}, f32[2,512,512]{2,1,0:T(8,128)}, f32[2,512,512]{2,1,0:T(8,128)}, f32[2,512,512]{2,1,0:T(8,128)}, f32[512,640]{1,0:T(8,128)S(1)}, /*index=5*/f32[512,640]{1,0:T(8,128)S(1)}) custom-call(s32[3,2]{1,0:T(4,128)S(1)} %pad_add_fusion.where_ref, f32[2,2,144,512]{3,2,1,0:T(8,128)S(1)} %copy-done.23, ...), custom_call_target="tpu_custom_call" | custom-call | tf_op jit(solution)/shard_map/pallas_call | solution.py:298
  88.7 1.9 collective-permute-start.13
  91.2 5.4 %collective-permute-done.11.came_ref = f32[512,640]{1,0:T(8,128)S(1)} collective-permute-done((f32[512,640]{1,0:T(8,128)S(1)}, f32[512,640]{1,0:T(8,128)S(1)}, u32[]{:S(2)}, u32[]{:S(2)}) %collective-permute-start.11) | collective-permute-done | bytes 1310752 | tf_op jit(solution)/shard_map/ppermute | solution.py:417
  96.7 1.2 shard_map.113.refs_1_.after_ref
  97.9 17.8 %all-to-all-start = ((f32[16,32,640]{2,1,0:T(8,128)}), f32[16,32,640]{2,1,0:T(8,128)S(1)}, u32[]{:S(2)}, u32[]{:S(2)}) async-start(f32[16,32,640]{2,1,0:T(8,128)} %bitcast.5), calls=%async_computation | async-start | bytes 2621440 | tf_op jit(solution)/shard_map/all_to_all | solution.py:500
  115.7 3.8 %collective-permute-start.12 = (f32[2,512,512]{2,1,0:T(8,128)}, f32[2,512,512]{2,1,0:T(8,128)}, u32[]{:S(2)}, u32[]{:S(2)}) collective-permute-start(f32[2,512,512]{2,1,0:T(8,128)} %shard_map.114), channel_id=1, source_target_pairs={{0,1},{1,2},{2,3},{3,4},{4,5},{5,6},{6,7},{8,9},{9,10},{10,11},{11... | collective-permute-start | bytes 6291464 | tf_op jit(solution)/shard_map/ppermute | solution.py:407
  119.5 1.6 copy-done.19
  121.1 3.9 %shard_map.115.refs_0_ = f32[2,512,512]{2,1,0:T(8,128)} custom-call(f32[2,512,512]{2,1,0:T(8,128)S(1)} %copy-done.19, f32[2,512,512]{2,1,0:T(8,128)} %collective-permute-done.13.corner_ref, f32[512,640]{1,0:T(8,128)} %shard_map.113.refs_1_.after_ref), custom_call_target="tpu_custom_call" | custom-call | tf_op jit(solution)/shard_map/pallas_call | solution.py:354
  125.0 4.9 %collective-permute-start.14 = (f32[2,512,512]{2,1,0:T(8,128)}, f32[2,512,512]{2,1,0:T(8,128)}, u32[]{:S(2)}, u32[]{:S(2)}) collective-permute-start(f32[2,512,512]{2,1,0:T(8,128)} %shard_map.115.refs_0_), channel_id=1, source_target_pairs={{0,8},{8,16},{16,24},{24,32},{32,40},{40,48},{48,56},{56,64},{64,7... | collective-permute-start | bytes 6291464 | tf_op jit(solution)/shard_map/ppermute | solution.py:407
  129.9 6.6 %all-to-all-done.terms_ref = f32[16,32,640]{2,1,0:T(8,128)S(1)} async-done(((f32[16,32,640]{2,1,0:T(8,128)}), f32[16,32,640]{2,1,0:T(8,128)S(1)}, u32[]{:S(2)}, u32[]{:S(2)}) %all-to-all-start) | async-done | bytes 1310752 | tf_op jit(solution)/shard_map/all_to_all | solution.py:500
  137.4 4.7 %all-to-all-start.1 = ((f32[4,32,640]{2,1,0:T(8,128)}), f32[4,32,640]{2,1,0:T(8,128)S(1)}, u32[]{:S(2)}, u32[]{:S(2)}) async-start(f32[4,32,640]{2,1,0:T(8,128)} %copy-done.21), calls=%async_computation.1 | async-start | bytes 655360 | tf_op jit(solution)/shard_map/all_to_all | solution.py:506
  142.9 3.9 %all-to-all-done.1.terms_ref = f32[4,32,640]{2,1,0:T(8,128)S(1)} async-done(((f32[4,32,640]{2,1,0:T(8,128)}), f32[4,32,640]{2,1,0:T(8,128)S(1)}, u32[]{:S(2)}, u32[]{:S(2)}) %all-to-all-start.1) | async-done | bytes 327712 | tf_op jit(solution)/shard_map/all_to_all | solution.py:506
  147.9 11.0 %all-to-all-start.2 = ((f32[16,32,512]{2,1,0:T(8,128)}), f32[16,32,512]{2,1,0:T(8,128)S(1)}, u32[]{:S(2)}, u32[]{:S(2)}) async-start(f32[16,32,512]{2,1,0:T(8,128)} %copy-done.13), calls=%async_computation.2 | async-start | bytes 2097152 | tf_op jit(solution)/shard_map/all_to_all | solution.py:510
  160.2 1.6 copy-done.18
  161.8 1.3 shard_map.112
  163.1 14.1 %collective-permute-done.14.above_ref = f32[2,512,512]{2,1,0:T(8,128)} collective-permute-done((f32[2,512,512]{2,1,0:T(8,128)}, f32[2,512,512]{2,1,0:T(8,128)}, u32[]{:S(2)}, u32[]{:S(2)}) %collective-permute-start.14) | collective-permute-done | bytes 2097184 | tf_op jit(solution)/shard_map/ppermute | solution.py:407
  177.2 4.3 %shard_map.116 = (f32[2,512,512]{2,1,0:T(8,128)}, f32[8,128]{1,0:T(8,128)S(1)}) custom-call(f32[1,1]{1,0:T(1,128)} %bitcast.3.scale_ref, f32[2,512,512]{2,1,0:T(8,128)S(1)} %get-tuple-element.42.base_ref, f32[2,512,512]{2,1,0:T(8,128)} %collective-permute-done.12.left_ref, f32[2,512,512]{2,1,0:T(8,128)} %collective-permute-done.14.above_ref), custom_call_target="tpu_custom_call" | custom-call | tf_op jit(solution)/shard_map/pallas_call | solution.py:445
  182.1 12.0 %all-to-all-done.2 = f32[16,32,512]{2,1,0:T(8,128)S(1)} async-done(((f32[16,32,512]{2,1,0:T(8,128)}), f32[16,32,512]{2,1,0:T(8,128)S(1)}, u32[]{:S(2)}, u32[]{:S(2)}) %all-to-all-start.2) | async-done | bytes 1048608 | tf_op jit(solution)/shard_map/all_to_all | solution.py:510
  195.1 2.2 %collective-permute-start.15 = (f32[512,512]{1,0:T(8,128)}, f32[512,512]{1,0:T(8,128)S(1)}, u32[]{:S(2)}, u32[]{:S(2)}) collective-permute-start(f32[512,512]{1,0:T(8,128)} %shard_map.119.mine_ref), channel_id=1, source_target_pairs={{0,1},{1,0},{2,3},{3,2},{4,5},{5,4},{6,7},{7,6},{8,9},{9,8},{10,11... | collective-permute-start | bytes 3145736 | tf_op jit(solution)/shard_map/ppermute | solution.py:417
  197.3 2.5 %collective-permute-done.15.other_ref = f32[512,512]{1,0:T(8,128)S(1)} collective-permute-done((f32[512,512]{1,0:T(8,128)}, f32[512,512]{1,0:T(8,128)S(1)}, u32[]{:S(2)}, u32[]{:S(2)}) %collective-permute-start.15) | collective-permute-done | bytes 1048608 | tf_op jit(solution)/shard_map/ppermute | solution.py:417
  199.8 1.2 copy-done.4
  201.0 1.5 shard_map.120
  (83 shorter events, 11.2 us)
Async XLA Ops:
  0.6 6.4 %copy-start = (f32[2,512,512]{2,1,0:T(8,128)S(1)}, f32[2,512,512]{2,1,0:T(8,128)}, u32[]{:S(2)}) copy-start(f32[2,512,512]{2,1,0:T(8,128)} %own_ref.11) | copy-start | bytes 6291460
  0.6 19.4 %copy-start.28 = (bf16[512,512]{1,0:T(8,128)(2,1)S(1)}, bf16[512,512]{1,0:T(8,128)(2,1)}, u32[]{:S(2)}) copy-start(bf16[512,512]{1,0:T(8,128)(2,1)} %constant.45.clone.order_ref) | copy-start | bytes 1572868
  0.7 9.9 %copy-start.33 = (s32[2,2]{1,0:T(2,128)S(1)}, s32[2,2]{1,0:T(2,128)}, u32[]{:S(2)}) copy-start(s32[2,2]{1,0:T(2,128)} %param.12) | copy-start | bytes 52
  0.7 45.7 %collective-permute-start = (f32[2,512,512]{2,1,0:T(8,128)}, f32[2,512,512]{2,1,0:T(8,128)}, u32[]{:S(2)}, u32[]{:S(2)}) collective-permute-start(f32[2,512,512]{2,1,0:T(8,128)} %own_ref.11), channel_id=1, source_target_pairs={{1,0},{2,1},{3,2},{4,3},{5,4},{6,5},{7,6},{9,8},{10,9},{11,10},{12... | collective-permute-start | bytes 6291464 | tf_op jit(solution)/shard_map/ppermute | solution.py:407
  5.7 27.9 %collective-permute-start.1 = (f32[2,144,512]{2,1,0:T(8,128)}, f32[2,144,512]{2,1,0:T(8,128)}, u32[]{:S(2)}, u32[]{:S(2)}) collective-permute-start(f32[2,144,512]{2,1,0:T(8,128)} %get-tuple-element.53), channel_id=1, source_target_pairs={{8,0},{16,8},{24,16},{32,24},{40,32},{48,40},{56,48},{64,56},{72,6... | collective-permute-start | bytes 1769480 | tf_op jit(solution)/shard_map/ppermute | solution.py:407
  7.1 13.0 %collective-permute-start.7 = (f32[2,96,512]{2,1,0:T(8,128)S(1)}, f32[2,96,512]{2,1,0:T(8,128)S(1)}, u32[]{:S(2)}, u32[]{:S(2)}) collective-permute-start(f32[2,96,512]{2,1,0:T(8,128)S(1)} %slice.27), channel_id=1, source_target_pairs={{0,8},{8,16},{16,24},{24,0},{1,9},{9,17},{17,25},{25,1},{2,10},{10... | collective-permute-start | bytes 1179656 | tf_op jit(solution)/shard_map/ppermute | solution.py:412
  9.2 32.8 %collective-permute-start.3 = (f32[2,144,512]{2,1,0:T(8,128)}, f32[2,144,512]{2,1,0:T(8,128)}, u32[]{:S(2)}, u32[]{:S(2)}) collective-permute-start(f32[2,144,512]{2,1,0:T(8,128)} %get-tuple-element.52), channel_id=1, source_target_pairs={{8,0},{16,8},{24,16},{32,24},{40,32},{48,40},{56,48},{64,56},{72,6... | collective-permute-start | bytes 1769480 | tf_op jit(solution)/shard_map/ppermute | solution.py:407
  20.0 18.0 %collective-permute-start.8 = (f32[2,96,512]{2,1,0:T(8,128)S(1)}, f32[2,96,512]{2,1,0:T(8,128)}, u32[]{:S(2)}, u32[]{:S(2)}) collective-permute-start(f32[2,96,512]{2,1,0:T(8,128)S(1)} %collective-permute-done.7), channel_id=1, source_target_pairs={{0,8},{8,16},{16,24},{24,0},{1,9},{9,17},{17,25},{25,1},{2,10},{10... | collective-permute-start | bytes 1179656 | tf_op jit(solution)/shard_map/ppermute | solution.py:412
  20.1 1.6 copy-start.16
  21.7 1.6 copy-start.17
  27.8 1.0 copy-start.5
  28.8 1.0 copy-start.8
  29.8 1.0 copy-start.11
  31.7 1.3 copy-start.20
  33.6 12.7 %copy-start.1 = (bf16[4,256,256]{2,1,0:T(8,128)(2,1)S(1)}, bf16[4,256,256]{2,1,0:T(8,128)(2,1)}, u32[]{:S(2)}) copy-start(bf16[4,256,256]{2,1,0:T(8,128)(2,1)} %constant.43.clone.mh_ref.refs_16_) | copy-start | bytes 1572868
  33.6 12.7 %copy-start.2 = (bf16[4,256,256]{2,1,0:T(8,128)(2,1)S(1)}, bf16[4,256,256]{2,1,0:T(8,128)(2,1)}, u32[]{:S(2)}) copy-start(bf16[4,256,256]{2,1,0:T(8,128)(2,1)} %constant.44.clone.ml_ref.refs_17_) | copy-start | bytes 1572868
  33.7 12.7 %collective-permute-start.2 = (f32[2,144,512]{2,1,0:T(8,128)}, f32[2,144,512]{2,1,0:T(8,128)S(1)}, u32[]{:S(2)}, u32[]{:S(2)}) collective-permute-start(f32[2,144,512]{2,1,0:T(8,128)} %shard_map.105.below_ref), channel_id=1, source_target_pairs={{1,0},{2,1},{3,2},{4,3},{5,4},{6,5},{7,6},{9,8},{10,9},{11,10},{12... | collective-permute-start | bytes 1769480 | tf_op jit(solution)/shard_map/ppermute | solution.py:407
  36.7 16.3 %collective-permute-start.5 = (f32[2,128,512]{2,1,0:T(8,128)S(1)}, f32[2,128,512]{2,1,0:T(8,128)}, u32[]{:S(2)}, u32[]{:S(2)}) collective-permute-start(f32[2,128,512]{2,1,0:T(8,128)S(1)} %slice.26), channel_id=1, source_target_pairs={{8,0},{16,8},{24,16},{32,24},{40,32},{48,40},{56,48},{64,56},{72,6... | collective-permute-start | bytes 1572872 | tf_op jit(solution)/shard_map/ppermute | solution.py:407
  38.0 16.9 %collective-permute-start.9 = (f32[2,96,512]{2,1,0:T(8,128)}, f32[2,96,512]{2,1,0:T(8,128)S(1)}, u32[]{:S(2)}, u32[]{:S(2)}) collective-permute-start(f32[2,96,512]{2,1,0:T(8,128)} %collective-permute-done.8), channel_id=1, source_target_pairs={{24,0},{0,8},{8,16},{48,24},{56,32},{32,40},{40,48},{80,56},{88,64... | collective-permute-start | bytes 1179656 | tf_op jit(solution)/shard_map/ppermute | solution.py:413
  42.0 15.2 %collective-permute-start.4 = (f32[2,144,512]{2,1,0:T(8,128)}, f32[2,144,512]{2,1,0:T(8,128)}, u32[]{:S(2)}, u32[]{:S(2)}) collective-permute-start(f32[2,144,512]{2,1,0:T(8,128)} %collective-permute-done.3.below_ref), channel_id=1, source_target_pairs={{1,0},{2,1},{3,2},{4,3},{5,4},{6,5},{7,6},{9,8},{10,9},{11,10},{12... | collective-permute-start | bytes 1769480 | tf_op jit(solution)/shard_map/ppermute | solution.py:407
  46.4 1.3 copy-start.6
  50.3 1.0 copy-start.22
  51.4 1.1 copy-start.24
  53.0 17.8 %collective-permute-start.6 = (f32[2,128,512]{2,1,0:T(8,128)}, f32[2,128,512]{2,1,0:T(8,128)S(1)}, u32[]{:S(2)}, u32[]{:S(2)}) collective-permute-start(f32[2,128,512]{2,1,0:T(8,128)} %shard_map.108.below_ref), channel_id=1, source_target_pairs={{1,0},{2,1},{3,2},{4,3},{5,4},{6,5},{7,6},{9,8},{10,9},{11,10},{12... | collective-permute-start | bytes 1572872 | tf_op jit(solution)/shard_map/ppermute | solution.py:407
  55.0 13.0 %collective-permute-start.10 = (f32[2,96,512]{2,1,0:T(8,128)S(1)}, f32[2,96,512]{2,1,0:T(8,128)S(1)}, u32[]{:S(2)}, u32[]{:S(2)}) collective-permute-start(f32[2,96,512]{2,1,0:T(8,128)S(1)} %collective-permute-done.9.below_ref), channel_id=1, source_target_pairs={{1,0},{2,1},{3,2},{4,3},{5,4},{6,5},{7,6},{9,8},{10,9},{11,10},{12... | collective-permute-start | bytes 1179656 | tf_op jit(solution)/shard_map/ppermute | solution.py:407
  57.2 1.3 copy-start.9
  58.5 9.4 %copy-start.15 = (f32[2,2,96,512]{3,2,1,0:T(8,128)S(1)}, f32[2,2,96,512]{3,2,1,0:T(8,128)}, u32[]{:S(2)}) copy-start(f32[2,2,96,512]{3,2,1,0:T(8,128)} %copy-done.14) | copy-start | bytes 2359300
  67.9 2.9 %copy-start.12 = (f32[2,2,128,512]{3,2,1,0:T(8,128)S(1)}, f32[2,2,128,512]{3,2,1,0:T(8,128)}, u32[]{:S(2)}) copy-start(f32[2,2,128,512]{3,2,1,0:T(8,128)} %copy-done.11) | copy-start | bytes 3145732
  70.8 3.2 %copy-start.7 = (f32[2,2,144,512]{3,2,1,0:T(8,128)S(1)}, f32[2,2,144,512]{3,2,1,0:T(8,128)}, u32[]{:S(2)}) copy-start(f32[2,2,144,512]{3,2,1,0:T(8,128)} %copy-done.5) | copy-start | bytes 3538948
  70.8 3.2 %copy-start.10 = (f32[2,2,144,512]{3,2,1,0:T(8,128)S(1)}, f32[2,2,144,512]{3,2,1,0:T(8,128)}, u32[]{:S(2)}) copy-start(f32[2,2,144,512]{3,2,1,0:T(8,128)} %copy-done.8) | copy-start | bytes 3538948
  70.9 3.2 %copy-start.23 = (f32[2,2,144,512]{3,2,1,0:T(8,128)S(1)}, f32[2,2,144,512]{3,2,1,0:T(8,128)}, u32[]{:S(2)}) copy-start(f32[2,2,144,512]{3,2,1,0:T(8,128)} %copy-done.22) | copy-start | bytes 3538948
  70.9 3.2 %copy-start.25 = (f32[2,2,144,512]{3,2,1,0:T(8,128)S(1)}, f32[2,2,144,512]{3,2,1,0:T(8,128)}, u32[]{:S(2)}) copy-start(f32[2,2,144,512]{3,2,1,0:T(8,128)} %copy-done.24) | copy-start | bytes 3538948
  70.9 3.2 %copy-start.26 = (bf16[4,256,256]{2,1,0:T(8,128)(2,1)S(1)}, bf16[4,256,256]{2,1,0:T(8,128)(2,1)}, u32[]{:S(2)}) copy-start(bf16[4,256,256]{2,1,0:T(8,128)(2,1)} %constant.41.clone.refs_14_) | copy-start | bytes 1572868
  70.9 3.4 %copy-start.27 = (bf16[4,256,256]{2,1,0:T(8,128)(2,1)S(1)}, bf16[4,256,256]{2,1,0:T(8,128)(2,1)}, u32[]{:S(2)}) copy-start(bf16[4,256,256]{2,1,0:T(8,128)(2,1)} %constant.42.clone.refs_15_) | copy-start | bytes 1572868
  70.9 3.4 %copy-start.30 = (f32[2,8,128]{2,1,0:T(8,128)S(1)}, f32[2,8,128]{2,1,0:T(8,128)}, u32[]{:S(2)}) copy-start(f32[2,8,128]{2,1,0:T(8,128)} %copy-done.29) | copy-start | bytes 24580
  88.7 30.8 %collective-permute-start.13 = (f32[2,512,512]{2,1,0:T(8,128)}, f32[2,512,512]{2,1,0:T(8,128)}, u32[]{:S(2)}, u32[]{:S(2)}) collective-permute-start(f32[2,512,512]{2,1,0:T(8,128)} %get-tuple-element.47), channel_id=1, source_target_pairs={{0,1},{1,2},{2,3},{3,4},{4,5},{5,6},{6,7},{8,9},{9,10},{10,11},{11... | collective-permute-start | bytes 6291464 | tf_op jit(solution)/shard_map/ppermute | solution.py:407
  90.7 6.0 %collective-permute-start.11 = (f32[512,640]{1,0:T(8,128)S(1)}, f32[512,640]{1,0:T(8,128)S(1)}, u32[]{:S(2)}, u32[]{:S(2)}) collective-permute-start(f32[512,640]{1,0:T(8,128)S(1)} %get-tuple-element.45), channel_id=1, source_target_pairs={{0,1},{1,0},{2,3},{3,2},{4,5},{5,4},{6,7},{7,6},{8,9},{9,8},{10,11... | collective-permute-start | bytes 3932168 | tf_op jit(solution)/shard_map/ppermute | solution.py:417
  97.9 38.7 %all-to-all-start = ((f32[16,32,640]{2,1,0:T(8,128)}), f32[16,32,640]{2,1,0:T(8,128)S(1)}, u32[]{:S(2)}, u32[]{:S(2)}) async-start(f32[16,32,640]{2,1,0:T(8,128)} %bitcast.5), calls=%async_computation | async-start | bytes 2621440 | tf_op jit(solution)/shard_map/all_to_all | solution.py:500
  115.7 47.4 %collective-permute-start.12 = (f32[2,512,512]{2,1,0:T(8,128)}, f32[2,512,512]{2,1,0:T(8,128)}, u32[]{:S(2)}, u32[]{:S(2)}) collective-permute-start(f32[2,512,512]{2,1,0:T(8,128)} %shard_map.114), channel_id=1, source_target_pairs={{0,1},{1,2},{2,3},{3,4},{4,5},{5,6},{6,7},{8,9},{9,10},{10,11},{11... | collective-permute-start | bytes 6291464 | tf_op jit(solution)/shard_map/ppermute | solution.py:407
  119.5 1.6 copy-start.19
  125.0 52.2 %collective-permute-start.14 = (f32[2,512,512]{2,1,0:T(8,128)}, f32[2,512,512]{2,1,0:T(8,128)}, u32[]{:S(2)}, u32[]{:S(2)}) collective-permute-start(f32[2,512,512]{2,1,0:T(8,128)} %shard_map.115.refs_0_), channel_id=1, source_target_pairs={{0,8},{8,16},{16,24},{24,32},{32,40},{40,48},{48,56},{56,64},{64,7... | collective-permute-start | bytes 6291464 | tf_op jit(solution)/shard_map/ppermute | solution.py:407
  137.4 9.4 %all-to-all-start.1 = ((f32[4,32,640]{2,1,0:T(8,128)}), f32[4,32,640]{2,1,0:T(8,128)S(1)}, u32[]{:S(2)}, u32[]{:S(2)}) async-start(f32[4,32,640]{2,1,0:T(8,128)} %copy-done.21), calls=%async_computation.1 | async-start | bytes 655360 | tf_op jit(solution)/shard_map/all_to_all | solution.py:506
  146.8 1.0 copy-start.13
  147.9 46.2 %all-to-all-start.2 = ((f32[16,32,512]{2,1,0:T(8,128)}), f32[16,32,512]{2,1,0:T(8,128)S(1)}, u32[]{:S(2)}, u32[]{:S(2)}) async-start(f32[16,32,512]{2,1,0:T(8,128)} %copy-done.13), calls=%async_computation.2 | async-start | bytes 2097152 | tf_op jit(solution)/shard_map/all_to_all | solution.py:510
  160.2 1.6 copy-start.18
  194.1 1.0 copy-start.3
  195.1 4.7 %collective-permute-start.15 = (f32[512,512]{1,0:T(8,128)}, f32[512,512]{1,0:T(8,128)S(1)}, u32[]{:S(2)}, u32[]{:S(2)}) collective-permute-start(f32[512,512]{1,0:T(8,128)} %shard_map.119.mine_ref), channel_id=1, source_target_pairs={{0,1},{1,0},{2,3},{3,2},{4,5},{5,4},{6,7},{7,6},{8,9},{9,8},{10,11... | collective-permute-start | bytes 3145736 | tf_op jit(solution)/shard_map/ppermute | solution.py:417
  199.8 1.2 copy-start.4
  (5 other events, 3.4 us)

commit v8 on v7

--- a/solution.py
+++ b/solution.py
@@ -407,12 +407,6 @@
     return lax.ppermute(value, axis, [(source, source + steps) for source in range(first, last)])
 
 
-def the_long_way(value):
-    for _ in range(2):
-        value = lax.ppermute(value, "x", [(x, (x + 1) % 4) for x in range(4)])
-    return lax.ppermute(value, ROW, [(r // 4 * 4 + (r + 2) % 4, r - 1) for r in range(1, 16)])
-
-
 def other_core(value):
     return lax.ppermute(value, "core", [(0, 1), (1, 0)])
 
@@ -482,8 +476,8 @@
     scale = 0.9 / (peaks[1, :1, :1] + 1e-06)
     specs, wrapped, tokens = [], [], []
     for k, piece in enumerate(pieces):
-        below = the_long_way(piece) if k == 3 else shifted(piece, ROW, -1)
-        if k in (0, 2):
+        below = shifted(piece, ROW, -1)
+        if k in (0, 3):
             (below,) = tied((below,), tokens[:1] if k else (peaks,))
         corner = shifted(below, COL, -1)
         spec, wrap, token = fore(k, where, object_field, right, below, corner, rolled[k], matrices)

time: 204 us -> 192 us (0.941)
  starting transfers between devices: 69.3 us -> 53.9 us
  waiting for transfers between devices: 61.8 us -> 64.2 us
    ppermute x11 -> x12, waiting for transfers between devices: 22.1 us -> 34.3 us  [shifted(): lax.ppermute(value, axis, [(source, source + steps) for source in range(f...]
    ppermute x3 -> x0, waiting for transfers between devices: 9.29 us -> none  [the longest x2 9.29 us: the_long_way(): value = lax.ppermute(value, 'x', [(x, (x + 1) % 4) for x in range(4)])]
    all_to_all x1, starting transfers between devices: 17.8 us -> 8.61 us  [on_device(): terms = lax.all_to_all(half.reshape(16, share, WIDE), ROW, 0, 0)]
    ppermute x3 -> x0, starting transfers between devices: 6.15 us -> none  [the longest x1 3.99 us: the_long_way(): lax.ppermute(value, ROW, [(r // 4 * 4 + (r + 2) % 4, r - 1) for r in rang...]
    all_to_all x1, waiting for transfers between devices: 6.62 us -> 1.74 us  [on_device(): terms = lax.all_to_all(half.reshape(16, share, WIDE), ROW, 0, 0)]
    all_to_all x1, waiting for transfers between devices: 3.86 us -> 7.84 us  [on_device(): terms = lax.all_to_all(terms, 'z', 0, 0)]
    ppermute x11 -> x12, starting transfers between devices: 26.9 us -> 30.1 us  [shifted(): lax.ppermute(value, axis, [(source, source + steps) for source in range(f...]
    all_to_all x1, starting transfers between devices: 11 us -> 8.6 us  [on_device(): mine = lax.all_to_all(shares, ROW, 0, 0).reshape(SIDE, SIDE)]
  transfers between devices with their start and end apart: 19 -> 17, of which waited for: 9 -> 9; matrix products, arithmetic and copies ran while one was open for 2% -> 3% of each run, Pallas kernels for 12% -> 13%
where the time goes in v8:
time: 192 us; the launch traced here: 191 us
  waiting for transfers between devices  64.2 us (33%)
  starting transfers between devices  53.9 us (28%)
  Pallas kernels  43.6 us (23%)
  local copies, waits for them, and re-layouts  27.5 us (14%)
    ppermute x12, waiting for transfers between devices, shifted(): lax.ppermute(value, axis, [(source, source + steps) for source in range(f...  34.3 us
    ppermute x12, starting transfers between devices, shifted(): lax.ppermute(value, axis, [(source, source + steps) for source in range(f...  30.1 us
    unnamed x72, local copies, waits for them, and re-layouts  22.8 us
    pallas_call x1, Pallas kernels, update(): pl.pallas_call(update_kernel, out_shape=out_shape, in_specs=[sm()] + [vm(...  14.5 us
    all_to_all x1, waiting for transfers between devices, on_device(): mine = lax.all_to_all(shares, ROW, 0, 0).reshape(SIDE, SIDE)  13.5 us
    pallas_call x4, Pallas kernels, fore(): pl.pallas_call(functools.partial(fore_kernel, piece), grid=(1,), out_shap...  12.3 us
    all_to_all x1, starting transfers between devices, on_device(): terms = lax.all_to_all(half.reshape(16, share, WIDE), ROW, 0, 0)  8.61 us
    all_to_all x1, starting transfers between devices, on_device(): mine = lax.all_to_all(shares, ROW, 0, 0).reshape(SIDE, SIDE)  8.6 us
  transfers between devices with their start and end apart: 17, of which 9 were waited for; matrix products, arithmetic and copies ran while one was open for 3% of the time, Pallas kernels for 13%

profile of v8, /device:TPU:33, one launch (start us, length us, event | category | flops | bytes accessed | tf_op | source)
XLA Modules:
  0.0 191.2 jit_solution(13815386446566678470)
XLA Ops:
  0.7 2.7 %collective-permute-start = (f32[2,512,512]{2,1,0:T(8,128)}, f32[2,512,512]{2,1,0:T(8,128)}, u32[]{:S(2)}, u32[]{:S(2)}) collective-permute-start(f32[2,512,512]{2,1,0:T(8,128)} %own_ref.11), channel_id=1, source_target_pairs={{1,0},{2,1},{3,2},{4,3},{5,4},{6,5},{7,6},{9,8},{10,9},{11,10},{12... | collective-permute-start | bytes 6291464 | tf_op jit(solution)/shard_map/ppermute | solution.py:407
  3.4 2.3 %fusion = (f32[2,144,512]{2,1,0:T(8,128)}, f32[2,144,512]{2,1,0:T(8,128)}) fusion(f32[2,512,512]{2,1,0:T(8,128)} %own_ref.11), kind=kLoop, calls=%fused_computation.5 | loop fusion | bytes 2359296 | tf_op jit(solution)/shard_map/slice | solution.py:473
  5.7 1.3 collective-permute-start.1
  7.0 1.3 collective-permute-start.3
  9.2 1.3 collective-permute-start.5
  10.8 1.6 copy-done.16
  12.4 1.6 copy-done.17
  14.0 4.5 %shard_map.104 = (f32[2,2,144,512]{3,2,1,0:T(8,128)S(1)}, f32[2,2,144,512]{3,2,1,0:T(8,128)S(1)}, f32[2,2,128,512]{3,2,1,0:T(8,128)S(1)}, f32[2,2,96,512]{3,2,1,...) custom-call(s32[3,2]{1,0:T(4,128)S(1)} %pad_add_fusion.where_ref, f32[2,512,512]{2,1,0:T(8,128)S(1)} %copy-done.16, ...), custom_call_target="tpu_custom_call" | custom-call | tf_op jit(solution)/shard_map/pallas_call | solution.py:277
  19.5 1.0 copy-done.8
  22.4 1.3 copy-done.20
  24.3 2.1 %collective-permute-start.2 = (f32[2,144,512]{2,1,0:T(8,128)}, f32[2,144,512]{2,1,0:T(8,128)S(1)}, u32[]{:S(2)}, u32[]{:S(2)}) collective-permute-start(f32[2,144,512]{2,1,0:T(8,128)} %shard_map.105.below_ref), channel_id=1, source_target_pairs={{1,0},{2,1},{3,2},{4,3},{5,4},{6,5},{7,6},{9,8},{10,9},{11,10},{12... | collective-permute-start | bytes 1769480 | tf_op jit(solution)/shard_map/ppermute | solution.py:407
  26.4 1.3 collective-permute-start.7
  27.7 7.8 %collective-permute-done.3.below_ref = f32[2,144,512]{2,1,0:T(8,128)} collective-permute-done((f32[2,144,512]{2,1,0:T(8,128)}, f32[2,144,512]{2,1,0:T(8,128)}, u32[]{:S(2)}, u32[]{:S(2)}) %collective-permute-start.3) | collective-permute-done | bytes 589856 | tf_op jit(solution)/shard_map/ppermute | solution.py:407
  35.5 3.1 %collective-permute-start.4 = (f32[2,144,512]{2,1,0:T(8,128)}, f32[2,144,512]{2,1,0:T(8,128)}, u32[]{:S(2)}, u32[]{:S(2)}) collective-permute-start(f32[2,144,512]{2,1,0:T(8,128)} %collective-permute-done.3.below_ref), channel_id=1, source_target_pairs={{1,0},{2,1},{3,2},{4,3},{5,4},{6,5},{7,6},{9,8},{10,9},{11,10},{12... | collective-permute-start | bytes 1769480 | tf_op jit(solution)/shard_map/ppermute | solution.py:407
  38.6 8.2 %collective-permute-done.5.below_ref = f32[2,128,512]{2,1,0:T(8,128)} collective-permute-done((f32[2,128,512]{2,1,0:T(8,128)}, f32[2,128,512]{2,1,0:T(8,128)}, u32[]{:S(2)}, u32[]{:S(2)}) %collective-permute-start.5) | collective-permute-done | bytes 524320 | tf_op jit(solution)/shard_map/ppermute | solution.py:407
  46.7 3.1 %collective-permute-start.6 = (f32[2,128,512]{2,1,0:T(8,128)}, f32[2,128,512]{2,1,0:T(8,128)}, u32[]{:S(2)}, u32[]{:S(2)}) collective-permute-start(f32[2,128,512]{2,1,0:T(8,128)} %collective-permute-done.5.below_ref), channel_id=1, source_target_pairs={{1,0},{2,1},{3,2},{4,3},{5,4},{6,5},{7,6},{9,8},{10,9},{11,10},{12... | collective-permute-start | bytes 1572872 | tf_op jit(solution)/shard_map/ppermute | solution.py:407
  49.9 1.3 copy-done.6
  51.1 2.7 %shard_map.106 = (f32[2,2,144,512]{3,2,1,0:T(8,128)S(1)}, f32[2,2,144,512]{3,2,1,0:T(8,128)S(1)}, f32[8,128]{1,0:T(8,128)S(1)}) custom-call(s32[3,2]{1,0:T(4,128)S(1)} %pad_add_fusion.where_ref, f32[2,512,512]{2,1,0:T(8,128)S(1)} %copy-done, f32[2,512,512]{2,1,0:T(8,128)} %collective-permute-done.right_ref, f32[2,144,512]{2,1,0:T(8,128)} %shard_map.105.below_ref, ...), custom_call_target="tpu_custom_call" | custom-call | tf_op jit(solution)/shard_map/pallas_call | solution.py:137
  54.9 1.1 copy-done.26
  57.3 2.1 %collective-permute-start.8 = (f32[2,96,512]{2,1,0:T(8,128)}, f32[2,96,512]{2,1,0:T(8,128)S(1)}, u32[]{:S(2)}, u32[]{:S(2)}) collective-permute-start(f32[2,96,512]{2,1,0:T(8,128)} %shard_map.109.below_ref), channel_id=1, source_target_pairs={{1,0},{2,1},{3,2},{4,3},{5,4},{6,5},{7,6},{9,8},{10,9},{11,10},{12... | collective-permute-start | bytes 1179656 | tf_op jit(solution)/shard_map/ppermute | solution.py:407
  59.4 1.3 copy-done.9
  60.6 3.3 %shard_map.107 = (f32[2,2,144,512]{3,2,1,0:T(8,128)S(1)}, f32[2,2,144,512]{3,2,1,0:T(8,128)S(1)}, f32[8,128]{1,0:T(8,128)}) custom-call(s32[3,2]{1,0:T(4,128)S(1)} %pad_add_fusion.where_ref, f32[2,512,512]{2,1,0:T(8,128)S(1)} %copy-done, f32[2,512,512]{2,1,0:T(8,128)} %collective-permute-done.right_ref, f32[2,144,512]{2,1,0:T(8,128)} %collective-permute-done.3.below_ref, ...), custom_call_target="tpu_custom_call" | custom-call | tf_op jit(solution)/shard_map/pallas_call | solution.py:137
  64.0 3.2 %shard_map.108 = (f32[2,2,128,512]{3,2,1,0:T(8,128)S(1)}, f32[2,2,128,512]{3,2,1,0:T(8,128)S(1)}, f32[8,128]{1,0:T(8,128)}) custom-call(s32[3,2]{1,0:T(4,128)S(1)} %pad_add_fusion.where_ref, f32[2,512,512]{2,1,0:T(8,128)S(1)} %copy-done, f32[2,512,512]{2,1,0:T(8,128)} %collective-permute-done.right_ref, f32[2,128,512]{2,1,0:T(8,128)} %collective-permute-done.5.below_ref, ...), custom_call_target="tpu_custom_call" | custom-call | tf_op jit(solution)/shard_map/pallas_call | solution.py:137
  67.3 3.0 %shard_map.110 = (f32[2,2,96,512]{3,2,1,0:T(8,128)S(1)}, f32[2,2,96,512]{3,2,1,0:T(8,128)S(1)}, f32[8,128]{1,0:T(8,128)}) custom-call(s32[3,2]{1,0:T(4,128)S(1)} %pad_add_fusion.where_ref, f32[2,512,512]{2,1,0:T(8,128)S(1)} %copy-done, f32[2,512,512]{2,1,0:T(8,128)} %collective-permute-done.right_ref, f32[2,96,512]{2,1,0:T(8,128)S(1)} %copy-done.22, ...), custom_call_target="tpu_custom_call" | custom-call | tf_op jit(solution)/shard_map/pallas_call | solution.py:137
  70.5 14.5 %shard_map.111 = (f32[2,512,512]{2,1,0:T(8,128)}, f32[2,512,512]{2,1,0:T(8,128)}, f32[2,512,512]{2,1,0:T(8,128)}, f32[2,512,512]{2,1,0:T(8,128)}, f32[512,640]{1,0:T(8,128)S(1)}, /*index=5*/f32[512,640]{1,0:T(8,128)S(1)}) custom-call(s32[3,2]{1,0:T(4,128)S(1)} %pad_add_fusion.where_ref, f32[2,2,144,512]{3,2,1,0:T(8,128)S(1)} %copy-done.25, ...), custom_call_target="tpu_custom_call" | custom-call | tf_op jit(solution)/shard_map/pallas_call | solution.py:298
  85.0 3.6 %collective-permute-start.11 = (f32[2,512,512]{2,1,0:T(8,128)}, f32[2,512,512]{2,1,0:T(8,128)}, u32[]{:S(2)}, u32[]{:S(2)}) collective-permute-start(f32[2,512,512]{2,1,0:T(8,128)} %get-tuple-element.47), channel_id=1, source_target_pairs={{0,1},{1,2},{2,3},{3,4},{4,5},{5,6},{6,7},{8,9},{9,10},{10,11},{11... | collective-permute-start | bytes 6291464 | tf_op jit(solution)/shard_map/ppermute | solution.py:407
  88.7 4.2 %collective-permute-done.9.came_ref = f32[512,640]{1,0:T(8,128)S(1)} collective-permute-done((f32[512,640]{1,0:T(8,128)S(1)}, f32[512,640]{1,0:T(8,128)S(1)}, u32[]{:S(2)}, u32[]{:S(2)}) %collective-permute-start.9) | collective-permute-done | bytes 1310752 | tf_op jit(solution)/shard_map/ppermute | solution.py:411
  92.9 1.2 shard_map.113.refs_1_.after_ref
  94.1 8.6 %all-to-all-start = ((f32[16,32,640]{2,1,0:T(8,128)}), f32[16,32,640]{2,1,0:T(8,128)S(1)}, u32[]{:S(2)}, u32[]{:S(2)}) async-start(f32[16,32,640]{2,1,0:T(8,128)} %bitcast.5), calls=%async_computation | async-start | bytes 2621440 | tf_op jit(solution)/shard_map/all_to_all | solution.py:494
  102.7 3.9 %collective-permute-start.10 = (f32[2,512,512]{2,1,0:T(8,128)}, f32[2,512,512]{2,1,0:T(8,128)}, u32[]{:S(2)}, u32[]{:S(2)}) collective-permute-start(f32[2,512,512]{2,1,0:T(8,128)} %shard_map.114), channel_id=1, source_target_pairs={{0,1},{1,2},{2,3},{3,4},{4,5},{5,6},{6,7},{8,9},{9,10},{10,11},{11... | collective-permute-start | bytes 6291464 | tf_op jit(solution)/shard_map/ppermute | solution.py:407
  106.6 5.3 %collective-permute-done.11.corner_ref = f32[2,512,512]{2,1,0:T(8,128)} collective-permute-done((f32[2,512,512]{2,1,0:T(8,128)}, f32[2,512,512]{2,1,0:T(8,128)}, u32[]{:S(2)}, u32[]{:S(2)}) %collective-permute-start.11) | collective-permute-done | bytes 2097184 | tf_op jit(solution)/shard_map/ppermute | solution.py:407
  111.9 1.6 copy-done.19
  113.5 3.9 %shard_map.115.refs_0_ = f32[2,512,512]{2,1,0:T(8,128)} custom-call(f32[2,512,512]{2,1,0:T(8,128)S(1)} %copy-done.19, f32[2,512,512]{2,1,0:T(8,128)} %collective-permute-done.11.corner_ref, f32[512,640]{1,0:T(8,128)} %shard_map.113.refs_1_.after_ref), custom_call_target="tpu_custom_call" | custom-call | tf_op jit(solution)/shard_map/pallas_call | solution.py:354
  117.4 4.5 %collective-permute-start.12 = (f32[2,512,512]{2,1,0:T(8,128)}, f32[2,512,512]{2,1,0:T(8,128)}, u32[]{:S(2)}, u32[]{:S(2)}) collective-permute-start(f32[2,512,512]{2,1,0:T(8,128)} %shard_map.115.refs_0_), channel_id=1, source_target_pairs={{0,8},{8,16},{16,24},{24,32},{32,40},{40,48},{48,56},{56,64},{64,7... | collective-permute-start | bytes 6291464 | tf_op jit(solution)/shard_map/ppermute | solution.py:407
  121.9 1.7 all-to-all-done.terms_ref
  124.4 4.8 %all-to-all-start.1 = ((f32[4,32,640]{2,1,0:T(8,128)}), f32[4,32,640]{2,1,0:T(8,128)S(1)}, u32[]{:S(2)}, u32[]{:S(2)}) async-start(f32[4,32,640]{2,1,0:T(8,128)} %copy-done.23), calls=%async_computation.1 | async-start | bytes 655360 | tf_op jit(solution)/shard_map/all_to_all | solution.py:500
  130.1 7.8 %all-to-all-done.1.terms_ref = f32[4,32,640]{2,1,0:T(8,128)S(1)} async-done(((f32[4,32,640]{2,1,0:T(8,128)}), f32[4,32,640]{2,1,0:T(8,128)S(1)}, u32[]{:S(2)}, u32[]{:S(2)}) %all-to-all-start.1) | async-done | bytes 327712 | tf_op jit(solution)/shard_map/all_to_all | solution.py:500
  138.0 1.0 copy-done.13
  139.1 8.6 %all-to-all-start.2 = ((f32[16,32,512]{2,1,0:T(8,128)}), f32[16,32,512]{2,1,0:T(8,128)S(1)}, u32[]{:S(2)}, u32[]{:S(2)}) async-start(f32[16,32,512]{2,1,0:T(8,128)} %copy-done.13), calls=%async_computation.2 | async-start | bytes 2097152 | tf_op jit(solution)/shard_map/all_to_all | solution.py:504
  149.0 1.6 copy-done.18
  150.6 1.3 shard_map.112
  151.9 13.1 %collective-permute-done.12.above_ref = f32[2,512,512]{2,1,0:T(8,128)} collective-permute-done((f32[2,512,512]{2,1,0:T(8,128)}, f32[2,512,512]{2,1,0:T(8,128)}, u32[]{:S(2)}, u32[]{:S(2)}) %collective-permute-start.12) | collective-permute-done | bytes 2097184 | tf_op jit(solution)/shard_map/ppermute | solution.py:407
  165.0 4.3 %shard_map.116 = (f32[2,512,512]{2,1,0:T(8,128)}, f32[8,128]{1,0:T(8,128)S(1)}) custom-call(f32[1,1]{1,0:T(1,128)} %bitcast.3.scale_ref, f32[2,512,512]{2,1,0:T(8,128)S(1)} %get-tuple-element.42.base_ref, f32[2,512,512]{2,1,0:T(8,128)} %collective-permute-done.10.left_ref, f32[2,512,512]{2,1,0:T(8,128)} %collective-permute-done.12.above_ref), custom_call_target="tpu_custom_call" | custom-call | tf_op jit(solution)/shard_map/pallas_call | solution.py:439
  169.9 13.5 %all-to-all-done.2 = f32[16,32,512]{2,1,0:T(8,128)S(1)} async-done(((f32[16,32,512]{2,1,0:T(8,128)}), f32[16,32,512]{2,1,0:T(8,128)S(1)}, u32[]{:S(2)}, u32[]{:S(2)}) %all-to-all-start.2) | async-done | bytes 1048608 | tf_op jit(solution)/shard_map/all_to_all | solution.py:504
  184.4 1.6 collective-permute-start.13
  186.0 2.5 %collective-permute-done.13.other_ref = f32[512,512]{1,0:T(8,128)S(1)} collective-permute-done((f32[512,512]{1,0:T(8,128)}, f32[512,512]{1,0:T(8,128)S(1)}, u32[]{:S(2)}, u32[]{:S(2)}) %collective-permute-start.13) | collective-permute-done | bytes 1048608 | tf_op jit(solution)/shard_map/ppermute | solution.py:411
  188.5 1.2 copy-done.4
  189.7 1.5 shard_map.120
  (83 shorter events, 11.2 us)
Async XLA Ops:
  0.6 7.7 %copy-start = (f32[2,512,512]{2,1,0:T(8,128)S(1)}, f32[2,512,512]{2,1,0:T(8,128)}, u32[]{:S(2)}) copy-start(f32[2,512,512]{2,1,0:T(8,128)} %own_ref.11) | copy-start | bytes 6291460
  0.6 10.1 %copy-start.30 = (bf16[512,512]{1,0:T(8,128)(2,1)S(1)}, bf16[512,512]{1,0:T(8,128)(2,1)}, u32[]{:S(2)}) copy-start(bf16[512,512]{1,0:T(8,128)(2,1)} %constant.45.clone.order_ref) | copy-start | bytes 1572868
  0.7 9.8 %copy-start.35 = (s32[2,2]{1,0:T(2,128)S(1)}, s32[2,2]{1,0:T(2,128)}, u32[]{:S(2)}) copy-start(s32[2,2]{1,0:T(2,128)} %param.12) | copy-start | bytes 52
  0.7 49.2 %collective-permute-start = (f32[2,512,512]{2,1,0:T(8,128)}, f32[2,512,512]{2,1,0:T(8,128)}, u32[]{:S(2)}, u32[]{:S(2)}) collective-permute-start(f32[2,512,512]{2,1,0:T(8,128)} %own_ref.11), channel_id=1, source_target_pairs={{1,0},{2,1},{3,2},{4,3},{5,4},{6,5},{7,6},{9,8},{10,9},{11,10},{12... | collective-permute-start | bytes 6291464 | tf_op jit(solution)/shard_map/ppermute | solution.py:407
  5.7 18.6 %collective-permute-start.1 = (f32[2,144,512]{2,1,0:T(8,128)}, f32[2,144,512]{2,1,0:T(8,128)}, u32[]{:S(2)}, u32[]{:S(2)}) collective-permute-start(f32[2,144,512]{2,1,0:T(8,128)} %get-tuple-element.53), channel_id=1, source_target_pairs={{8,0},{16,8},{24,16},{32,24},{40,32},{48,40},{56,48},{64,56},{72,6... | collective-permute-start | bytes 1769480 | tf_op jit(solution)/shard_map/ppermute | solution.py:407
  7.0 28.5 %collective-permute-start.3 = (f32[2,144,512]{2,1,0:T(8,128)}, f32[2,144,512]{2,1,0:T(8,128)}, u32[]{:S(2)}, u32[]{:S(2)}) collective-permute-start(f32[2,144,512]{2,1,0:T(8,128)} %get-tuple-element.52), channel_id=1, source_target_pairs={{8,0},{16,8},{24,16},{32,24},{40,32},{48,40},{56,48},{64,56},{72,6... | collective-permute-start | bytes 1769480 | tf_op jit(solution)/shard_map/ppermute | solution.py:407
  9.2 37.6 %collective-permute-start.5 = (f32[2,128,512]{2,1,0:T(8,128)}, f32[2,128,512]{2,1,0:T(8,128)}, u32[]{:S(2)}, u32[]{:S(2)}) collective-permute-start(f32[2,128,512]{2,1,0:T(8,128)} %slice.26), channel_id=1, source_target_pairs={{8,0},{16,8},{24,16},{32,24},{40,32},{48,40},{56,48},{64,56},{72,6... | collective-permute-start | bytes 1572872 | tf_op jit(solution)/shard_map/ppermute | solution.py:407
  10.8 1.6 copy-start.16
  12.4 1.6 copy-start.17
  18.5 1.0 copy-start.5
  19.5 1.0 copy-start.8
  20.5 1.0 copy-start.11
  21.5 0.9 copy-start.14
  22.4 1.3 copy-start.20
  24.3 25.5 %copy-start.1 = (bf16[4,256,256]{2,1,0:T(8,128)(2,1)S(1)}, bf16[4,256,256]{2,1,0:T(8,128)(2,1)}, u32[]{:S(2)}) copy-start(bf16[4,256,256]{2,1,0:T(8,128)(2,1)} %constant.43.clone.mh_ref.refs_16_) | copy-start | bytes 1572868
  24.3 25.5 %copy-start.2 = (bf16[4,256,256]{2,1,0:T(8,128)(2,1)S(1)}, bf16[4,256,256]{2,1,0:T(8,128)(2,1)}, u32[]{:S(2)}) copy-start(bf16[4,256,256]{2,1,0:T(8,128)(2,1)} %constant.44.clone.ml_ref.refs_17_) | copy-start | bytes 1572868
  24.3 25.5 %collective-permute-start.2 = (f32[2,144,512]{2,1,0:T(8,128)}, f32[2,144,512]{2,1,0:T(8,128)S(1)}, u32[]{:S(2)}, u32[]{:S(2)}) collective-permute-start(f32[2,144,512]{2,1,0:T(8,128)} %shard_map.105.below_ref), channel_id=1, source_target_pairs={{1,0},{2,1},{3,2},{4,3},{5,4},{6,5},{7,6},{9,8},{10,9},{11,10},{12... | collective-permute-start | bytes 1769480 | tf_op jit(solution)/shard_map/ppermute | solution.py:407
  26.4 30.1 %collective-permute-start.7 = (f32[2,96,512]{2,1,0:T(8,128)S(1)}, f32[2,96,512]{2,1,0:T(8,128)S(1)}, u32[]{:S(2)}, u32[]{:S(2)}) collective-permute-start(f32[2,96,512]{2,1,0:T(8,128)S(1)} %slice.27), channel_id=1, source_target_pairs={{8,0},{16,8},{24,16},{32,24},{40,32},{48,40},{56,48},{64,56},{72,6... | collective-permute-start | bytes 1179656 | tf_op jit(solution)/shard_map/ppermute | solution.py:407
  35.5 23.8 %collective-permute-start.4 = (f32[2,144,512]{2,1,0:T(8,128)}, f32[2,144,512]{2,1,0:T(8,128)}, u32[]{:S(2)}, u32[]{:S(2)}) collective-permute-start(f32[2,144,512]{2,1,0:T(8,128)} %collective-permute-done.3.below_ref), channel_id=1, source_target_pairs={{1,0},{2,1},{3,2},{4,3},{5,4},{6,5},{7,6},{9,8},{10,9},{11,10},{12... | collective-permute-start | bytes 1769480 | tf_op jit(solution)/shard_map/ppermute | solution.py:407
  46.7 17.2 %collective-permute-start.6 = (f32[2,128,512]{2,1,0:T(8,128)}, f32[2,128,512]{2,1,0:T(8,128)}, u32[]{:S(2)}, u32[]{:S(2)}) collective-permute-start(f32[2,128,512]{2,1,0:T(8,128)} %collective-permute-done.5.below_ref), channel_id=1, source_target_pairs={{1,0},{2,1},{3,2},{4,3},{5,4},{6,5},{7,6},{9,8},{10,9},{11,10},{12... | collective-permute-start | bytes 1572872 | tf_op jit(solution)/shard_map/ppermute | solution.py:407
  49.9 1.3 copy-start.6
  53.8 1.0 copy-start.24
  54.8 1.1 copy-start.26
  57.3 10.0 %collective-permute-start.8 = (f32[2,96,512]{2,1,0:T(8,128)}, f32[2,96,512]{2,1,0:T(8,128)S(1)}, u32[]{:S(2)}, u32[]{:S(2)}) collective-permute-start(f32[2,96,512]{2,1,0:T(8,128)} %shard_map.109.below_ref), channel_id=1, source_target_pairs={{1,0},{2,1},{3,2},{4,3},{5,4},{6,5},{7,6},{9,8},{10,9},{11,10},{12... | collective-permute-start | bytes 1179656 | tf_op jit(solution)/shard_map/ppermute | solution.py:407
  59.4 1.3 copy-start.9
  60.6 3.3 %copy-start.12 = (f32[2,2,128,512]{3,2,1,0:T(8,128)S(1)}, f32[2,2,128,512]{3,2,1,0:T(8,128)}, u32[]{:S(2)}) copy-start(f32[2,2,128,512]{3,2,1,0:T(8,128)} %copy-done.11) | copy-start | bytes 3145732
  64.0 3.3 %copy-start.15 = (f32[2,2,96,512]{3,2,1,0:T(8,128)S(1)}, f32[2,2,96,512]{3,2,1,0:T(8,128)}, u32[]{:S(2)}) copy-start(f32[2,2,96,512]{3,2,1,0:T(8,128)} %copy-done.14) | copy-start | bytes 2359300
  64.0 3.3 %copy-start.22 = (f32[2,96,512]{2,1,0:T(8,128)S(1)}, f32[2,96,512]{2,1,0:T(8,128)}, u32[]{:S(2)}) copy-start(f32[2,96,512]{2,1,0:T(8,128)} %shard_map.109.below_ref) | copy-start | bytes 1179652
  67.2 3.1 %copy-start.7 = (f32[2,2,144,512]{3,2,1,0:T(8,128)S(1)}, f32[2,2,144,512]{3,2,1,0:T(8,128)}, u32[]{:S(2)}) copy-start(f32[2,2,144,512]{3,2,1,0:T(8,128)} %copy-done.5) | copy-start | bytes 3538948
  67.3 3.1 %copy-start.10 = (f32[2,2,144,512]{3,2,1,0:T(8,128)S(1)}, f32[2,2,144,512]{3,2,1,0:T(8,128)}, u32[]{:S(2)}) copy-start(f32[2,2,144,512]{3,2,1,0:T(8,128)} %copy-done.8) | copy-start | bytes 3538948
  67.3 3.1 %copy-start.25 = (f32[2,2,144,512]{3,2,1,0:T(8,128)S(1)}, f32[2,2,144,512]{3,2,1,0:T(8,128)}, u32[]{:S(2)}) copy-start(f32[2,2,144,512]{3,2,1,0:T(8,128)} %copy-done.24) | copy-start | bytes 3538948
  67.3 3.1 %copy-start.27 = (f32[2,2,144,512]{3,2,1,0:T(8,128)S(1)}, f32[2,2,144,512]{3,2,1,0:T(8,128)}, u32[]{:S(2)}) copy-start(f32[2,2,144,512]{3,2,1,0:T(8,128)} %copy-done.26) | copy-start | bytes 3538948
  67.3 3.1 %copy-start.28 = (bf16[4,256,256]{2,1,0:T(8,128)(2,1)S(1)}, bf16[4,256,256]{2,1,0:T(8,128)(2,1)}, u32[]{:S(2)}) copy-start(bf16[4,256,256]{2,1,0:T(8,128)(2,1)} %constant.41.clone.refs_14_) | copy-start | bytes 1572868
  67.3 3.2 %copy-start.29 = (bf16[4,256,256]{2,1,0:T(8,128)(2,1)S(1)}, bf16[4,256,256]{2,1,0:T(8,128)(2,1)}, u32[]{:S(2)}) copy-start(bf16[4,256,256]{2,1,0:T(8,128)(2,1)} %constant.42.clone.refs_15_) | copy-start | bytes 1572868
  67.3 3.2 %copy-start.32 = (f32[2,8,128]{2,1,0:T(8,128)S(1)}, f32[2,8,128]{2,1,0:T(8,128)}, u32[]{:S(2)}) copy-start(f32[2,8,128]{2,1,0:T(8,128)} %copy-done.31) | copy-start | bytes 24580
  85.0 26.9 %collective-permute-start.11 = (f32[2,512,512]{2,1,0:T(8,128)}, f32[2,512,512]{2,1,0:T(8,128)}, u32[]{:S(2)}, u32[]{:S(2)}) collective-permute-start(f32[2,512,512]{2,1,0:T(8,128)} %get-tuple-element.47), channel_id=1, source_target_pairs={{0,1},{1,2},{2,3},{3,4},{4,5},{5,6},{6,7},{8,9},{9,10},{10,11},{11... | collective-permute-start | bytes 6291464 | tf_op jit(solution)/shard_map/ppermute | solution.py:407
  88.6 4.3 %collective-permute-start.9 = (f32[512,640]{1,0:T(8,128)S(1)}, f32[512,640]{1,0:T(8,128)S(1)}, u32[]{:S(2)}, u32[]{:S(2)}) collective-permute-start(f32[512,640]{1,0:T(8,128)S(1)} %get-tuple-element.45), channel_id=1, source_target_pairs={{0,1},{1,0},{2,3},{3,2},{4,5},{5,4},{6,7},{7,6},{8,9},{9,8},{10,11... | collective-permute-start | bytes 3932168 | tf_op jit(solution)/shard_map/ppermute | solution.py:411
  94.1 29.5 %all-to-all-start = ((f32[16,32,640]{2,1,0:T(8,128)}), f32[16,32,640]{2,1,0:T(8,128)S(1)}, u32[]{:S(2)}, u32[]{:S(2)}) async-start(f32[16,32,640]{2,1,0:T(8,128)} %bitcast.5), calls=%async_computation | async-start | bytes 2621440 | tf_op jit(solution)/shard_map/all_to_all | solution.py:494
  102.7 49.1 %collective-permute-start.10 = (f32[2,512,512]{2,1,0:T(8,128)}, f32[2,512,512]{2,1,0:T(8,128)}, u32[]{:S(2)}, u32[]{:S(2)}) collective-permute-start(f32[2,512,512]{2,1,0:T(8,128)} %shard_map.114), channel_id=1, source_target_pairs={{0,1},{1,2},{2,3},{3,4},{4,5},{5,6},{6,7},{8,9},{9,10},{10,11},{11... | collective-permute-start | bytes 6291464 | tf_op jit(solution)/shard_map/ppermute | solution.py:407
  111.9 1.6 copy-start.19
  117.4 47.6 %collective-permute-start.12 = (f32[2,512,512]{2,1,0:T(8,128)}, f32[2,512,512]{2,1,0:T(8,128)}, u32[]{:S(2)}, u32[]{:S(2)}) collective-permute-start(f32[2,512,512]{2,1,0:T(8,128)} %shard_map.115.refs_0_), channel_id=1, source_target_pairs={{0,8},{8,16},{16,24},{24,32},{32,40},{40,48},{48,56},{56,64},{64,7... | collective-permute-start | bytes 6291464 | tf_op jit(solution)/shard_map/ppermute | solution.py:407
  124.4 13.5 %all-to-all-start.1 = ((f32[4,32,640]{2,1,0:T(8,128)}), f32[4,32,640]{2,1,0:T(8,128)S(1)}, u32[]{:S(2)}, u32[]{:S(2)}) async-start(f32[4,32,640]{2,1,0:T(8,128)} %copy-done.23), calls=%async_computation.1 | async-start | bytes 655360 | tf_op jit(solution)/shard_map/all_to_all | solution.py:500
  138.0 1.0 copy-start.13
  139.1 44.3 %all-to-all-start.2 = ((f32[16,32,512]{2,1,0:T(8,128)}), f32[16,32,512]{2,1,0:T(8,128)S(1)}, u32[]{:S(2)}, u32[]{:S(2)}) async-start(f32[16,32,512]{2,1,0:T(8,128)} %copy-done.13), calls=%async_computation.2 | async-start | bytes 2097152 | tf_op jit(solution)/shard_map/all_to_all | solution.py:504
  149.0 1.6 copy-start.18
  183.4 1.0 copy-start.3
  184.4 4.1 %collective-permute-start.13 = (f32[512,512]{1,0:T(8,128)}, f32[512,512]{1,0:T(8,128)S(1)}, u32[]{:S(2)}, u32[]{:S(2)}) collective-permute-start(f32[512,512]{1,0:T(8,128)} %shard_map.119.mine_ref), channel_id=1, source_target_pairs={{0,1},{1,0},{2,3},{3,2},{4,5},{5,4},{6,7},{7,6},{8,9},{9,8},{10,11... | collective-permute-start | bytes 3145736 | tf_op jit(solution)/shard_map/ppermute | solution.py:411
  188.5 1.2 copy-start.4
  (5 other events, 3.3 us)
